TPU v7x, 512 devices: a whole 4x8x8 slice. The times are simulated.
512 devices in a mesh: kstr: 16 (over y, z_lo), pw: 32 (over x, z_hi, core).
Axes of the slice: x: 4, y: 8, z: 8 (z_hi: 4, z_lo: 2; z = z_hi * 2 + z_lo), core: 2. Of those that a mesh axis runs over, the one named last changes fastest.
Arguments:
- states_re: bfloat16 [16, 256, 16384], P('kstr', None, 'pw'), may hold values from -8 to 8
- states_im: bfloat16 [16, 256, 16384], P('kstr', None, 'pw'), may hold values from -8 to 8
- gmap: int32 [16384], P('pw'), may hold values from 0 to 16383, as said below
Outputs:
- new_re: bfloat16 [16, 256, 16384], P('kstr', None, 'pw')
- new_im: bfloat16 [16, 256, 16384], P('kstr', None, 'pw')
Inputs may be any that keep to these rules, and one draw needn't show every extreme that they name: gmap[G] = (G + o) mod 16384 for one offset o with 1 <= o < 16384.
All inputs are finite; a program needn't handle non-finite values.
Results may differ from a plain program's by a relative error of at most 0.008.
Values may be sent and summed in bfloat16 or wider, within the bound.
No kernel may reach another device: no remote copies, remote signals or barrier semaphores. Data moves between devices by JAX's collectives and lax.ppermute only.
A program may use at most 64 MiB of HBM per device.

v0:
```python
import jax
import jax.numpy as jnp
from jax import lax
from jax.sharding import PartitionSpec as P

NEWTON = 4
STEPS = 2


HIGH = lax.Precision.HIGHEST
EPS_SCALE = 1e-06
EPS_NORM = 1e-06
TAU_STEP = 0.25


def shifted(value, axis, by):
    count = lax.axis_size(axis)
    return lax.ppermute(value, axis, [(i, (i + by) % count) for i in range(count)])


def complex_mul(left, right):

    def matmul(first, second):
        return jnp.einsum("kij,kjl->kil", first, second, precision=HIGH)

    real = matmul(left[:, 0], right[:, 0]) - matmul(left[:, 1], right[:, 1])
    imag = matmul(left[:, 0], right[:, 1]) + matmul(left[:, 1], right[:, 0])
    return jnp.stack([real, imag], 1)


def start_inverse(whole):
    magnitude = jnp.sqrt(whole[:, 0] * whole[:, 0] + whole[:, 1] * whole[:, 1])
    colmax = jnp.max(jnp.sum(magnitude, axis=1), axis=1)
    rowmax = jnp.max(jnp.sum(magnitude, axis=2), axis=1)
    factor = (1.0 / (colmax * rowmax + EPS_SCALE))[:, None, None]
    return jnp.stack(
        [jnp.swapaxes(whole[:, 0], 1, 2) * factor, -jnp.swapaxes(whole[:, 1], 1, 2) * factor], 1
    )


def newton_full(whole):
    iterate = start_inverse(whole)
    for turn in range(NEWTON):
        iterate = 2.0 * iterate - complex_mul(iterate, complex_mul(whole, iterate))
    return iterate


def bf_product(form, left, right):
    return jnp.einsum(form, left, right, preferred_element_type=jnp.float32)


def dual_terms(rounded, states):
    real = bf_product("kmn,kmg->kng", rounded[:, 0], states[:, 0]) + bf_product(
        "kmn,kmg->kng", rounded[:, 1], states[:, 1]
    )
    imag = bf_product("kmn,kmg->kng", rounded[:, 0], states[:, 1]) - bf_product(
        "kmn,kmg->kng", rounded[:, 1], states[:, 0]
    )
    return jnp.stack([real, imag], 1).astype(jnp.bfloat16)


def rotate_columns(block, amount, width):
    blocks_off = amount // width
    rest = amount % width
    plane_size = lax.axis_size("pw")
    for bit in range((plane_size - 1).bit_length()):
        moved = shifted(block, "pw", -(1 << bit))
        block = jnp.where(jnp.bitwise_and(jnp.right_shift(blocks_off, bit), 1) == 1, moved, block)
    after = shifted(block, "pw", -1)
    joined = jnp.concatenate([block, after], block.ndim - 1)
    return lax.dynamic_slice_in_dim(joined, rest, width, block.ndim - 1)


def body(states_re, states_im, gmap):
    kpoints, bands, width = states_re.shape
    string_size = lax.axis_size("kstr")
    plane_size = lax.axis_size("pw")
    string_index = lax.axis_index("kstr")
    total_width = width * plane_size
    offset = jnp.mod(gmap[0] - lax.axis_index("pw") * width, total_width)
    back_offset = jnp.mod(total_width - offset, total_width)
    at_first = string_index == 0
    at_last = string_index == string_size - 1
    count_all = 2 * kpoints * string_size * bands * width * plane_size
    states = jnp.stack([states_re, states_im], 1)
    for step in range(STEPS):
        ahead = shifted(states, "kstr", -1)
        turned = rotate_columns(ahead, offset, width)
        ahead = jnp.where(at_last, turned, ahead)
        following = jnp.concatenate([states[1:], ahead], 0)
        s_re = bf_product("kmg,kng->kmn", states[:, 0], following[:, 0]) + bf_product(
            "kmg,kng->kmn", states[:, 1], following[:, 1]
        )
        s_im = bf_product("kmg,kng->kmn", states[:, 0], following[:, 1]) - bf_product(
            "kmg,kng->kmn", states[:, 1], following[:, 0]
        )
        partial_value = jnp.stack([s_re, s_im], 1)
        whole = lax.psum(partial_value, "pw") / (width * plane_size)
        inverse = newton_full(whole)
        rounded = inverse.astype(jnp.bfloat16)
        a_re = bf_product("kmn,kmg->kng", rounded[:, 0], following[:, 0]) - bf_product(
            "kmn,kmg->kng", rounded[:, 1], following[:, 1]
        )
        a_im = bf_product("kmn,kmg->kng", rounded[:, 0], following[:, 1]) + bf_product(
            "kmn,kmg->kng", rounded[:, 1], following[:, 0]
        )
        local_terms = dual_terms(rounded, states)
        arrived = shifted(local_terms, "kstr", 1)
        earlier = local_terms[:-1]
        placed = rotate_columns(arrived, back_offset, width)
        arrived = jnp.where(at_first, placed, arrived)
        incoming = jnp.concatenate([arrived, earlier], 0).astype(jnp.float32)
        g_re = a_im - incoming[:, 1]
        g_im = incoming[:, 0] - a_re
        total = lax.psum(jnp.sum(g_re * g_re + g_im * g_im), ("kstr", "pw"))
        rms = jnp.sqrt(total / count_all + EPS_NORM)
        new_re = (states[:, 0].astype(jnp.float32) + TAU_STEP * g_re / rms).astype(jnp.bfloat16)
        new_im = (states[:, 1].astype(jnp.float32) + TAU_STEP * g_im / rms).astype(jnp.bfloat16)
        states = jnp.stack([new_re, new_im], 1)
    return (states[:, 0], states[:, 1])


def solution(mesh):
    placed = (P("kstr", None, "pw"), P("kstr", None, "pw"), P("pw"))
    return jax.shard_map(
        body,
        mesh=mesh,
        in_specs=placed,
        out_specs=(P("kstr", None, "pw"), P("kstr", None, "pw")),
        check_vma=False,
    )
```

profile of v0, /device:TPU:1, one launch (start us, length us, event | category | flops | bytes accessed | tf_op | source)
XLA Modules:
  0.0 1402.9 jit_solution(1617140451742188734)
XLA Ops:
  8.3 7.7 collective-permute-start
  16.0 10.4 collective-permute-done
  26.5 3.6 collective-permute-start.1
  31.9 14.4 %collective-permute-done.1 = bf16[1,2,256,512]{3,2,1,0:T(8,128)(2,1)S(1)} collective-permute-done((bf16[1,2,256,512]{3,2,1,0:T(8,128)(2,1)S(1)}, bf16[1,2,256,512]{3,2,1,0:T(8,128)(2,1)S(1)}, u32[]{:S(2)}, u32[]{:S(2)}) %collective-permute-start.1) | collective-permute-done | bytes 524320 | tf_op jit(solution)/shard_map/ppermute | solution.py:18
  46.4 12.6 collective-permute-start.2
  59.0 13.9 collective-permute-done.2
  73.0 8.3 collective-permute-start.3
  81.3 22.1 %collective-permute-done.3 = bf16[1,2,256,512]{3,2,1,0:T(8,128)(2,1)S(1)} collective-permute-done((bf16[1,2,256,512]{3,2,1,0:T(8,128)(2,1)S(1)}, bf16[1,2,256,512]{3,2,1,0:T(8,128)(2,1)S(1)}, u32[]{:S(2)}, u32[]{:S(2)}) %collective-permute-start.3) | collective-permute-done | bytes 524320 | tf_op jit(solution)/shard_map/ppermute | solution.py:18
  105.3 12.9 collective-permute-done.4
  120.2 13.4 collective-permute-done.5
  133.7 4.3 collective-permute-start.6
  138.0 12.9 collective-permute-done.6
  154.4 291.2 %all-reduce.3.cloned.1.call-done = f32[1,2,256,256]{2,3,1,0:T(8,128)} async-done(((f32[1,2,256,256]{2,3,1,0:T(8,128)}), f32[1,2,256,256]{2,3,1,0:T(8,128)}) %all-reduce.3.cloned.1.call-update) | async-done | bytes 524304 | tf_op jit(solution)/shard_map/psum | solution.py:98
  469.9 14.7 %collective-permute-done.7 = bf16[1,2,256,512]{3,2,1,0:T(8,128)(2,1)S(1)} collective-permute-done((bf16[1,2,256,512]{3,2,1,0:T(8,128)(2,1)S(1)}, bf16[1,2,256,512]{3,2,1,0:T(8,128)(2,1)S(1)}, u32[]{:S(2)}, u32[]{:S(2)}) %collective-permute-start.7) | collective-permute-done | bytes 524320 | tf_op jit(solution)/shard_map/ppermute | solution.py:18
  484.6 3.1 collective-permute-start.8
  487.8 13.8 collective-permute-done.8
  501.7 5.1 collective-permute-start.9
  506.7 18.6 %collective-permute-done.9 = bf16[1,2,256,512]{3,2,1,0:T(8,128)(2,1)S(1)} collective-permute-done((bf16[1,2,256,512]{3,2,1,0:T(8,128)(2,1)S(1)}, bf16[1,2,256,512]{3,2,1,0:T(8,128)(2,1)S(1)}, u32[]{:S(2)}, u32[]{:S(2)}) %collective-permute-start.9) | collective-permute-done | bytes 524320 | tf_op jit(solution)/shard_map/ppermute | solution.py:18
  525.4 24.7 %collective-permute-start.10 = (bf16[1,2,256,512]{3,2,1,0:T(8,128)(2,1)S(1)}, bf16[1,2,256,512]{3,2,1,0:T(8,128)(2,1)S(1)}, u32[]{:S(2)}, u32[]{:S(2)}) collective-permute-start(bf16[1,2,256,512]{3,2,1,0:T(8,128)(2,1)S(1)} %broadcast_select_fusion.3), channel_id=1, source_target_pairs={{0,28},{1,29},{2,30},{3,31},{4,0},{5,1},{6,2},{7,3},{8,4},{9,5},{1... | collective-permute-start | bytes 1572872 | tf_op jit(solution)/shard_map/ppermute | solution.py:18
  550.2 9.8 collective-permute-done.10
  561.9 10.8 collective-permute-done.11
  574.8 9.5 collective-permute-done.12
  587.0 16.0 %collective-permute-done.13 = bf16[1,2,256,512]{3,2,1,0:T(8,128)(2,1)S(1)} collective-permute-done((bf16[1,2,256,512]{3,2,1,0:T(8,128)(2,1)S(1)}, bf16[1,2,256,512]{3,2,1,0:T(8,128)(2,1)S(1)}, u32[]{:S(2)}, u32[]{:S(2)}) %collective-permute-start.13) | collective-permute-done | bytes 524320 | tf_op jit(solution)/shard_map/ppermute | solution.py:18
  604.4 97.4 %psum.29 = f32[]{:T(128)} all-reduce(f32[]{:T(128)} %get-tuple-element.10), channel_id=1, replica_groups=mesh['kstr'=16,'pw'=32] {'kstr','pw'}, use_global_device_ids=true, to_apply=%region_6.7 | all-reduce | flops 1 | bytes 8 | tf_op jit(solution)/shard_map/psum | solution.py:115
  702.8 3.1 collective-permute-start.14
  705.9 11.6 collective-permute-done.14
  717.5 3.4 collective-permute-start.15
  720.9 10.2 collective-permute-done.15
  731.2 11.6 collective-permute-start.16
  742.9 17.5 %collective-permute-done.16 = bf16[1,2,256,512]{3,2,1,0:T(8,128)(2,1)S(1)} collective-permute-done((bf16[1,2,256,512]{3,2,1,0:T(8,128)(2,1)S(1)}, bf16[1,2,256,512]{3,2,1,0:T(8,128)(2,1)S(1)}, u32[]{:S(2)}, u32[]{:S(2)}) %collective-permute-start.16) | collective-permute-done | bytes 524320 | tf_op jit(solution)/shard_map/ppermute | solution.py:18
  762.3 18.9 %collective-permute-done.17 = bf16[1,2,256,512]{3,2,1,0:T(8,128)(2,1)S(1)} collective-permute-done((bf16[1,2,256,512]{3,2,1,0:T(8,128)(2,1)S(1)}, bf16[1,2,256,512]{3,2,1,0:T(8,128)(2,1)S(1)}, u32[]{:S(2)}, u32[]{:S(2)}) %collective-permute-start.17) | collective-permute-done | bytes 524320 | tf_op jit(solution)/shard_map/ppermute | solution.py:18
  783.2 8.0 collective-permute-done.18
  791.3 3.1 collective-permute-start.19
  794.4 11.0 collective-permute-done.19
  805.5 5.7 collective-permute-start.20
  811.2 15.5 %collective-permute-done.20 = bf16[1,2,256,512]{3,2,1,0:T(8,128)(2,1)S(1)} collective-permute-done((bf16[1,2,256,512]{3,2,1,0:T(8,128)(2,1)S(1)}, bf16[1,2,256,512]{3,2,1,0:T(8,128)(2,1)S(1)}, u32[]{:S(2)}, u32[]{:S(2)}) %collective-permute-start.20) | collective-permute-done | bytes 524320 | tf_op jit(solution)/shard_map/ppermute | solution.py:18
  829.1 308.6 %all-reduce.5.cloned.1.call-done = f32[1,2,256,256]{2,3,1,0:T(8,128)} async-done(((f32[1,2,256,256]{2,3,1,0:T(8,128)}), f32[1,2,256,256]{2,3,1,0:T(8,128)}) %all-reduce.5.cloned.1.call-update) | async-done | bytes 524304 | tf_op jit(solution)/shard_map/psum | solution.py:98
  1161.7 14.7 %collective-permute-done.21 = bf16[1,2,256,512]{3,2,1,0:T(8,128)(2,1)S(1)} collective-permute-done((bf16[1,2,256,512]{3,2,1,0:T(8,128)(2,1)S(1)}, bf16[1,2,256,512]{3,2,1,0:T(8,128)(2,1)S(1)}, u32[]{:S(2)}, u32[]{:S(2)}) %collective-permute-start.21) | collective-permute-done | bytes 524320 | tf_op jit(solution)/shard_map/ppermute | solution.py:18
  1176.4 3.1 collective-permute-start.22
  1179.5 13.9 collective-permute-done.22
  1193.4 5.1 collective-permute-start.23
  1198.5 18.6 %collective-permute-done.23 = bf16[1,2,256,512]{3,2,1,0:T(8,128)(2,1)S(1)} collective-permute-done((bf16[1,2,256,512]{3,2,1,0:T(8,128)(2,1)S(1)}, bf16[1,2,256,512]{3,2,1,0:T(8,128)(2,1)S(1)}, u32[]{:S(2)}, u32[]{:S(2)}) %collective-permute-start.23) | collective-permute-done | bytes 524320 | tf_op jit(solution)/shard_map/ppermute | solution.py:18
  1217.2 24.7 %collective-permute-start.24 = (bf16[1,2,256,512]{3,2,1,0:T(8,128)(2,1)S(1)}, bf16[1,2,256,512]{3,2,1,0:T(8,128)(2,1)S(1)}, u32[]{:S(2)}, u32[]{:S(2)}) collective-permute-start(bf16[1,2,256,512]{3,2,1,0:T(8,128)(2,1)S(1)} %broadcast_select_fusion.2), channel_id=1, source_target_pairs={{0,28},{1,29},{2,30},{3,31},{4,0},{5,1},{6,2},{7,3},{8,4},{9,5},{1... | collective-permute-start | bytes 1572872 | tf_op jit(solution)/shard_map/ppermute | solution.py:18
  1241.9 9.8 collective-permute-done.24
  1253.7 10.8 collective-permute-done.25
  1266.5 9.5 collective-permute-done.26
  1278.8 15.9 %collective-permute-done.27 = bf16[1,2,256,512]{3,2,1,0:T(8,128)(2,1)S(1)} collective-permute-done((bf16[1,2,256,512]{3,2,1,0:T(8,128)(2,1)S(1)}, bf16[1,2,256,512]{3,2,1,0:T(8,128)(2,1)S(1)}, u32[]{:S(2)}, u32[]{:S(2)}) %collective-permute-start.27) | collective-permute-done | bytes 524320 | tf_op jit(solution)/shard_map/ppermute | solution.py:18
  1296.2 97.3 %psum.31 = f32[]{:T(128)} all-reduce(f32[]{:T(128)} %get-tuple-element.12), channel_id=1, replica_groups=mesh['kstr'=16,'pw'=32] {'kstr','pw'}, use_global_device_ids=true, to_apply=%region_13.14 | all-reduce | flops 1 | bytes 8 | tf_op jit(solution)/shard_map/psum | solution.py:115
  (160 shorter events, 79.8 us)
Async XLA Ops:
  7.2 438.5 %all-reduce.3.cloned.1.call-start = ((), (), s32[]{:S(2)}) async-start(), calls=%async_computation | async-start | bytes 1048576 | tf_op jit(solution)/shard_map/psum | solution.py:98
  8.3 18.2 %collective-permute-start = (bf16[1,2,256,512]{3,2,1,0:T(8,128)(2,1)S(1)}, bf16[1,2,256,512]{3,2,1,0:T(8,128)(2,1)S(1)}, u32[]{:S(2)}, u32[]{:S(2)}) collective-permute-start(bf16[1,2,256,512]{3,2,1,0:T(8,128)(2,1)S(1)} %pad_maximum_fusion), channel_id=1, source_target_pairs={{0,480},{32,0},{64,32},{96,64},{128,96},{160,128},{192,160},{224,1... | collective-permute-start | bytes 1572872 | tf_op jit(solution)/shard_map/ppermute | solution.py:18
  26.5 19.8 %collective-permute-start.1 = (bf16[1,2,256,512]{3,2,1,0:T(8,128)(2,1)S(1)}, bf16[1,2,256,512]{3,2,1,0:T(8,128)(2,1)S(1)}, u32[]{:S(2)}, u32[]{:S(2)}) collective-permute-start(bf16[1,2,256,512]{3,2,1,0:T(8,128)(2,1)S(1)} %collective-permute-done), channel_id=1, source_target_pairs={{0,31},{1,0},{2,1},{3,2},{4,3},{5,4},{6,5},{7,6},{8,7},{9,8},{10,9... | collective-permute-start | bytes 1572872 | tf_op jit(solution)/shard_map/ppermute | solution.py:18
  46.4 26.5 %collective-permute-start.2 = (bf16[1,2,256,512]{3,2,1,0:T(8,128)(2,1)S(1)}, bf16[1,2,256,512]{3,2,1,0:T(8,128)(2,1)S(1)}, u32[]{:S(2)}, u32[]{:S(2)}) collective-permute-start(bf16[1,2,256,512]{3,2,1,0:T(8,128)(2,1)S(1)} %broadcast_select_fusion.11), channel_id=1, source_target_pairs={{0,30},{1,31},{2,0},{3,1},{4,2},{5,3},{6,4},{7,5},{8,6},{9,7},{10,... | collective-permute-start | bytes 1572872 | tf_op jit(solution)/shard_map/ppermute | solution.py:18
  73.0 30.4 %collective-permute-start.3 = (bf16[1,2,256,512]{3,2,1,0:T(8,128)(2,1)S(1)}, bf16[1,2,256,512]{3,2,1,0:T(8,128)(2,1)S(1)}, u32[]{:S(2)}, u32[]{:S(2)}) collective-permute-start(bf16[1,2,256,512]{3,2,1,0:T(8,128)(2,1)S(1)} %broadcast_select_fusion.13), channel_id=1, source_target_pairs={{0,28},{1,29},{2,30},{3,31},{4,0},{5,1},{6,2},{7,3},{8,4},{9,5},{1... | collective-permute-start | bytes 1572872 | tf_op jit(solution)/shard_map/ppermute | solution.py:18
  103.4 14.8 %collective-permute-start.4 = (bf16[1,2,256,512]{3,2,1,0:T(8,128)(2,1)S(1)}, bf16[1,2,256,512]{3,2,1,0:T(8,128)(2,1)S(1)}, u32[]{:S(2)}, u32[]{:S(2)}) collective-permute-start(bf16[1,2,256,512]{3,2,1,0:T(8,128)(2,1)S(1)} %broadcast_select_fusion.15), channel_id=1, source_target_pairs={{0,24},{1,25},{2,26},{3,27},{4,28},{5,29},{6,30},{7,31},{8,0},{9,1... | collective-permute-start | bytes 1572872 | tf_op jit(solution)/shard_map/ppermute | solution.py:18
  118.3 15.4 %collective-permute-start.5 = (bf16[1,2,256,512]{3,2,1,0:T(8,128)(2,1)S(1)}, bf16[1,2,256,512]{3,2,1,0:T(8,128)(2,1)S(1)}, u32[]{:S(2)}, u32[]{:S(2)}) collective-permute-start(bf16[1,2,256,512]{3,2,1,0:T(8,128)(2,1)S(1)} %broadcast_select_fusion.17), channel_id=1, source_target_pairs={{0,16},{1,17},{2,18},{3,19},{4,20},{5,21},{6,22},{7,23},{8,24},{9,... | collective-permute-start | bytes 1572872 | tf_op jit(solution)/shard_map/ppermute | solution.py:18
  133.7 17.2 %collective-permute-start.6 = (bf16[1,2,256,512]{3,2,1,0:T(8,128)(2,1)S(1)}, bf16[1,2,256,512]{3,2,1,0:T(8,128)(2,1)S(1)}, u32[]{:S(2)}, u32[]{:S(2)}) collective-permute-start(bf16[1,2,256,512]{3,2,1,0:T(8,128)(2,1)S(1)} %broadcast_select_fusion.19), channel_id=1, source_target_pairs={{0,31},{1,0},{2,1},{3,2},{4,3},{5,4},{6,5},{7,6},{8,7},{9,8},{10,9... | collective-permute-start | bytes 1572872 | tf_op jit(solution)/shard_map/ppermute | solution.py:18
  138.0 13.4 copy-start
  151.7 1.0 copy-start.1
  154.0 983.6 %all-reduce.5.cloned.1.call-start = ((), (), s32[]{:S(2)}) async-start(), calls=%async_computation.1 | async-start | bytes 1048576 | tf_op jit(solution)/shard_map/psum | solution.py:98
  467.5 17.2 %collective-permute-start.7 = (bf16[1,2,256,512]{3,2,1,0:T(8,128)(2,1)S(1)}, bf16[1,2,256,512]{3,2,1,0:T(8,128)(2,1)S(1)}, u32[]{:S(2)}, u32[]{:S(2)}) collective-permute-start(bf16[1,2,256,512]{3,2,1,0:T(8,128)(2,1)S(1)} %pad_maximum_fusion.2), channel_id=1, source_target_pairs={{0,32},{32,64},{64,96},{96,128},{128,160},{160,192},{192,224},{224... | collective-permute-start | bytes 1572872 | tf_op jit(solution)/shard_map/ppermute | solution.py:18
  484.6 17.0 %collective-permute-start.8 = (bf16[1,2,256,512]{3,2,1,0:T(8,128)(2,1)S(1)}, bf16[1,2,256,512]{3,2,1,0:T(8,128)(2,1)S(1)}, u32[]{:S(2)}, u32[]{:S(2)}) collective-permute-start(bf16[1,2,256,512]{3,2,1,0:T(8,128)(2,1)S(1)} %collective-permute-done.7), channel_id=1, source_target_pairs={{0,31},{1,0},{2,1},{3,2},{4,3},{5,4},{6,5},{7,6},{8,7},{9,8},{10,9... | collective-permute-start | bytes 1572872 | tf_op jit(solution)/shard_map/ppermute | solution.py:18
  501.7 23.7 %collective-permute-start.9 = (bf16[1,2,256,512]{3,2,1,0:T(8,128)(2,1)S(1)}, bf16[1,2,256,512]{3,2,1,0:T(8,128)(2,1)S(1)}, u32[]{:S(2)}, u32[]{:S(2)}) collective-permute-start(bf16[1,2,256,512]{3,2,1,0:T(8,128)(2,1)S(1)} %broadcast_select_fusion.1), channel_id=1, source_target_pairs={{0,30},{1,31},{2,0},{3,1},{4,2},{5,3},{6,4},{7,5},{8,6},{9,7},{10,... | collective-permute-start | bytes 1572872 | tf_op jit(solution)/shard_map/ppermute | solution.py:18
  525.4 34.6 %collective-permute-start.10 = (bf16[1,2,256,512]{3,2,1,0:T(8,128)(2,1)S(1)}, bf16[1,2,256,512]{3,2,1,0:T(8,128)(2,1)S(1)}, u32[]{:S(2)}, u32[]{:S(2)}) collective-permute-start(bf16[1,2,256,512]{3,2,1,0:T(8,128)(2,1)S(1)} %broadcast_select_fusion.3), channel_id=1, source_target_pairs={{0,28},{1,29},{2,30},{3,31},{4,0},{5,1},{6,2},{7,3},{8,4},{9,5},{1... | collective-permute-start | bytes 1572872 | tf_op jit(solution)/shard_map/ppermute | solution.py:18
  560.0 12.7 collective-permute-start.11
  572.8 11.4 collective-permute-start.12
  584.3 18.7 %collective-permute-start.13 = (bf16[1,2,256,512]{3,2,1,0:T(8,128)(2,1)S(1)}, bf16[1,2,256,512]{3,2,1,0:T(8,128)(2,1)S(1)}, u32[]{:S(2)}, u32[]{:S(2)}) collective-permute-start(bf16[1,2,256,512]{3,2,1,0:T(8,128)(2,1)S(1)} %broadcast_select_fusion.9), channel_id=1, source_target_pairs={{0,31},{1,0},{2,1},{3,2},{4,3},{5,4},{6,5},{7,6},{8,7},{9,8},{10,9... | collective-permute-start | bytes 1572872 | tf_op jit(solution)/shard_map/ppermute | solution.py:18
  702.8 14.7 %collective-permute-start.14 = (bf16[1,2,256,512]{3,2,1,0:T(8,128)(2,1)S(1)}, bf16[1,2,256,512]{3,2,1,0:T(8,128)(2,1)S(1)}, u32[]{:S(2)}, u32[]{:S(2)}) collective-permute-start(bf16[1,2,256,512]{3,2,1,0:T(8,128)(2,1)S(1)} %pad_maximum_fusion.3), channel_id=1, source_target_pairs={{0,480},{32,0},{64,32},{96,64},{128,96},{160,128},{192,160},{224,1... | collective-permute-start | bytes 1572872 | tf_op jit(solution)/shard_map/ppermute | solution.py:18
  717.5 13.7 collective-permute-start.15
  731.2 29.1 %collective-permute-start.16 = (bf16[1,2,256,512]{3,2,1,0:T(8,128)(2,1)S(1)}, bf16[1,2,256,512]{3,2,1,0:T(8,128)(2,1)S(1)}, u32[]{:S(2)}, u32[]{:S(2)}) collective-permute-start(bf16[1,2,256,512]{3,2,1,0:T(8,128)(2,1)S(1)} %broadcast_select_fusion.10), channel_id=1, source_target_pairs={{0,30},{1,31},{2,0},{3,1},{4,2},{5,3},{6,4},{7,5},{8,6},{9,7},{10,... | collective-permute-start | bytes 1572872 | tf_op jit(solution)/shard_map/ppermute | solution.py:18
  760.4 20.8 %collective-permute-start.17 = (bf16[1,2,256,512]{3,2,1,0:T(8,128)(2,1)S(1)}, bf16[1,2,256,512]{3,2,1,0:T(8,128)(2,1)S(1)}, u32[]{:S(2)}, u32[]{:S(2)}) collective-permute-start(bf16[1,2,256,512]{3,2,1,0:T(8,128)(2,1)S(1)} %broadcast_select_fusion.12), channel_id=1, source_target_pairs={{0,28},{1,29},{2,30},{3,31},{4,0},{5,1},{6,2},{7,3},{8,4},{9,5},{1... | collective-permute-start | bytes 1572872 | tf_op jit(solution)/shard_map/ppermute | solution.py:18
  781.3 9.9 collective-permute-start.18
  791.3 14.1 %collective-permute-start.19 = (bf16[1,2,256,512]{3,2,1,0:T(8,128)(2,1)S(1)}, bf16[1,2,256,512]{3,2,1,0:T(8,128)(2,1)S(1)}, u32[]{:S(2)}, u32[]{:S(2)}) collective-permute-start(bf16[1,2,256,512]{3,2,1,0:T(8,128)(2,1)S(1)} %broadcast_select_fusion.16), channel_id=1, source_target_pairs={{0,16},{1,17},{2,18},{3,19},{4,20},{5,21},{6,22},{7,23},{8,24},{9,... | collective-permute-start | bytes 1572872 | tf_op jit(solution)/shard_map/ppermute | solution.py:18
  805.5 21.2 %collective-permute-start.20 = (bf16[1,2,256,512]{3,2,1,0:T(8,128)(2,1)S(1)}, bf16[1,2,256,512]{3,2,1,0:T(8,128)(2,1)S(1)}, u32[]{:S(2)}, u32[]{:S(2)}) collective-permute-start(bf16[1,2,256,512]{3,2,1,0:T(8,128)(2,1)S(1)} %broadcast_select_fusion.18), channel_id=1, source_target_pairs={{0,31},{1,0},{2,1},{3,2},{4,3},{5,4},{6,5},{7,6},{8,7},{9,8},{10,9... | collective-permute-start | bytes 1572872 | tf_op jit(solution)/shard_map/ppermute | solution.py:18
  1159.3 17.2 %collective-permute-start.21 = (bf16[1,2,256,512]{3,2,1,0:T(8,128)(2,1)S(1)}, bf16[1,2,256,512]{3,2,1,0:T(8,128)(2,1)S(1)}, u32[]{:S(2)}, u32[]{:S(2)}) collective-permute-start(bf16[1,2,256,512]{3,2,1,0:T(8,128)(2,1)S(1)} %pad_maximum_fusion.5), channel_id=1, source_target_pairs={{0,32},{32,64},{64,96},{96,128},{128,160},{160,192},{192,224},{224... | collective-permute-start | bytes 1572872 | tf_op jit(solution)/shard_map/ppermute | solution.py:18
  1176.4 16.9 %collective-permute-start.22 = (bf16[1,2,256,512]{3,2,1,0:T(8,128)(2,1)S(1)}, bf16[1,2,256,512]{3,2,1,0:T(8,128)(2,1)S(1)}, u32[]{:S(2)}, u32[]{:S(2)}) collective-permute-start(bf16[1,2,256,512]{3,2,1,0:T(8,128)(2,1)S(1)} %collective-permute-done.21), channel_id=1, source_target_pairs={{0,31},{1,0},{2,1},{3,2},{4,3},{5,4},{6,5},{7,6},{8,7},{9,8},{10,9... | collective-permute-start | bytes 1572872 | tf_op jit(solution)/shard_map/ppermute | solution.py:18
  1193.4 23.7 %collective-permute-start.23 = (bf16[1,2,256,512]{3,2,1,0:T(8,128)(2,1)S(1)}, bf16[1,2,256,512]{3,2,1,0:T(8,128)(2,1)S(1)}, u32[]{:S(2)}, u32[]{:S(2)}) collective-permute-start(bf16[1,2,256,512]{3,2,1,0:T(8,128)(2,1)S(1)} %broadcast_select_fusion), channel_id=1, source_target_pairs={{0,30},{1,31},{2,0},{3,1},{4,2},{5,3},{6,4},{7,5},{8,6},{9,7},{10,... | collective-permute-start | bytes 1572872 | tf_op jit(solution)/shard_map/ppermute | solution.py:18
  1217.2 34.6 %collective-permute-start.24 = (bf16[1,2,256,512]{3,2,1,0:T(8,128)(2,1)S(1)}, bf16[1,2,256,512]{3,2,1,0:T(8,128)(2,1)S(1)}, u32[]{:S(2)}, u32[]{:S(2)}) collective-permute-start(bf16[1,2,256,512]{3,2,1,0:T(8,128)(2,1)S(1)} %broadcast_select_fusion.2), channel_id=1, source_target_pairs={{0,28},{1,29},{2,30},{3,31},{4,0},{5,1},{6,2},{7,3},{8,4},{9,5},{1... | collective-permute-start | bytes 1572872 | tf_op jit(solution)/shard_map/ppermute | solution.py:18
  1251.8 12.7 collective-permute-start.25
  1264.6 11.4 collective-permute-start.26
  1276.1 18.6 %collective-permute-start.27 = (bf16[1,2,256,512]{3,2,1,0:T(8,128)(2,1)S(1)}, bf16[1,2,256,512]{3,2,1,0:T(8,128)(2,1)S(1)}, u32[]{:S(2)}, u32[]{:S(2)}) collective-permute-start(bf16[1,2,256,512]{3,2,1,0:T(8,128)(2,1)S(1)} %broadcast_select_fusion.8), channel_id=1, source_target_pairs={{0,31},{1,0},{2,1},{3,2},{4,3},{5,4},{6,5},{7,6},{8,7},{9,8},{10,9... | collective-permute-start | bytes 1572872 | tf_op jit(solution)/shard_map/ppermute | solution.py:18
Sparse Core Ops, SparseCore 0:
  154.2 291.4 all-reduce.2
  829.2 308.4 all-reduce.4
where the time goes:
time: 1410 us; the launch traced here: 1400 us
  waiting for transfers between devices  979 us (69%)
  blocking collectives  195 us (14%)
  starting transfers between devices  154 us (11%)
  matrix products  38.9 us (3%)
  between operations  20.3 us (1%)
  other arithmetic  14.5 us (1%)
    psum x2, waiting for transfers between devices, body(): whole = lax.psum(partial_value, 'pw') / (width * plane_size)  600 us
    ppermute x28, waiting for transfers between devices, shifted(): lax.ppermute(value, axis, [(i, (i + by) % count) for i in range(count)])  379 us
    psum x2, blocking collectives, body(): total = lax.psum(jnp.sum(g_re * g_re + g_im * g_im), ('kstr', 'pw'))  195 us
    ppermute x28, starting transfers between devices, shifted(): lax.ppermute(value, axis, [(i, (i + by) % count) for i in range(count)])  153 us
    dot_general x64, matrix products, matmul(): return jnp.einsum('kij,kjl->kil', first, second, precision=HIGH)  31.5 us
  transfers between devices with their start and end apart: 30, of which 30 were waited for; matrix products, arithmetic and copies ran while one was open for 0% of the time, Pallas kernels for 0%

commit v1 on v0

v1 whole, which is shorter than its diff:
```python
import jax
import jax.numpy as jnp
from jax import lax
from jax.experimental import pallas as pl
from jax.experimental.pallas import tpu as pltpu
from jax.sharding import PartitionSpec as P

NEWTON = 4
NK = 16
NPW = 16384
NB = 256
PARTS = 32
EPS_SCALE = 1e-06
EPS_NORM = 1e-06
TAU_STEP = 0.25
F32 = jnp.float32
BF16 = jnp.bfloat16


def call(kernel, outs, *args, smem=0, flops=0):
    specs = [pl.BlockSpec(memory_space=pltpu.SMEM)] * smem
    specs += [pl.BlockSpec(memory_space=pltpu.VMEM)] * (len(args) - smem)
    single = not isinstance(outs, (tuple, list))
    outs = (outs,) if single else tuple(outs)
    moved = sum(a.size * a.dtype.itemsize for a in args) + sum(
        o.size * o.dtype.itemsize for o in outs
    )
    result = pl.pallas_call(
        kernel,
        out_shape=outs,
        in_specs=specs,
        out_specs=tuple(pl.BlockSpec(memory_space=pltpu.VMEM) for _ in outs),
        compiler_params=pltpu.CompilerParams(vmem_limit_bytes=36 * 1024 * 1024),
        cost_estimate=pl.CostEstimate(flops=flops, bytes_accessed=moved, transcendentals=0),
    )(*args)
    return result[0] if single else result


def shape(dims, dtype):
    return jax.ShapeDtypeStruct(dims, dtype)


def dot(left, right):
    return jnp.dot(left, right, preferred_element_type=F32)


def margin(left, right, out_ref):
    every = lax.dot_general(left, right, (((1,), (1,)), ((), ())), preferred_element_type=F32)
    out_ref[:NB, :] = (every[:NB, :NB] + every[NB:, NB:]).astype(out_ref.dtype)
    out_ref[NB:, :] = (every[:NB, NB:] - every[NB:, :NB]).astype(out_ref.dtype)


def margin_kernel(state_ref, next_ref, out_ref):
    margin(state_ref[...], next_ref[...], out_ref)


def rotate_kernel(amount_ref, block_ref, out_ref, rolled_ref):
    count, rows, width = block_ref.shape
    amount = amount_ref[0]
    first = amount // width
    rest = amount - first * width
    turn = lax.rem(width - rest, width)

    def roll(index, carry):
        rolled_ref[index] = pltpu.roll(block_ref[index].astype(F32), turn, 1)
        return carry

    lax.fori_loop(0, count, roll, 0, unroll=4)
    lane = lax.broadcasted_iota(jnp.int32, (rows, width), 1)

    def place(index, carry):
        here = lax.rem(index + first, count)
        after = lax.rem(index + first + 1, count)
        value = jnp.where(lane < width - rest, rolled_ref[here], rolled_ref[after])
        out_ref[index] = value.astype(BF16)
        return carry

    lax.fori_loop(0, count, place, 0, unroll=4)


def rotate(amount, block):
    return pl.pallas_call(
        rotate_kernel,
        out_shape=shape(block.shape, BF16),
        in_specs=[
            pl.BlockSpec(memory_space=pltpu.SMEM),
            pl.BlockSpec(memory_space=pltpu.VMEM),
        ],
        out_specs=pl.BlockSpec(memory_space=pltpu.VMEM),
        scratch_shapes=[pltpu.VMEM(block.shape, F32)],
        compiler_params=pltpu.CompilerParams(vmem_limit_bytes=36 * 1024 * 1024),
    )(amount, block)


def collect_kernel(parts_ref, out_ref):
    total = jnp.sum(parts_ref[...].astype(F32), axis=0) * (1.0 / NPW)
    out_ref[...] = jnp.broadcast_to(total.astype(out_ref.dtype)[None], out_ref.shape)


def spread_kernel(parts_ref, out_ref):
    total = jnp.sum(parts_ref[...], axis=0)
    out_ref[...] = jnp.broadcast_to(total[None], out_ref.shape)


def pieces(value, count):
    high = value.astype(BF16)
    if count == 1:
        return [high]
    return [high, (value - high.astype(F32)).astype(BF16)]


def newton_kernel(margin_ref, out_ref):
    stacked = margin_ref[...]
    whole = stacked.astype(F32)
    real, imag = whole[:NB], whole[NB:]
    magnitude = jnp.sqrt(real * real + imag * imag)
    colmax = jnp.max(jnp.sum(magnitude, axis=0, keepdims=True), axis=1, keepdims=True)
    rowmax = jnp.max(jnp.sum(magnitude, axis=1, keepdims=True), axis=0, keepdims=True)
    factor = 1.0 / (colmax * rowmax + EPS_SCALE)
    iterate = jnp.concatenate([real * factor, imag * factor], 1)

    for turn in range(NEWTON):
        parts = pieces(iterate, 2)
        product = None
        for part in parts:
            crossed = jnp.concatenate([part[:, NB:], -part[:, :NB]], 1)
            right = jnp.concatenate([part, crossed], 0)
            term = lax.dot_general(
                stacked, right, (((0,), (0,)), ((), ())), preferred_element_type=F32
            )
            product = term if product is None else product + term
        seconds = pieces(product, 2)
        change = None
        for j, second in enumerate(seconds):
            crossed = jnp.concatenate([-second[:, NB:], second[:, :NB]], 1)
            right = jnp.concatenate([second, crossed], 0)
            for i, part in enumerate(parts):
                if i + j < 2:
                    term = dot(part, right)
                    change = term if change is None else change + term
        iterate = 2.0 * iterate - change
    out_ref[...] = iterate.astype(BF16)


def slope(dual, following, dual_before, before):
    real, imag = dual[:, :NB], dual[:, NB:]
    forward = jnp.concatenate(
        [jnp.concatenate([-imag, real], 1), jnp.concatenate([-real, -imag], 1)], 0
    )
    real, imag = dual_before[:, :NB], dual_before[:, NB:]
    backward = jnp.concatenate(
        [jnp.concatenate([imag, real], 1), jnp.concatenate([-real, imag], 1)], 0
    )
    return dot(forward, following) - dot(backward, before).astype(BF16).astype(F32)


def squares(grad, count):
    part = grad[0:8]
    part = part * part
    for row in range(8, grad.shape[0], 8):
        more = grad[row : row + 8]
        part = part + more * more
    part = part[:, 0:128] + part[:, 128:256] + part[:, 256:384] + part[:, 384:512]
    return jnp.broadcast_to(part[None], (count, 8, 128))


def slopes_kernel(y_2, y_1, y0, y1, p_2, p_1, p0, p1, p2, g_1, g0, g1, total_ref):
    grad = slope(y0[...], p1[...], y_1[...], p_1[...])
    g0[...] = grad
    total_ref[...] = squares(grad, PARTS)
    g_1[...] = slope(y_1[...], p0[...], y_2[...], p_2[...])
    g1[...] = slope(y1[...], p2[...], y0[...], p0[...])


def last_slope_kernel(y_1, y0, p_1, p1, g0, total_ref):
    grad = slope(y0[...], p1[...], y_1[...], p_1[...])
    g0[...] = grad
    total_ref[...] = squares(grad, PARTS)


def step_size(total_ref):
    part = jnp.sum(total_ref[...], axis=0)
    total = jnp.sum(jnp.sum(part, axis=1, keepdims=True), axis=0, keepdims=True)
    return TAU_STEP / jnp.sqrt(total / (2 * NK * NB * NPW) + EPS_NORM)


def advance_kernel(total_ref, p_1, p0, p1, g_1, g0, g1, q_1, q0, q1, out_ref):
    size = step_size(total_ref)
    q_1[...] = (p_1[...].astype(F32) + size * g_1[...]).astype(BF16)
    here = (p0[...].astype(F32) + size * g0[...]).astype(BF16)
    ahead = (p1[...].astype(F32) + size * g1[...]).astype(BF16)
    q0[...] = here
    q1[...] = ahead
    margin(here, ahead, out_ref)


def finish_kernel(total_ref, p0, g0, re_ref, im_ref):
    size = step_size(total_ref)
    value = (p0[...].astype(F32) + size * g0[...]).astype(BF16)
    re_ref[...] = value[:NB]
    im_ref[...] = value[NB:]


def shifted(value, by):
    return lax.ppermute(value, "kstr", [(i, (i + by) % NK) for i in range(NK)])


def exchange(value, axis):
    return lax.all_to_all(value, axis, 0, 0, tiled=True)


def whole_margin(part):
    rows = 2 * NB // PARTS
    parts = exchange(part, "pw").reshape(PARTS, rows, NB)
    own = call(collect_kernel, shape((PARTS, rows, NB), BF16), parts)
    return exchange(own.reshape(2 * NB, NB), "pw")


def whole_total(part):
    parts = exchange(part, "pw")
    own = call(spread_kernel, shape((NK, 8, 128), F32), parts)
    return exchange(own, "kstr")


def inverse(whole):
    return call(newton_kernel, shape((NB, 2 * NB), BF16), whole)


def body(states_re, states_im, gmap):
    width = states_re.shape[2]
    row = lax.axis_index("kstr")
    offset = jnp.mod(gmap[0] - lax.axis_index("pw") * width, NPW)
    amount = jnp.where(row < NK // 2, offset, NPW - offset).astype(jnp.int32)
    state = jnp.concatenate([states_re[0], states_im[0]], 0)
    full = 2 * NB
    duals = shape((NB, full), BF16)
    fields = shape((full, width), BF16)
    grads = shape((full, width), F32)
    margins = shape((full, NB), BF16)
    totals = shape((PARTS, 8, 128), F32)

    blocks = exchange(state, "pw").reshape(PARTS, full // PARTS, width)
    turned = exchange(rotate(amount.reshape(1), blocks).reshape(full, width), "pw")

    p1 = shifted(jnp.where(row == 0, turned, state), -1)
    part = call(margin_kernel, margins, state, p1)
    state, turned, part = lax.optimization_barrier((state, turned, part))
    p_1 = shifted(jnp.where(row == NK - 1, turned, state), 1)
    p2 = shifted(jnp.where(row <= 1, turned, state), -2)
    p_2 = shifted(jnp.where(row >= NK - 2, turned, state), 2)

    y0 = inverse(whole_margin(part))
    y_1 = shifted(y0, 1)
    y1 = shifted(y0, -1)
    y_2 = shifted(y0, 2)
    g_1, g0, g1, total = call(
        slopes_kernel,
        (grads, grads, grads, totals),
        *(y_2, y_1, y0, y1, p_2, p_1, state, p1, p2),
    )
    total = whole_total(total)
    q_1, q0, q1, part = call(
        advance_kernel,
        (fields, fields, fields, margins),
        *(total, p_1, state, p1, g_1, g0, g1),
    )

    y0 = inverse(whole_margin(part))
    y_1 = shifted(y0, 1)
    g0, total = call(last_slope_kernel, (grads, totals), y_1, y0, q_1, q1)
    total = whole_total(total)
    half = shape((NB, width), BF16)
    new_re, new_im = call(finish_kernel, (half, half), total, q0, g0)
    return new_re[None], new_im[None]


def solution(mesh):
    placed = (P("kstr", None, "pw"), P("kstr", None, "pw"), P("pw"))
    return jax.shard_map(
        body,
        mesh=mesh,
        in_specs=placed,
        out_specs=(P("kstr", None, "pw"), P("kstr", None, "pw")),
        check_vma=False,
    )
```

time: 1410 us -> 264 us (0.19)
  waiting for transfers between devices: 979 us -> 77.5 us
  blocking collectives: 195 us -> 92 us
  starting transfers between devices: 154 us -> 66.5 us
  matrix products: 38.9 us -> 0 us
  Pallas kernels: 0 us -> 19.8 us
  between operations: 20.3 us -> 1.5 us
    psum x2 -> x0, waiting for transfers between devices: 600 us -> none  [body(): whole = lax.psum(partial_value, 'pw') / (width * plane_size)]
    ppermute x28 -> x8, waiting for transfers between devices: 379 us -> 28.6 us  [shifted(): return lax.ppermute(value, 'kstr', [(i, (i + by) % NK) for i in range(NK)])]
    psum x2 -> x0, blocking collectives: 195 us -> none  [body(): total = lax.psum(jnp.sum(g_re * g_re + g_im * g_im), ('kstr', 'pw'))]
    ppermute x28 -> x8, starting transfers between devices: 153 us -> 37.1 us  [shifted(): return lax.ppermute(value, 'kstr', [(i, (i + by) % NK) for i in range(NK)])]
    all_to_all x0 -> x6, blocking collectives: none -> 92 us  [exchange(): return lax.all_to_all(value, axis, 0, 0, tiled=True)]
    all_to_all x0 -> x4, waiting for transfers between devices: none -> 48.9 us  [exchange(): return lax.all_to_all(value, axis, 0, 0, tiled=True)]
    dot_general x88 -> x0, matrix products: 38.9 us -> none  [the longest x64 31.5 us: matmul(): return jnp.einsum('kij,kjl->kil', first, second, precision=HIGH)]
    all_to_all x0 -> x4, starting transfers between devices: none -> 29.4 us  [exchange(): return lax.all_to_all(value, axis, 0, 0, tiled=True)]
  transfers between devices with their start and end apart: 30 -> 12, of which waited for: 30 -> 9; matrix products, arithmetic and copies ran while one was open for 0% -> 1% of each run, Pallas kernels for 0% -> 2%
where the time goes in v1:
time: 264 us; the launch traced here: 263 us
  blocking collectives  92 us (35%)
  waiting for transfers between devices  77.5 us (29%)
  starting transfers between devices  66.5 us (25%)
  Pallas kernels  19.8 us (8%)
  other arithmetic  3.99 us (2%)
    all_to_all x6, blocking collectives, exchange(): return lax.all_to_all(value, axis, 0, 0, tiled=True)  92 us
    all_to_all x4, waiting for transfers between devices, exchange(): return lax.all_to_all(value, axis, 0, 0, tiled=True)  48.9 us
    ppermute x8, starting transfers between devices, shifted(): return lax.ppermute(value, 'kstr', [(i, (i + by) % NK) for i in range(NK)])  37.1 us
    all_to_all x4, starting transfers between devices, exchange(): return lax.all_to_all(value, axis, 0, 0, tiled=True)  29.4 us
    ppermute x8, waiting for transfers between devices, shifted(): return lax.ppermute(value, 'kstr', [(i, (i + by) % NK) for i in range(NK)])  28.6 us
    pallas_call x11, Pallas kernels, call(): pl.pallas_call(kernel, out_shape=outs, in_specs=specs, out_specs=tuple((p...  18.1 us
  transfers between devices with their start and end apart: 12, of which 9 were waited for; matrix products, arithmetic and copies ran while one was open for 1% of the time, Pallas kernels for 2%

profile of v1, /device:TPU:1, one launch (start us, length us, event | category | flops | bytes accessed | tf_op | source)
XLA Modules:
  0.0 262.6 jit_solution(10620699946068486349)
XLA Ops:
  0.6 1.9 pad_maximum_fusion.state_ref.p0
  2.5 14.4 %all-to-all-start = ((bf16[32,16,512]{2,1,0:T(8,128)(2,1)}), bf16[32,16,512]{2,1,0:T(8,128)(2,1)S(1)}, u32[]{:S(2)}, u32[]{:S(2)}) async-start(bf16[32,16,512]{2,1,0:T(8,128)(2,1)} %bitcast.4), calls=%async_computation | async-start | bytes 1048576 | tf_op jit(solution)/shard_map/all_to_all | solution.py:209
  16.9 1.2 slice.3
  18.8 15.4 %all-to-all-done.block_ref = bf16[32,16,512]{2,1,0:T(8,128)(2,1)S(1)} async-done(((bf16[32,16,512]{2,1,0:T(8,128)(2,1)}), bf16[32,16,512]{2,1,0:T(8,128)(2,1)S(1)}, u32[]{:S(2)}, u32[]{:S(2)}) %all-to-all-start) | async-done | bytes 524320 | tf_op jit(solution)/shard_map/all_to_all | solution.py:209
  34.2 1.7 shard_map.50
  35.9 0.0 copy-start
  35.9 0.0 copy-start.1
  35.9 5.0 %all-to-all-start.1 = ((bf16[32,16,512]{2,1,0:T(8,128)(2,1)}), bf16[32,16,512]{2,1,0:T(8,128)(2,1)S(1)}, u32[]{:S(2)}, u32[]{:S(2)}) async-start(bf16[32,16,512]{2,1,0:T(8,128)(2,1)} %shard_map.50), calls=%async_computation.1 | async-start | bytes 1048576 | tf_op jit(solution)/shard_map/all_to_all | solution.py:209
  40.9 16.6 %all-to-all-done.1 = bf16[32,16,512]{2,1,0:T(8,128)(2,1)S(1)} async-done(((bf16[32,16,512]{2,1,0:T(8,128)(2,1)}), bf16[32,16,512]{2,1,0:T(8,128)(2,1)S(1)}, u32[]{:S(2)}, u32[]{:S(2)}) %all-to-all-start.1) | async-done | bytes 524320 | tf_op jit(solution)/shard_map/all_to_all | solution.py:209
  57.6 0.0 copy-done
  57.6 0.0 copy-done.1
  57.6 0.2 broadcast_select_fusion.3
  57.7 8.2 %collective-permute-start = (bf16[512,512]{1,0:T(8,128)(2,1)S(1)}, bf16[512,512]{1,0:T(8,128)(2,1)S(1)}, u32[]{:S(2)}, u32[]{:S(2)}) collective-permute-start(bf16[512,512]{1,0:T(8,128)(2,1)S(1)} %broadcast_select_fusion.3), channel_id=1, source_target_pairs={{0,480},{32,0},{64,32},{96,64},{128,96},{160,128},{192,160},{224,1... | collective-permute-start | bytes 1572872 | tf_op jit(solution)/shard_map/ppermute | solution.py:205
  65.9 10.6 %collective-permute-done.next_ref.p1 = bf16[512,512]{1,0:T(8,128)(2,1)S(1)} collective-permute-done((bf16[512,512]{1,0:T(8,128)(2,1)S(1)}, bf16[512,512]{1,0:T(8,128)(2,1)S(1)}, u32[]{:S(2)}, u32[]{:S(2)}) %collective-permute-start) | collective-permute-done | bytes 524320 | tf_op jit(solution)/shard_map/ppermute | solution.py:205
  76.5 2.2 shard_map.51
  78.7 5.5 %all-to-all-start.2 = ((bf16[32,16,256]{2,1,0:T(8,128)(2,1)}), bf16[32,16,256]{2,1,0:T(8,128)(2,1)S(1)}, u32[]{:S(2)}, u32[]{:S(2)}) async-start(bf16[32,16,256]{2,1,0:T(8,128)(2,1)} %bitcast.6), calls=%async_computation.2 | async-start | bytes 524288 | tf_op jit(solution)/shard_map/all_to_all | solution.py:209
  84.2 1.9 broadcast_select_fusion
  86.2 3.0 %collective-permute-start.6 = (bf16[512,512]{1,0:T(8,128)(2,1)}, bf16[512,512]{1,0:T(8,128)(2,1)S(1)}, u32[]{:S(2)}, u32[]{:S(2)}) collective-permute-start(bf16[512,512]{1,0:T(8,128)(2,1)} %get-tuple-element.32), channel_id=1, source_target_pairs={{0,448},{32,480},{64,0},{96,32},{128,64},{160,96},{192,128},{224,1... | collective-permute-start | bytes 1572872 | tf_op jit(solution)/shard_map/ppermute | solution.py:205
  89.1 8.2 %all-to-all-done.2.parts_ref = bf16[32,16,256]{2,1,0:T(8,128)(2,1)S(1)} async-done(((bf16[32,16,256]{2,1,0:T(8,128)(2,1)}), bf16[32,16,256]{2,1,0:T(8,128)(2,1)S(1)}, u32[]{:S(2)}, u32[]{:S(2)}) %all-to-all-start.2) | async-done | bytes 262176 | tf_op jit(solution)/shard_map/all_to_all | solution.py:209
  97.3 0.8 shard_map.52
  98.1 4.4 %all-to-all-start.3 = ((bf16[32,16,256]{2,1,0:T(8,128)(2,1)}), bf16[32,16,256]{2,1,0:T(8,128)(2,1)S(1)}, u32[]{:S(2)}, u32[]{:S(2)}) async-start(bf16[32,16,256]{2,1,0:T(8,128)(2,1)} %shard_map.52), calls=%async_computation.3 | async-start | bytes 524288 | tf_op jit(solution)/shard_map/all_to_all | solution.py:209
  102.5 2.9 %collective-permute-start.5 = (bf16[512,512]{1,0:T(8,128)(2,1)S(1)}, bf16[512,512]{1,0:T(8,128)(2,1)S(1)}, u32[]{:S(2)}, u32[]{:S(2)}) collective-permute-start(bf16[512,512]{1,0:T(8,128)(2,1)S(1)} %get-tuple-element.33), channel_id=1, source_target_pairs={{0,32},{32,64},{64,96},{96,128},{128,160},{160,192},{192,224},{224... | collective-permute-start | bytes 1572872 | tf_op jit(solution)/shard_map/ppermute | solution.py:205
  105.4 1.9 collective-permute-start.4
  107.3 8.7 %all-to-all-done.3 = bf16[32,16,256]{2,1,0:T(8,128)(2,1)S(1)} async-done(((bf16[32,16,256]{2,1,0:T(8,128)(2,1)}), bf16[32,16,256]{2,1,0:T(8,128)(2,1)S(1)}, u32[]{:S(2)}, u32[]{:S(2)}) %all-to-all-start.3) | async-done | bytes 262176 | tf_op jit(solution)/shard_map/all_to_all | solution.py:209
  116.1 4.2 %shard_map.53.y0 = bf16[256,512]{1,0:T(8,128)(2,1)S(1)} custom-call(bf16[512,256]{1,0:T(8,128)(2,1)S(1)} %bitcast.13), custom_call_target="tpu_custom_call" | custom-call | bytes 524288 | tf_op jit(solution)/shard_map/pallas_call | solution.py:28
  120.2 15.5 %collective-permute-start.3 = (bf16[256,512]{1,0:T(8,128)(2,1)S(1)}, bf16[256,512]{1,0:T(8,128)(2,1)S(1)}, u32[]{:S(2)}, u32[]{:S(2)}) collective-permute-start(bf16[256,512]{1,0:T(8,128)(2,1)S(1)} %shard_map.53.y0), channel_id=1, source_target_pairs={{0,480},{32,0},{64,32},{96,64},{128,96},{160,128},{192,160},{224,1... | collective-permute-start | bytes 786440 | tf_op jit(solution)/shard_map/ppermute | solution.py:205
  135.7 1.9 collective-permute-start.2
  137.6 0.0 collective-permute-done.6.p2
  137.7 1.9 collective-permute-start.1
  139.6 0.0 collective-permute-done.5.p_1
  139.6 0.0 collective-permute-done.4.p_2
  139.6 1.6 collective-permute-done.3.y1
  141.2 5.9 %collective-permute-done.2.y_1 = bf16[256,512]{1,0:T(8,128)(2,1)S(1)} collective-permute-done((bf16[256,512]{1,0:T(8,128)(2,1)S(1)}, bf16[256,512]{1,0:T(8,128)(2,1)S(1)}, u32[]{:S(2)}, u32[]{:S(2)}) %collective-permute-start.2) | collective-permute-done | bytes 262176 | tf_op jit(solution)/shard_map/ppermute | solution.py:205
  147.0 1.0 collective-permute-done.1.y_2
  148.1 2.9 %shard_map.54 = (f32[512,512]{1,0:T(8,128)S(1)}, f32[512,512]{1,0:T(8,128)S(1)}, f32[512,512]{1,0:T(8,128)S(1)}, f32[32,8,128]{2,1,0:T(8,128)S(1)}) custom-call(bf16[256,512]{1,0:T(8,128)(2,1)S(1)} %collective-permute-done.1.y_2, bf16[256,512]{1,0:T(8,128)(2,1)S(1)} %collective-permute-done.2.y_1, bf16[256,512]{1,0:T(8,128)(2,1)S(1)} %shard_map.53.y0, ...), custom_call_target="tpu_custom_call" | custom-call | bytes 6946816 | tf_op jit(solution)/shard_map/pallas_call | solution.py:28
  151.0 15.2 %all_to_all.72.parts_ref = f32[32,8,128]{2,1,0:T(8,128)S(1)} all-to-all(f32[32,8,128]{2,1,0:T(8,128)S(1)} %get-tuple-element.20), channel_id=1, replica_groups=mesh['kstr'=16,'pw'=32] {'pw'}, dimensions={0} | all-to-all | bytes 262144 | tf_op jit(solution)/shard_map/all_to_all | solution.py:209
  166.2 16.0 %all_to_all.73.total_ref = f32[16,8,128]{2,1,0:T(8,128)S(1)} all-to-all(f32[16,8,128]{2,1,0:T(8,128)S(1)} %shard_map.55), channel_id=1, replica_groups=mesh['kstr'=16,'pw'=32] {'kstr'}, dimensions={0} | all-to-all | bytes 131072 | tf_op jit(solution)/shard_map/all_to_all | solution.py:209
  182.2 1.9 shard_map.56
  184.2 17.5 %all_to_all.74.parts_ref = bf16[32,16,256]{2,1,0:T(8,128)(2,1)S(1)} all-to-all(bf16[32,16,256]{2,1,0:T(8,128)(2,1)S(1)} %bitcast.15), channel_id=1, replica_groups=mesh['kstr'=16,'pw'=32] {'pw'}, dimensions={0} | all-to-all | bytes 524288 | tf_op jit(solution)/shard_map/all_to_all | solution.py:209
  201.7 0.1 shard_map.57
  201.8 17.1 %all_to_all.75 = bf16[32,16,256]{2,1,0:T(8,128)(2,1)S(1)} all-to-all(bf16[32,16,256]{2,1,0:T(8,128)(2,1)S(1)} %shard_map.57), channel_id=1, replica_groups=mesh['kstr'=16,'pw'=32] {'pw'}, dimensions={0} | all-to-all | bytes 524288 | tf_op jit(solution)/shard_map/all_to_all | solution.py:209
  218.9 4.2 %shard_map.58.y0 = bf16[256,512]{1,0:T(8,128)(2,1)S(1)} custom-call(bf16[512,256]{1,0:T(8,128)(2,1)S(1)} %bitcast.14), custom_call_target="tpu_custom_call" | custom-call | bytes 524288 | tf_op jit(solution)/shard_map/pallas_call | solution.py:28
  223.1 1.9 collective-permute-start.7
  225.0 9.5 %collective-permute-done.7.y_1 = bf16[256,512]{1,0:T(8,128)(2,1)S(1)} collective-permute-done((bf16[256,512]{1,0:T(8,128)(2,1)S(1)}, bf16[256,512]{1,0:T(8,128)(2,1)S(1)}, u32[]{:S(2)}, u32[]{:S(2)}) %collective-permute-start.7) | collective-permute-done | bytes 262176 | tf_op jit(solution)/shard_map/ppermute | solution.py:205
  234.5 0.7 shard_map.59
  235.3 15.6 %all_to_all.76.parts_ref = f32[32,8,128]{2,1,0:T(8,128)S(1)} all-to-all(f32[32,8,128]{2,1,0:T(8,128)S(1)} %get-tuple-element.27), channel_id=1, replica_groups=mesh['kstr'=16,'pw'=32] {'pw'}, dimensions={0} | all-to-all | bytes 262144 | tf_op jit(solution)/shard_map/all_to_all | solution.py:209
  251.0 10.5 %all_to_all.77.total_ref = f32[16,8,128]{2,1,0:T(8,128)S(1)} all-to-all(f32[16,8,128]{2,1,0:T(8,128)S(1)} %shard_map.60), channel_id=1, replica_groups=mesh['kstr'=16,'pw'=32] {'kstr'}, dimensions={0} | all-to-all | bytes 131072 | tf_op jit(solution)/shard_map/all_to_all | solution.py:209
  261.5 1.1 shard_map.61
  (2 shorter events, 0.1 us)
Async XLA Ops:
  2.5 31.7 %all-to-all-start = ((bf16[32,16,512]{2,1,0:T(8,128)(2,1)}), bf16[32,16,512]{2,1,0:T(8,128)(2,1)S(1)}, u32[]{:S(2)}, u32[]{:S(2)}) async-start(bf16[32,16,512]{2,1,0:T(8,128)(2,1)} %bitcast.4), calls=%async_computation | async-start | bytes 1048576 | tf_op jit(solution)/shard_map/all_to_all | solution.py:209
  35.9 21.7 %copy-start = (bf16[1,256,512]{2,1,0:T(8,128)(2,1)S(1)}, bf16[1,256,512]{2,1,0:T(8,128)(2,1)}, u32[]{:S(2)}) copy-start(bf16[1,256,512]{2,1,0:T(8,128)(2,1)} %param.4) | copy-start | bytes 786436
  35.9 21.7 %copy-start.1 = (bf16[1,256,512]{2,1,0:T(8,128)(2,1)S(1)}, bf16[1,256,512]{2,1,0:T(8,128)(2,1)}, u32[]{:S(2)}) copy-start(bf16[1,256,512]{2,1,0:T(8,128)(2,1)} %param.3) | copy-start | bytes 786436
  35.9 21.6 %all-to-all-start.1 = ((bf16[32,16,512]{2,1,0:T(8,128)(2,1)}), bf16[32,16,512]{2,1,0:T(8,128)(2,1)S(1)}, u32[]{:S(2)}, u32[]{:S(2)}) async-start(bf16[32,16,512]{2,1,0:T(8,128)(2,1)} %shard_map.50), calls=%async_computation.1 | async-start | bytes 1048576 | tf_op jit(solution)/shard_map/all_to_all | solution.py:209
  57.7 18.7 %collective-permute-start = (bf16[512,512]{1,0:T(8,128)(2,1)S(1)}, bf16[512,512]{1,0:T(8,128)(2,1)S(1)}, u32[]{:S(2)}, u32[]{:S(2)}) collective-permute-start(bf16[512,512]{1,0:T(8,128)(2,1)S(1)} %broadcast_select_fusion.3), channel_id=1, source_target_pairs={{0,480},{32,0},{64,32},{96,64},{128,96},{160,128},{192,160},{224,1... | collective-permute-start | bytes 1572872 | tf_op jit(solution)/shard_map/ppermute | solution.py:205
  78.7 18.6 %all-to-all-start.2 = ((bf16[32,16,256]{2,1,0:T(8,128)(2,1)}), bf16[32,16,256]{2,1,0:T(8,128)(2,1)S(1)}, u32[]{:S(2)}, u32[]{:S(2)}) async-start(bf16[32,16,256]{2,1,0:T(8,128)(2,1)} %bitcast.6), calls=%async_computation.2 | async-start | bytes 524288 | tf_op jit(solution)/shard_map/all_to_all | solution.py:209
  86.2 51.5 %collective-permute-start.6 = (bf16[512,512]{1,0:T(8,128)(2,1)}, bf16[512,512]{1,0:T(8,128)(2,1)S(1)}, u32[]{:S(2)}, u32[]{:S(2)}) collective-permute-start(bf16[512,512]{1,0:T(8,128)(2,1)} %get-tuple-element.32), channel_id=1, source_target_pairs={{0,448},{32,480},{64,0},{96,32},{128,64},{160,96},{192,128},{224,1... | collective-permute-start | bytes 1572872 | tf_op jit(solution)/shard_map/ppermute | solution.py:205
  98.1 18.0 %all-to-all-start.3 = ((bf16[32,16,256]{2,1,0:T(8,128)(2,1)}), bf16[32,16,256]{2,1,0:T(8,128)(2,1)S(1)}, u32[]{:S(2)}, u32[]{:S(2)}) async-start(bf16[32,16,256]{2,1,0:T(8,128)(2,1)} %shard_map.52), calls=%async_computation.3 | async-start | bytes 524288 | tf_op jit(solution)/shard_map/all_to_all | solution.py:209
  102.5 37.0 %collective-permute-start.5 = (bf16[512,512]{1,0:T(8,128)(2,1)S(1)}, bf16[512,512]{1,0:T(8,128)(2,1)S(1)}, u32[]{:S(2)}, u32[]{:S(2)}) collective-permute-start(bf16[512,512]{1,0:T(8,128)(2,1)S(1)} %get-tuple-element.33), channel_id=1, source_target_pairs={{0,32},{32,64},{64,96},{96,128},{128,160},{160,192},{192,224},{224... | collective-permute-start | bytes 1572872 | tf_op jit(solution)/shard_map/ppermute | solution.py:205
  105.4 34.2 %collective-permute-start.4 = (bf16[512,512]{1,0:T(8,128)(2,1)S(1)}, bf16[512,512]{1,0:T(8,128)(2,1)S(1)}, u32[]{:S(2)}, u32[]{:S(2)}) collective-permute-start(bf16[512,512]{1,0:T(8,128)(2,1)S(1)} %get-tuple-element.34), channel_id=1, source_target_pairs={{0,64},{32,96},{64,128},{96,160},{128,192},{160,224},{192,256},{22... | collective-permute-start | bytes 1572872 | tf_op jit(solution)/shard_map/ppermute | solution.py:205
  120.2 21.0 %collective-permute-start.3 = (bf16[256,512]{1,0:T(8,128)(2,1)S(1)}, bf16[256,512]{1,0:T(8,128)(2,1)S(1)}, u32[]{:S(2)}, u32[]{:S(2)}) collective-permute-start(bf16[256,512]{1,0:T(8,128)(2,1)S(1)} %shard_map.53.y0), channel_id=1, source_target_pairs={{0,480},{32,0},{64,32},{96,64},{128,96},{160,128},{192,160},{224,1... | collective-permute-start | bytes 786440 | tf_op jit(solution)/shard_map/ppermute | solution.py:205
  135.7 11.3 %collective-permute-start.2 = (bf16[256,512]{1,0:T(8,128)(2,1)S(1)}, bf16[256,512]{1,0:T(8,128)(2,1)S(1)}, u32[]{:S(2)}, u32[]{:S(2)}) collective-permute-start(bf16[256,512]{1,0:T(8,128)(2,1)S(1)} %shard_map.53.y0), channel_id=1, source_target_pairs={{0,32},{32,64},{64,96},{96,128},{128,160},{160,192},{192,224},{224... | collective-permute-start | bytes 786440 | tf_op jit(solution)/shard_map/ppermute | solution.py:205
  137.7 10.4 %collective-permute-start.1 = (bf16[256,512]{1,0:T(8,128)(2,1)S(1)}, bf16[256,512]{1,0:T(8,128)(2,1)S(1)}, u32[]{:S(2)}, u32[]{:S(2)}) collective-permute-start(bf16[256,512]{1,0:T(8,128)(2,1)S(1)} %shard_map.53.y0), channel_id=1, source_target_pairs={{0,64},{32,96},{64,128},{96,160},{128,192},{160,224},{192,256},{22... | collective-permute-start | bytes 786440 | tf_op jit(solution)/shard_map/ppermute | solution.py:205
  223.1 11.5 %collective-permute-start.7 = (bf16[256,512]{1,0:T(8,128)(2,1)S(1)}, bf16[256,512]{1,0:T(8,128)(2,1)S(1)}, u32[]{:S(2)}, u32[]{:S(2)}) collective-permute-start(bf16[256,512]{1,0:T(8,128)(2,1)S(1)} %shard_map.58.y0), channel_id=1, source_target_pairs={{0,32},{32,64},{64,96},{96,128},{128,160},{160,192},{192,224},{224... | collective-permute-start | bytes 786440 | tf_op jit(solution)/shard_map/ppermute | solution.py:205

commit v2 on v1

--- a/solution.py
+++ b/solution.py
@@ -30,7 +30,7 @@
         out_shape=outs,
         in_specs=specs,
         out_specs=tuple(pl.BlockSpec(memory_space=pltpu.VMEM) for _ in outs),
-        compiler_params=pltpu.CompilerParams(vmem_limit_bytes=36 * 1024 * 1024),
+        compiler_params=pltpu.CompilerParams(vmem_limit_bytes=14 * 1024 * 1024),
         cost_estimate=pl.CostEstimate(flops=flops, bytes_accessed=moved, transcendentals=0),
     )(*args)
     return result[0] if single else result
@@ -88,7 +88,7 @@
         ],
         out_specs=pl.BlockSpec(memory_space=pltpu.VMEM),
         scratch_shapes=[pltpu.VMEM(block.shape, F32)],
-        compiler_params=pltpu.CompilerParams(vmem_limit_bytes=36 * 1024 * 1024),
+        compiler_params=pltpu.CompilerParams(vmem_limit_bytes=14 * 1024 * 1024),
     )(amount, block)
 
 
@@ -164,15 +164,12 @@
     return jnp.broadcast_to(part[None], (count, 8, 128))
 
 
-def slopes_kernel(y_2, y_1, y0, y1, p_2, p_1, p0, p1, p2, g_1, g0, g1, total_ref):
-    grad = slope(y0[...], p1[...], y_1[...], p_1[...])
-    g0[...] = grad
-    total_ref[...] = squares(grad, PARTS)
+def sides_kernel(y_2, y_1, y0, y1, p_2, p0, p2, g_1, g1):
     g_1[...] = slope(y_1[...], p0[...], y_2[...], p_2[...])
     g1[...] = slope(y1[...], p2[...], y0[...], p0[...])
 
 
-def last_slope_kernel(y_1, y0, p_1, p1, g0, total_ref):
+def slope_kernel(y_1, y0, p_1, p1, g0, total_ref):
     grad = slope(y0[...], p1[...], y_1[...], p_1[...])
     g0[...] = grad
     total_ref[...] = squares(grad, PARTS)
@@ -251,14 +248,12 @@
 
     y0 = inverse(whole_margin(part))
     y_1 = shifted(y0, 1)
-    y1 = shifted(y0, -1)
-    y_2 = shifted(y0, 2)
-    g_1, g0, g1, total = call(
-        slopes_kernel,
-        (grads, grads, grads, totals),
-        *(y_2, y_1, y0, y1, p_2, p_1, state, p1, p2),
-    )
+    g0, total = call(slope_kernel, (grads, totals), y_1, y0, p_1, p1)
+    y0_later, total = lax.optimization_barrier((y0, total))
+    y1 = shifted(y0_later, -1)
+    y_2 = shifted(y0_later, 2)
     total = whole_total(total)
+    g_1, g1 = call(sides_kernel, (grads, grads), y_2, y_1, y0, y1, p_2, state, p2)
     q_1, q0, q1, part = call(
         advance_kernel,
         (fields, fields, fields, margins),
@@ -267,7 +262,7 @@
 
     y0 = inverse(whole_margin(part))
     y_1 = shifted(y0, 1)
-    g0, total = call(last_slope_kernel, (grads, totals), y_1, y0, q_1, q1)
+    g0, total = call(slope_kernel, (grads, totals), y_1, y0, q_1, q1)
     total = whole_total(total)
     half = shape((NB, width), BF16)
     new_re, new_im = call(finish_kernel, (half, half), total, q0, g0)

time: 264 us -> 267 us (1.011)
  blocking collectives: 92 us -> 61 us
  waiting for transfers between devices: 77.5 us -> 92.2 us
  starting transfers between devices: 66.5 us -> 79.5 us
  local copies, waits for them, and re-layouts: 1.2 us -> 6.22 us
    all_to_all x6 -> x4, blocking collectives: 92 us -> 61 us  [exchange(): return lax.all_to_all(value, axis, 0, 0, tiled=True)]
    all_to_all x4 -> x6, waiting for transfers between devices: 48.9 us -> 69.6 us  [exchange(): return lax.all_to_all(value, axis, 0, 0, tiled=True)]
    all_to_all x4 -> x6, starting transfers between devices: 29.4 us -> 40.3 us  [exchange(): return lax.all_to_all(value, axis, 0, 0, tiled=True)]
    ppermute x8, waiting for transfers between devices: 28.6 us -> 22.6 us  [shifted(): return lax.ppermute(value, 'kstr', [(i, (i + by) % NK) for i in range(NK)])]
    unnamed x4 -> x14, local copies, waits for them, and re-layouts: 0.01 us -> 5.02 us
    pallas_call x11 -> x12, Pallas kernels: 18.1 us -> 19.1 us  [call(): pl.pallas_call(kernel, out_shape=outs, in_specs=specs, out_specs=tuple((p...]
  transfers between devices with their start and end apart: 12 -> 14, of which waited for: 9 -> 9; matrix products, arithmetic and copies ran while one was open for 1% -> 1% of each run, Pallas kernels for 2% -> 3%
where the time goes in v2:
time: 267 us; the launch traced here: 265 us
  waiting for transfers between devices  92.2 us (35%)
  starting transfers between devices  79.5 us (30%)
  blocking collectives  61 us (23%)
  Pallas kernels  20.8 us (8%)
  local copies, waits for them, and re-layouts  6.22 us (2%)
  other arithmetic  4.17 us (2%)
    all_to_all x6, waiting for transfers between devices, exchange(): return lax.all_to_all(value, axis, 0, 0, tiled=True)  69.6 us
    all_to_all x4, blocking collectives, exchange(): return lax.all_to_all(value, axis, 0, 0, tiled=True)  61 us
    all_to_all x6, starting transfers between devices, exchange(): return lax.all_to_all(value, axis, 0, 0, tiled=True)  40.3 us
    ppermute x8, starting transfers between devices, shifted(): return lax.ppermute(value, 'kstr', [(i, (i + by) % NK) for i in range(NK)])  39.2 us
    ppermute x8, waiting for transfers between devices, shifted(): return lax.ppermute(value, 'kstr', [(i, (i + by) % NK) for i in range(NK)])  22.6 us
    pallas_call x12, Pallas kernels, call(): pl.pallas_call(kernel, out_shape=outs, in_specs=specs, out_specs=tuple((p...  19.1 us
  transfers between devices with their start and end apart: 14, of which 9 were waited for; matrix products, arithmetic and copies ran while one was open for 1% of the time, Pallas kernels for 3%

profile of v2, /device:TPU:1, one launch (start us, length us, event | category | flops | bytes accessed | tf_op | source)
XLA Modules:
  0.0 265.5 jit_solution(12863732132615220536)
XLA Ops:
  0.6 1.9 pad_maximum_fusion.state_ref.p0
  2.5 14.4 %all-to-all-start = ((bf16[32,16,512]{2,1,0:T(8,128)(2,1)}), bf16[32,16,512]{2,1,0:T(8,128)(2,1)S(1)}, u32[]{:S(2)}, u32[]{:S(2)}) async-start(bf16[32,16,512]{2,1,0:T(8,128)(2,1)} %bitcast.4), calls=%async_computation | async-start | bytes 1048576 | tf_op jit(solution)/shard_map/all_to_all | solution.py:206
  16.9 1.2 slice.3
  18.8 15.4 %all-to-all-done.block_ref = bf16[32,16,512]{2,1,0:T(8,128)(2,1)S(1)} async-done(((bf16[32,16,512]{2,1,0:T(8,128)(2,1)}), bf16[32,16,512]{2,1,0:T(8,128)(2,1)S(1)}, u32[]{:S(2)}, u32[]{:S(2)}) %all-to-all-start) | async-done | bytes 524320 | tf_op jit(solution)/shard_map/all_to_all | solution.py:206
  34.2 1.7 shard_map.50
  35.9 5.0 %all-to-all-start.1 = ((bf16[32,16,512]{2,1,0:T(8,128)(2,1)}), bf16[32,16,512]{2,1,0:T(8,128)(2,1)S(1)}, u32[]{:S(2)}, u32[]{:S(2)}) async-start(bf16[32,16,512]{2,1,0:T(8,128)(2,1)} %shard_map.50), calls=%async_computation.1 | async-start | bytes 1048576 | tf_op jit(solution)/shard_map/all_to_all | solution.py:206
  40.9 16.6 %all-to-all-done.1 = bf16[32,16,512]{2,1,0:T(8,128)(2,1)S(1)} async-done(((bf16[32,16,512]{2,1,0:T(8,128)(2,1)}), bf16[32,16,512]{2,1,0:T(8,128)(2,1)S(1)}, u32[]{:S(2)}, u32[]{:S(2)}) %all-to-all-start.1) | async-done | bytes 524320 | tf_op jit(solution)/shard_map/all_to_all | solution.py:206
  57.6 0.2 broadcast_select_fusion.3
  57.7 8.2 %collective-permute-start = (bf16[512,512]{1,0:T(8,128)(2,1)S(1)}, bf16[512,512]{1,0:T(8,128)(2,1)S(1)}, u32[]{:S(2)}, u32[]{:S(2)}) collective-permute-start(bf16[512,512]{1,0:T(8,128)(2,1)S(1)} %broadcast_select_fusion.3), channel_id=1, source_target_pairs={{0,480},{32,0},{64,32},{96,64},{128,96},{160,128},{192,160},{224,1... | collective-permute-start | bytes 1572872 | tf_op jit(solution)/shard_map/ppermute | solution.py:202
  65.9 10.6 %collective-permute-done.next_ref.p1 = bf16[512,512]{1,0:T(8,128)(2,1)S(1)} collective-permute-done((bf16[512,512]{1,0:T(8,128)(2,1)S(1)}, bf16[512,512]{1,0:T(8,128)(2,1)S(1)}, u32[]{:S(2)}, u32[]{:S(2)}) %collective-permute-start) | collective-permute-done | bytes 524320 | tf_op jit(solution)/shard_map/ppermute | solution.py:202
  76.5 2.2 shard_map.51
  78.7 5.5 %all-to-all-start.2 = ((bf16[32,16,256]{2,1,0:T(8,128)(2,1)}), bf16[32,16,256]{2,1,0:T(8,128)(2,1)S(1)}, u32[]{:S(2)}, u32[]{:S(2)}) async-start(bf16[32,16,256]{2,1,0:T(8,128)(2,1)} %bitcast.6), calls=%async_computation.2 | async-start | bytes 524288 | tf_op jit(solution)/shard_map/all_to_all | solution.py:206
  84.2 13.1 %all-to-all-done.2.parts_ref = bf16[32,16,256]{2,1,0:T(8,128)(2,1)S(1)} async-done(((bf16[32,16,256]{2,1,0:T(8,128)(2,1)}), bf16[32,16,256]{2,1,0:T(8,128)(2,1)S(1)}, u32[]{:S(2)}, u32[]{:S(2)}) %all-to-all-start.2) | async-done | bytes 262176 | tf_op jit(solution)/shard_map/all_to_all | solution.py:206
  97.3 0.8 shard_map.52
  98.1 4.4 %all-to-all-start.3 = ((bf16[32,16,256]{2,1,0:T(8,128)(2,1)}), bf16[32,16,256]{2,1,0:T(8,128)(2,1)S(1)}, u32[]{:S(2)}, u32[]{:S(2)}) async-start(bf16[32,16,256]{2,1,0:T(8,128)(2,1)} %shard_map.52), calls=%async_computation.3 | async-start | bytes 524288 | tf_op jit(solution)/shard_map/all_to_all | solution.py:206
  102.6 2.1 broadcast_select_fusion
  104.7 1.9 collective-permute-start.2
  106.6 8.7 %all-to-all-done.3 = bf16[32,16,256]{2,1,0:T(8,128)(2,1)S(1)} async-done(((bf16[32,16,256]{2,1,0:T(8,128)(2,1)}), bf16[32,16,256]{2,1,0:T(8,128)(2,1)S(1)}, u32[]{:S(2)}, u32[]{:S(2)}) %all-to-all-start.3) | async-done | bytes 262176 | tf_op jit(solution)/shard_map/all_to_all | solution.py:206
  115.3 4.1 %shard_map.53.y0 = bf16[256,512]{1,0:T(8,128)(2,1)S(1)} custom-call(bf16[512,256]{1,0:T(8,128)(2,1)S(1)} %bitcast.13), custom_call_target="tpu_custom_call" | custom-call | bytes 524288 | tf_op jit(solution)/shard_map/pallas_call | solution.py:28
  119.5 1.9 collective-permute-start.1
  121.4 19.5 %collective-permute-start.6 = (bf16[512,512]{1,0:T(8,128)(2,1)}, bf16[512,512]{1,0:T(8,128)(2,1)S(1)}, u32[]{:S(2)}, u32[]{:S(2)}) collective-permute-start(bf16[512,512]{1,0:T(8,128)(2,1)} %get-tuple-element.36), channel_id=1, source_target_pairs={{0,448},{32,480},{64,0},{96,32},{128,64},{160,96},{192,128},{224,1... | collective-permute-start | bytes 1572872 | tf_op jit(solution)/shard_map/ppermute | solution.py:202
  140.9 1.9 collective-permute-start.5
  142.8 2.5 collective-permute-done.1.y_1
  145.3 1.4 shard_map.54
  146.7 6.7 %all-to-all-start.4 = ((f32[32,8,128]{2,1,0:T(8,128)}), f32[32,8,128]{2,1,0:T(8,128)S(1)}, u32[]{:S(2)}, u32[]{:S(2)}) async-start(f32[32,8,128]{2,1,0:T(8,128)} %get-tuple-element.23), calls=%async_computation.4 | async-start | bytes 262144 | tf_op jit(solution)/shard_map/all_to_all | solution.py:206
  153.4 2.0 collective-permute-start.4
  155.4 1.9 collective-permute-start.3
  157.3 12.4 %all-to-all-done.4.parts_ref = f32[32,8,128]{2,1,0:T(8,128)S(1)} async-done(((f32[32,8,128]{2,1,0:T(8,128)}), f32[32,8,128]{2,1,0:T(8,128)S(1)}, u32[]{:S(2)}, u32[]{:S(2)}) %all-to-all-start.4) | async-done | bytes 131104 | tf_op jit(solution)/shard_map/all_to_all | solution.py:206
  169.8 0.6 copy-done.4
  170.4 4.2 %all-to-all-start.5 = ((f32[16,8,128]{2,1,0:T(8,128)}), f32[16,8,128]{2,1,0:T(8,128)S(1)}, u32[]{:S(2)}, u32[]{:S(2)}) async-start(f32[16,8,128]{2,1,0:T(8,128)} %copy-done.4), calls=%async_computation.5 | async-start | bytes 131072 | tf_op jit(solution)/shard_map/all_to_all | solution.py:206
  174.6 0.0 collective-permute-done.6.p2
  174.7 2.5 shard_map.56
  177.2 1.0 copy-done
  178.2 1.0 copy-done.2
  179.2 3.4 %all-to-all-done.5.total_ref = f32[16,8,128]{2,1,0:T(8,128)S(1)} async-done(((f32[16,8,128]{2,1,0:T(8,128)}), f32[16,8,128]{2,1,0:T(8,128)S(1)}, u32[]{:S(2)}, u32[]{:S(2)}) %all-to-all-start.5) | async-done | bytes 65568 | tf_op jit(solution)/shard_map/all_to_all | solution.py:206
  182.5 1.2 copy-done.1
  183.7 1.2 copy-done.3
  185.0 1.9 shard_map.57
  186.9 17.7 %all_to_all.72.parts_ref = bf16[32,16,256]{2,1,0:T(8,128)(2,1)S(1)} all-to-all(bf16[32,16,256]{2,1,0:T(8,128)(2,1)S(1)} %bitcast.15), channel_id=1, replica_groups=mesh['kstr'=16,'pw'=32] {'pw'}, dimensions={0} | all-to-all | bytes 524288 | tf_op jit(solution)/shard_map/all_to_all | solution.py:206
  204.6 0.1 shard_map.58
  204.6 17.1 %all_to_all.73 = bf16[32,16,256]{2,1,0:T(8,128)(2,1)S(1)} all-to-all(bf16[32,16,256]{2,1,0:T(8,128)(2,1)S(1)} %shard_map.58), channel_id=1, replica_groups=mesh['kstr'=16,'pw'=32] {'pw'}, dimensions={0} | all-to-all | bytes 524288 | tf_op jit(solution)/shard_map/all_to_all | solution.py:206
  221.7 4.2 %shard_map.59.y0 = bf16[256,512]{1,0:T(8,128)(2,1)S(1)} custom-call(bf16[512,256]{1,0:T(8,128)(2,1)S(1)} %bitcast.14), custom_call_target="tpu_custom_call" | custom-call | bytes 524288 | tf_op jit(solution)/shard_map/pallas_call | solution.py:28
  225.9 1.9 collective-permute-start.7
  227.8 9.6 %collective-permute-done.7.y_1 = bf16[256,512]{1,0:T(8,128)(2,1)S(1)} collective-permute-done((bf16[256,512]{1,0:T(8,128)(2,1)S(1)}, bf16[256,512]{1,0:T(8,128)(2,1)S(1)}, u32[]{:S(2)}, u32[]{:S(2)}) %collective-permute-start.7) | collective-permute-done | bytes 262176 | tf_op jit(solution)/shard_map/ppermute | solution.py:202
  237.4 0.7 shard_map.60
  238.1 15.6 %all_to_all.74.parts_ref = f32[32,8,128]{2,1,0:T(8,128)S(1)} all-to-all(f32[32,8,128]{2,1,0:T(8,128)S(1)} %get-tuple-element.31), channel_id=1, replica_groups=mesh['kstr'=16,'pw'=32] {'pw'}, dimensions={0} | all-to-all | bytes 262144 | tf_op jit(solution)/shard_map/all_to_all | solution.py:206
  253.8 10.5 %all_to_all.75.total_ref = f32[16,8,128]{2,1,0:T(8,128)S(1)} all-to-all(f32[16,8,128]{2,1,0:T(8,128)S(1)} %shard_map.61), channel_id=1, replica_groups=mesh['kstr'=16,'pw'=32] {'kstr'}, dimensions={0} | all-to-all | bytes 131072 | tf_op jit(solution)/shard_map/all_to_all | solution.py:206
  264.4 1.1 shard_map.62
  (15 shorter events, 0.1 us)
Async XLA Ops:
  2.5 31.7 %all-to-all-start = ((bf16[32,16,512]{2,1,0:T(8,128)(2,1)}), bf16[32,16,512]{2,1,0:T(8,128)(2,1)S(1)}, u32[]{:S(2)}, u32[]{:S(2)}) async-start(bf16[32,16,512]{2,1,0:T(8,128)(2,1)} %bitcast.4), calls=%async_computation | async-start | bytes 1048576 | tf_op jit(solution)/shard_map/all_to_all | solution.py:206
  35.9 21.7 %copy-start.5 = (bf16[1,256,512]{2,1,0:T(8,128)(2,1)S(1)}, bf16[1,256,512]{2,1,0:T(8,128)(2,1)}, u32[]{:S(2)}) copy-start(bf16[1,256,512]{2,1,0:T(8,128)(2,1)} %param.4) | copy-start | bytes 786436
  35.9 21.7 %copy-start.6 = (bf16[1,256,512]{2,1,0:T(8,128)(2,1)S(1)}, bf16[1,256,512]{2,1,0:T(8,128)(2,1)}, u32[]{:S(2)}) copy-start(bf16[1,256,512]{2,1,0:T(8,128)(2,1)} %param.3) | copy-start | bytes 786436
  35.9 21.6 %all-to-all-start.1 = ((bf16[32,16,512]{2,1,0:T(8,128)(2,1)}), bf16[32,16,512]{2,1,0:T(8,128)(2,1)S(1)}, u32[]{:S(2)}, u32[]{:S(2)}) async-start(bf16[32,16,512]{2,1,0:T(8,128)(2,1)} %shard_map.50), calls=%async_computation.1 | async-start | bytes 1048576 | tf_op jit(solution)/shard_map/all_to_all | solution.py:206
  57.7 18.7 %collective-permute-start = (bf16[512,512]{1,0:T(8,128)(2,1)S(1)}, bf16[512,512]{1,0:T(8,128)(2,1)S(1)}, u32[]{:S(2)}, u32[]{:S(2)}) collective-permute-start(bf16[512,512]{1,0:T(8,128)(2,1)S(1)} %broadcast_select_fusion.3), channel_id=1, source_target_pairs={{0,480},{32,0},{64,32},{96,64},{128,96},{160,128},{192,160},{224,1... | collective-permute-start | bytes 1572872 | tf_op jit(solution)/shard_map/ppermute | solution.py:202
  78.7 18.6 %all-to-all-start.2 = ((bf16[32,16,256]{2,1,0:T(8,128)(2,1)}), bf16[32,16,256]{2,1,0:T(8,128)(2,1)S(1)}, u32[]{:S(2)}, u32[]{:S(2)}) async-start(bf16[32,16,256]{2,1,0:T(8,128)(2,1)} %bitcast.6), calls=%async_computation.2 | async-start | bytes 524288 | tf_op jit(solution)/shard_map/all_to_all | solution.py:206
  98.1 17.2 %all-to-all-start.3 = ((bf16[32,16,256]{2,1,0:T(8,128)(2,1)}), bf16[32,16,256]{2,1,0:T(8,128)(2,1)S(1)}, u32[]{:S(2)}, u32[]{:S(2)}) async-start(bf16[32,16,256]{2,1,0:T(8,128)(2,1)} %shard_map.52), calls=%async_computation.3 | async-start | bytes 524288 | tf_op jit(solution)/shard_map/all_to_all | solution.py:206
  104.7 38.1 %collective-permute-start.2 = (bf16[512,512]{1,0:T(8,128)(2,1)S(1)}, bf16[512,512]{1,0:T(8,128)(2,1)S(1)}, u32[]{:S(2)}, u32[]{:S(2)}) collective-permute-start(bf16[512,512]{1,0:T(8,128)(2,1)S(1)} %get-tuple-element.38), channel_id=1, source_target_pairs={{0,32},{32,64},{64,96},{96,128},{128,160},{160,192},{192,224},{224... | collective-permute-start | bytes 1572872 | tf_op jit(solution)/shard_map/ppermute | solution.py:202
  119.5 25.8 %collective-permute-start.1 = (bf16[256,512]{1,0:T(8,128)(2,1)S(1)}, bf16[256,512]{1,0:T(8,128)(2,1)S(1)}, u32[]{:S(2)}, u32[]{:S(2)}) collective-permute-start(bf16[256,512]{1,0:T(8,128)(2,1)S(1)} %shard_map.53.y0), channel_id=1, source_target_pairs={{0,32},{32,64},{64,96},{96,128},{128,160},{160,192},{192,224},{224... | collective-permute-start | bytes 786440 | tf_op jit(solution)/shard_map/ppermute | solution.py:202
  121.4 53.2 %collective-permute-start.6 = (bf16[512,512]{1,0:T(8,128)(2,1)}, bf16[512,512]{1,0:T(8,128)(2,1)S(1)}, u32[]{:S(2)}, u32[]{:S(2)}) collective-permute-start(bf16[512,512]{1,0:T(8,128)(2,1)} %get-tuple-element.36), channel_id=1, source_target_pairs={{0,448},{32,480},{64,0},{96,32},{128,64},{160,96},{192,128},{224,1... | collective-permute-start | bytes 1572872 | tf_op jit(solution)/shard_map/ppermute | solution.py:202
  140.9 33.8 %collective-permute-start.5 = (bf16[512,512]{1,0:T(8,128)(2,1)}, bf16[512,512]{1,0:T(8,128)(2,1)}, u32[]{:S(2)}, u32[]{:S(2)}) collective-permute-start(bf16[512,512]{1,0:T(8,128)(2,1)} %get-tuple-element.37), channel_id=1, source_target_pairs={{0,64},{32,96},{64,128},{96,160},{128,192},{160,224},{192,256},{22... | collective-permute-start | bytes 1572872 | tf_op jit(solution)/shard_map/ppermute | solution.py:202
  146.7 23.0 %all-to-all-start.4 = ((f32[32,8,128]{2,1,0:T(8,128)}), f32[32,8,128]{2,1,0:T(8,128)S(1)}, u32[]{:S(2)}, u32[]{:S(2)}) async-start(f32[32,8,128]{2,1,0:T(8,128)} %get-tuple-element.23), calls=%async_computation.4 | async-start | bytes 262144 | tf_op jit(solution)/shard_map/all_to_all | solution.py:206
  153.4 21.2 %collective-permute-start.4 = (bf16[256,512]{1,0:T(8,128)(2,1)S(1)}, bf16[256,512]{1,0:T(8,128)(2,1)S(1)}, u32[]{:S(2)}, u32[]{:S(2)}) collective-permute-start(bf16[256,512]{1,0:T(8,128)(2,1)S(1)} %shard_map.53.y0), channel_id=1, source_target_pairs={{0,480},{32,0},{64,32},{96,64},{128,96},{160,128},{192,160},{224,1... | collective-permute-start | bytes 786440 | tf_op jit(solution)/shard_map/ppermute | solution.py:202
  155.4 19.2 %collective-permute-start.3 = (bf16[256,512]{1,0:T(8,128)(2,1)S(1)}, bf16[256,512]{1,0:T(8,128)(2,1)}, u32[]{:S(2)}, u32[]{:S(2)}) collective-permute-start(bf16[256,512]{1,0:T(8,128)(2,1)S(1)} %shard_map.53.y0), channel_id=1, source_target_pairs={{0,64},{32,96},{64,128},{96,160},{128,192},{160,224},{192,256},{22... | collective-permute-start | bytes 786440 | tf_op jit(solution)/shard_map/ppermute | solution.py:202
  169.8 0.6 copy-start.4
  170.4 12.1 %all-to-all-start.5 = ((f32[16,8,128]{2,1,0:T(8,128)}), f32[16,8,128]{2,1,0:T(8,128)S(1)}, u32[]{:S(2)}, u32[]{:S(2)}) async-start(f32[16,8,128]{2,1,0:T(8,128)} %copy-done.4), calls=%async_computation.5 | async-start | bytes 131072 | tf_op jit(solution)/shard_map/all_to_all | solution.py:206
  177.2 1.0 copy-start
  178.2 1.0 copy-start.2
  182.5 1.2 copy-start.1
  183.7 1.2 copy-start.3
  225.9 11.5 %collective-permute-start.7 = (bf16[256,512]{1,0:T(8,128)(2,1)S(1)}, bf16[256,512]{1,0:T(8,128)(2,1)S(1)}, u32[]{:S(2)}, u32[]{:S(2)}) collective-permute-start(bf16[256,512]{1,0:T(8,128)(2,1)S(1)} %shard_map.59.y0), channel_id=1, source_target_pairs={{0,32},{32,64},{64,96},{96,128},{128,160},{160,192},{192,224},{224... | collective-permute-start | bytes 786440 | tf_op jit(solution)/shard_map/ppermute | solution.py:202

commit v3 on v2

--- a/solution.py
+++ b/solution.py
@@ -17,7 +17,7 @@
 BF16 = jnp.bfloat16
 
 
-def call(kernel, outs, *args, smem=0, flops=0):
+def call(kernel, outs, *args, smem=0, flops=0, scratch=()):
     specs = [pl.BlockSpec(memory_space=pltpu.SMEM)] * smem
     specs += [pl.BlockSpec(memory_space=pltpu.VMEM)] * (len(args) - smem)
     single = not isinstance(outs, (tuple, list))
@@ -30,6 +30,7 @@
         out_shape=outs,
         in_specs=specs,
         out_specs=tuple(pl.BlockSpec(memory_space=pltpu.VMEM) for _ in outs),
+        scratch_shapes=list(scratch),
         compiler_params=pltpu.CompilerParams(vmem_limit_bytes=14 * 1024 * 1024),
         cost_estimate=pl.CostEstimate(flops=flops, bytes_accessed=moved, transcendentals=0),
     )(*args)
@@ -50,8 +51,19 @@
     out_ref[NB:, :] = (every[:NB, NB:] - every[NB:, :NB]).astype(out_ref.dtype)
 
 
-def margin_kernel(state_ref, next_ref, out_ref):
-    margin(state_ref[...], next_ref[...], out_ref)
+def choose(flag, yes_ref, no_ref, out_ref):
+    @pl.when(flag == 1)
+    def _():
+        out_ref[...] = yes_ref[...]
+
+    @pl.when(flag != 1)
+    def _():
+        out_ref[...] = no_ref[...]
+
+
+def margin_kernel(flags, state_ref, next_ref, closing_ref, out_ref, chosen_ref):
+    choose(flags[3], closing_ref, next_ref, chosen_ref)
+    margin(state_ref[...], chosen_ref[...], out_ref)
 
 
 def rotate_kernel(amount_ref, block_ref, out_ref, rolled_ref):
@@ -164,9 +176,9 @@
     return jnp.broadcast_to(part[None], (count, 8, 128))
 
 
-def sides_kernel(y_2, y_1, y0, y1, p_2, p0, p2, g_1, g1):
-    g_1[...] = slope(y_1[...], p0[...], y_2[...], p_2[...])
-    g1[...] = slope(y1[...], p2[...], y0[...], p0[...])
+def first_slope_kernel(flags, y_1, y0, p_1, closing, p1, g0, total_ref, chosen_ref):
+    choose(flags[0], closing, p_1, chosen_ref)
+    slope_kernel(y_1, y0, chosen_ref, p1, g0, total_ref)
 
 
 def slope_kernel(y_1, y0, p_1, p1, g0, total_ref):
@@ -181,14 +193,20 @@
     return TAU_STEP / jnp.sqrt(total / (2 * NK * NB * NPW) + EPS_NORM)
 
 
-def advance_kernel(total_ref, p_1, p0, p1, g_1, g0, g1, q_1, q0, q1, out_ref):
-    size = step_size(total_ref)
-    q_1[...] = (p_1[...].astype(F32) + size * g_1[...]).astype(BF16)
+def advance_kernel(
+    flags, total, y_2, y_1, y0, y1, p_2, p_1, p0, p1, p2, closing, g0, q_1, q0, q1, part, far
+):
+    size = step_size(total)
     here = (p0[...].astype(F32) + size * g0[...]).astype(BF16)
-    ahead = (p1[...].astype(F32) + size * g1[...]).astype(BF16)
     q0[...] = here
+    choose(flags[2], closing, p2, far)
+    grad = slope(y1[...], far[...], y0[...], p0[...])
+    ahead = (p1[...].astype(F32) + size * grad).astype(BF16)
     q1[...] = ahead
-    margin(here, ahead, out_ref)
+    margin(here, ahead, part)
+    choose(flags[1], closing, p_2, far)
+    grad = slope(y_1[...], p0[...], y_2[...], far[...])
+    q_1[...] = (p_1[...].astype(F32) + size * grad).astype(BF16)
 
 
 def finish_kernel(total_ref, p0, g0, re_ref, im_ref):
@@ -236,28 +254,39 @@
     margins = shape((full, NB), BF16)
     totals = shape((PARTS, 8, 128), F32)
 
+    flags = jnp.stack([row == 0, row <= 1, row >= NK - 2, row == NK - 1]).astype(jnp.int32)
+
     blocks = exchange(state, "pw").reshape(PARTS, full // PARTS, width)
-    turned = exchange(rotate(amount.reshape(1), blocks).reshape(full, width), "pw")
-
-    p1 = shifted(jnp.where(row == 0, turned, state), -1)
-    part = call(margin_kernel, margins, state, p1)
-    state, turned, part = lax.optimization_barrier((state, turned, part))
-    p_1 = shifted(jnp.where(row == NK - 1, turned, state), 1)
-    p2 = shifted(jnp.where(row <= 1, turned, state), -2)
-    p_2 = shifted(jnp.where(row >= NK - 2, turned, state), 2)
-
-    y0 = inverse(whole_margin(part))
+    p2, p_2 = shifted(state, -2), shifted(state, 2)
+    blocks, p2, p_2, state = lax.optimization_barrier((blocks, p2, p_2, state))
+    turned = rotate(amount.reshape(1), blocks).reshape(full, width)
+    turned, state = lax.optimization_barrier((turned, state))
+    turned = exchange(turned, "pw")
+    p1, p_1 = shifted(state, -1), shifted(state, 1)
+    turned, p1, p_1 = lax.optimization_barrier((turned, p1, p_1))
+
+    end = NK - 1
+    near = lax.ppermute(turned, "kstr", [(0, end), (end, 0)])
+    part, p1 = call(margin_kernel, (margins, fields), flags, state, p1, near, smem=1)
+    turned, part = lax.optimization_barrier((turned, part))
+    far = lax.ppermute(turned, "kstr", [(0, end - 1), (1, end), (end - 1, 0), (end, 1)])
+    whole, far = lax.optimization_barrier((whole_margin(part), far))
+
+    y0 = inverse(whole)
     y_1 = shifted(y0, 1)
-    g0, total = call(slope_kernel, (grads, totals), y_1, y0, p_1, p1)
+    g0, total, p_1 = call(
+        first_slope_kernel, (grads, totals, fields), flags, y_1, y0, p_1, near, p1, smem=1
+    )
     y0_later, total = lax.optimization_barrier((y0, total))
     y1 = shifted(y0_later, -1)
     y_2 = shifted(y0_later, 2)
     total = whole_total(total)
-    g_1, g1 = call(sides_kernel, (grads, grads), y_2, y_1, y0, y1, p_2, state, p2)
     q_1, q0, q1, part = call(
         advance_kernel,
         (fields, fields, fields, margins),
-        *(total, p_1, state, p1, g_1, g0, g1),
+        *(flags, total, y_2, y_1, y0, y1, p_2, p_1, state, p1, p2, far, g0),
+        smem=1,
+        scratch=(pltpu.VMEM((full, width), BF16),),
     )
 
     y0 = inverse(whole_margin(part))

time: 267 us -> 283 us (1.060)
  waiting for transfers between devices: 92.2 us -> 111 us
    ppermute x8, waiting for transfers between devices: 22.6 us -> 56.8 us  [shifted(): return lax.ppermute(value, 'kstr', [(i, (i + by) % NK) for i in range(NK)])]
    all_to_all x6, waiting for transfers between devices: 69.6 us -> 42.3 us  [exchange(): return lax.all_to_all(value, axis, 0, 0, tiled=True)]
    ppermute x8, starting transfers between devices: 39.2 us -> 23.2 us  [shifted(): return lax.ppermute(value, 'kstr', [(i, (i + by) % NK) for i in range(NK)])]
    ppermute x0 -> x2, waiting for transfers between devices: none -> 11.7 us  [the longest x1 11.7 us: body(): near = lax.ppermute(turned, 'kstr', [(0, end), (end, 0)])]
    all_to_all x6, starting transfers between devices: 40.3 us -> 48.4 us  [exchange(): return lax.all_to_all(value, axis, 0, 0, tiled=True)]
    ppermute x0 -> x2, starting transfers between devices: none -> 6.93 us  [the longest x1 5.01 us: body(): near = lax.ppermute(turned, 'kstr', [(0, end), (end, 0)])]
    pallas_call x12 -> x11, Pallas kernels: 19.1 us -> 19.8 us  [call(): pl.pallas_call(kernel, out_shape=outs, in_specs=specs, out_specs=tuple((p...]
  transfers between devices with their start and end apart: 14 -> 16, of which waited for: 9 -> 11; matrix products, arithmetic and copies ran while one was open for 1% -> 0% of each run, Pallas kernels for 3% -> 1%
where the time goes in v3:
time: 283 us; the launch traced here: 282 us
  waiting for transfers between devices  111 us (39%)
  starting transfers between devices  78.5 us (28%)
  blocking collectives  60.6 us (21%)
  Pallas kernels  21.5 us (8%)
  local copies, waits for them, and re-layouts  6.77 us (2%)
    all_to_all x4, blocking collectives, exchange(): return lax.all_to_all(value, axis, 0, 0, tiled=True)  60.6 us
    ppermute x8, waiting for transfers between devices, shifted(): return lax.ppermute(value, 'kstr', [(i, (i + by) % NK) for i in range(NK)])  56.8 us
    all_to_all x6, starting transfers between devices, exchange(): return lax.all_to_all(value, axis, 0, 0, tiled=True)  48.4 us
    all_to_all x6, waiting for transfers between devices, exchange(): return lax.all_to_all(value, axis, 0, 0, tiled=True)  42.3 us
    ppermute x8, starting transfers between devices, shifted(): return lax.ppermute(value, 'kstr', [(i, (i + by) % NK) for i in range(NK)])  23.2 us
    pallas_call x11, Pallas kernels, call(): pl.pallas_call(kernel, out_shape=outs, in_specs=specs, out_specs=tuple((p...  19.8 us
    ppermute x1, waiting for transfers between devices, body(): near = lax.ppermute(turned, 'kstr', [(0, end), (end, 0)])  11.7 us
  transfers between devices with their start and end apart: 16, of which 11 were waited for; matrix products, arithmetic and copies ran while one was open for 0% of the time, Pallas kernels for 1%

profile of v3, /device:TPU:1, one launch (start us, length us, event | category | flops | bytes accessed | tf_op | source)
XLA Modules:
  0.0 281.7 jit_solution(6778512399515531261)
XLA Ops:
  0.6 1.9 pad_maximum_fusion.state_ref.p0
  2.5 14.4 %all-to-all-start = ((bf16[32,16,512]{2,1,0:T(8,128)(2,1)}), bf16[32,16,512]{2,1,0:T(8,128)(2,1)S(1)}, u32[]{:S(2)}, u32[]{:S(2)}) async-start(bf16[32,16,512]{2,1,0:T(8,128)(2,1)} %bitcast.8), calls=%async_computation | async-start | bytes 1048576 | tf_op jit(solution)/shard_map/all_to_all | solution.py:224
  16.9 3.2 %collective-permute-start.1 = (bf16[512,512]{1,0:T(8,128)(2,1)}, bf16[512,512]{1,0:T(8,128)(2,1)S(1)}, u32[]{:S(2)}, u32[]{:S(2)}) collective-permute-start(bf16[512,512]{1,0:T(8,128)(2,1)} %pad_maximum_fusion.state_ref.p0), channel_id=1, source_target_pairs={{0,64},{32,96},{64,128},{96,160},{128,192},{160,224},{192,256},{22... | collective-permute-start | bytes 1572872 | tf_op jit(solution)/shard_map/ppermute | solution.py:220
  20.1 3.8 %collective-permute-start = (bf16[512,512]{1,0:T(8,128)(2,1)}, bf16[512,512]{1,0:T(8,128)(2,1)S(1)}, u32[]{:S(2)}, u32[]{:S(2)}) collective-permute-start(bf16[512,512]{1,0:T(8,128)(2,1)} %pad_maximum_fusion.state_ref.p0), channel_id=1, source_target_pairs={{0,448},{32,480},{64,0},{96,32},{128,64},{160,96},{192,128},{224,1... | collective-permute-start | bytes 1572872 | tf_op jit(solution)/shard_map/ppermute | solution.py:220
  24.0 1.2 slice.3
  25.8 8.5 %collective-permute-done.1.p_2 = bf16[512,512]{1,0:T(8,128)(2,1)S(1)} collective-permute-done((bf16[512,512]{1,0:T(8,128)(2,1)}, bf16[512,512]{1,0:T(8,128)(2,1)S(1)}, u32[]{:S(2)}, u32[]{:S(2)}) %collective-permute-start.1) | collective-permute-done | bytes 524320 | tf_op jit(solution)/shard_map/ppermute | solution.py:220
  34.4 1.0 collective-permute-done.p2
  35.3 1.7 shard_map.50
  37.1 10.7 %all-to-all-start.1 = ((bf16[32,16,512]{2,1,0:T(8,128)(2,1)}), bf16[32,16,512]{2,1,0:T(8,128)(2,1)S(1)}, u32[]{:S(2)}, u32[]{:S(2)}) async-start(bf16[32,16,512]{2,1,0:T(8,128)(2,1)} %bitcast.10), calls=%async_computation.1 | async-start | bytes 1048576 | tf_op jit(solution)/shard_map/all_to_all | solution.py:224
  47.7 3.1 %collective-permute-start.3 = (bf16[512,512]{1,0:T(8,128)(2,1)}, bf16[512,512]{1,0:T(8,128)(2,1)S(1)}, u32[]{:S(2)}, u32[]{:S(2)}) collective-permute-start(bf16[512,512]{1,0:T(8,128)(2,1)} %pad_maximum_fusion.state_ref.p0), channel_id=1, source_target_pairs={{0,32},{32,64},{64,96},{96,128},{128,160},{160,192},{192,224},{224... | collective-permute-start | bytes 1572872 | tf_op jit(solution)/shard_map/ppermute | solution.py:220
  50.9 4.8 %collective-permute-start.2 = (bf16[512,512]{1,0:T(8,128)(2,1)}, bf16[512,512]{1,0:T(8,128)(2,1)S(1)}, u32[]{:S(2)}, u32[]{:S(2)}) collective-permute-start(bf16[512,512]{1,0:T(8,128)(2,1)} %pad_maximum_fusion.state_ref.p0), channel_id=1, source_target_pairs={{0,480},{32,0},{64,32},{96,64},{128,96},{160,128},{192,160},{224,1... | collective-permute-start | bytes 1572872 | tf_op jit(solution)/shard_map/ppermute | solution.py:220
  55.6 26.3 %collective-permute-done.3.p_1 = bf16[512,512]{1,0:T(8,128)(2,1)S(1)} collective-permute-done((bf16[512,512]{1,0:T(8,128)(2,1)}, bf16[512,512]{1,0:T(8,128)(2,1)S(1)}, u32[]{:S(2)}, u32[]{:S(2)}) %collective-permute-start.3) | collective-permute-done | bytes 524320 | tf_op jit(solution)/shard_map/ppermute | solution.py:220
  81.9 1.8 collective-permute-done.2.next_ref
  83.7 5.0 %collective-permute-start.4 = (bf16[512,512]{1,0:T(8,128)(2,1)S(1)}, bf16[512,512]{1,0:T(8,128)(2,1)S(1)}, u32[]{:S(2)}, u32[]{:S(2)}) collective-permute-start(bf16[512,512]{1,0:T(8,128)(2,1)S(1)} %bitcast.21), channel_id=1, source_target_pairs={{0,480},{480,0},{1,481},{481,1},{2,482},{482,2},{3,483},{483,3},{4... | collective-permute-start | bytes 1572872 | tf_op jit(solution)/shard_map/ppermute | solution.py:269
  88.8 11.7 %collective-permute-done.4.closing_ref.closing = bf16[512,512]{1,0:T(8,128)(2,1)S(1)} collective-permute-done((bf16[512,512]{1,0:T(8,128)(2,1)S(1)}, bf16[512,512]{1,0:T(8,128)(2,1)S(1)}, u32[]{:S(2)}, u32[]{:S(2)}) %collective-permute-start.4) | collective-permute-done | bytes 524320 | tf_op jit(solution)/shard_map/ppermute | solution.py:269
  100.5 2.3 shard_map.51
  102.8 10.5 %all-to-all-start.2 = ((bf16[32,16,256]{2,1,0:T(8,128)(2,1)}), bf16[32,16,256]{2,1,0:T(8,128)(2,1)S(1)}, u32[]{:S(2)}, u32[]{:S(2)}) async-start(bf16[32,16,256]{2,1,0:T(8,128)(2,1)} %bitcast.12), calls=%async_computation.2 | async-start | bytes 524288 | tf_op jit(solution)/shard_map/all_to_all | solution.py:224
  113.3 1.9 collective-permute-start.5
  115.2 10.5 %all-to-all-done.2.parts_ref = bf16[32,16,256]{2,1,0:T(8,128)(2,1)S(1)} async-done(((bf16[32,16,256]{2,1,0:T(8,128)(2,1)}), bf16[32,16,256]{2,1,0:T(8,128)(2,1)S(1)}, u32[]{:S(2)}, u32[]{:S(2)}) %all-to-all-start.2) | async-done | bytes 262176 | tf_op jit(solution)/shard_map/all_to_all | solution.py:224
  125.8 0.8 shard_map.52
  126.5 3.9 %all-to-all-start.3 = ((bf16[32,16,256]{2,1,0:T(8,128)(2,1)}), bf16[32,16,256]{2,1,0:T(8,128)(2,1)S(1)}, u32[]{:S(2)}, u32[]{:S(2)}) async-start(bf16[32,16,256]{2,1,0:T(8,128)(2,1)} %shard_map.52), calls=%async_computation.3 | async-start | bytes 524288 | tf_op jit(solution)/shard_map/all_to_all | solution.py:224
  130.5 12.8 %all-to-all-done.3 = bf16[32,16,256]{2,1,0:T(8,128)(2,1)S(1)} async-done(((bf16[32,16,256]{2,1,0:T(8,128)(2,1)}), bf16[32,16,256]{2,1,0:T(8,128)(2,1)S(1)}, u32[]{:S(2)}, u32[]{:S(2)}) %all-to-all-start.3) | async-done | bytes 262176 | tf_op jit(solution)/shard_map/all_to_all | solution.py:224
  143.3 4.2 %shard_map.53.y0 = bf16[256,512]{1,0:T(8,128)(2,1)S(1)} custom-call(bf16[512,256]{1,0:T(8,128)(2,1)S(1)} %bitcast.18), custom_call_target="tpu_custom_call" | custom-call | bytes 524288 | tf_op jit(solution)/shard_map/pallas_call | solution.py:28
  147.4 1.9 collective-permute-start.6
  149.4 9.6 %collective-permute-done.6.y_1 = bf16[256,512]{1,0:T(8,128)(2,1)S(1)} collective-permute-done((bf16[256,512]{1,0:T(8,128)(2,1)S(1)}, bf16[256,512]{1,0:T(8,128)(2,1)S(1)}, u32[]{:S(2)}, u32[]{:S(2)}) %collective-permute-start.6) | collective-permute-done | bytes 262176 | tf_op jit(solution)/shard_map/ppermute | solution.py:220
  159.0 2.0 shard_map.54
  161.0 0.8 copy-done.6
  161.8 5.3 %all-to-all-start.4 = ((f32[32,8,128]{2,1,0:T(8,128)}), f32[32,8,128]{2,1,0:T(8,128)S(1)}, u32[]{:S(2)}, u32[]{:S(2)}) async-start(f32[32,8,128]{2,1,0:T(8,128)} %get-tuple-element.43), calls=%async_computation.4 | async-start | bytes 262144 | tf_op jit(solution)/shard_map/all_to_all | solution.py:224
  167.1 2.6 collective-permute-start.8
  169.7 1.9 collective-permute-start.7
  171.6 11.8 %all-to-all-done.4.parts_ref = f32[32,8,128]{2,1,0:T(8,128)S(1)} async-done(((f32[32,8,128]{2,1,0:T(8,128)}), f32[32,8,128]{2,1,0:T(8,128)S(1)}, u32[]{:S(2)}, u32[]{:S(2)}) %all-to-all-start.4) | async-done | bytes 131104 | tf_op jit(solution)/shard_map/all_to_all | solution.py:224
  184.1 3.5 %all-to-all-start.5 = ((f32[16,8,128]{2,1,0:T(8,128)}), f32[16,8,128]{2,1,0:T(8,128)S(1)}, u32[]{:S(2)}, u32[]{:S(2)}) async-start(f32[16,8,128]{2,1,0:T(8,128)} %shard_map.55), calls=%async_computation.5 | async-start | bytes 131072 | tf_op jit(solution)/shard_map/all_to_all | solution.py:224
  187.6 0.7 copy-done.8
  188.3 7.2 %all-to-all-done.5.total = f32[16,8,128]{2,1,0:T(8,128)S(1)} async-done(((f32[16,8,128]{2,1,0:T(8,128)}), f32[16,8,128]{2,1,0:T(8,128)S(1)}, u32[]{:S(2)}, u32[]{:S(2)}) %all-to-all-start.5) | async-done | bytes 65568 | tf_op jit(solution)/shard_map/all_to_all | solution.py:224
  195.5 1.0 copy-done.3
  196.6 1.0 copy-done.5
  197.6 1.0 copy-done.7
  198.6 0.9 copy-done.9
  199.6 3.9 %shard_map.56 = (bf16[512,512]{1,0:T(8,128)(2,1)S(1)}, bf16[512,512]{1,0:T(8,128)(2,1)S(1)}, bf16[512,512]{1,0:T(8,128)(2,1)S(1)}, bf16[512,256]{1,0:T(8,128)(2,1)S(1)}) custom-call(s32[4]{0:T(128)S(1)} %add_convert_fusion.flags, f32[16,8,128]{2,1,0:T(8,128)S(1)} %all-to-all-done.5.total, bf16[256,512]{1,0:T(8,128)(2,1)S(1)} %copy-done.9, ...), custom_call_target="tpu_custom_call" | custom-call | bytes 7143440 | tf_op jit(solution)/shard_map/pallas_call | solution.py:28
  203.4 17.4 %all_to_all.76.parts_ref = bf16[32,16,256]{2,1,0:T(8,128)(2,1)S(1)} all-to-all(bf16[32,16,256]{2,1,0:T(8,128)(2,1)S(1)} %bitcast.20), channel_id=1, replica_groups=mesh['kstr'=16,'pw'=32] {'pw'}, dimensions={0} | all-to-all | bytes 524288 | tf_op jit(solution)/shard_map/all_to_all | solution.py:224
  220.9 17.2 %all_to_all.77 = bf16[32,16,256]{2,1,0:T(8,128)(2,1)S(1)} all-to-all(bf16[32,16,256]{2,1,0:T(8,128)(2,1)S(1)} %shard_map.57), channel_id=1, replica_groups=mesh['kstr'=16,'pw'=32] {'pw'}, dimensions={0} | all-to-all | bytes 524288 | tf_op jit(solution)/shard_map/all_to_all | solution.py:224
  238.0 4.2 %shard_map.58.y0 = bf16[256,512]{1,0:T(8,128)(2,1)S(1)} custom-call(bf16[512,256]{1,0:T(8,128)(2,1)S(1)} %bitcast.19), custom_call_target="tpu_custom_call" | custom-call | bytes 524288 | tf_op jit(solution)/shard_map/pallas_call | solution.py:28
  242.2 1.9 collective-permute-start.9
  244.1 9.6 %collective-permute-done.9.y_1 = bf16[256,512]{1,0:T(8,128)(2,1)S(1)} collective-permute-done((bf16[256,512]{1,0:T(8,128)(2,1)S(1)}, bf16[256,512]{1,0:T(8,128)(2,1)S(1)}, u32[]{:S(2)}, u32[]{:S(2)}) %collective-permute-start.9) | collective-permute-done | bytes 262176 | tf_op jit(solution)/shard_map/ppermute | solution.py:220
  253.7 0.7 shard_map.59
  254.5 15.6 %all_to_all.78.parts_ref = f32[32,8,128]{2,1,0:T(8,128)S(1)} all-to-all(f32[32,8,128]{2,1,0:T(8,128)S(1)} %get-tuple-element.53), channel_id=1, replica_groups=mesh['kstr'=16,'pw'=32] {'pw'}, dimensions={0} | all-to-all | bytes 262144 | tf_op jit(solution)/shard_map/all_to_all | solution.py:224
  270.1 10.5 %all_to_all.79.total_ref = f32[16,8,128]{2,1,0:T(8,128)S(1)} all-to-all(f32[16,8,128]{2,1,0:T(8,128)S(1)} %shard_map.60), channel_id=1, replica_groups=mesh['kstr'=16,'pw'=32] {'kstr'}, dimensions={0} | all-to-all | bytes 131072 | tf_op jit(solution)/shard_map/all_to_all | solution.py:224
  280.6 1.1 shard_map.61
  (23 shorter events, 0.9 us)
Async XLA Ops:
  2.5 32.9 %all-to-all-start = ((bf16[32,16,512]{2,1,0:T(8,128)(2,1)}), bf16[32,16,512]{2,1,0:T(8,128)(2,1)S(1)}, u32[]{:S(2)}, u32[]{:S(2)}) async-start(bf16[32,16,512]{2,1,0:T(8,128)(2,1)} %bitcast.8), calls=%async_computation | async-start | bytes 1048576 | tf_op jit(solution)/shard_map/all_to_all | solution.py:224
  16.9 17.4 %collective-permute-start.1 = (bf16[512,512]{1,0:T(8,128)(2,1)}, bf16[512,512]{1,0:T(8,128)(2,1)S(1)}, u32[]{:S(2)}, u32[]{:S(2)}) collective-permute-start(bf16[512,512]{1,0:T(8,128)(2,1)} %pad_maximum_fusion.state_ref.p0), channel_id=1, source_target_pairs={{0,64},{32,96},{64,128},{96,160},{128,192},{160,224},{192,256},{22... | collective-permute-start | bytes 1572872 | tf_op jit(solution)/shard_map/ppermute | solution.py:220
  20.1 15.2 %collective-permute-start = (bf16[512,512]{1,0:T(8,128)(2,1)}, bf16[512,512]{1,0:T(8,128)(2,1)S(1)}, u32[]{:S(2)}, u32[]{:S(2)}) collective-permute-start(bf16[512,512]{1,0:T(8,128)(2,1)} %pad_maximum_fusion.state_ref.p0), channel_id=1, source_target_pairs={{0,448},{32,480},{64,0},{96,32},{128,64},{160,96},{192,128},{224,1... | collective-permute-start | bytes 1572872 | tf_op jit(solution)/shard_map/ppermute | solution.py:220
  34.4 2.7 copy-start
  35.3 1.7 copy-start.2
  37.1 46.7 %all-to-all-start.1 = ((bf16[32,16,512]{2,1,0:T(8,128)(2,1)}), bf16[32,16,512]{2,1,0:T(8,128)(2,1)S(1)}, u32[]{:S(2)}, u32[]{:S(2)}) async-start(bf16[32,16,512]{2,1,0:T(8,128)(2,1)} %bitcast.10), calls=%async_computation.1 | async-start | bytes 1048576 | tf_op jit(solution)/shard_map/all_to_all | solution.py:224
  47.7 34.2 %collective-permute-start.3 = (bf16[512,512]{1,0:T(8,128)(2,1)}, bf16[512,512]{1,0:T(8,128)(2,1)S(1)}, u32[]{:S(2)}, u32[]{:S(2)}) collective-permute-start(bf16[512,512]{1,0:T(8,128)(2,1)} %pad_maximum_fusion.state_ref.p0), channel_id=1, source_target_pairs={{0,32},{32,64},{64,96},{96,128},{128,160},{160,192},{192,224},{224... | collective-permute-start | bytes 1572872 | tf_op jit(solution)/shard_map/ppermute | solution.py:220
  50.9 32.9 %collective-permute-start.2 = (bf16[512,512]{1,0:T(8,128)(2,1)}, bf16[512,512]{1,0:T(8,128)(2,1)S(1)}, u32[]{:S(2)}, u32[]{:S(2)}) collective-permute-start(bf16[512,512]{1,0:T(8,128)(2,1)} %pad_maximum_fusion.state_ref.p0), channel_id=1, source_target_pairs={{0,480},{32,0},{64,32},{96,64},{128,96},{160,128},{192,160},{224,1... | collective-permute-start | bytes 1572872 | tf_op jit(solution)/shard_map/ppermute | solution.py:220
  83.7 16.8 %collective-permute-start.4 = (bf16[512,512]{1,0:T(8,128)(2,1)S(1)}, bf16[512,512]{1,0:T(8,128)(2,1)S(1)}, u32[]{:S(2)}, u32[]{:S(2)}) collective-permute-start(bf16[512,512]{1,0:T(8,128)(2,1)S(1)} %bitcast.21), channel_id=1, source_target_pairs={{0,480},{480,0},{1,481},{481,1},{2,482},{482,2},{3,483},{483,3},{4... | collective-permute-start | bytes 1572872 | tf_op jit(solution)/shard_map/ppermute | solution.py:269
  102.8 23.0 %all-to-all-start.2 = ((bf16[32,16,256]{2,1,0:T(8,128)(2,1)}), bf16[32,16,256]{2,1,0:T(8,128)(2,1)S(1)}, u32[]{:S(2)}, u32[]{:S(2)}) async-start(bf16[32,16,256]{2,1,0:T(8,128)(2,1)} %bitcast.12), calls=%async_computation.2 | async-start | bytes 524288 | tf_op jit(solution)/shard_map/all_to_all | solution.py:224
  113.3 17.1 %collective-permute-start.5 = (bf16[512,512]{1,0:T(8,128)(2,1)S(1)}, bf16[512,512]{1,0:T(8,128)(2,1)S(1)}, u32[]{:S(2)}, u32[]{:S(2)}) collective-permute-start(bf16[512,512]{1,0:T(8,128)(2,1)S(1)} %bitcast.22), channel_id=1, source_target_pairs={{0,448},{32,480},{448,0},{480,32},{1,449},{33,481},{449,1},{481,33... | collective-permute-start | bytes 1572872 | tf_op jit(solution)/shard_map/ppermute | solution.py:272
  126.5 16.8 %all-to-all-start.3 = ((bf16[32,16,256]{2,1,0:T(8,128)(2,1)}), bf16[32,16,256]{2,1,0:T(8,128)(2,1)S(1)}, u32[]{:S(2)}, u32[]{:S(2)}) async-start(bf16[32,16,256]{2,1,0:T(8,128)(2,1)} %shard_map.52), calls=%async_computation.3 | async-start | bytes 524288 | tf_op jit(solution)/shard_map/all_to_all | solution.py:224
  130.5 28.5 %copy-start.4 = (bf16[512,512]{1,0:T(8,128)(2,1)}, bf16[512,512]{1,0:T(8,128)(2,1)S(1)}, u32[]{:S(2)}) copy-start(bf16[512,512]{1,0:T(8,128)(2,1)S(1)} %collective-permute-done.5.closing) | copy-start | bytes 1572868
  147.4 11.5 %collective-permute-start.6 = (bf16[256,512]{1,0:T(8,128)(2,1)S(1)}, bf16[256,512]{1,0:T(8,128)(2,1)S(1)}, u32[]{:S(2)}, u32[]{:S(2)}) collective-permute-start(bf16[256,512]{1,0:T(8,128)(2,1)S(1)} %shard_map.53.y0), channel_id=1, source_target_pairs={{0,32},{32,64},{64,96},{96,128},{128,160},{160,192},{192,224},{224... | collective-permute-start | bytes 786440 | tf_op jit(solution)/shard_map/ppermute | solution.py:220
  161.0 0.8 copy-start.6
  161.8 33.7 %copy-start.1 = (bf16[512,512]{1,0:T(8,128)(2,1)S(1)}, bf16[512,512]{1,0:T(8,128)(2,1)}, u32[]{:S(2)}) copy-start(bf16[512,512]{1,0:T(8,128)(2,1)} %copy-done) | copy-start | bytes 1572868
  161.8 21.7 %all-to-all-start.4 = ((f32[32,8,128]{2,1,0:T(8,128)}), f32[32,8,128]{2,1,0:T(8,128)S(1)}, u32[]{:S(2)}, u32[]{:S(2)}) async-start(f32[32,8,128]{2,1,0:T(8,128)} %get-tuple-element.43), calls=%async_computation.4 | async-start | bytes 262144 | tf_op jit(solution)/shard_map/all_to_all | solution.py:224
  167.1 20.5 %collective-permute-start.8 = (bf16[256,512]{1,0:T(8,128)(2,1)S(1)}, bf16[256,512]{1,0:T(8,128)(2,1)S(1)}, u32[]{:S(2)}, u32[]{:S(2)}) collective-permute-start(bf16[256,512]{1,0:T(8,128)(2,1)S(1)} %shard_map.53.y0), channel_id=1, source_target_pairs={{0,480},{32,0},{64,32},{96,64},{128,96},{160,128},{192,160},{224,1... | collective-permute-start | bytes 786440 | tf_op jit(solution)/shard_map/ppermute | solution.py:220
  169.7 17.9 %collective-permute-start.7 = (bf16[256,512]{1,0:T(8,128)(2,1)S(1)}, bf16[256,512]{1,0:T(8,128)(2,1)S(1)}, u32[]{:S(2)}, u32[]{:S(2)}) collective-permute-start(bf16[256,512]{1,0:T(8,128)(2,1)S(1)} %shard_map.53.y0), channel_id=1, source_target_pairs={{0,64},{32,96},{64,128},{96,160},{128,192},{160,224},{192,256},{22... | collective-permute-start | bytes 786440 | tf_op jit(solution)/shard_map/ppermute | solution.py:220
  184.1 11.4 %all-to-all-start.5 = ((f32[16,8,128]{2,1,0:T(8,128)}), f32[16,8,128]{2,1,0:T(8,128)S(1)}, u32[]{:S(2)}, u32[]{:S(2)}) async-start(f32[16,8,128]{2,1,0:T(8,128)} %shard_map.55), calls=%async_computation.5 | async-start | bytes 131072 | tf_op jit(solution)/shard_map/all_to_all | solution.py:224
  187.6 0.7 copy-start.8
  195.5 1.0 copy-start.3
  196.6 1.0 copy-start.5
  197.6 1.0 copy-start.7
  198.6 0.9 copy-start.9
  242.2 11.5 %collective-permute-start.9 = (bf16[256,512]{1,0:T(8,128)(2,1)S(1)}, bf16[256,512]{1,0:T(8,128)(2,1)S(1)}, u32[]{:S(2)}, u32[]{:S(2)}) collective-permute-start(bf16[256,512]{1,0:T(8,128)(2,1)S(1)} %shard_map.58.y0), channel_id=1, source_target_pairs={{0,32},{32,64},{64,96},{96,128},{128,160},{160,192},{192,224},{224... | collective-permute-start | bytes 786440 | tf_op jit(solution)/shard_map/ppermute | solution.py:220

commit v4 on v3

--- a/solution.py
+++ b/solution.py
@@ -10,6 +10,7 @@
 NPW = 16384
 NB = 256
 PARTS = 32
+CHUNK = 2 * NB // PARTS
 EPS_SCALE = 1e-06
 EPS_NORM = 1e-06
 TAU_STEP = 0.25
@@ -45,10 +46,10 @@
     return jnp.dot(left, right, preferred_element_type=F32)
 
 
-def margin(left, right, out_ref):
+def margin(left, right):
     every = lax.dot_general(left, right, (((1,), (1,)), ((), ())), preferred_element_type=F32)
-    out_ref[:NB, :] = (every[:NB, :NB] + every[NB:, NB:]).astype(out_ref.dtype)
-    out_ref[NB:, :] = (every[:NB, NB:] - every[NB:, :NB]).astype(out_ref.dtype)
+    real = every[:NB, :NB] + every[NB:, NB:]
+    return jnp.concatenate([real, every[:NB, NB:] - every[NB:, :NB]], 0)
 
 
 def choose(flag, yes_ref, no_ref, out_ref):
@@ -61,9 +62,8 @@
         out_ref[...] = no_ref[...]
 
 
-def margin_kernel(flags, state_ref, next_ref, closing_ref, out_ref, chosen_ref):
-    choose(flags[3], closing_ref, next_ref, chosen_ref)
-    margin(state_ref[...], chosen_ref[...], out_ref)
+def margin_kernel(state_ref, next_ref, out_ref):
+    out_ref[...] = margin(state_ref[...], next_ref[...]).astype(BF16)
 
 
 def rotate_kernel(amount_ref, block_ref, out_ref, rolled_ref):
@@ -104,9 +104,26 @@
     )(amount, block)
 
 
-def collect_kernel(parts_ref, out_ref):
+def collect_kernel(parts_ref, out_ref, kept_ref):
     total = jnp.sum(parts_ref[...].astype(F32), axis=0) * (1.0 / NPW)
-    out_ref[...] = jnp.broadcast_to(total.astype(out_ref.dtype)[None], out_ref.shape)
+    kept_ref[...] = total
+    out_ref[...] = jnp.broadcast_to(total.astype(BF16)[None], out_ref.shape)
+
+
+def collect_orders_kernel(parts_ref, first_ref, second_ref, squares_ref):
+    total = jnp.sum(parts_ref[...].astype(F32), axis=0)
+    for half in range(2):
+        lanes = pl.ds(128 * half, 128)
+        first_ref[:, lanes] = total[CHUNK * half : CHUNK * (half + 1)] * (1.0 / NPW)
+        second_ref[:, lanes] = total[CHUNK * (2 + half) : CHUNK * (3 + half)] * (1.0 / NPW)
+    part = total[4 * CHUNK : 4 * CHUNK + 8] + total[4 * CHUNK + 8 :]
+    squares_ref[...] = jnp.broadcast_to(part[None], squares_ref.shape)
+
+
+def combine_kernel(total_ref, kept_ref, first_ref, second_ref, out_ref):
+    size = step_size(total_ref)
+    value = kept_ref[...] + size * (first_ref[...] + size * second_ref[...])
+    out_ref[...] = jnp.broadcast_to(value.astype(BF16)[None], out_ref.shape)
 
 
 def spread_kernel(parts_ref, out_ref):
@@ -132,7 +149,8 @@
     iterate = jnp.concatenate([real * factor, imag * factor], 1)
 
     for turn in range(NEWTON):
-        parts = pieces(iterate, 2)
+        terms = 1 if turn < NEWTON // 2 else 2
+        parts = pieces(iterate, terms)
         product = None
         for part in parts:
             crossed = jnp.concatenate([part[:, NB:], -part[:, :NB]], 1)
@@ -141,13 +159,13 @@
                 stacked, right, (((0,), (0,)), ((), ())), preferred_element_type=F32
             )
             product = term if product is None else product + term
-        seconds = pieces(product, 2)
+        seconds = pieces(product, terms)
         change = None
         for j, second in enumerate(seconds):
             crossed = jnp.concatenate([-second[:, NB:], second[:, :NB]], 1)
             right = jnp.concatenate([second, crossed], 0)
             for i, part in enumerate(parts):
-                if i + j < 2:
+                if i + j < terms:
                     term = dot(part, right)
                     change = term if change is None else change + term
         iterate = 2.0 * iterate - change
@@ -166,25 +184,40 @@
     return dot(forward, following) - dot(backward, before).astype(BF16).astype(F32)
 
 
-def squares(grad, count):
+def squares(grad):
     part = grad[0:8]
     part = part * part
     for row in range(8, grad.shape[0], 8):
         more = grad[row : row + 8]
         part = part + more * more
-    part = part[:, 0:128] + part[:, 128:256] + part[:, 256:384] + part[:, 384:512]
-    return jnp.broadcast_to(part[None], (count, 8, 128))
-
-
-def first_slope_kernel(flags, y_1, y0, p_1, closing, p1, g0, total_ref, chosen_ref):
-    choose(flags[0], closing, p_1, chosen_ref)
-    slope_kernel(y_1, y0, chosen_ref, p1, g0, total_ref)
+    return part[:, 0:128] + part[:, 128:256] + part[:, 256:384] + part[:, 384:512]
+
+
+def orders_kernel(flags, y_1, y0, y1, p_1, p0, p1, p2, closing, g0, g1, out_ref, far):
+    grad = slope(y0[...], p1[...], y_1[...], p_1[...])
+    g0[...] = grad
+    part = squares(grad)
+    high = part.astype(BF16).astype(F32)
+    pair = jnp.concatenate([high, part - high], 0).astype(BF16)
+    here = grad.astype(BF16)
+    choose(flags[2], closing, p2, far)
+    ahead = slope(y1[...], far[...], y0[...], p0[...]).astype(BF16)
+    g1[...] = ahead
+    first = (margin(here, p1[...]) + margin(p0[...], ahead)).astype(BF16)
+    second = margin(here, ahead).astype(BF16)
+    for part in range(PARTS):
+        rows = slice(CHUNK * part, CHUNK * (part + 1))
+        for index, value in enumerate((first, second)):
+            for half in range(2):
+                at = pl.ds(CHUNK * (2 * index + half), CHUNK)
+                out_ref[part, at, :] = value[rows, 128 * half : 128 * (half + 1)]
+        out_ref[part, pl.ds(4 * CHUNK, CHUNK), :] = pair
 
 
 def slope_kernel(y_1, y0, p_1, p1, g0, total_ref):
     grad = slope(y0[...], p1[...], y_1[...], p_1[...])
     g0[...] = grad
-    total_ref[...] = squares(grad, PARTS)
+    total_ref[...] = jnp.broadcast_to(squares(grad)[None], total_ref.shape)
 
 
 def step_size(total_ref):
@@ -193,17 +226,10 @@
     return TAU_STEP / jnp.sqrt(total / (2 * NK * NB * NPW) + EPS_NORM)
 
 
-def advance_kernel(
-    flags, total, y_2, y_1, y0, y1, p_2, p_1, p0, p1, p2, closing, g0, q_1, q0, q1, part, far
-):
+def advance_kernel(flags, total, y_2, y_1, p_2, p_1, p0, p1, closing, g0, g1, q_1, q0, q1, far):
     size = step_size(total)
-    here = (p0[...].astype(F32) + size * g0[...]).astype(BF16)
-    q0[...] = here
-    choose(flags[2], closing, p2, far)
-    grad = slope(y1[...], far[...], y0[...], p0[...])
-    ahead = (p1[...].astype(F32) + size * grad).astype(BF16)
-    q1[...] = ahead
-    margin(here, ahead, part)
+    q0[...] = (p0[...].astype(F32) + size * g0[...]).astype(BF16)
+    q1[...] = (p1[...].astype(F32) + size * g1[...].astype(F32)).astype(BF16)
     choose(flags[1], closing, p_2, far)
     grad = slope(y_1[...], p0[...], y_2[...], far[...])
     q_1[...] = (p_1[...].astype(F32) + size * grad).astype(BF16)
@@ -222,13 +248,6 @@
 
 def exchange(value, axis):
     return lax.all_to_all(value, axis, 0, 0, tiled=True)
-
-
-def whole_margin(part):
-    rows = 2 * NB // PARTS
-    parts = exchange(part, "pw").reshape(PARTS, rows, NB)
-    own = call(collect_kernel, shape((PARTS, rows, NB), BF16), parts)
-    return exchange(own.reshape(2 * NB, NB), "pw")
 
 
 def whole_total(part):
@@ -248,50 +267,61 @@
     amount = jnp.where(row < NK // 2, offset, NPW - offset).astype(jnp.int32)
     state = jnp.concatenate([states_re[0], states_im[0]], 0)
     full = 2 * NB
+    end = NK - 1
     duals = shape((NB, full), BF16)
     fields = shape((full, width), BF16)
     grads = shape((full, width), F32)
-    margins = shape((full, NB), BF16)
-    totals = shape((PARTS, 8, 128), F32)
-
-    flags = jnp.stack([row == 0, row <= 1, row >= NK - 2, row == NK - 1]).astype(jnp.int32)
-
-    blocks = exchange(state, "pw").reshape(PARTS, full // PARTS, width)
+    chunk = shape((CHUNK, NB), F32)
+    chunks = shape((PARTS, CHUNK, NB), BF16)
+    far_scratch = (pltpu.VMEM((full, width), BF16),)
+    flags = jnp.stack([row == 0, row <= 1, row >= NK - 2, row == end]).astype(jnp.int32)
+
+    blocks = exchange(state, "pw").reshape(PARTS, CHUNK, width)
     p2, p_2 = shifted(state, -2), shifted(state, 2)
     blocks, p2, p_2, state = lax.optimization_barrier((blocks, p2, p_2, state))
-    turned = rotate(amount.reshape(1), blocks).reshape(full, width)
-    turned, state = lax.optimization_barrier((turned, state))
-    turned = exchange(turned, "pw")
-    p1, p_1 = shifted(state, -1), shifted(state, 1)
-    turned, p1, p_1 = lax.optimization_barrier((turned, p1, p_1))
-
-    end = NK - 1
-    near = lax.ppermute(turned, "kstr", [(0, end), (end, 0)])
-    part, p1 = call(margin_kernel, (margins, fields), flags, state, p1, near, smem=1)
-    turned, part = lax.optimization_barrier((turned, part))
+    turned = exchange(rotate(amount.reshape(1), blocks).reshape(full, width), "pw")
+    p1 = shifted(jnp.where(row == 0, turned, state), -1)
+
+    part = call(margin_kernel, shape((full, NB), BF16), state, p1)
+    state, turned, part = lax.optimization_barrier((state, turned, part))
+    parts = exchange(part, "pw").reshape(PARTS, CHUNK, NB)
+    p_1 = shifted(jnp.where(row == end, turned, state), 1)
+    parts, p_1, turned = lax.optimization_barrier((parts, p_1, turned))
+    own, kept = call(collect_kernel, (chunks, chunk), parts)
+    whole = exchange(own.reshape(full, NB), "pw")
     far = lax.ppermute(turned, "kstr", [(0, end - 1), (1, end), (end - 1, 0), (end, 1)])
-    whole, far = lax.optimization_barrier((whole_margin(part), far))
+    whole, far = lax.optimization_barrier((whole, far))
 
     y0 = inverse(whole)
     y_1 = shifted(y0, 1)
-    g0, total, p_1 = call(
-        first_slope_kernel, (grads, totals, fields), flags, y_1, y0, p_1, near, p1, smem=1
-    )
-    y0_later, total = lax.optimization_barrier((y0, total))
-    y1 = shifted(y0_later, -1)
-    y_2 = shifted(y0_later, 2)
-    total = whole_total(total)
-    q_1, q0, q1, part = call(
+    y1 = shifted(y0, -1)
+    g0, g1, part = call(
+        orders_kernel,
+        (grads, fields, shape((PARTS, 5 * CHUNK, 128), BF16)),
+        *(flags, y_1, y0, y1, p_1, state, p1, p2, far),
+        smem=1,
+        scratch=far_scratch,
+    )
+    y0, part = lax.optimization_barrier((y0, part))
+    y_2 = shifted(y0, 2)
+    parts = exchange(part, "pw")
+    first, second, total = call(
+        collect_orders_kernel, (chunk, chunk, shape((NK, 8, 128), F32)), parts
+    )
+    total = exchange(total, "kstr")
+    own = call(combine_kernel, chunks, total, kept, first, second)
+    whole = exchange(own.reshape(full, NB), "pw")
+    q_1, q0, q1 = call(
         advance_kernel,
-        (fields, fields, fields, margins),
-        *(flags, total, y_2, y_1, y0, y1, p_2, p_1, state, p1, p2, far, g0),
+        (fields, fields, fields),
+        *(flags, total, y_2, y_1, p_2, p_1, state, p1, far, g0, g1),
         smem=1,
-        scratch=(pltpu.VMEM((full, width), BF16),),
-    )
-
-    y0 = inverse(whole_margin(part))
+        scratch=far_scratch,
+    )
+
+    y0 = inverse(whole)
     y_1 = shifted(y0, 1)
-    g0, total = call(slope_kernel, (grads, totals), y_1, y0, q_1, q1)
+    g0, total = call(slope_kernel, (grads, shape((PARTS, 8, 128), F32)), y_1, y0, q_1, q1)
     total = whole_total(total)
     half = shape((NB, width), BF16)
     new_re, new_im = call(finish_kernel, (half, half), total, q0, g0)

time: 283 us -> 260 us (0.919)
  waiting for transfers between devices: 111 us -> 68.9 us
  blocking collectives: 60.6 us -> 102 us
  starting transfers between devices: 78.5 us -> 61 us
  Pallas kernels: 21.5 us -> 18.5 us
    all_to_all x4 -> x6, blocking collectives: 60.6 us -> 102 us  [exchange(): return lax.all_to_all(value, axis, 0, 0, tiled=True)]
    all_to_all x6 -> x3, starting transfers between devices: 48.4 us -> 30.4 us  [exchange(): return lax.all_to_all(value, axis, 0, 0, tiled=True)]
    ppermute x8, waiting for transfers between devices: 56.8 us -> 40.7 us  [shifted(): return lax.ppermute(value, 'kstr', [(i, (i + by) % NK) for i in range(NK)])]
    all_to_all x6 -> x3, waiting for transfers between devices: 42.3 us -> 28.2 us  [exchange(): return lax.all_to_all(value, axis, 0, 0, tiled=True)]
    ppermute x1 -> x0, waiting for transfers between devices: 11.7 us -> none  [body(): near = lax.ppermute(turned, 'kstr', [(0, end), (end, 0)])]
    ppermute x8, starting transfers between devices: 23.2 us -> 28.6 us  [shifted(): return lax.ppermute(value, 'kstr', [(i, (i + by) % NK) for i in range(NK)])]
    ppermute x1 -> x0, starting transfers between devices: 5.01 us -> none  [body(): near = lax.ppermute(turned, 'kstr', [(0, end), (end, 0)])]
    pallas_call x11, Pallas kernels: 19.8 us -> 16.8 us  [call(): pl.pallas_call(kernel, out_shape=outs, in_specs=specs, out_specs=tuple((p...]
  transfers between devices with their start and end apart: 16 -> 12, of which waited for: 11 -> 8; matrix products, arithmetic and copies ran while one was open for 0% -> 0% of each run, Pallas kernels for 1% -> 2%
where the time goes in v4:
time: 260 us; the launch traced here: 259 us
  blocking collectives  102 us (39%)
  waiting for transfers between devices  68.9 us (27%)
  starting transfers between devices  61 us (23%)
  Pallas kernels  18.5 us (7%)
  local copies, waits for them, and re-layouts  3.98 us (2%)
  other arithmetic  3.15 us (1%)
    all_to_all x6, blocking collectives, exchange(): return lax.all_to_all(value, axis, 0, 0, tiled=True)  102 us
    ppermute x8, waiting for transfers between devices, shifted(): return lax.ppermute(value, 'kstr', [(i, (i + by) % NK) for i in range(NK)])  40.7 us
    all_to_all x3, starting transfers between devices, exchange(): return lax.all_to_all(value, axis, 0, 0, tiled=True)  30.4 us
    ppermute x8, starting transfers between devices, shifted(): return lax.ppermute(value, 'kstr', [(i, (i + by) % NK) for i in range(NK)])  28.6 us
    all_to_all x3, waiting for transfers between devices, exchange(): return lax.all_to_all(value, axis, 0, 0, tiled=True)  28.2 us
    pallas_call x11, Pallas kernels, call(): pl.pallas_call(kernel, out_shape=outs, in_specs=specs, out_specs=tuple((p...  16.8 us
  transfers between devices with their start and end apart: 12, of which 8 were waited for; matrix products, arithmetic and copies ran while one was open for 0% of the time, Pallas kernels for 2%

profile of v4, /device:TPU:1, one launch (start us, length us, event | category | flops | bytes accessed | tf_op | source)
XLA Modules:
  0.0 259.1 jit_solution(6785814413694566416)
XLA Ops:
  0.6 1.9 pad_maximum_fusion.state_ref.p0
  2.5 14.4 %all-to-all-start = ((bf16[32,16,512]{2,1,0:T(8,128)(2,1)}), bf16[32,16,512]{2,1,0:T(8,128)(2,1)S(1)}, u32[]{:S(2)}, u32[]{:S(2)}) async-start(bf16[32,16,512]{2,1,0:T(8,128)(2,1)} %bitcast.2), calls=%async_computation | async-start | bytes 1048576 | tf_op jit(solution)/shard_map/all_to_all | solution.py:250
  16.9 5.1 %collective-permute-start = (bf16[512,512]{1,0:T(8,128)(2,1)}, bf16[512,512]{1,0:T(8,128)(2,1)S(1)}, u32[]{:S(2)}, u32[]{:S(2)}) collective-permute-start(bf16[512,512]{1,0:T(8,128)(2,1)} %pad_maximum_fusion.state_ref.p0), channel_id=1, source_target_pairs={{0,448},{32,480},{64,0},{96,32},{128,64},{160,96},{192,128},{224,1... | collective-permute-start | bytes 1572872 | tf_op jit(solution)/shard_map/ppermute | solution.py:246
  22.0 1.9 collective-permute-start.1
  24.0 1.2 slice.3
  25.8 7.6 %collective-permute-done.p2 = bf16[512,512]{1,0:T(8,128)(2,1)S(1)} collective-permute-done((bf16[512,512]{1,0:T(8,128)(2,1)}, bf16[512,512]{1,0:T(8,128)(2,1)S(1)}, u32[]{:S(2)}, u32[]{:S(2)}) %collective-permute-start) | collective-permute-done | bytes 524320 | tf_op jit(solution)/shard_map/ppermute | solution.py:246
  33.4 4.9 %collective-permute-done.1.p_2 = bf16[512,512]{1,0:T(8,128)(2,1)S(1)} collective-permute-done((bf16[512,512]{1,0:T(8,128)(2,1)}, bf16[512,512]{1,0:T(8,128)(2,1)S(1)}, u32[]{:S(2)}, u32[]{:S(2)}) %collective-permute-start.1) | collective-permute-done | bytes 524320 | tf_op jit(solution)/shard_map/ppermute | solution.py:246
  38.3 0.0 all-to-all-done.block_ref
  38.3 1.7 shard_map.50
  40.1 10.8 %all-to-all-start.1 = ((bf16[32,16,512]{2,1,0:T(8,128)(2,1)}), bf16[32,16,512]{2,1,0:T(8,128)(2,1)S(1)}, u32[]{:S(2)}, u32[]{:S(2)}) async-start(bf16[32,16,512]{2,1,0:T(8,128)(2,1)} %shard_map.50), calls=%async_computation.1 | async-start | bytes 1048576 | tf_op jit(solution)/shard_map/all_to_all | solution.py:250
  50.9 17.2 %all-to-all-done.1 = bf16[32,16,512]{2,1,0:T(8,128)(2,1)S(1)} async-done(((bf16[32,16,512]{2,1,0:T(8,128)(2,1)}), bf16[32,16,512]{2,1,0:T(8,128)(2,1)S(1)}, u32[]{:S(2)}, u32[]{:S(2)}) %all-to-all-start.1) | async-done | bytes 524320 | tf_op jit(solution)/shard_map/all_to_all | solution.py:250
  68.1 0.1 broadcast_select_fusion.1
  68.2 5.4 %collective-permute-start.2 = (bf16[512,512]{1,0:T(8,128)(2,1)S(1)}, bf16[512,512]{1,0:T(8,128)(2,1)S(1)}, u32[]{:S(2)}, u32[]{:S(2)}) collective-permute-start(bf16[512,512]{1,0:T(8,128)(2,1)S(1)} %broadcast_select_fusion.1), channel_id=1, source_target_pairs={{0,480},{32,0},{64,32},{96,64},{128,96},{160,128},{192,160},{224,1... | collective-permute-start | bytes 1572872 | tf_op jit(solution)/shard_map/ppermute | solution.py:246
  73.6 12.4 %collective-permute-done.2.next_ref.p1 = bf16[512,512]{1,0:T(8,128)(2,1)S(1)} collective-permute-done((bf16[512,512]{1,0:T(8,128)(2,1)S(1)}, bf16[512,512]{1,0:T(8,128)(2,1)S(1)}, u32[]{:S(2)}, u32[]{:S(2)}) %collective-permute-start.2) | collective-permute-done | bytes 524320 | tf_op jit(solution)/shard_map/ppermute | solution.py:246
  86.0 1.5 shard_map.51
  87.5 1.1 broadcast_select_fusion
  88.6 3.9 %collective-permute-start.3 = (bf16[512,512]{1,0:T(8,128)(2,1)S(1)}, bf16[512,512]{1,0:T(8,128)(2,1)S(1)}, u32[]{:S(2)}, u32[]{:S(2)}) collective-permute-start(bf16[512,512]{1,0:T(8,128)(2,1)S(1)} %broadcast_select_fusion), channel_id=1, source_target_pairs={{0,32},{32,64},{64,96},{96,128},{128,160},{160,192},{192,224},{224... | collective-permute-start | bytes 1572872 | tf_op jit(solution)/shard_map/ppermute | solution.py:246
  92.6 19.5 %all_to_all.64.parts_ref = bf16[32,16,256]{2,1,0:T(8,128)(2,1)S(1)} all-to-all(bf16[32,16,256]{2,1,0:T(8,128)(2,1)S(1)} %bitcast.16), channel_id=1, replica_groups=mesh['kstr'=16,'pw'=32] {'pw'}, dimensions={0} | all-to-all | bytes 524288 | tf_op jit(solution)/shard_map/all_to_all | solution.py:250
  112.1 0.0 collective-permute-done.3.p_1
  112.1 1.9 collective-permute-start.4
  114.0 0.1 shard_map.52
  114.1 20.4 %all_to_all.65 = bf16[32,16,256]{2,1,0:T(8,128)(2,1)S(1)} all-to-all(bf16[32,16,256]{2,1,0:T(8,128)(2,1)S(1)} %get-tuple-element.37), channel_id=1, replica_groups=mesh['kstr'=16,'pw'=32] {'pw'}, dimensions={0} | all-to-all | bytes 524288 | tf_op jit(solution)/shard_map/all_to_all | solution.py:250
  134.5 3.3 %shard_map.53.y0 = bf16[256,512]{1,0:T(8,128)(2,1)S(1)} custom-call(bf16[512,256]{1,0:T(8,128)(2,1)S(1)} %bitcast.18), custom_call_target="tpu_custom_call" | custom-call | bytes 524288 | tf_op jit(solution)/shard_map/pallas_call | solution.py:29
  137.8 3.6 %collective-permute-start.5 = (bf16[256,512]{1,0:T(8,128)(2,1)S(1)}, bf16[256,512]{1,0:T(8,128)(2,1)S(1)}, u32[]{:S(2)}, u32[]{:S(2)}) collective-permute-start(bf16[256,512]{1,0:T(8,128)(2,1)S(1)} %shard_map.53.y0), channel_id=1, source_target_pairs={{0,32},{32,64},{64,96},{96,128},{128,160},{160,192},{192,224},{224... | collective-permute-start | bytes 786440 | tf_op jit(solution)/shard_map/ppermute | solution.py:246
  141.4 4.3 %collective-permute-start.6 = (bf16[256,512]{1,0:T(8,128)(2,1)S(1)}, bf16[256,512]{1,0:T(8,128)(2,1)S(1)}, u32[]{:S(2)}, u32[]{:S(2)}) collective-permute-start(bf16[256,512]{1,0:T(8,128)(2,1)S(1)} %shard_map.53.y0), channel_id=1, source_target_pairs={{0,480},{32,0},{64,32},{96,64},{128,96},{160,128},{192,160},{224,1... | collective-permute-start | bytes 786440 | tf_op jit(solution)/shard_map/ppermute | solution.py:246
  145.7 0.1 add_convert_fusion.flags
  145.8 6.7 %collective-permute-done.5.y_1 = bf16[256,512]{1,0:T(8,128)(2,1)S(1)} collective-permute-done((bf16[256,512]{1,0:T(8,128)(2,1)S(1)}, bf16[256,512]{1,0:T(8,128)(2,1)S(1)}, u32[]{:S(2)}, u32[]{:S(2)}) %collective-permute-start.5) | collective-permute-done | bytes 262176 | tf_op jit(solution)/shard_map/ppermute | solution.py:246
  152.5 3.7 %collective-permute-done.6.y1 = bf16[256,512]{1,0:T(8,128)(2,1)S(1)} collective-permute-done((bf16[256,512]{1,0:T(8,128)(2,1)S(1)}, bf16[256,512]{1,0:T(8,128)(2,1)S(1)}, u32[]{:S(2)}, u32[]{:S(2)}) %collective-permute-start.6) | collective-permute-done | bytes 262176 | tf_op jit(solution)/shard_map/ppermute | solution.py:246
  156.2 1.0 copy-done.6
  157.2 3.9 %shard_map.54 = (f32[512,512]{1,0:T(8,128)S(1)}, bf16[512,512]{1,0:T(8,128)(2,1)S(1)}, bf16[32,80,128]{2,1,0:T(8,128)(2,1)S(1)}) custom-call(s32[4]{0:T(128)S(1)} %add_convert_fusion.flags, bf16[256,512]{1,0:T(8,128)(2,1)S(1)} %collective-permute-done.5.y_1, bf16[256,512]{1,0:T(8,128)(2,1)S(1)} %shard_map.53.y0, ...), custom_call_target="tpu_custom_call" | custom-call | bytes 5636112 | tf_op jit(solution)/shard_map/pallas_call | solution.py:29
  161.1 24.2 %all_to_all.66.parts_ref = bf16[32,80,128]{2,1,0:T(8,128)(2,1)S(1)} all-to-all(bf16[32,80,128]{2,1,0:T(8,128)(2,1)S(1)} %get-tuple-element.44), channel_id=1, replica_groups=mesh['kstr'=16,'pw'=32] {'pw'}, dimensions={0} | all-to-all | bytes 1310720 | tf_op jit(solution)/shard_map/all_to_all | solution.py:250
  185.3 0.1 shard_map.55
  185.4 11.7 %all_to_all.67.total_ref.total = f32[16,8,128]{2,1,0:T(8,128)S(1)} all-to-all(f32[16,8,128]{2,1,0:T(8,128)S(1)} %get-tuple-element.45), channel_id=1, replica_groups=mesh['kstr'=16,'pw'=32] {'kstr'}, dimensions={0} | all-to-all | bytes 131072 | tf_op jit(solution)/shard_map/all_to_all | solution.py:250
  197.1 0.1 shard_map.56
  197.2 0.0 copy-start
  197.2 0.7 copy-done
  197.9 5.2 %all-to-all-start.6 = ((bf16[32,16,256]{2,1,0:T(8,128)(2,1)}), bf16[32,16,256]{2,1,0:T(8,128)(2,1)S(1)}, u32[]{:S(2)}, u32[]{:S(2)}) async-start(bf16[32,16,256]{2,1,0:T(8,128)(2,1)} %copy-done), calls=%async_computation.6 | async-start | bytes 524288 | tf_op jit(solution)/shard_map/all_to_all | solution.py:250
  203.1 2.1 collective-permute-start.8
  205.2 10.9 %all-to-all-done.6 = bf16[32,16,256]{2,1,0:T(8,128)(2,1)S(1)} async-done(((bf16[32,16,256]{2,1,0:T(8,128)(2,1)}), bf16[32,16,256]{2,1,0:T(8,128)(2,1)S(1)}, u32[]{:S(2)}, u32[]{:S(2)}) %all-to-all-start.6) | async-done | bytes 262176 | tf_op jit(solution)/shard_map/all_to_all | solution.py:250
  216.2 3.3 %shard_map.57.y0 = bf16[256,512]{1,0:T(8,128)(2,1)S(1)} custom-call(bf16[512,256]{1,0:T(8,128)(2,1)S(1)} %bitcast.17), custom_call_target="tpu_custom_call" | custom-call | bytes 524288 | tf_op jit(solution)/shard_map/pallas_call | solution.py:29
  219.5 2.3 collective-permute-start.7
  221.8 1.0 copy-done.4
  222.9 2.6 %shard_map.58 = (bf16[512,512]{1,0:T(8,128)(2,1)S(1)}, bf16[512,512]{1,0:T(8,128)(2,1)S(1)}, bf16[512,512]{1,0:T(8,128)(2,1)S(1)}) custom-call(s32[4]{0:T(128)S(1)} %add_convert_fusion.flags, f32[16,8,128]{2,1,0:T(8,128)S(1)} %all_to_all.67.total_ref.total, bf16[256,512]{1,0:T(8,128)(2,1)} %collective-permute-done.8.y_2, ...), custom_call_target="tpu_custom_call" | custom-call | bytes 6357008 | tf_op jit(solution)/shard_map/pallas_call | solution.py:29
  225.5 5.4 %collective-permute-done.7.y_1 = bf16[256,512]{1,0:T(8,128)(2,1)S(1)} collective-permute-done((bf16[256,512]{1,0:T(8,128)(2,1)S(1)}, bf16[256,512]{1,0:T(8,128)(2,1)S(1)}, u32[]{:S(2)}, u32[]{:S(2)}) %collective-permute-start.7) | collective-permute-done | bytes 262176 | tf_op jit(solution)/shard_map/ppermute | solution.py:246
  230.9 0.7 shard_map.59
  231.7 15.7 %all_to_all.68.parts_ref = f32[32,8,128]{2,1,0:T(8,128)S(1)} all-to-all(f32[32,8,128]{2,1,0:T(8,128)S(1)} %get-tuple-element.55), channel_id=1, replica_groups=mesh['kstr'=16,'pw'=32] {'pw'}, dimensions={0} | all-to-all | bytes 262144 | tf_op jit(solution)/shard_map/all_to_all | solution.py:250
  247.4 10.5 %all_to_all.69.total_ref = f32[16,8,128]{2,1,0:T(8,128)S(1)} all-to-all(f32[16,8,128]{2,1,0:T(8,128)S(1)} %shard_map.60), channel_id=1, replica_groups=mesh['kstr'=16,'pw'=32] {'kstr'}, dimensions={0} | all-to-all | bytes 131072 | tf_op jit(solution)/shard_map/all_to_all | solution.py:250
  258.0 1.1 shard_map.61
  (13 shorter events, 0.1 us)
Async XLA Ops:
  2.5 35.8 %all-to-all-start = ((bf16[32,16,512]{2,1,0:T(8,128)(2,1)}), bf16[32,16,512]{2,1,0:T(8,128)(2,1)S(1)}, u32[]{:S(2)}, u32[]{:S(2)}) async-start(bf16[32,16,512]{2,1,0:T(8,128)(2,1)} %bitcast.2), calls=%async_computation | async-start | bytes 1048576 | tf_op jit(solution)/shard_map/all_to_all | solution.py:250
  16.9 16.5 %collective-permute-start = (bf16[512,512]{1,0:T(8,128)(2,1)}, bf16[512,512]{1,0:T(8,128)(2,1)S(1)}, u32[]{:S(2)}, u32[]{:S(2)}) collective-permute-start(bf16[512,512]{1,0:T(8,128)(2,1)} %pad_maximum_fusion.state_ref.p0), channel_id=1, source_target_pairs={{0,448},{32,480},{64,0},{96,32},{128,64},{160,96},{192,128},{224,1... | collective-permute-start | bytes 1572872 | tf_op jit(solution)/shard_map/ppermute | solution.py:246
  22.0 16.3 %collective-permute-start.1 = (bf16[512,512]{1,0:T(8,128)(2,1)}, bf16[512,512]{1,0:T(8,128)(2,1)S(1)}, u32[]{:S(2)}, u32[]{:S(2)}) collective-permute-start(bf16[512,512]{1,0:T(8,128)(2,1)} %pad_maximum_fusion.state_ref.p0), channel_id=1, source_target_pairs={{0,64},{32,96},{64,128},{96,160},{128,192},{160,224},{192,256},{22... | collective-permute-start | bytes 1572872 | tf_op jit(solution)/shard_map/ppermute | solution.py:246
  33.4 6.6 %copy-start.5 = (bf16[512,512]{1,0:T(8,128)(2,1)}, bf16[512,512]{1,0:T(8,128)(2,1)S(1)}, u32[]{:S(2)}) copy-start(bf16[512,512]{1,0:T(8,128)(2,1)S(1)} %collective-permute-done.p2) | copy-start | bytes 1572868
  38.3 1.7 copy-start.1
  40.1 28.0 %all-to-all-start.1 = ((bf16[32,16,512]{2,1,0:T(8,128)(2,1)}), bf16[32,16,512]{2,1,0:T(8,128)(2,1)S(1)}, u32[]{:S(2)}, u32[]{:S(2)}) async-start(bf16[32,16,512]{2,1,0:T(8,128)(2,1)} %shard_map.50), calls=%async_computation.1 | async-start | bytes 1048576 | tf_op jit(solution)/shard_map/all_to_all | solution.py:250
  68.2 17.8 %collective-permute-start.2 = (bf16[512,512]{1,0:T(8,128)(2,1)S(1)}, bf16[512,512]{1,0:T(8,128)(2,1)S(1)}, u32[]{:S(2)}, u32[]{:S(2)}) collective-permute-start(bf16[512,512]{1,0:T(8,128)(2,1)S(1)} %broadcast_select_fusion.1), channel_id=1, source_target_pairs={{0,480},{32,0},{64,32},{96,64},{128,96},{160,128},{192,160},{224,1... | collective-permute-start | bytes 1572872 | tf_op jit(solution)/shard_map/ppermute | solution.py:246
  88.6 23.5 %collective-permute-start.3 = (bf16[512,512]{1,0:T(8,128)(2,1)S(1)}, bf16[512,512]{1,0:T(8,128)(2,1)S(1)}, u32[]{:S(2)}, u32[]{:S(2)}) collective-permute-start(bf16[512,512]{1,0:T(8,128)(2,1)S(1)} %broadcast_select_fusion), channel_id=1, source_target_pairs={{0,32},{32,64},{64,96},{96,128},{128,160},{160,192},{192,224},{224... | collective-permute-start | bytes 1572872 | tf_op jit(solution)/shard_map/ppermute | solution.py:246
  112.1 22.4 %collective-permute-start.4 = (bf16[512,512]{1,0:T(8,128)(2,1)S(1)}, bf16[512,512]{1,0:T(8,128)(2,1)S(1)}, u32[]{:S(2)}, u32[]{:S(2)}) collective-permute-start(bf16[512,512]{1,0:T(8,128)(2,1)S(1)} %bitcast.20), channel_id=1, source_target_pairs={{0,448},{32,480},{448,0},{480,32},{1,449},{33,481},{449,1},{481,33... | collective-permute-start | bytes 1572872 | tf_op jit(solution)/shard_map/ppermute | solution.py:292
  137.8 14.6 %collective-permute-start.5 = (bf16[256,512]{1,0:T(8,128)(2,1)S(1)}, bf16[256,512]{1,0:T(8,128)(2,1)S(1)}, u32[]{:S(2)}, u32[]{:S(2)}) collective-permute-start(bf16[256,512]{1,0:T(8,128)(2,1)S(1)} %shard_map.53.y0), channel_id=1, source_target_pairs={{0,32},{32,64},{64,96},{96,128},{128,160},{160,192},{192,224},{224... | collective-permute-start | bytes 786440 | tf_op jit(solution)/shard_map/ppermute | solution.py:246
  141.4 14.8 %collective-permute-start.6 = (bf16[256,512]{1,0:T(8,128)(2,1)S(1)}, bf16[256,512]{1,0:T(8,128)(2,1)S(1)}, u32[]{:S(2)}, u32[]{:S(2)}) collective-permute-start(bf16[256,512]{1,0:T(8,128)(2,1)S(1)} %shard_map.53.y0), channel_id=1, source_target_pairs={{0,480},{32,0},{64,32},{96,64},{128,96},{160,128},{192,160},{224,1... | collective-permute-start | bytes 786440 | tf_op jit(solution)/shard_map/ppermute | solution.py:246
  156.2 1.0 copy-start.6
  161.1 24.2 %copy-start.3 = (bf16[512,512]{1,0:T(8,128)(2,1)}, bf16[512,512]{1,0:T(8,128)(2,1)S(1)}, u32[]{:S(2)}) copy-start(bf16[512,512]{1,0:T(8,128)(2,1)S(1)} %get-tuple-element.52.g1) | copy-start | bytes 1572868
  197.2 0.7 copy-start
  197.9 18.3 %all-to-all-start.6 = ((bf16[32,16,256]{2,1,0:T(8,128)(2,1)}), bf16[32,16,256]{2,1,0:T(8,128)(2,1)S(1)}, u32[]{:S(2)}, u32[]{:S(2)}) async-start(bf16[32,16,256]{2,1,0:T(8,128)(2,1)} %copy-done), calls=%async_computation.6 | async-start | bytes 524288 | tf_op jit(solution)/shard_map/all_to_all | solution.py:250
  203.1 18.7 %collective-permute-start.8 = (bf16[256,512]{1,0:T(8,128)(2,1)S(1)}, bf16[256,512]{1,0:T(8,128)(2,1)}, u32[]{:S(2)}, u32[]{:S(2)}) collective-permute-start(bf16[256,512]{1,0:T(8,128)(2,1)S(1)} %shard_map.53.y0), channel_id=1, source_target_pairs={{0,64},{32,96},{64,128},{96,160},{128,192},{160,224},{192,256},{22... | collective-permute-start | bytes 786440 | tf_op jit(solution)/shard_map/ppermute | solution.py:246
  216.2 5.7 %copy-start.2 = (bf16[512,512]{1,0:T(8,128)(2,1)S(1)}, bf16[512,512]{1,0:T(8,128)(2,1)}, u32[]{:S(2)}) copy-start(bf16[512,512]{1,0:T(8,128)(2,1)} %copy-done.1) | copy-start | bytes 1572868
  219.5 11.5 %collective-permute-start.7 = (bf16[256,512]{1,0:T(8,128)(2,1)S(1)}, bf16[256,512]{1,0:T(8,128)(2,1)S(1)}, u32[]{:S(2)}, u32[]{:S(2)}) collective-permute-start(bf16[256,512]{1,0:T(8,128)(2,1)S(1)} %shard_map.57.y0), channel_id=1, source_target_pairs={{0,32},{32,64},{64,96},{96,128},{128,160},{160,192},{192,224},{224... | collective-permute-start | bytes 786440 | tf_op jit(solution)/shard_map/ppermute | solution.py:246
  221.8 1.0 copy-start.4

commit v5 on v4

--- a/solution.py
+++ b/solution.py
@@ -66,42 +66,46 @@
     out_ref[...] = margin(state_ref[...], next_ref[...]).astype(BF16)
 
 
-def rotate_kernel(amount_ref, block_ref, out_ref, rolled_ref):
-    count, rows, width = block_ref.shape
-    amount = amount_ref[0]
-    first = amount // width
-    rest = amount - first * width
-    turn = lax.rem(width - rest, width)
-
-    def roll(index, carry):
-        rolled_ref[index] = pltpu.roll(block_ref[index].astype(F32), turn, 1)
-        return carry
-
-    lax.fori_loop(0, count, roll, 0, unroll=4)
-    lane = lax.broadcasted_iota(jnp.int32, (rows, width), 1)
-
-    def place(index, carry):
-        here = lax.rem(index + first, count)
-        after = lax.rem(index + first + 1, count)
-        value = jnp.where(lane < width - rest, rolled_ref[here], rolled_ref[after])
-        out_ref[index] = value.astype(BF16)
-        return carry
-
-    lax.fori_loop(0, count, place, 0, unroll=4)
-
-
-def rotate(amount, block):
-    return pl.pallas_call(
-        rotate_kernel,
-        out_shape=shape(block.shape, BF16),
-        in_specs=[
-            pl.BlockSpec(memory_space=pltpu.SMEM),
-            pl.BlockSpec(memory_space=pltpu.VMEM),
-        ],
-        out_specs=pl.BlockSpec(memory_space=pltpu.VMEM),
-        scratch_shapes=[pltpu.VMEM(block.shape, F32)],
-        compiler_params=pltpu.CompilerParams(vmem_limit_bytes=14 * 1024 * 1024),
-    )(amount, block)
+def first_margin_kernel(flags, state_ref, next_ref, closing_ref, out_ref, chosen_ref):
+    choose(flags[3], closing_ref, next_ref, chosen_ref)
+    margin_kernel(state_ref, chosen_ref, out_ref)
+
+
+def merge_kernel(bounds, state_ref, beside_ref, out_ref):
+    lane = lax.broadcasted_iota(jnp.int32, (CHUNK, state_ref.shape[1]), 1)
+    own = (lane >= bounds[0]) & (lane < bounds[1])
+    for row in range(0, state_ref.shape[0], CHUNK):
+        rows = pl.ds(row, CHUNK)
+        value = jnp.where(own, state_ref[rows, :].astype(F32), beside_ref[rows, :].astype(F32))
+        out_ref[rows, :] = pltpu.roll(value, bounds[2], 1).astype(BF16)
+
+
+def place(row, column):
+    return row * PARTS + column % PARTS
+
+
+def beside_pairs():
+    pairs = []
+    for j in range(PARTS):
+        pairs += [(place(row, j), place(row, j - 1)) for row in (0, 1)]
+        pairs += [(place(row, j), place(row, j + 1)) for row in (NK - 2, NK - 1)]
+    return pairs
+
+
+def closing_pairs(by):
+    pairs = []
+    for j in range(PARTS):
+        for row in (0, 1):
+            pairs.append((place(row, j), place(NK - 1 - row, j - by)))
+            pairs.append((place(NK - 1 - row, j), place(row, j + by)))
+    return pairs
+
+
+def close_string(value, blocks):
+    def branch(by):
+        return lambda block: lax.ppermute(block, ("kstr", "pw"), closing_pairs(by))
+
+    return lax.switch(blocks, [branch(by) for by in range(PARTS)], value)
 
 
 def collect_kernel(parts_ref, out_ref, kept_ref):
@@ -193,14 +197,17 @@
     return part[:, 0:128] + part[:, 128:256] + part[:, 256:384] + part[:, 384:512]
 
 
-def orders_kernel(flags, y_1, y0, y1, p_1, p0, p1, p2, closing, g0, g1, out_ref, far):
+def orders_kernel(
+    flags, y_1, y0, y1, before, p0, p1, p2, closing, beyond, g0, g1, p_1, out_ref, far
+):
+    choose(flags[0], closing, before, p_1)
     grad = slope(y0[...], p1[...], y_1[...], p_1[...])
     g0[...] = grad
     part = squares(grad)
     high = part.astype(BF16).astype(F32)
     pair = jnp.concatenate([high, part - high], 0).astype(BF16)
     here = grad.astype(BF16)
-    choose(flags[2], closing, p2, far)
+    choose(flags[2], beyond, p2, far)
     ahead = slope(y1[...], far[...], y0[...], p0[...]).astype(BF16)
     g1[...] = ahead
     first = (margin(here, p1[...]) + margin(p0[...], ahead)).astype(BF16)
@@ -264,7 +271,16 @@
     width = states_re.shape[2]
     row = lax.axis_index("kstr")
     offset = jnp.mod(gmap[0] - lax.axis_index("pw") * width, NPW)
-    amount = jnp.where(row < NK // 2, offset, NPW - offset).astype(jnp.int32)
+    blocks = offset // width
+    rest = offset - blocks * width
+    first = row < NK // 2
+    bounds = jnp.stack(
+        [
+            jnp.where(first, rest, 0),
+            jnp.where(first, width, width - rest),
+            jnp.where(first, jnp.mod(width - rest, width), rest),
+        ]
+    ).astype(jnp.int32)
     state = jnp.concatenate([states_re[0], states_im[0]], 0)
     full = 2 * NB
     end = NK - 1
@@ -276,29 +292,30 @@
     far_scratch = (pltpu.VMEM((full, width), BF16),)
     flags = jnp.stack([row == 0, row <= 1, row >= NK - 2, row == end]).astype(jnp.int32)
 
-    blocks = exchange(state, "pw").reshape(PARTS, CHUNK, width)
-    p2, p_2 = shifted(state, -2), shifted(state, 2)
-    blocks, p2, p_2, state = lax.optimization_barrier((blocks, p2, p_2, state))
-    turned = exchange(rotate(amount.reshape(1), blocks).reshape(full, width), "pw")
-    p1 = shifted(jnp.where(row == 0, turned, state), -1)
-
-    part = call(margin_kernel, shape((full, NB), BF16), state, p1)
-    state, turned, part = lax.optimization_barrier((state, turned, part))
+    beside = lax.ppermute(state, ("kstr", "pw"), beside_pairs())
+    p1, p_2 = shifted(state, -1), shifted(state, 2)
+    merged = call(merge_kernel, fields, bounds, state, beside, smem=1)
+    near = close_string(merged, blocks)
+    near, p1, p_2 = lax.optimization_barrier((near, p1, p_2))
+
+    part, p1 = call(first_margin_kernel, (shape((full, NB), BF16), fields), flags, state, p1, near, smem=1)
+    state, near, part = lax.optimization_barrier((state, near, part))
     parts = exchange(part, "pw").reshape(PARTS, CHUNK, NB)
-    p_1 = shifted(jnp.where(row == end, turned, state), 1)
-    parts, p_1, turned = lax.optimization_barrier((parts, p_1, turned))
+    p_1 = shifted(state, 1)
+    parts, p_1, near, p1 = lax.optimization_barrier((parts, p_1, near, p1))
+    p2 = shifted(p1, -1)
     own, kept = call(collect_kernel, (chunks, chunk), parts)
     whole = exchange(own.reshape(full, NB), "pw")
-    far = lax.ppermute(turned, "kstr", [(0, end - 1), (1, end), (end - 1, 0), (end, 1)])
-    whole, far = lax.optimization_barrier((whole, far))
+    far = lax.ppermute(near, "kstr", [(0, 1), (1, 0), (end - 1, end), (end, end - 1)])
+    whole, far, p2 = lax.optimization_barrier((whole, far, p2))
 
     y0 = inverse(whole)
     y_1 = shifted(y0, 1)
     y1 = shifted(y0, -1)
-    g0, g1, part = call(
+    g0, g1, p_1, part = call(
         orders_kernel,
-        (grads, fields, shape((PARTS, 5 * CHUNK, 128), BF16)),
-        *(flags, y_1, y0, y1, p_1, state, p1, p2, far),
+        (grads, fields, fields, shape((PARTS, 5 * CHUNK, 128), BF16)),
+        *(flags, y_1, y0, y1, p_1, state, p1, p2, near, far),
         smem=1,
         scratch=far_scratch,
     )

time: 260 us -> 254 us (0.977)
  blocking collectives: 102 us -> 140 us
  waiting for transfers between devices: 68.9 us -> 34.2 us
  starting transfers between devices: 61 us -> 54 us
    all_to_all x6, blocking collectives: 102 us -> 140 us  [exchange(): return lax.all_to_all(value, axis, 0, 0, tiled=True)]
    ppermute x8, waiting for transfers between devices: 40.7 us -> 15.1 us  [shifted(): return lax.ppermute(value, 'kstr', [(i, (i + by) % NK) for i in range(NK)])]
    all_to_all x3 -> x1, starting transfers between devices: 30.4 us -> 5.73 us  [exchange(): return lax.all_to_all(value, axis, 0, 0, tiled=True)]
    ppermute x1 -> x3, starting transfers between devices: 1.93 us -> 22.3 us  [the longest x1 11.6 us: branch(): return lambda block: lax.ppermute(block, ('kstr', 'pw'), closing_pairs(by))]
    all_to_all x3 -> x1, waiting for transfers between devices: 28.2 us -> 10.8 us  [exchange(): return lax.all_to_all(value, axis, 0, 0, tiled=True)]
    ppermute x1 -> x3, waiting for transfers between devices: 0.01 us -> 8.24 us  [the longest x1 7.61 us: branch(): return lambda block: lax.ppermute(block, ('kstr', 'pw'), closing_pairs(by))]
    ppermute x8, starting transfers between devices: 28.6 us -> 25.9 us  [shifted(): return lax.ppermute(value, 'kstr', [(i, (i + by) % NK) for i in range(NK)])]
    pallas_call x11 -> x12, Pallas kernels: 16.8 us -> 17.5 us  [call(): pl.pallas_call(kernel, out_shape=outs, in_specs=specs, out_specs=tuple((p...]
  transfers between devices with their start and end apart: 12 -> 12, of which waited for: 8 -> 6; matrix products, arithmetic and copies ran while one was open for 0% -> 1% of each run, Pallas kernels for 2% -> 3%
where the time goes in v5:
time: 254 us; the launch traced here: 253 us
  blocking collectives  140 us (55%)
  starting transfers between devices  54 us (21%)
  waiting for transfers between devices  34.2 us (13%)
  Pallas kernels  17.5 us (7%)
  local copies, waits for them, and re-layouts  4.78 us (2%)
    all_to_all x6, blocking collectives, exchange(): return lax.all_to_all(value, axis, 0, 0, tiled=True)  140 us
    ppermute x8, starting transfers between devices, shifted(): return lax.ppermute(value, 'kstr', [(i, (i + by) % NK) for i in range(NK)])  25.9 us
    pallas_call x12, Pallas kernels, call(): pl.pallas_call(kernel, out_shape=outs, in_specs=specs, out_specs=tuple((p...  17.5 us
    ppermute x8, waiting for transfers between devices, shifted(): return lax.ppermute(value, 'kstr', [(i, (i + by) % NK) for i in range(NK)])  15.1 us
    ppermute x1, starting transfers between devices, branch(): return lambda block: lax.ppermute(block, ('kstr', 'pw'), closing_pairs(by))  11.6 us
    all_to_all x1, waiting for transfers between devices, exchange(): return lax.all_to_all(value, axis, 0, 0, tiled=True)  10.8 us
    ppermute x1, starting transfers between devices, body(): beside = lax.ppermute(state, ('kstr', 'pw'), beside_pairs())  8.79 us
    ppermute x1, waiting for transfers between devices, branch(): return lambda block: lax.ppermute(block, ('kstr', 'pw'), closing_pairs(by))  7.61 us
  transfers between devices with their start and end apart: 12, of which 6 were waited for; matrix products, arithmetic and copies ran while one was open for 1% of the time, Pallas kernels for 3%

profile of v5, /device:TPU:1, one launch (start us, length us, event | category | flops | bytes accessed | tf_op | source)
XLA Modules:
  0.0 253.0 jit_solution(7875697482853701377)
XLA Ops:
  0.6 1.1 pad_maximum_fusion.state_ref.p0
  1.7 8.8 %collective-permute-start.32 = (bf16[512,512]{1,0:T(8,128)(2,1)S(1)}, bf16[512,512]{1,0:T(8,128)(2,1)S(1)}, u32[]{:S(2)}, u32[]{:S(2)}) collective-permute-start(bf16[512,512]{1,0:T(8,128)(2,1)S(1)} %pad_maximum_fusion.state_ref.p0), channel_id=1, source_target_pairs={{0,31},{32,63},{448,449},{480,481},{1,0},{33,32},{449,450},{481,48... | collective-permute-start | bytes 1572872 | tf_op jit(solution)/shard_map/ppermute | solution.py:295
  10.5 1.9 collective-permute-start.34
  12.4 5.3 %collective-permute-start.33 = (bf16[512,512]{1,0:T(8,128)(2,1)S(1)}, bf16[512,512]{1,0:T(8,128)(2,1)S(1)}, u32[]{:S(2)}, u32[]{:S(2)}) collective-permute-start(bf16[512,512]{1,0:T(8,128)(2,1)S(1)} %pad_maximum_fusion.state_ref.p0), channel_id=1, source_target_pairs={{0,480},{32,0},{64,32},{96,64},{128,96},{160,128},{192,160},{224,1... | collective-permute-start | bytes 1572872 | tf_op jit(solution)/shard_map/ppermute | solution.py:253
  17.8 1.2 slice.3
  19.7 0.1 pad_add_fusion.bounds
  19.7 0.1 add_convert_fusion.flags
  19.8 0.6 collective-permute-done.32.beside_ref
  20.5 0.8 shard_map.50
  21.3 19.2 %conditional.1 = (bf16[512,512]{1,0:T(8,128)(2,1)}) conditional(s32[]{:T(128)} %clamp.3, bf16[512,512]{1,0:T(8,128)(2,1)S(1)} %shard_map.50, bf16[512,512]{1,0:T(8,128)(2,1)S(1)} %shard_map.50, bf16[512,512]{1,0:T(8,128)(2,1)S(1)} %shard_map.50, bf16[512,512]{1,0:T(8,128)(2,1)S(1)} %shard_map.50, ...), branch_computations={%region_0.1_spmd, %region_1.2_spmd, %region_2.3_spmd, %region_3.4_... | conditional | bytes 2097200 | solution.py:108
  21.3 11.6 %collective-permute-start = (bf16[512,512]{1,0:T(8,128)(2,1)S(1)}, bf16[512,512]{1,0:T(8,128)(2,1)}, u32[]{:S(2)}, u32[]{:S(2)}) collective-permute-start(bf16[512,512]{1,0:T(8,128)(2,1)S(1)} %param), channel_id=1, source_target_pairs={{0,480},{480,0},{32,448},{448,32},{1,481},{481,1},{33,449},{449,33... | collective-permute-start | bytes 1572872 | tf_op jit(solution)/shard_map/cond/branch_0_fun/ppermute | solution.py:106
  32.9 7.6 %collective-permute-done = bf16[512,512]{1,0:T(8,128)(2,1)} collective-permute-done((bf16[512,512]{1,0:T(8,128)(2,1)S(1)}, bf16[512,512]{1,0:T(8,128)(2,1)}, u32[]{:S(2)}, u32[]{:S(2)}) %collective-permute-start) | collective-permute-done | bytes 524320 | tf_op jit(solution)/shard_map/cond/branch_0_fun/ppermute | solution.py:106
  40.5 0.8 copy-done.1
  41.3 0.0 collective-permute-done.33.next_ref
  41.3 1.6 shard_map.51
  42.9 2.0 collective-permute-start.35
  44.8 46.5 %all_to_all.46.parts_ref = bf16[32,16,256]{2,1,0:T(8,128)(2,1)S(1)} all-to-all(bf16[32,16,256]{2,1,0:T(8,128)(2,1)S(1)} %bitcast.17), channel_id=1, replica_groups=mesh['kstr'=16,'pw'=32] {'pw'}, dimensions={0} | all-to-all | bytes 524288 | tf_op jit(solution)/shard_map/all_to_all | solution.py:257
  91.4 1.9 collective-permute-start.36
  93.3 5.4 %collective-permute-start.37 = (bf16[512,512]{1,0:T(8,128)(2,1)S(1)}, bf16[512,512]{1,0:T(8,128)(2,1)S(1)}, u32[]{:S(2)}, u32[]{:S(2)}) collective-permute-start(bf16[512,512]{1,0:T(8,128)(2,1)S(1)} %get-tuple-element.110.p1), channel_id=1, source_target_pairs={{0,480},{32,0},{64,32},{96,64},{128,96},{160,128},{192,160},{224,1... | collective-permute-start | bytes 1572872 | tf_op jit(solution)/shard_map/ppermute | solution.py:253
  98.7 0.1 shard_map.52
  98.7 24.5 %all_to_all.47 = bf16[32,16,256]{2,1,0:T(8,128)(2,1)S(1)} all-to-all(bf16[32,16,256]{2,1,0:T(8,128)(2,1)S(1)} %get-tuple-element.108), channel_id=1, replica_groups=mesh['kstr'=16,'pw'=32] {'pw'}, dimensions={0} | all-to-all | bytes 524288 | tf_op jit(solution)/shard_map/all_to_all | solution.py:257
  123.2 0.0 collective-permute-done.37.p2
  123.2 3.3 %shard_map.53.y0 = bf16[256,512]{1,0:T(8,128)(2,1)S(1)} custom-call(bf16[512,256]{1,0:T(8,128)(2,1)S(1)} %bitcast.16), custom_call_target="tpu_custom_call" | custom-call | bytes 524288 | tf_op jit(solution)/shard_map/pallas_call | solution.py:29
  126.5 5.0 %collective-permute-start.39 = (bf16[256,512]{1,0:T(8,128)(2,1)S(1)}, bf16[256,512]{1,0:T(8,128)(2,1)S(1)}, u32[]{:S(2)}, u32[]{:S(2)}) collective-permute-start(bf16[256,512]{1,0:T(8,128)(2,1)S(1)} %shard_map.53.y0), channel_id=1, source_target_pairs={{0,480},{32,0},{64,32},{96,64},{128,96},{160,128},{192,160},{224,1... | collective-permute-start | bytes 786440 | tf_op jit(solution)/shard_map/ppermute | solution.py:253
  131.6 1.9 collective-permute-start.38
  133.5 4.5 %collective-permute-done.39.y1 = bf16[256,512]{1,0:T(8,128)(2,1)S(1)} collective-permute-done((bf16[256,512]{1,0:T(8,128)(2,1)S(1)}, bf16[256,512]{1,0:T(8,128)(2,1)S(1)}, u32[]{:S(2)}, u32[]{:S(2)}) %collective-permute-start.39) | collective-permute-done | bytes 262176 | tf_op jit(solution)/shard_map/ppermute | solution.py:253
  138.0 5.9 %collective-permute-done.38.y_1 = bf16[256,512]{1,0:T(8,128)(2,1)S(1)} collective-permute-done((bf16[256,512]{1,0:T(8,128)(2,1)S(1)}, bf16[256,512]{1,0:T(8,128)(2,1)S(1)}, u32[]{:S(2)}, u32[]{:S(2)}) %collective-permute-start.38) | collective-permute-done | bytes 262176 | tf_op jit(solution)/shard_map/ppermute | solution.py:253
  143.9 3.9 %shard_map.54 = (f32[512,512]{1,0:T(8,128)S(1)}, bf16[512,512]{1,0:T(8,128)(2,1)S(1)}, bf16[512,512]{1,0:T(8,128)(2,1)S(1)}, bf16[32,80,128]{2,1,0:T(8,128)(2,1)S(1)}) custom-call(s32[4]{0:T(128)S(1)} %add_convert_fusion.flags, bf16[256,512]{1,0:T(8,128)(2,1)S(1)} %collective-permute-done.38.y_1, bf16[256,512]{1,0:T(8,128)(2,1)S(1)} %shard_map.53.y0, ...), custom_call_target="tpu_custom_call" | custom-call | bytes 6684688 | tf_op jit(solution)/shard_map/pallas_call | solution.py:29
  147.8 30.1 %all_to_all.48.parts_ref = bf16[32,80,128]{2,1,0:T(8,128)(2,1)S(1)} all-to-all(bf16[32,80,128]{2,1,0:T(8,128)(2,1)S(1)} %get-tuple-element.116), channel_id=1, replica_groups=mesh['kstr'=16,'pw'=32] {'pw'}, dimensions={0} | all-to-all | bytes 1310720 | tf_op jit(solution)/shard_map/all_to_all | solution.py:257
  177.9 0.1 shard_map.55
  178.0 12.4 %all_to_all.49.total_ref.total = f32[16,8,128]{2,1,0:T(8,128)S(1)} all-to-all(f32[16,8,128]{2,1,0:T(8,128)S(1)} %get-tuple-element.117), channel_id=1, replica_groups=mesh['kstr'=16,'pw'=32] {'kstr'}, dimensions={0} | all-to-all | bytes 131072 | tf_op jit(solution)/shard_map/all_to_all | solution.py:257
  190.4 0.1 shard_map.56
  190.5 0.0 copy-start
  190.5 0.7 copy-done
  191.2 5.7 %all-to-all-start.4 = ((bf16[32,16,256]{2,1,0:T(8,128)(2,1)}), bf16[32,16,256]{2,1,0:T(8,128)(2,1)S(1)}, u32[]{:S(2)}, u32[]{:S(2)}) async-start(bf16[32,16,256]{2,1,0:T(8,128)(2,1)} %copy-done), calls=%async_computation.4 | async-start | bytes 524288 | tf_op jit(solution)/shard_map/all_to_all | solution.py:257
  197.0 2.3 collective-permute-start.41
  199.3 10.8 %all-to-all-done.4 = bf16[32,16,256]{2,1,0:T(8,128)(2,1)S(1)} async-done(((bf16[32,16,256]{2,1,0:T(8,128)(2,1)}), bf16[32,16,256]{2,1,0:T(8,128)(2,1)S(1)}, u32[]{:S(2)}, u32[]{:S(2)}) %all-to-all-start.4) | async-done | bytes 262176 | tf_op jit(solution)/shard_map/all_to_all | solution.py:257
  210.1 3.3 %shard_map.57.y0 = bf16[256,512]{1,0:T(8,128)(2,1)S(1)} custom-call(bf16[512,256]{1,0:T(8,128)(2,1)S(1)} %bitcast.15), custom_call_target="tpu_custom_call" | custom-call | bytes 524288 | tf_op jit(solution)/shard_map/pallas_call | solution.py:29
  213.4 2.2 collective-permute-start.40
  215.6 0.0 collective-permute-done.41.y_2
  215.6 1.0 copy-done.4
  216.6 1.0 copy-done.6
  217.7 2.4 shard_map.58
  220.1 4.7 %collective-permute-done.40.y_1 = bf16[256,512]{1,0:T(8,128)(2,1)S(1)} collective-permute-done((bf16[256,512]{1,0:T(8,128)(2,1)S(1)}, bf16[256,512]{1,0:T(8,128)(2,1)S(1)}, u32[]{:S(2)}, u32[]{:S(2)}) %collective-permute-start.40) | collective-permute-done | bytes 262176 | tf_op jit(solution)/shard_map/ppermute | solution.py:253
  224.9 0.7 shard_map.59
  225.6 15.7 %all_to_all.50.parts_ref = f32[32,8,128]{2,1,0:T(8,128)S(1)} all-to-all(f32[32,8,128]{2,1,0:T(8,128)S(1)} %get-tuple-element.128), channel_id=1, replica_groups=mesh['kstr'=16,'pw'=32] {'pw'}, dimensions={0} | all-to-all | bytes 262144 | tf_op jit(solution)/shard_map/all_to_all | solution.py:257
  241.4 10.5 %all_to_all.51.total_ref = f32[16,8,128]{2,1,0:T(8,128)S(1)} all-to-all(f32[16,8,128]{2,1,0:T(8,128)S(1)} %shard_map.60), channel_id=1, replica_groups=mesh['kstr'=16,'pw'=32] {'kstr'}, dimensions={0} | all-to-all | bytes 131072 | tf_op jit(solution)/shard_map/all_to_all | solution.py:257
  251.9 1.1 shard_map.61
  (13 shorter events, 0.1 us)
Async XLA Ops:
  1.7 18.8 %collective-permute-start.32 = (bf16[512,512]{1,0:T(8,128)(2,1)S(1)}, bf16[512,512]{1,0:T(8,128)(2,1)S(1)}, u32[]{:S(2)}, u32[]{:S(2)}) collective-permute-start(bf16[512,512]{1,0:T(8,128)(2,1)S(1)} %pad_maximum_fusion.state_ref.p0), channel_id=1, source_target_pairs={{0,31},{32,63},{448,449},{480,481},{1,0},{33,32},{449,450},{481,48... | collective-permute-start | bytes 1572872 | tf_op jit(solution)/shard_map/ppermute | solution.py:295
  10.5 30.0 %collective-permute-start.34 = (bf16[512,512]{1,0:T(8,128)(2,1)S(1)}, bf16[512,512]{1,0:T(8,128)(2,1)S(1)}, u32[]{:S(2)}, u32[]{:S(2)}) collective-permute-start(bf16[512,512]{1,0:T(8,128)(2,1)S(1)} %pad_maximum_fusion.state_ref.p0), channel_id=1, source_target_pairs={{0,64},{32,96},{64,128},{96,160},{128,192},{160,224},{192,256},{22... | collective-permute-start | bytes 1572872 | tf_op jit(solution)/shard_map/ppermute | solution.py:253
  12.4 28.9 %collective-permute-start.33 = (bf16[512,512]{1,0:T(8,128)(2,1)S(1)}, bf16[512,512]{1,0:T(8,128)(2,1)S(1)}, u32[]{:S(2)}, u32[]{:S(2)}) collective-permute-start(bf16[512,512]{1,0:T(8,128)(2,1)S(1)} %pad_maximum_fusion.state_ref.p0), channel_id=1, source_target_pairs={{0,480},{32,0},{64,32},{96,64},{128,96},{160,128},{192,160},{224,1... | collective-permute-start | bytes 1572872 | tf_op jit(solution)/shard_map/ppermute | solution.py:253
  21.3 19.2 %collective-permute-start = (bf16[512,512]{1,0:T(8,128)(2,1)S(1)}, bf16[512,512]{1,0:T(8,128)(2,1)}, u32[]{:S(2)}, u32[]{:S(2)}) collective-permute-start(bf16[512,512]{1,0:T(8,128)(2,1)S(1)} %param), channel_id=1, source_target_pairs={{0,480},{480,0},{32,448},{448,32},{1,481},{481,1},{33,449},{449,33... | collective-permute-start | bytes 1572872 | tf_op jit(solution)/shard_map/cond/branch_0_fun/ppermute | solution.py:106
  40.5 0.8 copy-start.1
  42.9 48.5 %collective-permute-start.35 = (bf16[512,512]{1,0:T(8,128)(2,1)S(1)}, bf16[512,512]{1,0:T(8,128)(2,1)S(1)}, u32[]{:S(2)}, u32[]{:S(2)}) collective-permute-start(bf16[512,512]{1,0:T(8,128)(2,1)S(1)} %pad_maximum_fusion.state_ref.p0), channel_id=1, source_target_pairs={{0,32},{32,64},{64,96},{96,128},{128,160},{160,192},{192,224},{224... | collective-permute-start | bytes 1572872 | tf_op jit(solution)/shard_map/ppermute | solution.py:253
  91.4 31.8 %collective-permute-start.36 = (bf16[512,512]{1,0:T(8,128)(2,1)}, bf16[512,512]{1,0:T(8,128)(2,1)S(1)}, u32[]{:S(2)}, u32[]{:S(2)}) collective-permute-start(bf16[512,512]{1,0:T(8,128)(2,1)} %get-tuple-element.133.closing_ref.closing), channel_id=1, source_target_pairs={{0,32},{32,0},{448,480},{480,448},{1,33},{33,1},{449,481},{481,449... | collective-permute-start | bytes 1572872 | tf_op jit(solution)/shard_map/ppermute | solution.py:309
  93.3 29.9 %collective-permute-start.37 = (bf16[512,512]{1,0:T(8,128)(2,1)S(1)}, bf16[512,512]{1,0:T(8,128)(2,1)S(1)}, u32[]{:S(2)}, u32[]{:S(2)}) collective-permute-start(bf16[512,512]{1,0:T(8,128)(2,1)S(1)} %get-tuple-element.110.p1), channel_id=1, source_target_pairs={{0,480},{32,0},{64,32},{96,64},{128,96},{160,128},{192,160},{224,1... | collective-permute-start | bytes 1572872 | tf_op jit(solution)/shard_map/ppermute | solution.py:253
  126.5 11.4 %collective-permute-start.39 = (bf16[256,512]{1,0:T(8,128)(2,1)S(1)}, bf16[256,512]{1,0:T(8,128)(2,1)S(1)}, u32[]{:S(2)}, u32[]{:S(2)}) collective-permute-start(bf16[256,512]{1,0:T(8,128)(2,1)S(1)} %shard_map.53.y0), channel_id=1, source_target_pairs={{0,480},{32,0},{64,32},{96,64},{128,96},{160,128},{192,160},{224,1... | collective-permute-start | bytes 786440 | tf_op jit(solution)/shard_map/ppermute | solution.py:253
  131.6 12.3 %collective-permute-start.38 = (bf16[256,512]{1,0:T(8,128)(2,1)S(1)}, bf16[256,512]{1,0:T(8,128)(2,1)S(1)}, u32[]{:S(2)}, u32[]{:S(2)}) collective-permute-start(bf16[256,512]{1,0:T(8,128)(2,1)S(1)} %shard_map.53.y0), channel_id=1, source_target_pairs={{0,32},{32,64},{64,96},{96,128},{128,160},{160,192},{192,224},{224... | collective-permute-start | bytes 786440 | tf_op jit(solution)/shard_map/ppermute | solution.py:253
  147.8 30.1 %copy-start.3 = (bf16[512,512]{1,0:T(8,128)(2,1)}, bf16[512,512]{1,0:T(8,128)(2,1)S(1)}, u32[]{:S(2)}) copy-start(bf16[512,512]{1,0:T(8,128)(2,1)S(1)} %get-tuple-element.125.g1) | copy-start | bytes 1572868
  147.8 30.1 %copy-start.5 = (bf16[512,512]{1,0:T(8,128)(2,1)}, bf16[512,512]{1,0:T(8,128)(2,1)S(1)}, u32[]{:S(2)}) copy-start(bf16[512,512]{1,0:T(8,128)(2,1)S(1)} %get-tuple-element.123.p_1) | copy-start | bytes 1572868
  190.5 0.7 copy-start
  191.2 18.9 %all-to-all-start.4 = ((bf16[32,16,256]{2,1,0:T(8,128)(2,1)}), bf16[32,16,256]{2,1,0:T(8,128)(2,1)S(1)}, u32[]{:S(2)}, u32[]{:S(2)}) async-start(bf16[32,16,256]{2,1,0:T(8,128)(2,1)} %copy-done), calls=%async_computation.4 | async-start | bytes 524288 | tf_op jit(solution)/shard_map/all_to_all | solution.py:257
  197.0 18.6 %collective-permute-start.41 = (bf16[256,512]{1,0:T(8,128)(2,1)S(1)}, bf16[256,512]{1,0:T(8,128)(2,1)}, u32[]{:S(2)}, u32[]{:S(2)}) collective-permute-start(bf16[256,512]{1,0:T(8,128)(2,1)S(1)} %shard_map.53.y0), channel_id=1, source_target_pairs={{0,64},{32,96},{64,128},{96,160},{128,192},{160,224},{192,256},{22... | collective-permute-start | bytes 786440 | tf_op jit(solution)/shard_map/ppermute | solution.py:253
  210.1 5.5 %copy-start.2 = (bf16[512,512]{1,0:T(8,128)(2,1)S(1)}, bf16[512,512]{1,0:T(8,128)(2,1)}, u32[]{:S(2)}) copy-start(bf16[512,512]{1,0:T(8,128)(2,1)} %copy-done.1) | copy-start | bytes 1572868
  213.4 11.5 %collective-permute-start.40 = (bf16[256,512]{1,0:T(8,128)(2,1)S(1)}, bf16[256,512]{1,0:T(8,128)(2,1)S(1)}, u32[]{:S(2)}, u32[]{:S(2)}) collective-permute-start(bf16[256,512]{1,0:T(8,128)(2,1)S(1)} %shard_map.57.y0), channel_id=1, source_target_pairs={{0,32},{32,64},{64,96},{96,128},{128,160},{160,192},{192,224},{224... | collective-permute-start | bytes 786440 | tf_op jit(solution)/shard_map/ppermute | solution.py:253
  215.6 1.0 copy-start.4
  216.6 1.0 copy-start.6

commit v6 on v5

--- a/solution.py
+++ b/solution.py
@@ -294,20 +294,20 @@
 
     beside = lax.ppermute(state, ("kstr", "pw"), beside_pairs())
     p1, p_2 = shifted(state, -1), shifted(state, 2)
+    p2 = shifted(state, -2)
     merged = call(merge_kernel, fields, bounds, state, beside, smem=1)
     near = close_string(merged, blocks)
-    near, p1, p_2 = lax.optimization_barrier((near, p1, p_2))
+    near, p1, p2, p_2 = lax.optimization_barrier((near, p1, p2, p_2))
 
     part, p1 = call(first_margin_kernel, (shape((full, NB), BF16), fields), flags, state, p1, near, smem=1)
     state, near, part = lax.optimization_barrier((state, near, part))
     parts = exchange(part, "pw").reshape(PARTS, CHUNK, NB)
     p_1 = shifted(state, 1)
-    parts, p_1, near, p1 = lax.optimization_barrier((parts, p_1, near, p1))
-    p2 = shifted(p1, -1)
+    parts, p_1, near = lax.optimization_barrier((parts, p_1, near))
     own, kept = call(collect_kernel, (chunks, chunk), parts)
     whole = exchange(own.reshape(full, NB), "pw")
     far = lax.ppermute(near, "kstr", [(0, 1), (1, 0), (end - 1, end), (end, end - 1)])
-    whole, far, p2 = lax.optimization_barrier((whole, far, p2))
+    whole, far = lax.optimization_barrier((whole, far))
 
     y0 = inverse(whole)
     y_1 = shifted(y0, 1)

time: 254 us -> 245 us (0.965)
  blocking collectives: 140 us -> 114 us
  waiting for transfers between devices: 34.2 us -> 42.9 us
  starting transfers between devices: 54 us -> 62.3 us
    all_to_all x6, blocking collectives: 140 us -> 114 us  [exchange(): return lax.all_to_all(value, axis, 0, 0, tiled=True)]
    ppermute x8, starting transfers between devices: 25.9 us -> 40.8 us  [shifted(): return lax.ppermute(value, 'kstr', [(i, (i + by) % NK) for i in range(NK)])]
    ppermute x1, waiting for transfers between devices: 7.61 us -> 17.7 us  [branch(): return lambda block: lax.ppermute(block, ('kstr', 'pw'), closing_pairs(by))]
    ppermute x1, starting transfers between devices: 11.6 us -> 2.84 us  [branch(): return lambda block: lax.ppermute(block, ('kstr', 'pw'), closing_pairs(by))]
  transfers between devices with their start and end apart: 12 -> 12, of which waited for: 6 -> 5; matrix products, arithmetic and copies ran while one was open for 1% -> 1% of each run, Pallas kernels for 3% -> 3%
where the time goes in v6:
time: 245 us; the launch traced here: 244 us
  blocking collectives  114 us (47%)
  starting transfers between devices  62.3 us (25%)
  waiting for transfers between devices  42.9 us (18%)
  Pallas kernels  17.7 us (7%)
  local copies, waits for them, and re-layouts  4.8 us (2%)
    all_to_all x6, blocking collectives, exchange(): return lax.all_to_all(value, axis, 0, 0, tiled=True)  114 us
    ppermute x8, starting transfers between devices, shifted(): return lax.ppermute(value, 'kstr', [(i, (i + by) % NK) for i in range(NK)])  40.8 us
    ppermute x1, waiting for transfers between devices, branch(): return lambda block: lax.ppermute(block, ('kstr', 'pw'), closing_pairs(by))  17.7 us
    pallas_call x12, Pallas kernels, call(): pl.pallas_call(kernel, out_shape=outs, in_specs=specs, out_specs=tuple((p...  17.7 us
    ppermute x8, waiting for transfers between devices, shifted(): return lax.ppermute(value, 'kstr', [(i, (i + by) % NK) for i in range(NK)])  14.3 us
    all_to_all x1, waiting for transfers between devices, exchange(): return lax.all_to_all(value, axis, 0, 0, tiled=True)  10.8 us
    ppermute x1, starting transfers between devices, body(): beside = lax.ppermute(state, ('kstr', 'pw'), beside_pairs())  8.79 us
    all_to_all x1, starting transfers between devices, exchange(): return lax.all_to_all(value, axis, 0, 0, tiled=True)  5.74 us
  transfers between devices with their start and end apart: 12, of which 5 were waited for; matrix products, arithmetic and copies ran while one was open for 1% of the time, Pallas kernels for 3%

profile of v6, /device:TPU:1, one launch (start us, length us, event | category | flops | bytes accessed | tf_op | source)
XLA Modules:
  0.0 244.0 jit_solution(6707653753380934632)
XLA Ops:
  0.6 1.1 pad_maximum_fusion.state_ref.p0
  1.7 8.8 %collective-permute-start.32 = (bf16[512,512]{1,0:T(8,128)(2,1)S(1)}, bf16[512,512]{1,0:T(8,128)(2,1)S(1)}, u32[]{:S(2)}, u32[]{:S(2)}) collective-permute-start(bf16[512,512]{1,0:T(8,128)(2,1)S(1)} %pad_maximum_fusion.state_ref.p0), channel_id=1, source_target_pairs={{0,31},{32,63},{448,449},{480,481},{1,0},{33,32},{449,450},{481,48... | collective-permute-start | bytes 1572872 | tf_op jit(solution)/shard_map/ppermute | solution.py:295
  10.5 1.9 collective-permute-start.35
  12.4 13.6 %collective-permute-start.34 = (bf16[512,512]{1,0:T(8,128)(2,1)S(1)}, bf16[512,512]{1,0:T(8,128)(2,1)S(1)}, u32[]{:S(2)}, u32[]{:S(2)}) collective-permute-start(bf16[512,512]{1,0:T(8,128)(2,1)S(1)} %pad_maximum_fusion.state_ref.p0), channel_id=1, source_target_pairs={{0,448},{32,480},{64,0},{96,32},{128,64},{160,96},{192,128},{224,1... | collective-permute-start | bytes 1572872 | tf_op jit(solution)/shard_map/ppermute | solution.py:253
  26.0 6.3 %collective-permute-start.33 = (bf16[512,512]{1,0:T(8,128)(2,1)S(1)}, bf16[512,512]{1,0:T(8,128)(2,1)S(1)}, u32[]{:S(2)}, u32[]{:S(2)}) collective-permute-start(bf16[512,512]{1,0:T(8,128)(2,1)S(1)} %pad_maximum_fusion.state_ref.p0), channel_id=1, source_target_pairs={{0,480},{32,0},{64,32},{96,64},{128,96},{160,128},{192,160},{224,1... | collective-permute-start | bytes 1572872 | tf_op jit(solution)/shard_map/ppermute | solution.py:253
  32.3 1.2 slice.3
  34.2 0.1 pad_add_fusion.bounds
  34.3 0.1 add_convert_fusion.flags
  34.3 0.0 collective-permute-done.32.beside_ref
  34.3 0.8 shard_map.50
  35.2 20.6 %conditional.1 = (bf16[512,512]{1,0:T(8,128)(2,1)}) conditional(s32[]{:T(128)} %clamp.3, bf16[512,512]{1,0:T(8,128)(2,1)S(1)} %shard_map.50, bf16[512,512]{1,0:T(8,128)(2,1)S(1)} %shard_map.50, bf16[512,512]{1,0:T(8,128)(2,1)S(1)} %shard_map.50, bf16[512,512]{1,0:T(8,128)(2,1)S(1)} %shard_map.50, ...), branch_computations={%region_0.1_spmd, %region_1.2_spmd, %region_2.3_spmd, %region_3.4_... | conditional | bytes 2097200 | solution.py:108
  35.2 2.8 %collective-permute-start.24 = (bf16[512,512]{1,0:T(8,128)(2,1)S(1)}, bf16[512,512]{1,0:T(8,128)(2,1)}, u32[]{:S(2)}, u32[]{:S(2)}) collective-permute-start(bf16[512,512]{1,0:T(8,128)(2,1)S(1)} %param.24), channel_id=1, source_target_pairs={{0,488},{480,24},{32,456},{448,56},{1,489},{481,25},{33,457},{449,... | collective-permute-start | bytes 1572872 | tf_op jit(solution)/shard_map/cond/branch_24_fun/ppermute | solution.py:106
  38.1 17.7 %collective-permute-done.24 = bf16[512,512]{1,0:T(8,128)(2,1)} collective-permute-done((bf16[512,512]{1,0:T(8,128)(2,1)S(1)}, bf16[512,512]{1,0:T(8,128)(2,1)}, u32[]{:S(2)}, u32[]{:S(2)}) %collective-permute-start.24) | collective-permute-done | bytes 524320 | tf_op jit(solution)/shard_map/cond/branch_24_fun/ppermute | solution.py:106
  55.8 0.8 copy-done.1
  56.6 0.0 collective-permute-done.33.next_ref
  56.6 1.7 shard_map.51
  58.4 8.1 %collective-permute-start.36 = (bf16[512,512]{1,0:T(8,128)(2,1)S(1)}, bf16[512,512]{1,0:T(8,128)(2,1)S(1)}, u32[]{:S(2)}, u32[]{:S(2)}) collective-permute-start(bf16[512,512]{1,0:T(8,128)(2,1)S(1)} %pad_maximum_fusion.state_ref.p0), channel_id=1, source_target_pairs={{0,32},{32,64},{64,96},{96,128},{128,160},{160,192},{192,224},{224... | collective-permute-start | bytes 1572872 | tf_op jit(solution)/shard_map/ppermute | solution.py:253
  66.5 25.9 %all_to_all.46.parts_ref = bf16[32,16,256]{2,1,0:T(8,128)(2,1)S(1)} all-to-all(bf16[32,16,256]{2,1,0:T(8,128)(2,1)S(1)} %bitcast.17), channel_id=1, replica_groups=mesh['kstr'=16,'pw'=32] {'pw'}, dimensions={0} | all-to-all | bytes 524288 | tf_op jit(solution)/shard_map/all_to_all | solution.py:257
  92.4 0.0 collective-permute-done.36.before
  92.4 4.2 %collective-permute-start.37 = (bf16[512,512]{1,0:T(8,128)(2,1)}, bf16[512,512]{1,0:T(8,128)(2,1)S(1)}, u32[]{:S(2)}, u32[]{:S(2)}) collective-permute-start(bf16[512,512]{1,0:T(8,128)(2,1)} %get-tuple-element.131.closing_ref.closing), channel_id=1, source_target_pairs={{0,32},{32,0},{448,480},{480,448},{1,33},{33,1},{449,481},{481,449... | collective-permute-start | bytes 1572872 | tf_op jit(solution)/shard_map/ppermute | solution.py:309
  96.6 0.1 shard_map.52
  96.7 20.2 %all_to_all.47 = bf16[32,16,256]{2,1,0:T(8,128)(2,1)S(1)} all-to-all(bf16[32,16,256]{2,1,0:T(8,128)(2,1)S(1)} %get-tuple-element.106), channel_id=1, replica_groups=mesh['kstr'=16,'pw'=32] {'pw'}, dimensions={0} | all-to-all | bytes 524288 | tf_op jit(solution)/shard_map/all_to_all | solution.py:257
  116.9 0.0 collective-permute-done.37.beyond.closing
  116.9 3.3 %shard_map.53.y0 = bf16[256,512]{1,0:T(8,128)(2,1)S(1)} custom-call(bf16[512,256]{1,0:T(8,128)(2,1)S(1)} %bitcast.16), custom_call_target="tpu_custom_call" | custom-call | bytes 524288 | tf_op jit(solution)/shard_map/pallas_call | solution.py:29
  120.2 4.6 %collective-permute-start.39 = (bf16[256,512]{1,0:T(8,128)(2,1)S(1)}, bf16[256,512]{1,0:T(8,128)(2,1)S(1)}, u32[]{:S(2)}, u32[]{:S(2)}) collective-permute-start(bf16[256,512]{1,0:T(8,128)(2,1)S(1)} %shard_map.53.y0), channel_id=1, source_target_pairs={{0,480},{32,0},{64,32},{96,64},{128,96},{160,128},{192,160},{224,1... | collective-permute-start | bytes 786440 | tf_op jit(solution)/shard_map/ppermute | solution.py:253
  124.8 1.9 collective-permute-start.38
  126.7 3.4 %collective-permute-done.39.y1 = bf16[256,512]{1,0:T(8,128)(2,1)S(1)} collective-permute-done((bf16[256,512]{1,0:T(8,128)(2,1)S(1)}, bf16[256,512]{1,0:T(8,128)(2,1)S(1)}, u32[]{:S(2)}, u32[]{:S(2)}) %collective-permute-start.39) | collective-permute-done | bytes 262176 | tf_op jit(solution)/shard_map/ppermute | solution.py:253
  130.1 6.2 %collective-permute-done.38.y_1 = bf16[256,512]{1,0:T(8,128)(2,1)S(1)} collective-permute-done((bf16[256,512]{1,0:T(8,128)(2,1)S(1)}, bf16[256,512]{1,0:T(8,128)(2,1)S(1)}, u32[]{:S(2)}, u32[]{:S(2)}) %collective-permute-start.38) | collective-permute-done | bytes 262176 | tf_op jit(solution)/shard_map/ppermute | solution.py:253
  136.3 3.9 %shard_map.54 = (f32[512,512]{1,0:T(8,128)S(1)}, bf16[512,512]{1,0:T(8,128)(2,1)S(1)}, bf16[512,512]{1,0:T(8,128)(2,1)S(1)}, bf16[32,80,128]{2,1,0:T(8,128)(2,1)S(1)}) custom-call(s32[4]{0:T(128)S(1)} %add_convert_fusion.flags, bf16[256,512]{1,0:T(8,128)(2,1)S(1)} %collective-permute-done.38.y_1, bf16[256,512]{1,0:T(8,128)(2,1)S(1)} %shard_map.53.y0, ...), custom_call_target="tpu_custom_call" | custom-call | bytes 6684688 | tf_op jit(solution)/shard_map/pallas_call | solution.py:29
  140.2 28.6 %all_to_all.48.parts_ref = bf16[32,80,128]{2,1,0:T(8,128)(2,1)S(1)} all-to-all(bf16[32,80,128]{2,1,0:T(8,128)(2,1)S(1)} %get-tuple-element.114), channel_id=1, replica_groups=mesh['kstr'=16,'pw'=32] {'pw'}, dimensions={0} | all-to-all | bytes 1310720 | tf_op jit(solution)/shard_map/all_to_all | solution.py:257
  168.8 0.1 shard_map.55
  168.9 12.5 %all_to_all.49.total_ref.total = f32[16,8,128]{2,1,0:T(8,128)S(1)} all-to-all(f32[16,8,128]{2,1,0:T(8,128)S(1)} %get-tuple-element.115), channel_id=1, replica_groups=mesh['kstr'=16,'pw'=32] {'kstr'}, dimensions={0} | all-to-all | bytes 131072 | tf_op jit(solution)/shard_map/all_to_all | solution.py:257
  181.4 0.1 shard_map.56
  181.5 0.0 copy-start
  181.5 0.7 copy-done
  182.2 5.7 %all-to-all-start.4 = ((bf16[32,16,256]{2,1,0:T(8,128)(2,1)}), bf16[32,16,256]{2,1,0:T(8,128)(2,1)S(1)}, u32[]{:S(2)}, u32[]{:S(2)}) async-start(bf16[32,16,256]{2,1,0:T(8,128)(2,1)} %copy-done), calls=%async_computation.4 | async-start | bytes 524288 | tf_op jit(solution)/shard_map/all_to_all | solution.py:257
  188.0 2.3 collective-permute-start.41
  190.3 10.8 %all-to-all-done.4 = bf16[32,16,256]{2,1,0:T(8,128)(2,1)S(1)} async-done(((bf16[32,16,256]{2,1,0:T(8,128)(2,1)}), bf16[32,16,256]{2,1,0:T(8,128)(2,1)S(1)}, u32[]{:S(2)}, u32[]{:S(2)}) %all-to-all-start.4) | async-done | bytes 262176 | tf_op jit(solution)/shard_map/all_to_all | solution.py:257
  201.1 3.3 %shard_map.57.y0 = bf16[256,512]{1,0:T(8,128)(2,1)S(1)} custom-call(bf16[512,256]{1,0:T(8,128)(2,1)S(1)} %bitcast.15), custom_call_target="tpu_custom_call" | custom-call | bytes 524288 | tf_op jit(solution)/shard_map/pallas_call | solution.py:29
  204.4 2.2 collective-permute-start.40
  206.6 1.0 copy-done.6
  207.6 1.0 copy-done.8
  208.7 2.4 %shard_map.58 = (bf16[512,512]{1,0:T(8,128)(2,1)S(1)}, bf16[512,512]{1,0:T(8,128)(2,1)S(1)}, bf16[512,512]{1,0:T(8,128)(2,1)S(1)}) custom-call(s32[4]{0:T(128)S(1)} %add_convert_fusion.flags, f32[16,8,128]{2,1,0:T(8,128)S(1)} %all_to_all.49.total_ref.total, bf16[256,512]{1,0:T(8,128)(2,1)} %collective-permute-done.41.y_2, ...), custom_call_target="tpu_custom_call" | custom-call | bytes 6357008 | tf_op jit(solution)/shard_map/pallas_call | solution.py:29
  211.1 4.7 %collective-permute-done.40.y_1 = bf16[256,512]{1,0:T(8,128)(2,1)S(1)} collective-permute-done((bf16[256,512]{1,0:T(8,128)(2,1)S(1)}, bf16[256,512]{1,0:T(8,128)(2,1)S(1)}, u32[]{:S(2)}, u32[]{:S(2)}) %collective-permute-start.40) | collective-permute-done | bytes 262176 | tf_op jit(solution)/shard_map/ppermute | solution.py:253
  215.9 0.7 shard_map.59
  216.6 15.7 %all_to_all.50.parts_ref = f32[32,8,128]{2,1,0:T(8,128)S(1)} all-to-all(f32[32,8,128]{2,1,0:T(8,128)S(1)} %get-tuple-element.126), channel_id=1, replica_groups=mesh['kstr'=16,'pw'=32] {'pw'}, dimensions={0} | all-to-all | bytes 262144 | tf_op jit(solution)/shard_map/all_to_all | solution.py:257
  232.4 10.5 %all_to_all.51.total_ref = f32[16,8,128]{2,1,0:T(8,128)S(1)} all-to-all(f32[16,8,128]{2,1,0:T(8,128)S(1)} %shard_map.60), channel_id=1, replica_groups=mesh['kstr'=16,'pw'=32] {'kstr'}, dimensions={0} | all-to-all | bytes 131072 | tf_op jit(solution)/shard_map/all_to_all | solution.py:257
  243.0 1.1 shard_map.61
  (17 shorter events, 0.1 us)
Async XLA Ops:
  1.7 32.6 %collective-permute-start.32 = (bf16[512,512]{1,0:T(8,128)(2,1)S(1)}, bf16[512,512]{1,0:T(8,128)(2,1)S(1)}, u32[]{:S(2)}, u32[]{:S(2)}) collective-permute-start(bf16[512,512]{1,0:T(8,128)(2,1)S(1)} %pad_maximum_fusion.state_ref.p0), channel_id=1, source_target_pairs={{0,31},{32,63},{448,449},{480,481},{1,0},{33,32},{449,450},{481,48... | collective-permute-start | bytes 1572872 | tf_op jit(solution)/shard_map/ppermute | solution.py:295
  10.5 45.3 %collective-permute-start.35 = (bf16[512,512]{1,0:T(8,128)(2,1)S(1)}, bf16[512,512]{1,0:T(8,128)(2,1)S(1)}, u32[]{:S(2)}, u32[]{:S(2)}) collective-permute-start(bf16[512,512]{1,0:T(8,128)(2,1)S(1)} %pad_maximum_fusion.state_ref.p0), channel_id=1, source_target_pairs={{0,64},{32,96},{64,128},{96,160},{128,192},{160,224},{192,256},{22... | collective-permute-start | bytes 1572872 | tf_op jit(solution)/shard_map/ppermute | solution.py:253
  12.4 44.2 %collective-permute-start.34 = (bf16[512,512]{1,0:T(8,128)(2,1)S(1)}, bf16[512,512]{1,0:T(8,128)(2,1)S(1)}, u32[]{:S(2)}, u32[]{:S(2)}) collective-permute-start(bf16[512,512]{1,0:T(8,128)(2,1)S(1)} %pad_maximum_fusion.state_ref.p0), channel_id=1, source_target_pairs={{0,448},{32,480},{64,0},{96,32},{128,64},{160,96},{192,128},{224,1... | collective-permute-start | bytes 1572872 | tf_op jit(solution)/shard_map/ppermute | solution.py:253
  26.0 30.6 %collective-permute-start.33 = (bf16[512,512]{1,0:T(8,128)(2,1)S(1)}, bf16[512,512]{1,0:T(8,128)(2,1)S(1)}, u32[]{:S(2)}, u32[]{:S(2)}) collective-permute-start(bf16[512,512]{1,0:T(8,128)(2,1)S(1)} %pad_maximum_fusion.state_ref.p0), channel_id=1, source_target_pairs={{0,480},{32,0},{64,32},{96,64},{128,96},{160,128},{192,160},{224,1... | collective-permute-start | bytes 1572872 | tf_op jit(solution)/shard_map/ppermute | solution.py:253
  35.2 20.6 %collective-permute-start.24 = (bf16[512,512]{1,0:T(8,128)(2,1)S(1)}, bf16[512,512]{1,0:T(8,128)(2,1)}, u32[]{:S(2)}, u32[]{:S(2)}) collective-permute-start(bf16[512,512]{1,0:T(8,128)(2,1)S(1)} %param.24), channel_id=1, source_target_pairs={{0,488},{480,24},{32,456},{448,56},{1,489},{481,25},{33,457},{449,... | collective-permute-start | bytes 1572872 | tf_op jit(solution)/shard_map/cond/branch_24_fun/ppermute | solution.py:106
  55.8 0.8 copy-start.1
  56.6 1.8 copy-start.3
  58.4 34.0 %collective-permute-start.36 = (bf16[512,512]{1,0:T(8,128)(2,1)S(1)}, bf16[512,512]{1,0:T(8,128)(2,1)S(1)}, u32[]{:S(2)}, u32[]{:S(2)}) collective-permute-start(bf16[512,512]{1,0:T(8,128)(2,1)S(1)} %pad_maximum_fusion.state_ref.p0), channel_id=1, source_target_pairs={{0,32},{32,64},{64,96},{96,128},{128,160},{160,192},{192,224},{224... | collective-permute-start | bytes 1572872 | tf_op jit(solution)/shard_map/ppermute | solution.py:253
  92.4 24.5 %collective-permute-start.37 = (bf16[512,512]{1,0:T(8,128)(2,1)}, bf16[512,512]{1,0:T(8,128)(2,1)S(1)}, u32[]{:S(2)}, u32[]{:S(2)}) collective-permute-start(bf16[512,512]{1,0:T(8,128)(2,1)} %get-tuple-element.131.closing_ref.closing), channel_id=1, source_target_pairs={{0,32},{32,0},{448,480},{480,448},{1,33},{33,1},{449,481},{481,449... | collective-permute-start | bytes 1572872 | tf_op jit(solution)/shard_map/ppermute | solution.py:309
  96.6 39.6 %copy-start.4 = (bf16[512,512]{1,0:T(8,128)(2,1)S(1)}, bf16[512,512]{1,0:T(8,128)(2,1)}, u32[]{:S(2)}) copy-start(bf16[512,512]{1,0:T(8,128)(2,1)} %copy-done.3) | copy-start | bytes 1572868
  120.2 9.9 %collective-permute-start.39 = (bf16[256,512]{1,0:T(8,128)(2,1)S(1)}, bf16[256,512]{1,0:T(8,128)(2,1)S(1)}, u32[]{:S(2)}, u32[]{:S(2)}) collective-permute-start(bf16[256,512]{1,0:T(8,128)(2,1)S(1)} %shard_map.53.y0), channel_id=1, source_target_pairs={{0,480},{32,0},{64,32},{96,64},{128,96},{160,128},{192,160},{224,1... | collective-permute-start | bytes 786440 | tf_op jit(solution)/shard_map/ppermute | solution.py:253
  124.8 11.5 %collective-permute-start.38 = (bf16[256,512]{1,0:T(8,128)(2,1)S(1)}, bf16[256,512]{1,0:T(8,128)(2,1)S(1)}, u32[]{:S(2)}, u32[]{:S(2)}) collective-permute-start(bf16[256,512]{1,0:T(8,128)(2,1)S(1)} %shard_map.53.y0), channel_id=1, source_target_pairs={{0,32},{32,64},{64,96},{96,128},{128,160},{160,192},{192,224},{224... | collective-permute-start | bytes 786440 | tf_op jit(solution)/shard_map/ppermute | solution.py:253
  140.2 28.6 %copy-start.5 = (bf16[512,512]{1,0:T(8,128)(2,1)}, bf16[512,512]{1,0:T(8,128)(2,1)S(1)}, u32[]{:S(2)}) copy-start(bf16[512,512]{1,0:T(8,128)(2,1)S(1)} %get-tuple-element.123.g1) | copy-start | bytes 1572868
  140.2 28.6 %copy-start.7 = (bf16[512,512]{1,0:T(8,128)(2,1)}, bf16[512,512]{1,0:T(8,128)(2,1)S(1)}, u32[]{:S(2)}) copy-start(bf16[512,512]{1,0:T(8,128)(2,1)S(1)} %get-tuple-element.121.p_1) | copy-start | bytes 1572868
  181.5 0.7 copy-start
  182.2 18.9 %all-to-all-start.4 = ((bf16[32,16,256]{2,1,0:T(8,128)(2,1)}), bf16[32,16,256]{2,1,0:T(8,128)(2,1)S(1)}, u32[]{:S(2)}, u32[]{:S(2)}) async-start(bf16[32,16,256]{2,1,0:T(8,128)(2,1)} %copy-done), calls=%async_computation.4 | async-start | bytes 524288 | tf_op jit(solution)/shard_map/all_to_all | solution.py:257
  188.0 18.6 %collective-permute-start.41 = (bf16[256,512]{1,0:T(8,128)(2,1)S(1)}, bf16[256,512]{1,0:T(8,128)(2,1)}, u32[]{:S(2)}, u32[]{:S(2)}) collective-permute-start(bf16[256,512]{1,0:T(8,128)(2,1)S(1)} %shard_map.53.y0), channel_id=1, source_target_pairs={{0,64},{32,96},{64,128},{96,160},{128,192},{160,224},{192,256},{22... | collective-permute-start | bytes 786440 | tf_op jit(solution)/shard_map/ppermute | solution.py:253
  201.1 5.5 %copy-start.2 = (bf16[512,512]{1,0:T(8,128)(2,1)S(1)}, bf16[512,512]{1,0:T(8,128)(2,1)}, u32[]{:S(2)}) copy-start(bf16[512,512]{1,0:T(8,128)(2,1)} %copy-done.1) | copy-start | bytes 1572868
  204.4 11.5 %collective-permute-start.40 = (bf16[256,512]{1,0:T(8,128)(2,1)S(1)}, bf16[256,512]{1,0:T(8,128)(2,1)S(1)}, u32[]{:S(2)}, u32[]{:S(2)}) collective-permute-start(bf16[256,512]{1,0:T(8,128)(2,1)S(1)} %shard_map.57.y0), channel_id=1, source_target_pairs={{0,32},{32,64},{64,96},{96,128},{128,160},{160,192},{192,224},{224... | collective-permute-start | bytes 786440 | tf_op jit(solution)/shard_map/ppermute | solution.py:253
  206.6 1.0 copy-start.6
  207.6 1.0 copy-start.8

commit v7 on v6

--- a/solution.py
+++ b/solution.py
@@ -293,17 +293,16 @@
     flags = jnp.stack([row == 0, row <= 1, row >= NK - 2, row == end]).astype(jnp.int32)
 
     beside = lax.ppermute(state, ("kstr", "pw"), beside_pairs())
-    p1, p_2 = shifted(state, -1), shifted(state, 2)
+    p1, p_1, p_2 = shifted(state, -1), shifted(state, 1), shifted(state, 2)
     p2 = shifted(state, -2)
     merged = call(merge_kernel, fields, bounds, state, beside, smem=1)
     near = close_string(merged, blocks)
-    near, p1, p2, p_2 = lax.optimization_barrier((near, p1, p2, p_2))
+    near, p1, p_1, p2, p_2 = lax.optimization_barrier((near, p1, p_1, p2, p_2))
 
     part, p1 = call(first_margin_kernel, (shape((full, NB), BF16), fields), flags, state, p1, near, smem=1)
-    state, near, part = lax.optimization_barrier((state, near, part))
+    near, part = lax.optimization_barrier((near, part))
     parts = exchange(part, "pw").reshape(PARTS, CHUNK, NB)
-    p_1 = shifted(state, 1)
-    parts, p_1, near = lax.optimization_barrier((parts, p_1, near))
+    parts, near = lax.optimization_barrier((parts, near))
     own, kept = call(collect_kernel, (chunks, chunk), parts)
     whole = exchange(own.reshape(full, NB), "pw")
     far = lax.ppermute(near, "kstr", [(0, 1), (1, 0), (end - 1, end), (end, end - 1)])

time: 245 us -> 248 us (1.012)
  blocking collectives: 114 us -> 119 us
    all_to_all x6, blocking collectives: 114 us -> 119 us  [exchange(): return lax.all_to_all(value, axis, 0, 0, tiled=True)]
    ppermute x8, starting transfers between devices: 40.8 us -> 36.1 us  [shifted(): return lax.ppermute(value, 'kstr', [(i, (i + by) % NK) for i in range(NK)])]
    ppermute x1, waiting for transfers between devices: 17.7 us -> 13.8 us  [branch(): return lambda block: lax.ppermute(block, ('kstr', 'pw'), closing_pairs(by))]
    ppermute x8, waiting for transfers between devices: 14.3 us -> 18.2 us  [shifted(): return lax.ppermute(value, 'kstr', [(i, (i + by) % NK) for i in range(NK)])]
    ppermute x1, starting transfers between devices: 2.84 us -> 6.33 us  [branch(): return lambda block: lax.ppermute(block, ('kstr', 'pw'), closing_pairs(by))]
  transfers between devices with their start and end apart: 12 -> 12, of which waited for: 5 -> 6; matrix products, arithmetic and copies ran while one was open for 1% -> 1% of each run, Pallas kernels for 3% -> 3%
where the time goes in v7:
time: 248 us; the launch traced here: 247 us
  blocking collectives  119 us (48%)
  starting transfers between devices  60.5 us (24%)
  waiting for transfers between devices  42.8 us (17%)
  Pallas kernels  17.5 us (7%)
  local copies, waits for them, and re-layouts  4.8 us (2%)
    all_to_all x6, blocking collectives, exchange(): return lax.all_to_all(value, axis, 0, 0, tiled=True)  119 us
    ppermute x8, starting transfers between devices, shifted(): return lax.ppermute(value, 'kstr', [(i, (i + by) % NK) for i in range(NK)])  36.1 us
    ppermute x8, waiting for transfers between devices, shifted(): return lax.ppermute(value, 'kstr', [(i, (i + by) % NK) for i in range(NK)])  18.2 us
    pallas_call x12, Pallas kernels, call(): pl.pallas_call(kernel, out_shape=outs, in_specs=specs, out_specs=tuple((p...  17.5 us
    ppermute x1, waiting for transfers between devices, branch(): return lambda block: lax.ppermute(block, ('kstr', 'pw'), closing_pairs(by))  13.8 us
    all_to_all x1, waiting for transfers between devices, exchange(): return lax.all_to_all(value, axis, 0, 0, tiled=True)  10.8 us
    ppermute x1, starting transfers between devices, body(): beside = lax.ppermute(state, ('kstr', 'pw'), beside_pairs())  8.79 us
    ppermute x1, starting transfers between devices, branch(): return lambda block: lax.ppermute(block, ('kstr', 'pw'), closing_pairs(by))  6.33 us
  transfers between devices with their start and end apart: 12, of which 6 were waited for; matrix products, arithmetic and copies ran while one was open for 1% of the time, Pallas kernels for 3%

profile of v7, /device:TPU:1, one launch (start us, length us, event | category | flops | bytes accessed | tf_op | source)
XLA Modules:
  0.0 247.5 jit_solution(6443010293879922781)
XLA Ops:
  0.6 1.1 pad_maximum_fusion.state_ref.p0
  1.7 8.8 %collective-permute-start.32 = (bf16[512,512]{1,0:T(8,128)(2,1)S(1)}, bf16[512,512]{1,0:T(8,128)(2,1)S(1)}, u32[]{:S(2)}, u32[]{:S(2)}) collective-permute-start(bf16[512,512]{1,0:T(8,128)(2,1)S(1)} %pad_maximum_fusion.state_ref.p0), channel_id=1, source_target_pairs={{0,31},{32,63},{448,449},{480,481},{1,0},{33,32},{449,450},{481,48... | collective-permute-start | bytes 1572872 | tf_op jit(solution)/shard_map/ppermute | solution.py:295
  10.5 1.9 collective-permute-start.36
  12.4 13.6 %collective-permute-start.35 = (bf16[512,512]{1,0:T(8,128)(2,1)S(1)}, bf16[512,512]{1,0:T(8,128)(2,1)S(1)}, u32[]{:S(2)}, u32[]{:S(2)}) collective-permute-start(bf16[512,512]{1,0:T(8,128)(2,1)S(1)} %pad_maximum_fusion.state_ref.p0), channel_id=1, source_target_pairs={{0,448},{32,480},{64,0},{96,32},{128,64},{160,96},{192,128},{224,1... | collective-permute-start | bytes 1572872 | tf_op jit(solution)/shard_map/ppermute | solution.py:253
  26.0 3.7 %collective-permute-start.34 = (bf16[512,512]{1,0:T(8,128)(2,1)S(1)}, bf16[512,512]{1,0:T(8,128)(2,1)S(1)}, u32[]{:S(2)}, u32[]{:S(2)}) collective-permute-start(bf16[512,512]{1,0:T(8,128)(2,1)S(1)} %pad_maximum_fusion.state_ref.p0), channel_id=1, source_target_pairs={{0,32},{32,64},{64,96},{96,128},{128,160},{160,192},{192,224},{224... | collective-permute-start | bytes 1572872 | tf_op jit(solution)/shard_map/ppermute | solution.py:253
  29.7 4.5 %collective-permute-start.33 = (bf16[512,512]{1,0:T(8,128)(2,1)S(1)}, bf16[512,512]{1,0:T(8,128)(2,1)S(1)}, u32[]{:S(2)}, u32[]{:S(2)}) collective-permute-start(bf16[512,512]{1,0:T(8,128)(2,1)S(1)} %pad_maximum_fusion.state_ref.p0), channel_id=1, source_target_pairs={{0,480},{32,0},{64,32},{96,64},{128,96},{160,128},{192,160},{224,1... | collective-permute-start | bytes 1572872 | tf_op jit(solution)/shard_map/ppermute | solution.py:253
  34.2 1.2 slice.3
  36.1 0.1 pad_add_fusion.bounds
  36.2 0.1 add_convert_fusion.flags
  36.3 0.0 collective-permute-done.32.beside_ref
  36.3 0.8 shard_map.50
  37.1 20.2 %conditional.1 = (bf16[512,512]{1,0:T(8,128)(2,1)}) conditional(s32[]{:T(128)} %clamp.3, bf16[512,512]{1,0:T(8,128)(2,1)S(1)} %shard_map.50, bf16[512,512]{1,0:T(8,128)(2,1)S(1)} %shard_map.50, bf16[512,512]{1,0:T(8,128)(2,1)S(1)} %shard_map.50, bf16[512,512]{1,0:T(8,128)(2,1)S(1)} %shard_map.50, ...), branch_computations={%region_0.1_spmd, %region_1.2_spmd, %region_2.3_spmd, %region_3.4_... | conditional | bytes 2097200 | solution.py:108
  37.1 6.3 %collective-permute-start.9 = (bf16[512,512]{1,0:T(8,128)(2,1)S(1)}, bf16[512,512]{1,0:T(8,128)(2,1)}, u32[]{:S(2)}, u32[]{:S(2)}) collective-permute-start(bf16[512,512]{1,0:T(8,128)(2,1)S(1)} %param.9), channel_id=1, source_target_pairs={{0,503},{480,9},{32,471},{448,41},{1,504},{481,10},{33,472},{449,4... | collective-permute-start | bytes 1572872 | tf_op jit(solution)/shard_map/cond/branch_9_fun/ppermute | solution.py:106
  43.5 13.8 %collective-permute-done.9 = bf16[512,512]{1,0:T(8,128)(2,1)} collective-permute-done((bf16[512,512]{1,0:T(8,128)(2,1)S(1)}, bf16[512,512]{1,0:T(8,128)(2,1)}, u32[]{:S(2)}, u32[]{:S(2)}) %collective-permute-start.9) | collective-permute-done | bytes 524320 | tf_op jit(solution)/shard_map/cond/branch_9_fun/ppermute | solution.py:106
  57.3 0.0 collective-permute-done.36.p_2
  57.3 0.8 copy-done.1
  58.1 0.0 collective-permute-done.35.p2
  58.1 3.5 %collective-permute-done.33.next_ref = bf16[512,512]{1,0:T(8,128)(2,1)S(1)} collective-permute-done((bf16[512,512]{1,0:T(8,128)(2,1)S(1)}, bf16[512,512]{1,0:T(8,128)(2,1)S(1)}, u32[]{:S(2)}, u32[]{:S(2)}) %collective-permute-start.33) | collective-permute-done | bytes 524320 | tf_op jit(solution)/shard_map/ppermute | solution.py:253
  61.6 1.6 shard_map.51
  63.2 32.2 %all_to_all.46.parts_ref = bf16[32,16,256]{2,1,0:T(8,128)(2,1)S(1)} all-to-all(bf16[32,16,256]{2,1,0:T(8,128)(2,1)S(1)} %bitcast.17), channel_id=1, replica_groups=mesh['kstr'=16,'pw'=32] {'pw'}, dimensions={0} | all-to-all | bytes 524288 | tf_op jit(solution)/shard_map/all_to_all | solution.py:257
  95.4 3.5 %collective-permute-start.37 = (bf16[512,512]{1,0:T(8,128)(2,1)}, bf16[512,512]{1,0:T(8,128)(2,1)S(1)}, u32[]{:S(2)}, u32[]{:S(2)}) collective-permute-start(bf16[512,512]{1,0:T(8,128)(2,1)} %get-tuple-element.129.closing_ref.closing), channel_id=1, source_target_pairs={{0,32},{32,0},{448,480},{480,448},{1,33},{33,1},{449,481},{481,449... | collective-permute-start | bytes 1572872 | tf_op jit(solution)/shard_map/ppermute | solution.py:308
  99.0 0.1 shard_map.52
  99.0 19.2 %all_to_all.47 = bf16[32,16,256]{2,1,0:T(8,128)(2,1)S(1)} all-to-all(bf16[32,16,256]{2,1,0:T(8,128)(2,1)S(1)} %get-tuple-element.104), channel_id=1, replica_groups=mesh['kstr'=16,'pw'=32] {'pw'}, dimensions={0} | all-to-all | bytes 524288 | tf_op jit(solution)/shard_map/all_to_all | solution.py:257
  118.2 3.3 %shard_map.53.y0 = bf16[256,512]{1,0:T(8,128)(2,1)S(1)} custom-call(bf16[512,256]{1,0:T(8,128)(2,1)S(1)} %bitcast.16), custom_call_target="tpu_custom_call" | custom-call | bytes 524288 | tf_op jit(solution)/shard_map/pallas_call | solution.py:29
  121.5 6.0 %collective-permute-start.39 = (bf16[256,512]{1,0:T(8,128)(2,1)S(1)}, bf16[256,512]{1,0:T(8,128)(2,1)S(1)}, u32[]{:S(2)}, u32[]{:S(2)}) collective-permute-start(bf16[256,512]{1,0:T(8,128)(2,1)S(1)} %shard_map.53.y0), channel_id=1, source_target_pairs={{0,480},{32,0},{64,32},{96,64},{128,96},{160,128},{192,160},{224,1... | collective-permute-start | bytes 786440 | tf_op jit(solution)/shard_map/ppermute | solution.py:253
  127.6 1.9 collective-permute-start.38
  129.5 4.0 %collective-permute-done.39.y1 = bf16[256,512]{1,0:T(8,128)(2,1)S(1)} collective-permute-done((bf16[256,512]{1,0:T(8,128)(2,1)S(1)}, bf16[256,512]{1,0:T(8,128)(2,1)S(1)}, u32[]{:S(2)}, u32[]{:S(2)}) %collective-permute-start.39) | collective-permute-done | bytes 262176 | tf_op jit(solution)/shard_map/ppermute | solution.py:253
  133.4 6.0 %collective-permute-done.38.y_1 = bf16[256,512]{1,0:T(8,128)(2,1)S(1)} collective-permute-done((bf16[256,512]{1,0:T(8,128)(2,1)S(1)}, bf16[256,512]{1,0:T(8,128)(2,1)S(1)}, u32[]{:S(2)}, u32[]{:S(2)}) %collective-permute-start.38) | collective-permute-done | bytes 262176 | tf_op jit(solution)/shard_map/ppermute | solution.py:253
  139.4 3.9 %shard_map.54 = (f32[512,512]{1,0:T(8,128)S(1)}, bf16[512,512]{1,0:T(8,128)(2,1)S(1)}, bf16[512,512]{1,0:T(8,128)(2,1)S(1)}, bf16[32,80,128]{2,1,0:T(8,128)(2,1)S(1)}) custom-call(s32[4]{0:T(128)S(1)} %add_convert_fusion.flags, bf16[256,512]{1,0:T(8,128)(2,1)S(1)} %collective-permute-done.38.y_1, bf16[256,512]{1,0:T(8,128)(2,1)S(1)} %shard_map.53.y0, ...), custom_call_target="tpu_custom_call" | custom-call | bytes 6684688 | tf_op jit(solution)/shard_map/pallas_call | solution.py:29
  143.4 28.6 %all_to_all.48.parts_ref = bf16[32,80,128]{2,1,0:T(8,128)(2,1)S(1)} all-to-all(bf16[32,80,128]{2,1,0:T(8,128)(2,1)S(1)} %get-tuple-element.112), channel_id=1, replica_groups=mesh['kstr'=16,'pw'=32] {'pw'}, dimensions={0} | all-to-all | bytes 1310720 | tf_op jit(solution)/shard_map/all_to_all | solution.py:257
  172.0 0.1 shard_map.55
  172.1 12.7 %all_to_all.49.total_ref.total = f32[16,8,128]{2,1,0:T(8,128)S(1)} all-to-all(f32[16,8,128]{2,1,0:T(8,128)S(1)} %get-tuple-element.113), channel_id=1, replica_groups=mesh['kstr'=16,'pw'=32] {'kstr'}, dimensions={0} | all-to-all | bytes 131072 | tf_op jit(solution)/shard_map/all_to_all | solution.py:257
  184.8 0.1 shard_map.56
  185.0 0.0 copy-start
  185.0 0.7 copy-done
  185.7 5.7 %all-to-all-start.4 = ((bf16[32,16,256]{2,1,0:T(8,128)(2,1)}), bf16[32,16,256]{2,1,0:T(8,128)(2,1)S(1)}, u32[]{:S(2)}, u32[]{:S(2)}) async-start(bf16[32,16,256]{2,1,0:T(8,128)(2,1)} %copy-done), calls=%async_computation.4 | async-start | bytes 524288 | tf_op jit(solution)/shard_map/all_to_all | solution.py:257
  191.4 2.3 collective-permute-start.41
  193.7 10.8 %all-to-all-done.4 = bf16[32,16,256]{2,1,0:T(8,128)(2,1)S(1)} async-done(((bf16[32,16,256]{2,1,0:T(8,128)(2,1)}), bf16[32,16,256]{2,1,0:T(8,128)(2,1)S(1)}, u32[]{:S(2)}, u32[]{:S(2)}) %all-to-all-start.4) | async-done | bytes 262176 | tf_op jit(solution)/shard_map/all_to_all | solution.py:257
  204.6 3.3 %shard_map.57.y0 = bf16[256,512]{1,0:T(8,128)(2,1)S(1)} custom-call(bf16[512,256]{1,0:T(8,128)(2,1)S(1)} %bitcast.15), custom_call_target="tpu_custom_call" | custom-call | bytes 524288 | tf_op jit(solution)/shard_map/pallas_call | solution.py:29
  207.9 2.2 collective-permute-start.40
  210.1 1.0 copy-done.8
  211.1 1.0 copy-done.10
  212.1 2.4 shard_map.58
  214.6 4.7 %collective-permute-done.40.y_1 = bf16[256,512]{1,0:T(8,128)(2,1)S(1)} collective-permute-done((bf16[256,512]{1,0:T(8,128)(2,1)S(1)}, bf16[256,512]{1,0:T(8,128)(2,1)S(1)}, u32[]{:S(2)}, u32[]{:S(2)}) %collective-permute-start.40) | collective-permute-done | bytes 262176 | tf_op jit(solution)/shard_map/ppermute | solution.py:253
  219.3 0.7 shard_map.59
  220.1 15.7 %all_to_all.50.parts_ref = f32[32,8,128]{2,1,0:T(8,128)S(1)} all-to-all(f32[32,8,128]{2,1,0:T(8,128)S(1)} %get-tuple-element.124), channel_id=1, replica_groups=mesh['kstr'=16,'pw'=32] {'pw'}, dimensions={0} | all-to-all | bytes 262144 | tf_op jit(solution)/shard_map/all_to_all | solution.py:257
  235.8 10.5 %all_to_all.51.total_ref = f32[16,8,128]{2,1,0:T(8,128)S(1)} all-to-all(f32[16,8,128]{2,1,0:T(8,128)S(1)} %shard_map.60), channel_id=1, replica_groups=mesh['kstr'=16,'pw'=32] {'kstr'}, dimensions={0} | all-to-all | bytes 131072 | tf_op jit(solution)/shard_map/all_to_all | solution.py:257
  246.4 1.1 shard_map.61
  (21 shorter events, 0.1 us)
Async XLA Ops:
  1.7 34.6 %collective-permute-start.32 = (bf16[512,512]{1,0:T(8,128)(2,1)S(1)}, bf16[512,512]{1,0:T(8,128)(2,1)S(1)}, u32[]{:S(2)}, u32[]{:S(2)}) collective-permute-start(bf16[512,512]{1,0:T(8,128)(2,1)S(1)} %pad_maximum_fusion.state_ref.p0), channel_id=1, source_target_pairs={{0,31},{32,63},{448,449},{480,481},{1,0},{33,32},{449,450},{481,48... | collective-permute-start | bytes 1572872 | tf_op jit(solution)/shard_map/ppermute | solution.py:295
  10.5 46.8 %collective-permute-start.36 = (bf16[512,512]{1,0:T(8,128)(2,1)S(1)}, bf16[512,512]{1,0:T(8,128)(2,1)S(1)}, u32[]{:S(2)}, u32[]{:S(2)}) collective-permute-start(bf16[512,512]{1,0:T(8,128)(2,1)S(1)} %pad_maximum_fusion.state_ref.p0), channel_id=1, source_target_pairs={{0,64},{32,96},{64,128},{96,160},{128,192},{160,224},{192,256},{22... | collective-permute-start | bytes 1572872 | tf_op jit(solution)/shard_map/ppermute | solution.py:253
  12.4 45.7 %collective-permute-start.35 = (bf16[512,512]{1,0:T(8,128)(2,1)S(1)}, bf16[512,512]{1,0:T(8,128)(2,1)S(1)}, u32[]{:S(2)}, u32[]{:S(2)}) collective-permute-start(bf16[512,512]{1,0:T(8,128)(2,1)S(1)} %pad_maximum_fusion.state_ref.p0), channel_id=1, source_target_pairs={{0,448},{32,480},{64,0},{96,32},{128,64},{160,96},{192,128},{224,1... | collective-permute-start | bytes 1572872 | tf_op jit(solution)/shard_map/ppermute | solution.py:253
  26.0 32.1 %collective-permute-start.34 = (bf16[512,512]{1,0:T(8,128)(2,1)S(1)}, bf16[512,512]{1,0:T(8,128)(2,1)S(1)}, u32[]{:S(2)}, u32[]{:S(2)}) collective-permute-start(bf16[512,512]{1,0:T(8,128)(2,1)S(1)} %pad_maximum_fusion.state_ref.p0), channel_id=1, source_target_pairs={{0,32},{32,64},{64,96},{96,128},{128,160},{160,192},{192,224},{224... | collective-permute-start | bytes 1572872 | tf_op jit(solution)/shard_map/ppermute | solution.py:253
  29.7 31.9 %collective-permute-start.33 = (bf16[512,512]{1,0:T(8,128)(2,1)S(1)}, bf16[512,512]{1,0:T(8,128)(2,1)S(1)}, u32[]{:S(2)}, u32[]{:S(2)}) collective-permute-start(bf16[512,512]{1,0:T(8,128)(2,1)S(1)} %pad_maximum_fusion.state_ref.p0), channel_id=1, source_target_pairs={{0,480},{32,0},{64,32},{96,64},{128,96},{160,128},{192,160},{224,1... | collective-permute-start | bytes 1572872 | tf_op jit(solution)/shard_map/ppermute | solution.py:253
  37.1 20.1 %collective-permute-start.9 = (bf16[512,512]{1,0:T(8,128)(2,1)S(1)}, bf16[512,512]{1,0:T(8,128)(2,1)}, u32[]{:S(2)}, u32[]{:S(2)}) collective-permute-start(bf16[512,512]{1,0:T(8,128)(2,1)S(1)} %param.9), channel_id=1, source_target_pairs={{0,503},{480,9},{32,471},{448,41},{1,504},{481,10},{33,472},{449,4... | collective-permute-start | bytes 1572872 | tf_op jit(solution)/shard_map/cond/branch_9_fun/ppermute | solution.py:106
  57.3 0.8 copy-start.1
  58.1 5.1 %copy-start.3 = (bf16[512,512]{1,0:T(8,128)(2,1)}, bf16[512,512]{1,0:T(8,128)(2,1)S(1)}, u32[]{:S(2)}) copy-start(bf16[512,512]{1,0:T(8,128)(2,1)S(1)} %collective-permute-done.35.p2) | copy-start | bytes 1572868
  58.1 5.1 %copy-start.5 = (bf16[512,512]{1,0:T(8,128)(2,1)}, bf16[512,512]{1,0:T(8,128)(2,1)S(1)}, u32[]{:S(2)}) copy-start(bf16[512,512]{1,0:T(8,128)(2,1)S(1)} %collective-permute-done.34.before) | copy-start | bytes 1572868
  95.4 22.8 %collective-permute-start.37 = (bf16[512,512]{1,0:T(8,128)(2,1)}, bf16[512,512]{1,0:T(8,128)(2,1)S(1)}, u32[]{:S(2)}, u32[]{:S(2)}) collective-permute-start(bf16[512,512]{1,0:T(8,128)(2,1)} %get-tuple-element.129.closing_ref.closing), channel_id=1, source_target_pairs={{0,32},{32,0},{448,480},{480,448},{1,33},{33,1},{449,481},{481,449... | collective-permute-start | bytes 1572872 | tf_op jit(solution)/shard_map/ppermute | solution.py:308
  99.0 40.4 %copy-start.4 = (bf16[512,512]{1,0:T(8,128)(2,1)S(1)}, bf16[512,512]{1,0:T(8,128)(2,1)}, u32[]{:S(2)}) copy-start(bf16[512,512]{1,0:T(8,128)(2,1)} %copy-done.3) | copy-start | bytes 1572868
  99.0 40.4 %copy-start.6 = (bf16[512,512]{1,0:T(8,128)(2,1)S(1)}, bf16[512,512]{1,0:T(8,128)(2,1)}, u32[]{:S(2)}) copy-start(bf16[512,512]{1,0:T(8,128)(2,1)} %copy-done.5) | copy-start | bytes 1572868
  121.5 11.9 %collective-permute-start.39 = (bf16[256,512]{1,0:T(8,128)(2,1)S(1)}, bf16[256,512]{1,0:T(8,128)(2,1)S(1)}, u32[]{:S(2)}, u32[]{:S(2)}) collective-permute-start(bf16[256,512]{1,0:T(8,128)(2,1)S(1)} %shard_map.53.y0), channel_id=1, source_target_pairs={{0,480},{32,0},{64,32},{96,64},{128,96},{160,128},{192,160},{224,1... | collective-permute-start | bytes 786440 | tf_op jit(solution)/shard_map/ppermute | solution.py:253
  127.6 11.9 %collective-permute-start.38 = (bf16[256,512]{1,0:T(8,128)(2,1)S(1)}, bf16[256,512]{1,0:T(8,128)(2,1)S(1)}, u32[]{:S(2)}, u32[]{:S(2)}) collective-permute-start(bf16[256,512]{1,0:T(8,128)(2,1)S(1)} %shard_map.53.y0), channel_id=1, source_target_pairs={{0,32},{32,64},{64,96},{96,128},{128,160},{160,192},{192,224},{224... | collective-permute-start | bytes 786440 | tf_op jit(solution)/shard_map/ppermute | solution.py:253
  143.4 28.7 %copy-start.7 = (bf16[512,512]{1,0:T(8,128)(2,1)}, bf16[512,512]{1,0:T(8,128)(2,1)S(1)}, u32[]{:S(2)}) copy-start(bf16[512,512]{1,0:T(8,128)(2,1)S(1)} %get-tuple-element.121.g1) | copy-start | bytes 1572868
  143.4 28.6 %copy-start.9 = (bf16[512,512]{1,0:T(8,128)(2,1)}, bf16[512,512]{1,0:T(8,128)(2,1)S(1)}, u32[]{:S(2)}) copy-start(bf16[512,512]{1,0:T(8,128)(2,1)S(1)} %get-tuple-element.119.p_1) | copy-start | bytes 1572868
  185.0 0.7 copy-start
  185.7 18.9 %all-to-all-start.4 = ((bf16[32,16,256]{2,1,0:T(8,128)(2,1)}), bf16[32,16,256]{2,1,0:T(8,128)(2,1)S(1)}, u32[]{:S(2)}, u32[]{:S(2)}) async-start(bf16[32,16,256]{2,1,0:T(8,128)(2,1)} %copy-done), calls=%async_computation.4 | async-start | bytes 524288 | tf_op jit(solution)/shard_map/all_to_all | solution.py:257
  191.4 18.6 %collective-permute-start.41 = (bf16[256,512]{1,0:T(8,128)(2,1)S(1)}, bf16[256,512]{1,0:T(8,128)(2,1)}, u32[]{:S(2)}, u32[]{:S(2)}) collective-permute-start(bf16[256,512]{1,0:T(8,128)(2,1)S(1)} %shard_map.53.y0), channel_id=1, source_target_pairs={{0,64},{32,96},{64,128},{96,160},{128,192},{160,224},{192,256},{22... | collective-permute-start | bytes 786440 | tf_op jit(solution)/shard_map/ppermute | solution.py:253
  204.6 5.5 %copy-start.2 = (bf16[512,512]{1,0:T(8,128)(2,1)S(1)}, bf16[512,512]{1,0:T(8,128)(2,1)}, u32[]{:S(2)}) copy-start(bf16[512,512]{1,0:T(8,128)(2,1)} %copy-done.1) | copy-start | bytes 1572868
  207.9 11.5 %collective-permute-start.40 = (bf16[256,512]{1,0:T(8,128)(2,1)S(1)}, bf16[256,512]{1,0:T(8,128)(2,1)S(1)}, u32[]{:S(2)}, u32[]{:S(2)}) collective-permute-start(bf16[256,512]{1,0:T(8,128)(2,1)S(1)} %shard_map.57.y0), channel_id=1, source_target_pairs={{0,32},{32,64},{64,96},{96,128},{128,160},{160,192},{192,224},{224... | collective-permute-start | bytes 786440 | tf_op jit(solution)/shard_map/ppermute | solution.py:253
  210.0 1.0 copy-start.8
  211.1 1.0 copy-start.10

commit v8 on v6

--- a/solution.py
+++ b/solution.py
@@ -98,6 +98,8 @@
         for row in (0, 1):
             pairs.append((place(row, j), place(NK - 1 - row, j - by)))
             pairs.append((place(NK - 1 - row, j), place(row, j + by)))
+    for row in range(2, NK - 2):
+        pairs += [(place(row, j), place(row, j)) for j in range(PARTS)]
     return pairs
 
 

time: 245 us -> 244 us (level)
  starting transfers between devices: 62.3 us -> 49 us
  waiting for transfers between devices: 42.9 us -> 50.7 us
  blocking collectives: 114 us -> 118 us
    ppermute x8, starting transfers between devices: 40.8 us -> 22.8 us  [shifted(): return lax.ppermute(value, 'kstr', [(i, (i + by) % NK) for i in range(NK)])]
    ppermute x1, waiting for transfers between devices: 17.7 us -> 24.8 us  [branch(): return lambda block: lax.ppermute(block, ('kstr', 'pw'), closing_pairs(by))]
    ppermute x1, starting transfers between devices: 2.84 us -> 9.85 us  [branch(): return lambda block: lax.ppermute(block, ('kstr', 'pw'), closing_pairs(by))]
    all_to_all x6, blocking collectives: 114 us -> 118 us  [exchange(): return lax.all_to_all(value, axis, 0, 0, tiled=True)]
where the time goes in v8:
time: 244 us; the launch traced here: 243 us
  blocking collectives  118 us (48%)
  waiting for transfers between devices  50.7 us (21%)
  starting transfers between devices  49 us (20%)
  Pallas kernels  17.7 us (7%)
  local copies, waits for them, and re-layouts  4.8 us (2%)
    all_to_all x6, blocking collectives, exchange(): return lax.all_to_all(value, axis, 0, 0, tiled=True)  118 us
    ppermute x1, waiting for transfers between devices, branch(): return lambda block: lax.ppermute(block, ('kstr', 'pw'), closing_pairs(by))  24.8 us
    ppermute x8, starting transfers between devices, shifted(): return lax.ppermute(value, 'kstr', [(i, (i + by) % NK) for i in range(NK)])  22.8 us
    pallas_call x12, Pallas kernels, call(): pl.pallas_call(kernel, out_shape=outs, in_specs=specs, out_specs=tuple((p...  17.7 us
    ppermute x8, waiting for transfers between devices, shifted(): return lax.ppermute(value, 'kstr', [(i, (i + by) % NK) for i in range(NK)])  15 us
    all_to_all x1, waiting for transfers between devices, exchange(): return lax.all_to_all(value, axis, 0, 0, tiled=True)  10.8 us
    ppermute x1, starting transfers between devices, branch(): return lambda block: lax.ppermute(block, ('kstr', 'pw'), closing_pairs(by))  9.85 us
    ppermute x1, starting transfers between devices, body(): beside = lax.ppermute(state, ('kstr', 'pw'), beside_pairs())  8.79 us
  transfers between devices with their start and end apart: 12, of which 5 were waited for; matrix products, arithmetic and copies ran while one was open for 1% of the time, Pallas kernels for 3%

profile of v8, /device:TPU:1, one launch (start us, length us, event | category | flops | bytes accessed | tf_op | source)
XLA Modules:
  0.0 243.4 jit_solution(13800745129162227704)
XLA Ops:
  0.6 1.1 pad_maximum_fusion.state_ref.p0
  1.7 8.8 %collective-permute-start.32 = (bf16[512,512]{1,0:T(8,128)(2,1)S(1)}, bf16[512,512]{1,0:T(8,128)(2,1)S(1)}, u32[]{:S(2)}, u32[]{:S(2)}) collective-permute-start(bf16[512,512]{1,0:T(8,128)(2,1)S(1)} %pad_maximum_fusion.state_ref.p0), channel_id=1, source_target_pairs={{0,31},{32,63},{448,449},{480,481},{1,0},{33,32},{449,450},{481,48... | collective-permute-start | bytes 1572872 | tf_op jit(solution)/shard_map/ppermute | solution.py:297
  10.5 1.9 collective-permute-start.35
  12.4 4.6 %collective-permute-start.34 = (bf16[512,512]{1,0:T(8,128)(2,1)S(1)}, bf16[512,512]{1,0:T(8,128)(2,1)S(1)}, u32[]{:S(2)}, u32[]{:S(2)}) collective-permute-start(bf16[512,512]{1,0:T(8,128)(2,1)S(1)} %pad_maximum_fusion.state_ref.p0), channel_id=1, source_target_pairs={{0,448},{32,480},{64,0},{96,32},{128,64},{160,96},{192,128},{224,1... | collective-permute-start | bytes 1572872 | tf_op jit(solution)/shard_map/ppermute | solution.py:255
  17.0 4.1 %collective-permute-start.33 = (bf16[512,512]{1,0:T(8,128)(2,1)S(1)}, bf16[512,512]{1,0:T(8,128)(2,1)S(1)}, u32[]{:S(2)}, u32[]{:S(2)}) collective-permute-start(bf16[512,512]{1,0:T(8,128)(2,1)S(1)} %pad_maximum_fusion.state_ref.p0), channel_id=1, source_target_pairs={{0,480},{32,0},{64,32},{96,64},{128,96},{160,128},{192,160},{224,1... | collective-permute-start | bytes 1572872 | tf_op jit(solution)/shard_map/ppermute | solution.py:255
  21.1 1.2 slice.3
  23.0 0.1 pad_add_fusion.bounds
  23.1 0.1 add_convert_fusion.flags
  23.2 0.0 collective-permute-done.32.beside_ref
  23.2 0.8 shard_map.50
  24.0 34.7 %conditional.1 = (bf16[512,512]{1,0:T(8,128)(2,1)}) conditional(s32[]{:T(128)} %clamp.3, bf16[512,512]{1,0:T(8,128)(2,1)S(1)} %shard_map.50, bf16[512,512]{1,0:T(8,128)(2,1)S(1)} %shard_map.50, bf16[512,512]{1,0:T(8,128)(2,1)S(1)} %shard_map.50, bf16[512,512]{1,0:T(8,128)(2,1)S(1)} %shard_map.50, ...), branch_computations={%region_0.1_spmd, %region_1.2_spmd, %region_2.3_spmd, %region_3.4_... | conditional | bytes 2097200 | solution.py:110
  24.1 9.9 %collective-permute-start.19 = (bf16[512,512]{1,0:T(8,128)(2,1)S(1)}, bf16[512,512]{1,0:T(8,128)(2,1)}, u32[]{:S(2)}, u32[]{:S(2)}) collective-permute-start(bf16[512,512]{1,0:T(8,128)(2,1)S(1)} %param.19), channel_id=1, source_target_pairs={{0,493},{480,19},{32,461},{448,51},{1,494},{481,20},{33,462},{449,... | collective-permute-start | bytes 1572872 | tf_op jit(solution)/shard_map/cond/branch_19_fun/ppermute | solution.py:108
  33.9 24.8 %collective-permute-done.19 = bf16[512,512]{1,0:T(8,128)(2,1)} collective-permute-done((bf16[512,512]{1,0:T(8,128)(2,1)S(1)}, bf16[512,512]{1,0:T(8,128)(2,1)}, u32[]{:S(2)}, u32[]{:S(2)}) %collective-permute-start.19) | collective-permute-done | bytes 524320 | tf_op jit(solution)/shard_map/cond/branch_19_fun/ppermute | solution.py:108
  58.7 0.0 collective-permute-done.35.p_2
  58.8 0.8 copy-done.1
  59.6 0.0 collective-permute-done.34.p2
  59.6 0.0 collective-permute-done.33.next_ref
  59.6 1.8 shard_map.51
  61.4 2.3 collective-permute-start.36
  63.6 28.9 %all_to_all.46.parts_ref = bf16[32,16,256]{2,1,0:T(8,128)(2,1)S(1)} all-to-all(bf16[32,16,256]{2,1,0:T(8,128)(2,1)S(1)} %bitcast.17), channel_id=1, replica_groups=mesh['kstr'=16,'pw'=32] {'pw'}, dimensions={0} | all-to-all | bytes 524288 | tf_op jit(solution)/shard_map/all_to_all | solution.py:259
  92.5 1.9 collective-permute-start.37
  94.4 0.1 shard_map.52
  94.5 22.0 %all_to_all.47 = bf16[32,16,256]{2,1,0:T(8,128)(2,1)S(1)} all-to-all(bf16[32,16,256]{2,1,0:T(8,128)(2,1)S(1)} %get-tuple-element.106), channel_id=1, replica_groups=mesh['kstr'=16,'pw'=32] {'pw'}, dimensions={0} | all-to-all | bytes 524288 | tf_op jit(solution)/shard_map/all_to_all | solution.py:259
  116.5 3.3 %shard_map.53.y0 = bf16[256,512]{1,0:T(8,128)(2,1)S(1)} custom-call(bf16[512,256]{1,0:T(8,128)(2,1)S(1)} %bitcast.16), custom_call_target="tpu_custom_call" | custom-call | bytes 524288 | tf_op jit(solution)/shard_map/pallas_call | solution.py:29
  119.8 3.5 %collective-permute-start.39 = (bf16[256,512]{1,0:T(8,128)(2,1)S(1)}, bf16[256,512]{1,0:T(8,128)(2,1)S(1)}, u32[]{:S(2)}, u32[]{:S(2)}) collective-permute-start(bf16[256,512]{1,0:T(8,128)(2,1)S(1)} %shard_map.53.y0), channel_id=1, source_target_pairs={{0,480},{32,0},{64,32},{96,64},{128,96},{160,128},{192,160},{224,1... | collective-permute-start | bytes 786440 | tf_op jit(solution)/shard_map/ppermute | solution.py:255
  123.3 1.9 collective-permute-start.38
  125.3 4.2 %collective-permute-done.39.y1 = bf16[256,512]{1,0:T(8,128)(2,1)S(1)} collective-permute-done((bf16[256,512]{1,0:T(8,128)(2,1)S(1)}, bf16[256,512]{1,0:T(8,128)(2,1)S(1)}, u32[]{:S(2)}, u32[]{:S(2)}) %collective-permute-start.39) | collective-permute-done | bytes 262176 | tf_op jit(solution)/shard_map/ppermute | solution.py:255
  129.5 6.1 %collective-permute-done.38.y_1 = bf16[256,512]{1,0:T(8,128)(2,1)S(1)} collective-permute-done((bf16[256,512]{1,0:T(8,128)(2,1)S(1)}, bf16[256,512]{1,0:T(8,128)(2,1)S(1)}, u32[]{:S(2)}, u32[]{:S(2)}) %collective-permute-start.38) | collective-permute-done | bytes 262176 | tf_op jit(solution)/shard_map/ppermute | solution.py:255
  135.5 3.9 %shard_map.54 = (f32[512,512]{1,0:T(8,128)S(1)}, bf16[512,512]{1,0:T(8,128)(2,1)S(1)}, bf16[512,512]{1,0:T(8,128)(2,1)S(1)}, bf16[32,80,128]{2,1,0:T(8,128)(2,1)S(1)}) custom-call(s32[4]{0:T(128)S(1)} %add_convert_fusion.flags, bf16[256,512]{1,0:T(8,128)(2,1)S(1)} %collective-permute-done.38.y_1, bf16[256,512]{1,0:T(8,128)(2,1)S(1)} %shard_map.53.y0, ...), custom_call_target="tpu_custom_call" | custom-call | bytes 6684688 | tf_op jit(solution)/shard_map/pallas_call | solution.py:29
  139.5 28.3 %all_to_all.48.parts_ref = bf16[32,80,128]{2,1,0:T(8,128)(2,1)S(1)} all-to-all(bf16[32,80,128]{2,1,0:T(8,128)(2,1)S(1)} %get-tuple-element.114), channel_id=1, replica_groups=mesh['kstr'=16,'pw'=32] {'pw'}, dimensions={0} | all-to-all | bytes 1310720 | tf_op jit(solution)/shard_map/all_to_all | solution.py:259
  167.8 0.1 shard_map.55
  167.9 12.8 %all_to_all.49.total_ref.total = f32[16,8,128]{2,1,0:T(8,128)S(1)} all-to-all(f32[16,8,128]{2,1,0:T(8,128)S(1)} %get-tuple-element.115), channel_id=1, replica_groups=mesh['kstr'=16,'pw'=32] {'kstr'}, dimensions={0} | all-to-all | bytes 131072 | tf_op jit(solution)/shard_map/all_to_all | solution.py:259
  180.7 0.1 shard_map.56
  180.9 0.0 copy-start
  180.9 0.7 copy-done
  181.6 5.7 %all-to-all-start.4 = ((bf16[32,16,256]{2,1,0:T(8,128)(2,1)}), bf16[32,16,256]{2,1,0:T(8,128)(2,1)S(1)}, u32[]{:S(2)}, u32[]{:S(2)}) async-start(bf16[32,16,256]{2,1,0:T(8,128)(2,1)} %copy-done), calls=%async_computation.4 | async-start | bytes 524288 | tf_op jit(solution)/shard_map/all_to_all | solution.py:259
  187.3 2.3 collective-permute-start.41
  189.6 10.8 %all-to-all-done.4 = bf16[32,16,256]{2,1,0:T(8,128)(2,1)S(1)} async-done(((bf16[32,16,256]{2,1,0:T(8,128)(2,1)}), bf16[32,16,256]{2,1,0:T(8,128)(2,1)S(1)}, u32[]{:S(2)}, u32[]{:S(2)}) %all-to-all-start.4) | async-done | bytes 262176 | tf_op jit(solution)/shard_map/all_to_all | solution.py:259
  200.5 3.3 %shard_map.57.y0 = bf16[256,512]{1,0:T(8,128)(2,1)S(1)} custom-call(bf16[512,256]{1,0:T(8,128)(2,1)S(1)} %bitcast.15), custom_call_target="tpu_custom_call" | custom-call | bytes 524288 | tf_op jit(solution)/shard_map/pallas_call | solution.py:29
  203.8 2.2 collective-permute-start.40
  206.0 1.0 copy-done.6
  207.0 1.0 copy-done.8
  208.1 2.4 %shard_map.58 = (bf16[512,512]{1,0:T(8,128)(2,1)S(1)}, bf16[512,512]{1,0:T(8,128)(2,1)S(1)}, bf16[512,512]{1,0:T(8,128)(2,1)S(1)}) custom-call(s32[4]{0:T(128)S(1)} %add_convert_fusion.flags, f32[16,8,128]{2,1,0:T(8,128)S(1)} %all_to_all.49.total_ref.total, bf16[256,512]{1,0:T(8,128)(2,1)} %collective-permute-done.41.y_2, ...), custom_call_target="tpu_custom_call" | custom-call | bytes 6357008 | tf_op jit(solution)/shard_map/pallas_call | solution.py:29
  210.5 4.7 %collective-permute-done.40.y_1 = bf16[256,512]{1,0:T(8,128)(2,1)S(1)} collective-permute-done((bf16[256,512]{1,0:T(8,128)(2,1)S(1)}, bf16[256,512]{1,0:T(8,128)(2,1)S(1)}, u32[]{:S(2)}, u32[]{:S(2)}) %collective-permute-start.40) | collective-permute-done | bytes 262176 | tf_op jit(solution)/shard_map/ppermute | solution.py:255
  215.2 0.7 shard_map.59
  216.0 15.7 %all_to_all.50.parts_ref = f32[32,8,128]{2,1,0:T(8,128)S(1)} all-to-all(f32[32,8,128]{2,1,0:T(8,128)S(1)} %get-tuple-element.126), channel_id=1, replica_groups=mesh['kstr'=16,'pw'=32] {'pw'}, dimensions={0} | all-to-all | bytes 262144 | tf_op jit(solution)/shard_map/all_to_all | solution.py:259
  231.8 10.5 %all_to_all.51.total_ref = f32[16,8,128]{2,1,0:T(8,128)S(1)} all-to-all(f32[16,8,128]{2,1,0:T(8,128)S(1)} %shard_map.60), channel_id=1, replica_groups=mesh['kstr'=16,'pw'=32] {'kstr'}, dimensions={0} | all-to-all | bytes 131072 | tf_op jit(solution)/shard_map/all_to_all | solution.py:259
  242.3 1.1 shard_map.61
  (17 shorter events, 0.1 us)
Async XLA Ops:
  1.7 21.5 %collective-permute-start.32 = (bf16[512,512]{1,0:T(8,128)(2,1)S(1)}, bf16[512,512]{1,0:T(8,128)(2,1)S(1)}, u32[]{:S(2)}, u32[]{:S(2)}) collective-permute-start(bf16[512,512]{1,0:T(8,128)(2,1)S(1)} %pad_maximum_fusion.state_ref.p0), channel_id=1, source_target_pairs={{0,31},{32,63},{448,449},{480,481},{1,0},{33,32},{449,450},{481,48... | collective-permute-start | bytes 1572872 | tf_op jit(solution)/shard_map/ppermute | solution.py:297
  10.5 48.3 %collective-permute-start.35 = (bf16[512,512]{1,0:T(8,128)(2,1)S(1)}, bf16[512,512]{1,0:T(8,128)(2,1)S(1)}, u32[]{:S(2)}, u32[]{:S(2)}) collective-permute-start(bf16[512,512]{1,0:T(8,128)(2,1)S(1)} %pad_maximum_fusion.state_ref.p0), channel_id=1, source_target_pairs={{0,64},{32,96},{64,128},{96,160},{128,192},{160,224},{192,256},{22... | collective-permute-start | bytes 1572872 | tf_op jit(solution)/shard_map/ppermute | solution.py:255
  12.4 47.2 %collective-permute-start.34 = (bf16[512,512]{1,0:T(8,128)(2,1)S(1)}, bf16[512,512]{1,0:T(8,128)(2,1)S(1)}, u32[]{:S(2)}, u32[]{:S(2)}) collective-permute-start(bf16[512,512]{1,0:T(8,128)(2,1)S(1)} %pad_maximum_fusion.state_ref.p0), channel_id=1, source_target_pairs={{0,448},{32,480},{64,0},{96,32},{128,64},{160,96},{192,128},{224,1... | collective-permute-start | bytes 1572872 | tf_op jit(solution)/shard_map/ppermute | solution.py:255
  17.0 42.6 %collective-permute-start.33 = (bf16[512,512]{1,0:T(8,128)(2,1)S(1)}, bf16[512,512]{1,0:T(8,128)(2,1)S(1)}, u32[]{:S(2)}, u32[]{:S(2)}) collective-permute-start(bf16[512,512]{1,0:T(8,128)(2,1)S(1)} %pad_maximum_fusion.state_ref.p0), channel_id=1, source_target_pairs={{0,480},{32,0},{64,32},{96,64},{128,96},{160,128},{192,160},{224,1... | collective-permute-start | bytes 1572872 | tf_op jit(solution)/shard_map/ppermute | solution.py:255
  24.1 34.7 %collective-permute-start.19 = (bf16[512,512]{1,0:T(8,128)(2,1)S(1)}, bf16[512,512]{1,0:T(8,128)(2,1)}, u32[]{:S(2)}, u32[]{:S(2)}) collective-permute-start(bf16[512,512]{1,0:T(8,128)(2,1)S(1)} %param.19), channel_id=1, source_target_pairs={{0,493},{480,19},{32,461},{448,51},{1,494},{481,20},{33,462},{449,... | collective-permute-start | bytes 1572872 | tf_op jit(solution)/shard_map/cond/branch_19_fun/ppermute | solution.py:108
  58.8 0.8 copy-start.1
  59.6 1.8 copy-start.3
  61.4 31.2 %collective-permute-start.36 = (bf16[512,512]{1,0:T(8,128)(2,1)S(1)}, bf16[512,512]{1,0:T(8,128)(2,1)S(1)}, u32[]{:S(2)}, u32[]{:S(2)}) collective-permute-start(bf16[512,512]{1,0:T(8,128)(2,1)S(1)} %pad_maximum_fusion.state_ref.p0), channel_id=1, source_target_pairs={{0,32},{32,64},{64,96},{96,128},{128,160},{160,192},{192,224},{224... | collective-permute-start | bytes 1572872 | tf_op jit(solution)/shard_map/ppermute | solution.py:255
  92.5 24.0 %collective-permute-start.37 = (bf16[512,512]{1,0:T(8,128)(2,1)}, bf16[512,512]{1,0:T(8,128)(2,1)S(1)}, u32[]{:S(2)}, u32[]{:S(2)}) collective-permute-start(bf16[512,512]{1,0:T(8,128)(2,1)} %get-tuple-element.131.closing_ref.closing), channel_id=1, source_target_pairs={{0,32},{32,0},{448,480},{480,448},{1,33},{33,1},{449,481},{481,449... | collective-permute-start | bytes 1572872 | tf_op jit(solution)/shard_map/ppermute | solution.py:311
  94.5 41.0 %copy-start.4 = (bf16[512,512]{1,0:T(8,128)(2,1)S(1)}, bf16[512,512]{1,0:T(8,128)(2,1)}, u32[]{:S(2)}) copy-start(bf16[512,512]{1,0:T(8,128)(2,1)} %copy-done.3) | copy-start | bytes 1572868
  119.8 9.7 %collective-permute-start.39 = (bf16[256,512]{1,0:T(8,128)(2,1)S(1)}, bf16[256,512]{1,0:T(8,128)(2,1)S(1)}, u32[]{:S(2)}, u32[]{:S(2)}) collective-permute-start(bf16[256,512]{1,0:T(8,128)(2,1)S(1)} %shard_map.53.y0), channel_id=1, source_target_pairs={{0,480},{32,0},{64,32},{96,64},{128,96},{160,128},{192,160},{224,1... | collective-permute-start | bytes 786440 | tf_op jit(solution)/shard_map/ppermute | solution.py:255
  123.3 12.2 %collective-permute-start.38 = (bf16[256,512]{1,0:T(8,128)(2,1)S(1)}, bf16[256,512]{1,0:T(8,128)(2,1)S(1)}, u32[]{:S(2)}, u32[]{:S(2)}) collective-permute-start(bf16[256,512]{1,0:T(8,128)(2,1)S(1)} %shard_map.53.y0), channel_id=1, source_target_pairs={{0,32},{32,64},{64,96},{96,128},{128,160},{160,192},{192,224},{224... | collective-permute-start | bytes 786440 | tf_op jit(solution)/shard_map/ppermute | solution.py:255
  139.5 28.3 %copy-start.5 = (bf16[512,512]{1,0:T(8,128)(2,1)}, bf16[512,512]{1,0:T(8,128)(2,1)S(1)}, u32[]{:S(2)}) copy-start(bf16[512,512]{1,0:T(8,128)(2,1)S(1)} %get-tuple-element.123.g1) | copy-start | bytes 1572868
  139.5 28.3 %copy-start.7 = (bf16[512,512]{1,0:T(8,128)(2,1)}, bf16[512,512]{1,0:T(8,128)(2,1)S(1)}, u32[]{:S(2)}) copy-start(bf16[512,512]{1,0:T(8,128)(2,1)S(1)} %get-tuple-element.121.p_1) | copy-start | bytes 1572868
  180.9 0.7 copy-start
  181.6 18.9 %all-to-all-start.4 = ((bf16[32,16,256]{2,1,0:T(8,128)(2,1)}), bf16[32,16,256]{2,1,0:T(8,128)(2,1)S(1)}, u32[]{:S(2)}, u32[]{:S(2)}) async-start(bf16[32,16,256]{2,1,0:T(8,128)(2,1)} %copy-done), calls=%async_computation.4 | async-start | bytes 524288 | tf_op jit(solution)/shard_map/all_to_all | solution.py:259
  187.3 18.6 %collective-permute-start.41 = (bf16[256,512]{1,0:T(8,128)(2,1)S(1)}, bf16[256,512]{1,0:T(8,128)(2,1)}, u32[]{:S(2)}, u32[]{:S(2)}) collective-permute-start(bf16[256,512]{1,0:T(8,128)(2,1)S(1)} %shard_map.53.y0), channel_id=1, source_target_pairs={{0,64},{32,96},{64,128},{96,160},{128,192},{160,224},{192,256},{22... | collective-permute-start | bytes 786440 | tf_op jit(solution)/shard_map/ppermute | solution.py:255
  200.5 5.5 %copy-start.2 = (bf16[512,512]{1,0:T(8,128)(2,1)S(1)}, bf16[512,512]{1,0:T(8,128)(2,1)}, u32[]{:S(2)}) copy-start(bf16[512,512]{1,0:T(8,128)(2,1)} %copy-done.1) | copy-start | bytes 1572868
  203.8 11.5 %collective-permute-start.40 = (bf16[256,512]{1,0:T(8,128)(2,1)S(1)}, bf16[256,512]{1,0:T(8,128)(2,1)S(1)}, u32[]{:S(2)}, u32[]{:S(2)}) collective-permute-start(bf16[256,512]{1,0:T(8,128)(2,1)S(1)} %shard_map.57.y0), channel_id=1, source_target_pairs={{0,32},{32,64},{64,96},{96,128},{128,160},{160,192},{192,224},{224... | collective-permute-start | bytes 786440 | tf_op jit(solution)/shard_map/ppermute | solution.py:255
  206.0 1.0 copy-start.6
  207.0 1.0 copy-start.8

commit v9 on v8

--- a/solution.py
+++ b/solution.py
@@ -303,13 +303,12 @@
 
     part, p1 = call(first_margin_kernel, (shape((full, NB), BF16), fields), flags, state, p1, near, smem=1)
     state, near, part = lax.optimization_barrier((state, near, part))
+    p_1 = shifted(state, 1)
+    far = lax.ppermute(near, "kstr", [(0, 1), (1, 0), (end - 1, end), (end, end - 1)])
     parts = exchange(part, "pw").reshape(PARTS, CHUNK, NB)
-    p_1 = shifted(state, 1)
-    parts, p_1, near = lax.optimization_barrier((parts, p_1, near))
     own, kept = call(collect_kernel, (chunks, chunk), parts)
     whole = exchange(own.reshape(full, NB), "pw")
-    far = lax.ppermute(near, "kstr", [(0, 1), (1, 0), (end - 1, end), (end, end - 1)])
-    whole, far = lax.optimization_barrier((whole, far))
+    whole, far, p_1 = lax.optimization_barrier((whole, far, p_1))
 
     y0 = inverse(whole)
     y_1 = shifted(y0, 1)

time: 244 us -> 241 us (0.988); the launches traced: 243 us -> 238 us
  blocking collectives: 118 us -> 63.7 us
  starting transfers between devices: 49 us -> 79.1 us
  waiting for transfers between devices: 50.7 us -> 66.5 us
    all_to_all x6 -> x4, blocking collectives: 118 us -> 63.7 us  [exchange(): return lax.all_to_all(value, axis, 0, 0, tiled=True)]
    all_to_all x1 -> x3, starting transfers between devices: 5.73 us -> 29.9 us  [exchange(): return lax.all_to_all(value, axis, 0, 0, tiled=True)]
    ppermute x1, waiting for transfers between devices: 0.01 us -> 14.5 us  [body(): lax.ppermute(near, 'kstr', [(0, 1), (1, 0), (end - 1, end), (end, end - 1)])]
    all_to_all x1 -> x3, waiting for transfers between devices: 10.8 us -> 22.9 us  [exchange(): return lax.all_to_all(value, axis, 0, 0, tiled=True)]
    ppermute x1, waiting for transfers between devices: 24.8 us -> 14.9 us  [branch(): return lambda block: lax.ppermute(block, ('kstr', 'pw'), closing_pairs(by))]
    ppermute x1, starting transfers between devices: 1.91 us -> 7.14 us  [body(): lax.ppermute(near, 'kstr', [(0, 1), (1, 0), (end - 1, end), (end, end - 1)])]
    unnamed x18 -> x22, local copies, waits for them, and re-layouts: 3.61 us -> 5.43 us
  transfers between devices with their start and end apart: 12 -> 14, of which waited for: 5 -> 8; matrix products, arithmetic and copies ran while one was open for 1% -> 1% of each run, Pallas kernels for 3% -> 3%
where the time goes in v9:
time: 241 us; the launch traced here: 238 us
  starting transfers between devices  79.1 us (33%)
  waiting for transfers between devices  66.5 us (28%)
  blocking collectives  63.7 us (26%)
  Pallas kernels  19.1 us (8%)
  local copies, waits for them, and re-layouts  6.63 us (3%)
    all_to_all x4, blocking collectives, exchange(): return lax.all_to_all(value, axis, 0, 0, tiled=True)  63.7 us
    all_to_all x3, starting transfers between devices, exchange(): return lax.all_to_all(value, axis, 0, 0, tiled=True)  29.9 us
    ppermute x8, starting transfers between devices, shifted(): return lax.ppermute(value, 'kstr', [(i, (i + by) % NK) for i in range(NK)])  24 us
    all_to_all x3, waiting for transfers between devices, exchange(): return lax.all_to_all(value, axis, 0, 0, tiled=True)  22.9 us
    pallas_call x12, Pallas kernels, call(): pl.pallas_call(kernel, out_shape=outs, in_specs=specs, out_specs=tuple((p...  19.1 us
    ppermute x1, waiting for transfers between devices, branch(): return lambda block: lax.ppermute(block, ('kstr', 'pw'), closing_pairs(by))  14.9 us
    ppermute x1, waiting for transfers between devices, body(): lax.ppermute(near, 'kstr', [(0, 1), (1, 0), (end - 1, end), (end, end - 1)])  14.5 us
    ppermute x8, waiting for transfers between devices, shifted(): return lax.ppermute(value, 'kstr', [(i, (i + by) % NK) for i in range(NK)])  14.3 us
  transfers between devices with their start and end apart: 14, of which 8 were waited for; matrix products, arithmetic and copies ran while one was open for 1% of the time, Pallas kernels for 3%

profile of v9, /device:TPU:1, one launch (start us, length us, event | category | flops | bytes accessed | tf_op | source)
XLA Modules:
  0.0 237.8 jit_solution(5564357131729548537)
XLA Ops:
  0.6 1.1 pad_maximum_fusion.state_ref.p0
  1.7 8.8 %collective-permute-start.32 = (bf16[512,512]{1,0:T(8,128)(2,1)S(1)}, bf16[512,512]{1,0:T(8,128)(2,1)S(1)}, u32[]{:S(2)}, u32[]{:S(2)}) collective-permute-start(bf16[512,512]{1,0:T(8,128)(2,1)S(1)} %pad_maximum_fusion.state_ref.p0), channel_id=1, source_target_pairs={{0,31},{32,63},{448,449},{480,481},{1,0},{33,32},{449,450},{481,48... | collective-permute-start | bytes 1572872 | tf_op jit(solution)/shard_map/ppermute | solution.py:297
  10.5 1.9 collective-permute-start.35
  12.4 4.6 %collective-permute-start.34 = (bf16[512,512]{1,0:T(8,128)(2,1)S(1)}, bf16[512,512]{1,0:T(8,128)(2,1)S(1)}, u32[]{:S(2)}, u32[]{:S(2)}) collective-permute-start(bf16[512,512]{1,0:T(8,128)(2,1)S(1)} %pad_maximum_fusion.state_ref.p0), channel_id=1, source_target_pairs={{0,448},{32,480},{64,0},{96,32},{128,64},{160,96},{192,128},{224,1... | collective-permute-start | bytes 1572872 | tf_op jit(solution)/shard_map/ppermute | solution.py:255
  17.0 4.1 %collective-permute-start.33 = (bf16[512,512]{1,0:T(8,128)(2,1)S(1)}, bf16[512,512]{1,0:T(8,128)(2,1)S(1)}, u32[]{:S(2)}, u32[]{:S(2)}) collective-permute-start(bf16[512,512]{1,0:T(8,128)(2,1)S(1)} %pad_maximum_fusion.state_ref.p0), channel_id=1, source_target_pairs={{0,480},{32,0},{64,32},{96,64},{128,96},{160,128},{192,160},{224,1... | collective-permute-start | bytes 1572872 | tf_op jit(solution)/shard_map/ppermute | solution.py:255
  21.1 1.2 slice.3
  23.0 0.1 pad_add_fusion.bounds
  23.1 0.1 add_convert_fusion.flags
  23.2 0.8 shard_map.50
  24.0 24.2 %conditional.1 = (bf16[512,512]{1,0:T(8,128)(2,1)}) conditional(s32[]{:T(128)} %clamp.3, bf16[512,512]{1,0:T(8,128)(2,1)S(1)} %shard_map.50, bf16[512,512]{1,0:T(8,128)(2,1)S(1)} %shard_map.50, bf16[512,512]{1,0:T(8,128)(2,1)S(1)} %shard_map.50, bf16[512,512]{1,0:T(8,128)(2,1)S(1)} %shard_map.50, ...), branch_computations={%region_0.1_spmd, %region_1.2_spmd, %region_2.3_spmd, %region_3.4_... | conditional | bytes 2097200 | solution.py:110
  24.1 9.2 %collective-permute-start.10 = (bf16[512,512]{1,0:T(8,128)(2,1)S(1)}, bf16[512,512]{1,0:T(8,128)(2,1)}, u32[]{:S(2)}, u32[]{:S(2)}) collective-permute-start(bf16[512,512]{1,0:T(8,128)(2,1)S(1)} %param.10), channel_id=1, source_target_pairs={{0,502},{480,10},{32,470},{448,42},{1,503},{481,11},{33,471},{449,... | collective-permute-start | bytes 1572872 | tf_op jit(solution)/shard_map/cond/branch_10_fun/ppermute | solution.py:108
  33.3 14.9 %collective-permute-done.10 = bf16[512,512]{1,0:T(8,128)(2,1)} collective-permute-done((bf16[512,512]{1,0:T(8,128)(2,1)S(1)}, bf16[512,512]{1,0:T(8,128)(2,1)}, u32[]{:S(2)}, u32[]{:S(2)}) %collective-permute-start.10) | collective-permute-done | bytes 524320 | tf_op jit(solution)/shard_map/cond/branch_10_fun/ppermute | solution.py:108
  48.2 0.8 copy-done.1
  49.0 2.5 %shard_map.51 = (bf16[512,256]{1,0:T(8,128)(2,1)}, bf16[512,512]{1,0:T(8,128)(2,1)S(1)}) custom-call(s32[4]{0:T(128)S(1)} %add_convert_fusion.flags, bf16[512,512]{1,0:T(8,128)(2,1)S(1)} %pad_maximum_fusion.state_ref.p0, bf16[512,512]{1,0:T(8,128)(2,1)S(1)} %collective-permute-done.33.next_ref, bf16[512,512]{1,0:T(8,128)(2,1)} %get-tuple-element.127.closing_ref.closing), custom_call_target="tpu_custom_call" | custom-call | bytes 2359312 | tf_op jit(solution)/shard_map/pallas_call | solution.py:29
  51.5 17.5 %all-to-all-start = ((bf16[32,16,256]{2,1,0:T(8,128)(2,1)}), bf16[32,16,256]{2,1,0:T(8,128)(2,1)S(1)}, u32[]{:S(2)}, u32[]{:S(2)}) async-start(bf16[32,16,256]{2,1,0:T(8,128)(2,1)} %bitcast.10), calls=%async_computation | async-start | bytes 524288 | tf_op jit(solution)/shard_map/all_to_all | solution.py:259
  69.0 7.1 %collective-permute-start.36 = (bf16[512,512]{1,0:T(8,128)(2,1)}, bf16[512,512]{1,0:T(8,128)(2,1)S(1)}, u32[]{:S(2)}, u32[]{:S(2)}) collective-permute-start(bf16[512,512]{1,0:T(8,128)(2,1)} %get-tuple-element.127.closing_ref.closing), channel_id=1, source_target_pairs={{0,32},{32,0},{448,480},{480,448},{1,33},{33,1},{449,481},{481,449... | collective-permute-start | bytes 1572872 | tf_op jit(solution)/shard_map/ppermute | solution.py:307
  76.1 1.9 collective-permute-start.37
  78.1 3.4 %all-to-all-done.parts_ref = bf16[32,16,256]{2,1,0:T(8,128)(2,1)S(1)} async-done(((bf16[32,16,256]{2,1,0:T(8,128)(2,1)}), bf16[32,16,256]{2,1,0:T(8,128)(2,1)S(1)}, u32[]{:S(2)}, u32[]{:S(2)}) %all-to-all-start) | async-done | bytes 262176 | tf_op jit(solution)/shard_map/all_to_all | solution.py:259
  81.4 0.8 shard_map.52
  82.2 6.7 %all-to-all-start.1 = ((bf16[32,16,256]{2,1,0:T(8,128)(2,1)}), bf16[32,16,256]{2,1,0:T(8,128)(2,1)S(1)}, u32[]{:S(2)}, u32[]{:S(2)}) async-start(bf16[32,16,256]{2,1,0:T(8,128)(2,1)} %get-tuple-element.101), calls=%async_computation.1 | async-start | bytes 524288 | tf_op jit(solution)/shard_map/all_to_all | solution.py:259
  88.9 14.5 %collective-permute-done.36.beyond.closing = bf16[512,512]{1,0:T(8,128)(2,1)S(1)} collective-permute-done((bf16[512,512]{1,0:T(8,128)(2,1)}, bf16[512,512]{1,0:T(8,128)(2,1)S(1)}, u32[]{:S(2)}, u32[]{:S(2)}) %collective-permute-start.36) | collective-permute-done | bytes 524320 | tf_op jit(solution)/shard_map/ppermute | solution.py:307
  103.3 0.8 copy-done.9
  104.1 8.6 %all-to-all-done.1 = bf16[32,16,256]{2,1,0:T(8,128)(2,1)S(1)} async-done(((bf16[32,16,256]{2,1,0:T(8,128)(2,1)}), bf16[32,16,256]{2,1,0:T(8,128)(2,1)S(1)}, u32[]{:S(2)}, u32[]{:S(2)}) %all-to-all-start.1) | async-done | bytes 262176 | tf_op jit(solution)/shard_map/all_to_all | solution.py:259
  112.8 3.3 %shard_map.53.y0 = bf16[256,512]{1,0:T(8,128)(2,1)S(1)} custom-call(bf16[512,256]{1,0:T(8,128)(2,1)S(1)} %bitcast.15), custom_call_target="tpu_custom_call" | custom-call | bytes 524288 | tf_op jit(solution)/shard_map/pallas_call | solution.py:29
  116.1 5.1 %collective-permute-start.39 = (bf16[256,512]{1,0:T(8,128)(2,1)S(1)}, bf16[256,512]{1,0:T(8,128)(2,1)S(1)}, u32[]{:S(2)}, u32[]{:S(2)}) collective-permute-start(bf16[256,512]{1,0:T(8,128)(2,1)S(1)} %shard_map.53.y0), channel_id=1, source_target_pairs={{0,480},{32,0},{64,32},{96,64},{128,96},{160,128},{192,160},{224,1... | collective-permute-start | bytes 786440 | tf_op jit(solution)/shard_map/ppermute | solution.py:255
  121.3 1.9 collective-permute-start.38
  123.2 3.6 %collective-permute-done.39.y1 = bf16[256,512]{1,0:T(8,128)(2,1)S(1)} collective-permute-done((bf16[256,512]{1,0:T(8,128)(2,1)S(1)}, bf16[256,512]{1,0:T(8,128)(2,1)S(1)}, u32[]{:S(2)}, u32[]{:S(2)}) %collective-permute-start.39) | collective-permute-done | bytes 262176 | tf_op jit(solution)/shard_map/ppermute | solution.py:255
  126.8 5.9 %collective-permute-done.38.y_1 = bf16[256,512]{1,0:T(8,128)(2,1)S(1)} collective-permute-done((bf16[256,512]{1,0:T(8,128)(2,1)S(1)}, bf16[256,512]{1,0:T(8,128)(2,1)S(1)}, u32[]{:S(2)}, u32[]{:S(2)}) %collective-permute-start.38) | collective-permute-done | bytes 262176 | tf_op jit(solution)/shard_map/ppermute | solution.py:255
  132.7 1.0 copy-done.4
  133.7 3.9 %shard_map.54 = (f32[512,512]{1,0:T(8,128)S(1)}, bf16[512,512]{1,0:T(8,128)(2,1)S(1)}, bf16[512,512]{1,0:T(8,128)(2,1)S(1)}, bf16[32,80,128]{2,1,0:T(8,128)(2,1)S(1)}) custom-call(s32[4]{0:T(128)S(1)} %add_convert_fusion.flags, bf16[256,512]{1,0:T(8,128)(2,1)S(1)} %collective-permute-done.38.y_1, bf16[256,512]{1,0:T(8,128)(2,1)S(1)} %shard_map.53.y0, ...), custom_call_target="tpu_custom_call" | custom-call | bytes 6684688 | tf_op jit(solution)/shard_map/pallas_call | solution.py:29
  137.7 23.5 %all_to_all.46.parts_ref = bf16[32,80,128]{2,1,0:T(8,128)(2,1)S(1)} all-to-all(bf16[32,80,128]{2,1,0:T(8,128)(2,1)S(1)} %get-tuple-element.110), channel_id=1, replica_groups=mesh['kstr'=16,'pw'=32] {'pw'}, dimensions={0} | all-to-all | bytes 1310720 | tf_op jit(solution)/shard_map/all_to_all | solution.py:259
  161.2 0.1 shard_map.55
  161.3 13.9 %all_to_all.47.total_ref.total = f32[16,8,128]{2,1,0:T(8,128)S(1)} all-to-all(f32[16,8,128]{2,1,0:T(8,128)S(1)} %get-tuple-element.111), channel_id=1, replica_groups=mesh['kstr'=16,'pw'=32] {'kstr'}, dimensions={0} | all-to-all | bytes 131072 | tf_op jit(solution)/shard_map/all_to_all | solution.py:259
  175.2 0.1 shard_map.56
  175.3 0.7 copy-done
  176.0 5.7 %all-to-all-start.4 = ((bf16[32,16,256]{2,1,0:T(8,128)(2,1)}), bf16[32,16,256]{2,1,0:T(8,128)(2,1)S(1)}, u32[]{:S(2)}, u32[]{:S(2)}) async-start(bf16[32,16,256]{2,1,0:T(8,128)(2,1)} %copy-done), calls=%async_computation.4 | async-start | bytes 524288 | tf_op jit(solution)/shard_map/all_to_all | solution.py:259
  181.8 2.3 collective-permute-start.41
  184.1 10.8 %all-to-all-done.4 = bf16[32,16,256]{2,1,0:T(8,128)(2,1)S(1)} async-done(((bf16[32,16,256]{2,1,0:T(8,128)(2,1)}), bf16[32,16,256]{2,1,0:T(8,128)(2,1)S(1)}, u32[]{:S(2)}, u32[]{:S(2)}) %all-to-all-start.4) | async-done | bytes 262176 | tf_op jit(solution)/shard_map/all_to_all | solution.py:259
  194.9 3.3 %shard_map.57.y0 = bf16[256,512]{1,0:T(8,128)(2,1)S(1)} custom-call(bf16[512,256]{1,0:T(8,128)(2,1)S(1)} %bitcast.16), custom_call_target="tpu_custom_call" | custom-call | bytes 524288 | tf_op jit(solution)/shard_map/pallas_call | solution.py:29
  198.2 2.2 collective-permute-start.40
  200.4 1.0 copy-done.6
  201.4 1.0 copy-done.8
  202.5 2.4 %shard_map.58 = (bf16[512,512]{1,0:T(8,128)(2,1)S(1)}, bf16[512,512]{1,0:T(8,128)(2,1)S(1)}, bf16[512,512]{1,0:T(8,128)(2,1)S(1)}) custom-call(s32[4]{0:T(128)S(1)} %add_convert_fusion.flags, f32[16,8,128]{2,1,0:T(8,128)S(1)} %all_to_all.47.total_ref.total, bf16[256,512]{1,0:T(8,128)(2,1)} %collective-permute-done.41.y_2, ...), custom_call_target="tpu_custom_call" | custom-call | bytes 6357008 | tf_op jit(solution)/shard_map/pallas_call | solution.py:29
  204.9 4.7 %collective-permute-done.40.y_1 = bf16[256,512]{1,0:T(8,128)(2,1)S(1)} collective-permute-done((bf16[256,512]{1,0:T(8,128)(2,1)S(1)}, bf16[256,512]{1,0:T(8,128)(2,1)S(1)}, u32[]{:S(2)}, u32[]{:S(2)}) %collective-permute-start.40) | collective-permute-done | bytes 262176 | tf_op jit(solution)/shard_map/ppermute | solution.py:255
  209.7 0.7 shard_map.59
  210.4 15.7 %all_to_all.48.parts_ref = f32[32,8,128]{2,1,0:T(8,128)S(1)} all-to-all(f32[32,8,128]{2,1,0:T(8,128)S(1)} %get-tuple-element.122), channel_id=1, replica_groups=mesh['kstr'=16,'pw'=32] {'pw'}, dimensions={0} | all-to-all | bytes 262144 | tf_op jit(solution)/shard_map/all_to_all | solution.py:259
  226.2 10.5 %all_to_all.49.total_ref = f32[16,8,128]{2,1,0:T(8,128)S(1)} all-to-all(f32[16,8,128]{2,1,0:T(8,128)S(1)} %shard_map.60), channel_id=1, replica_groups=mesh['kstr'=16,'pw'=32] {'kstr'}, dimensions={0} | all-to-all | bytes 131072 | tf_op jit(solution)/shard_map/all_to_all | solution.py:259
  236.7 1.1 shard_map.61
  (23 shorter events, 0.1 us)
Async XLA Ops:
  1.7 21.5 %collective-permute-start.32 = (bf16[512,512]{1,0:T(8,128)(2,1)S(1)}, bf16[512,512]{1,0:T(8,128)(2,1)S(1)}, u32[]{:S(2)}, u32[]{:S(2)}) collective-permute-start(bf16[512,512]{1,0:T(8,128)(2,1)S(1)} %pad_maximum_fusion.state_ref.p0), channel_id=1, source_target_pairs={{0,31},{32,63},{448,449},{480,481},{1,0},{33,32},{449,450},{481,48... | collective-permute-start | bytes 1572872 | tf_op jit(solution)/shard_map/ppermute | solution.py:297
  10.5 37.7 %collective-permute-start.35 = (bf16[512,512]{1,0:T(8,128)(2,1)S(1)}, bf16[512,512]{1,0:T(8,128)(2,1)S(1)}, u32[]{:S(2)}, u32[]{:S(2)}) collective-permute-start(bf16[512,512]{1,0:T(8,128)(2,1)S(1)} %pad_maximum_fusion.state_ref.p0), channel_id=1, source_target_pairs={{0,64},{32,96},{64,128},{96,160},{128,192},{160,224},{192,256},{22... | collective-permute-start | bytes 1572872 | tf_op jit(solution)/shard_map/ppermute | solution.py:255
  12.4 36.6 %collective-permute-start.34 = (bf16[512,512]{1,0:T(8,128)(2,1)S(1)}, bf16[512,512]{1,0:T(8,128)(2,1)S(1)}, u32[]{:S(2)}, u32[]{:S(2)}) collective-permute-start(bf16[512,512]{1,0:T(8,128)(2,1)S(1)} %pad_maximum_fusion.state_ref.p0), channel_id=1, source_target_pairs={{0,448},{32,480},{64,0},{96,32},{128,64},{160,96},{192,128},{224,1... | collective-permute-start | bytes 1572872 | tf_op jit(solution)/shard_map/ppermute | solution.py:255
  17.0 32.0 %collective-permute-start.33 = (bf16[512,512]{1,0:T(8,128)(2,1)S(1)}, bf16[512,512]{1,0:T(8,128)(2,1)S(1)}, u32[]{:S(2)}, u32[]{:S(2)}) collective-permute-start(bf16[512,512]{1,0:T(8,128)(2,1)S(1)} %pad_maximum_fusion.state_ref.p0), channel_id=1, source_target_pairs={{0,480},{32,0},{64,32},{96,64},{128,96},{160,128},{192,160},{224,1... | collective-permute-start | bytes 1572872 | tf_op jit(solution)/shard_map/ppermute | solution.py:255
  24.1 24.2 %collective-permute-start.10 = (bf16[512,512]{1,0:T(8,128)(2,1)S(1)}, bf16[512,512]{1,0:T(8,128)(2,1)}, u32[]{:S(2)}, u32[]{:S(2)}) collective-permute-start(bf16[512,512]{1,0:T(8,128)(2,1)S(1)} %param.10), channel_id=1, source_target_pairs={{0,502},{480,10},{32,470},{448,42},{1,503},{481,11},{33,471},{449,... | collective-permute-start | bytes 1572872 | tf_op jit(solution)/shard_map/cond/branch_10_fun/ppermute | solution.py:108
  48.2 0.8 copy-start.1
  49.0 2.5 %copy-start.3 = (bf16[512,512]{1,0:T(8,128)(2,1)}, bf16[512,512]{1,0:T(8,128)(2,1)S(1)}, u32[]{:S(2)}) copy-start(bf16[512,512]{1,0:T(8,128)(2,1)S(1)} %collective-permute-done.34.p2) | copy-start | bytes 1572868
  51.5 29.9 %all-to-all-start = ((bf16[32,16,256]{2,1,0:T(8,128)(2,1)}), bf16[32,16,256]{2,1,0:T(8,128)(2,1)S(1)}, u32[]{:S(2)}, u32[]{:S(2)}) async-start(bf16[32,16,256]{2,1,0:T(8,128)(2,1)} %bitcast.10), calls=%async_computation | async-start | bytes 524288 | tf_op jit(solution)/shard_map/all_to_all | solution.py:259
  69.0 34.4 %collective-permute-start.36 = (bf16[512,512]{1,0:T(8,128)(2,1)}, bf16[512,512]{1,0:T(8,128)(2,1)S(1)}, u32[]{:S(2)}, u32[]{:S(2)}) collective-permute-start(bf16[512,512]{1,0:T(8,128)(2,1)} %get-tuple-element.127.closing_ref.closing), channel_id=1, source_target_pairs={{0,32},{32,0},{448,480},{480,448},{1,33},{33,1},{449,481},{481,449... | collective-permute-start | bytes 1572872 | tf_op jit(solution)/shard_map/ppermute | solution.py:307
  76.1 27.2 %collective-permute-start.37 = (bf16[512,512]{1,0:T(8,128)(2,1)S(1)}, bf16[512,512]{1,0:T(8,128)(2,1)S(1)}, u32[]{:S(2)}, u32[]{:S(2)}) collective-permute-start(bf16[512,512]{1,0:T(8,128)(2,1)S(1)} %pad_maximum_fusion.state_ref.p0), channel_id=1, source_target_pairs={{0,32},{32,64},{64,96},{96,128},{128,160},{160,192},{192,224},{224... | collective-permute-start | bytes 1572872 | tf_op jit(solution)/shard_map/ppermute | solution.py:255
  82.2 30.6 %all-to-all-start.1 = ((bf16[32,16,256]{2,1,0:T(8,128)(2,1)}), bf16[32,16,256]{2,1,0:T(8,128)(2,1)S(1)}, u32[]{:S(2)}, u32[]{:S(2)}) async-start(bf16[32,16,256]{2,1,0:T(8,128)(2,1)} %get-tuple-element.101), calls=%async_computation.1 | async-start | bytes 524288 | tf_op jit(solution)/shard_map/all_to_all | solution.py:259
  103.3 0.8 copy-start.9
  112.8 19.9 %copy-start.10 = (bf16[512,512]{1,0:T(8,128)(2,1)S(1)}, bf16[512,512]{1,0:T(8,128)(2,1)}, u32[]{:S(2)}) copy-start(bf16[512,512]{1,0:T(8,128)(2,1)} %copy-done.9) | copy-start | bytes 1572868
  116.1 10.7 %collective-permute-start.39 = (bf16[256,512]{1,0:T(8,128)(2,1)S(1)}, bf16[256,512]{1,0:T(8,128)(2,1)S(1)}, u32[]{:S(2)}, u32[]{:S(2)}) collective-permute-start(bf16[256,512]{1,0:T(8,128)(2,1)S(1)} %shard_map.53.y0), channel_id=1, source_target_pairs={{0,480},{32,0},{64,32},{96,64},{128,96},{160,128},{192,160},{224,1... | collective-permute-start | bytes 786440 | tf_op jit(solution)/shard_map/ppermute | solution.py:255
  121.3 11.4 %collective-permute-start.38 = (bf16[256,512]{1,0:T(8,128)(2,1)S(1)}, bf16[256,512]{1,0:T(8,128)(2,1)S(1)}, u32[]{:S(2)}, u32[]{:S(2)}) collective-permute-start(bf16[256,512]{1,0:T(8,128)(2,1)S(1)} %shard_map.53.y0), channel_id=1, source_target_pairs={{0,32},{32,64},{64,96},{96,128},{128,160},{160,192},{192,224},{224... | collective-permute-start | bytes 786440 | tf_op jit(solution)/shard_map/ppermute | solution.py:255
  132.7 1.0 copy-start.4
  137.6 23.5 %copy-start.5 = (bf16[512,512]{1,0:T(8,128)(2,1)}, bf16[512,512]{1,0:T(8,128)(2,1)S(1)}, u32[]{:S(2)}) copy-start(bf16[512,512]{1,0:T(8,128)(2,1)S(1)} %get-tuple-element.119.g1) | copy-start | bytes 1572868
  137.7 23.5 %copy-start.7 = (bf16[512,512]{1,0:T(8,128)(2,1)}, bf16[512,512]{1,0:T(8,128)(2,1)S(1)}, u32[]{:S(2)}) copy-start(bf16[512,512]{1,0:T(8,128)(2,1)S(1)} %get-tuple-element.117.p_1) | copy-start | bytes 1572868
  175.3 0.7 copy-start
  176.0 18.9 %all-to-all-start.4 = ((bf16[32,16,256]{2,1,0:T(8,128)(2,1)}), bf16[32,16,256]{2,1,0:T(8,128)(2,1)S(1)}, u32[]{:S(2)}, u32[]{:S(2)}) async-start(bf16[32,16,256]{2,1,0:T(8,128)(2,1)} %copy-done), calls=%async_computation.4 | async-start | bytes 524288 | tf_op jit(solution)/shard_map/all_to_all | solution.py:259
  181.8 18.6 %collective-permute-start.41 = (bf16[256,512]{1,0:T(8,128)(2,1)S(1)}, bf16[256,512]{1,0:T(8,128)(2,1)}, u32[]{:S(2)}, u32[]{:S(2)}) collective-permute-start(bf16[256,512]{1,0:T(8,128)(2,1)S(1)} %shard_map.53.y0), channel_id=1, source_target_pairs={{0,64},{32,96},{64,128},{96,160},{128,192},{160,224},{192,256},{22... | collective-permute-start | bytes 786440 | tf_op jit(solution)/shard_map/ppermute | solution.py:255
  194.9 5.5 %copy-start.2 = (bf16[512,512]{1,0:T(8,128)(2,1)S(1)}, bf16[512,512]{1,0:T(8,128)(2,1)}, u32[]{:S(2)}) copy-start(bf16[512,512]{1,0:T(8,128)(2,1)} %copy-done.1) | copy-start | bytes 1572868
  198.2 11.5 %collective-permute-start.40 = (bf16[256,512]{1,0:T(8,128)(2,1)S(1)}, bf16[256,512]{1,0:T(8,128)(2,1)S(1)}, u32[]{:S(2)}, u32[]{:S(2)}) collective-permute-start(bf16[256,512]{1,0:T(8,128)(2,1)S(1)} %shard_map.57.y0), channel_id=1, source_target_pairs={{0,32},{32,64},{64,96},{96,128},{128,160},{160,192},{192,224},{224... | collective-permute-start | bytes 786440 | tf_op jit(solution)/shard_map/ppermute | solution.py:255
  200.4 1.0 copy-start.6
  201.4 1.0 copy-start.8

commit v10 on v9

--- a/solution.py
+++ b/solution.py
@@ -304,13 +304,14 @@
     part, p1 = call(first_margin_kernel, (shape((full, NB), BF16), fields), flags, state, p1, near, smem=1)
     state, near, part = lax.optimization_barrier((state, near, part))
     p_1 = shifted(state, 1)
-    far = lax.ppermute(near, "kstr", [(0, 1), (1, 0), (end - 1, end), (end, end - 1)])
     parts = exchange(part, "pw").reshape(PARTS, CHUNK, NB)
     own, kept = call(collect_kernel, (chunks, chunk), parts)
+    own, near = lax.optimization_barrier((own, near))
+    far = lax.ppermute(near, "kstr", [(0, 1), (1, 0), (end - 1, end), (end, end - 1)])
     whole = exchange(own.reshape(full, NB), "pw")
-    whole, far, p_1 = lax.optimization_barrier((whole, far, p_1))
-
-    y0 = inverse(whole)
+    whole, p_1 = lax.optimization_barrier((whole, p_1))
+
+    y0, far = lax.optimization_barrier((inverse(whole), far))
     y_1 = shifted(y0, 1)
     y1 = shifted(y0, -1)
     g0, g1, p_1, part = call(

time: 241 us -> 241 us (level)
  starting transfers between devices: 79.1 us -> 69.6 us
  waiting for transfers between devices: 66.5 us -> 73.2 us
  blocking collectives: 63.7 us -> 68.5 us
    all_to_all x3, waiting for transfers between devices: 22.9 us -> 39.7 us  [exchange(): return lax.all_to_all(value, axis, 0, 0, tiled=True)]
    ppermute x1, waiting for transfers between devices: 14.5 us -> 0.01 us  [body(): lax.ppermute(near, 'kstr', [(0, 1), (1, 0), (end - 1, end), (end, end - 1)])]
    all_to_all x3, starting transfers between devices: 29.9 us -> 23.9 us  [exchange(): return lax.all_to_all(value, axis, 0, 0, tiled=True)]
    ppermute x1, starting transfers between devices: 7.14 us -> 1.91 us  [body(): lax.ppermute(near, 'kstr', [(0, 1), (1, 0), (end - 1, end), (end, end - 1)])]
    all_to_all x4, blocking collectives: 63.7 us -> 68.5 us  [exchange(): return lax.all_to_all(value, axis, 0, 0, tiled=True)]
    ppermute x8, waiting for transfers between devices: 14.3 us -> 17.6 us  [shifted(): return lax.ppermute(value, 'kstr', [(i, (i + by) % NK) for i in range(NK)])]
  transfers between devices with their start and end apart: 14 -> 14, of which waited for: 8 -> 8; matrix products, arithmetic and copies ran while one was open for 1% -> 1% of each run, Pallas kernels for 3% -> 4%
where the time goes in v10:
time: 241 us; the launch traced here: 240 us
  waiting for transfers between devices  73.2 us (30%)
  starting transfers between devices  69.6 us (29%)
  blocking collectives  68.5 us (28%)
  Pallas kernels  19.1 us (8%)
  local copies, waits for them, and re-layouts  6.63 us (3%)
    all_to_all x4, blocking collectives, exchange(): return lax.all_to_all(value, axis, 0, 0, tiled=True)  68.5 us
    all_to_all x3, waiting for transfers between devices, exchange(): return lax.all_to_all(value, axis, 0, 0, tiled=True)  39.7 us
    ppermute x8, starting transfers between devices, shifted(): return lax.ppermute(value, 'kstr', [(i, (i + by) % NK) for i in range(NK)])  25.9 us
    all_to_all x3, starting transfers between devices, exchange(): return lax.all_to_all(value, axis, 0, 0, tiled=True)  23.9 us
    pallas_call x12, Pallas kernels, call(): pl.pallas_call(kernel, out_shape=outs, in_specs=specs, out_specs=tuple((p...  19.1 us
    ppermute x8, waiting for transfers between devices, shifted(): return lax.ppermute(value, 'kstr', [(i, (i + by) % NK) for i in range(NK)])  17.6 us
    ppermute x1, waiting for transfers between devices, branch(): return lambda block: lax.ppermute(block, ('kstr', 'pw'), closing_pairs(by))  15.9 us
    ppermute x1, starting transfers between devices, branch(): return lambda block: lax.ppermute(block, ('kstr', 'pw'), closing_pairs(by))  9.08 us
  transfers between devices with their start and end apart: 14, of which 8 were waited for; matrix products, arithmetic and copies ran while one was open for 1% of the time, Pallas kernels for 4%

profile of v10, /device:TPU:1, one launch (start us, length us, event | category | flops | bytes accessed | tf_op | source)
XLA Modules:
  0.0 239.9 jit_solution(6442818450484592941)
XLA Ops:
  0.6 1.1 pad_maximum_fusion.state_ref.p0
  1.7 8.8 %collective-permute-start.32 = (bf16[512,512]{1,0:T(8,128)(2,1)S(1)}, bf16[512,512]{1,0:T(8,128)(2,1)S(1)}, u32[]{:S(2)}, u32[]{:S(2)}) collective-permute-start(bf16[512,512]{1,0:T(8,128)(2,1)S(1)} %pad_maximum_fusion.state_ref.p0), channel_id=1, source_target_pairs={{0,31},{32,63},{448,449},{480,481},{1,0},{33,32},{449,450},{481,48... | collective-permute-start | bytes 1572872 | tf_op jit(solution)/shard_map/ppermute | solution.py:297
  10.5 1.9 collective-permute-start.35
  12.4 4.6 %collective-permute-start.34 = (bf16[512,512]{1,0:T(8,128)(2,1)S(1)}, bf16[512,512]{1,0:T(8,128)(2,1)S(1)}, u32[]{:S(2)}, u32[]{:S(2)}) collective-permute-start(bf16[512,512]{1,0:T(8,128)(2,1)S(1)} %pad_maximum_fusion.state_ref.p0), channel_id=1, source_target_pairs={{0,448},{32,480},{64,0},{96,32},{128,64},{160,96},{192,128},{224,1... | collective-permute-start | bytes 1572872 | tf_op jit(solution)/shard_map/ppermute | solution.py:255
  17.0 4.1 %collective-permute-start.33 = (bf16[512,512]{1,0:T(8,128)(2,1)S(1)}, bf16[512,512]{1,0:T(8,128)(2,1)S(1)}, u32[]{:S(2)}, u32[]{:S(2)}) collective-permute-start(bf16[512,512]{1,0:T(8,128)(2,1)S(1)} %pad_maximum_fusion.state_ref.p0), channel_id=1, source_target_pairs={{0,480},{32,0},{64,32},{96,64},{128,96},{160,128},{192,160},{224,1... | collective-permute-start | bytes 1572872 | tf_op jit(solution)/shard_map/ppermute | solution.py:255
  21.1 1.2 slice.3
  23.0 0.1 pad_add_fusion.bounds
  23.1 0.1 add_convert_fusion.flags
  23.2 0.8 shard_map.50
  24.0 25.0 %conditional.1 = (bf16[512,512]{1,0:T(8,128)(2,1)}) conditional(s32[]{:T(128)} %clamp.3, bf16[512,512]{1,0:T(8,128)(2,1)S(1)} %shard_map.50, bf16[512,512]{1,0:T(8,128)(2,1)S(1)} %shard_map.50, bf16[512,512]{1,0:T(8,128)(2,1)S(1)} %shard_map.50, bf16[512,512]{1,0:T(8,128)(2,1)S(1)} %shard_map.50, ...), branch_computations={%region_0.1_spmd, %region_1.2_spmd, %region_2.3_spmd, %region_3.4_... | conditional | bytes 2097200 | solution.py:110
  24.1 9.1 %collective-permute-start.15 = (bf16[512,512]{1,0:T(8,128)(2,1)S(1)}, bf16[512,512]{1,0:T(8,128)(2,1)}, u32[]{:S(2)}, u32[]{:S(2)}) collective-permute-start(bf16[512,512]{1,0:T(8,128)(2,1)S(1)} %param.15), channel_id=1, source_target_pairs={{0,497},{480,15},{32,465},{448,47},{1,498},{481,16},{33,466},{449,... | collective-permute-start | bytes 1572872 | tf_op jit(solution)/shard_map/cond/branch_15_fun/ppermute | solution.py:108
  33.1 15.9 %collective-permute-done.15 = bf16[512,512]{1,0:T(8,128)(2,1)} collective-permute-done((bf16[512,512]{1,0:T(8,128)(2,1)S(1)}, bf16[512,512]{1,0:T(8,128)(2,1)}, u32[]{:S(2)}, u32[]{:S(2)}) %collective-permute-start.15) | collective-permute-done | bytes 524320 | tf_op jit(solution)/shard_map/cond/branch_15_fun/ppermute | solution.py:108
  49.0 0.8 copy-done.1
  49.9 2.5 %shard_map.51 = (bf16[512,256]{1,0:T(8,128)(2,1)}, bf16[512,512]{1,0:T(8,128)(2,1)S(1)}) custom-call(s32[4]{0:T(128)S(1)} %add_convert_fusion.flags, bf16[512,512]{1,0:T(8,128)(2,1)S(1)} %pad_maximum_fusion.state_ref.p0, bf16[512,512]{1,0:T(8,128)(2,1)S(1)} %collective-permute-done.33.next_ref, bf16[512,512]{1,0:T(8,128)(2,1)} %get-tuple-element.133.closing_ref.closing), custom_call_target="tpu_custom_call" | custom-call | bytes 2359312 | tf_op jit(solution)/shard_map/pallas_call | solution.py:29
  52.3 14.4 %all-to-all-start = ((bf16[32,16,256]{2,1,0:T(8,128)(2,1)}), bf16[32,16,256]{2,1,0:T(8,128)(2,1)S(1)}, u32[]{:S(2)}, u32[]{:S(2)}) async-start(bf16[32,16,256]{2,1,0:T(8,128)(2,1)} %bitcast.10), calls=%async_computation | async-start | bytes 524288 | tf_op jit(solution)/shard_map/all_to_all | solution.py:259
  66.7 1.9 collective-permute-start.36
  68.7 10.6 %all-to-all-done.parts_ref = bf16[32,16,256]{2,1,0:T(8,128)(2,1)S(1)} async-done(((bf16[32,16,256]{2,1,0:T(8,128)(2,1)}), bf16[32,16,256]{2,1,0:T(8,128)(2,1)S(1)}, u32[]{:S(2)}, u32[]{:S(2)}) %all-to-all-start) | async-done | bytes 262176 | tf_op jit(solution)/shard_map/all_to_all | solution.py:259
  79.2 0.8 shard_map.52
  80.0 1.9 collective-permute-start.37
  81.9 3.9 %all-to-all-start.1 = ((bf16[32,16,256]{2,1,0:T(8,128)(2,1)}), bf16[32,16,256]{2,1,0:T(8,128)(2,1)S(1)}, u32[]{:S(2)}, u32[]{:S(2)}) async-start(bf16[32,16,256]{2,1,0:T(8,128)(2,1)} %get-tuple-element.106), calls=%async_computation.1 | async-start | bytes 524288 | tf_op jit(solution)/shard_map/all_to_all | solution.py:259
  85.8 2.3 collective-permute-done.36.before
  88.1 0.8 copy-done.9
  88.9 18.4 %all-to-all-done.1 = bf16[32,16,256]{2,1,0:T(8,128)(2,1)S(1)} async-done(((bf16[32,16,256]{2,1,0:T(8,128)(2,1)}), bf16[32,16,256]{2,1,0:T(8,128)(2,1)S(1)}, u32[]{:S(2)}, u32[]{:S(2)}) %all-to-all-start.1) | async-done | bytes 262176 | tf_op jit(solution)/shard_map/all_to_all | solution.py:259
  107.3 3.3 %shard_map.53.y0 = bf16[256,512]{1,0:T(8,128)(2,1)S(1)} custom-call(bf16[512,256]{1,0:T(8,128)(2,1)S(1)} %bitcast.16), custom_call_target="tpu_custom_call" | custom-call | bytes 524288 | tf_op jit(solution)/shard_map/pallas_call | solution.py:29
  110.6 7.1 %collective-permute-start.39 = (bf16[256,512]{1,0:T(8,128)(2,1)S(1)}, bf16[256,512]{1,0:T(8,128)(2,1)S(1)}, u32[]{:S(2)}, u32[]{:S(2)}) collective-permute-start(bf16[256,512]{1,0:T(8,128)(2,1)S(1)} %shard_map.53.y0), channel_id=1, source_target_pairs={{0,480},{32,0},{64,32},{96,64},{128,96},{160,128},{192,160},{224,1... | collective-permute-start | bytes 786440 | tf_op jit(solution)/shard_map/ppermute | solution.py:255
  117.7 1.9 collective-permute-start.38
  119.6 4.2 %collective-permute-done.39.y1 = bf16[256,512]{1,0:T(8,128)(2,1)S(1)} collective-permute-done((bf16[256,512]{1,0:T(8,128)(2,1)S(1)}, bf16[256,512]{1,0:T(8,128)(2,1)S(1)}, u32[]{:S(2)}, u32[]{:S(2)}) %collective-permute-start.39) | collective-permute-done | bytes 262176 | tf_op jit(solution)/shard_map/ppermute | solution.py:255
  123.8 6.3 %collective-permute-done.38.y_1 = bf16[256,512]{1,0:T(8,128)(2,1)S(1)} collective-permute-done((bf16[256,512]{1,0:T(8,128)(2,1)S(1)}, bf16[256,512]{1,0:T(8,128)(2,1)S(1)}, u32[]{:S(2)}, u32[]{:S(2)}) %collective-permute-start.38) | collective-permute-done | bytes 262176 | tf_op jit(solution)/shard_map/ppermute | solution.py:255
  130.1 1.0 copy-done.4
  131.1 3.9 %shard_map.54 = (f32[512,512]{1,0:T(8,128)S(1)}, bf16[512,512]{1,0:T(8,128)(2,1)S(1)}, bf16[512,512]{1,0:T(8,128)(2,1)S(1)}, bf16[32,80,128]{2,1,0:T(8,128)(2,1)S(1)}) custom-call(s32[4]{0:T(128)S(1)} %add_convert_fusion.flags, bf16[256,512]{1,0:T(8,128)(2,1)S(1)} %collective-permute-done.38.y_1, bf16[256,512]{1,0:T(8,128)(2,1)S(1)} %shard_map.53.y0, ...), custom_call_target="tpu_custom_call" | custom-call | bytes 6684688 | tf_op jit(solution)/shard_map/pallas_call | solution.py:29
  135.0 27.9 %all_to_all.46.parts_ref = bf16[32,80,128]{2,1,0:T(8,128)(2,1)S(1)} all-to-all(bf16[32,80,128]{2,1,0:T(8,128)(2,1)S(1)} %get-tuple-element.116), channel_id=1, replica_groups=mesh['kstr'=16,'pw'=32] {'pw'}, dimensions={0} | all-to-all | bytes 1310720 | tf_op jit(solution)/shard_map/all_to_all | solution.py:259
  162.9 0.1 shard_map.55
  163.0 14.4 %all_to_all.47.total_ref.total = f32[16,8,128]{2,1,0:T(8,128)S(1)} all-to-all(f32[16,8,128]{2,1,0:T(8,128)S(1)} %get-tuple-element.117), channel_id=1, replica_groups=mesh['kstr'=16,'pw'=32] {'kstr'}, dimensions={0} | all-to-all | bytes 131072 | tf_op jit(solution)/shard_map/all_to_all | solution.py:259
  177.5 0.1 shard_map.56
  177.6 0.7 copy-done
  178.3 5.6 %all-to-all-start.4 = ((bf16[32,16,256]{2,1,0:T(8,128)(2,1)}), bf16[32,16,256]{2,1,0:T(8,128)(2,1)S(1)}, u32[]{:S(2)}, u32[]{:S(2)}) async-start(bf16[32,16,256]{2,1,0:T(8,128)(2,1)} %copy-done), calls=%async_computation.4 | async-start | bytes 524288 | tf_op jit(solution)/shard_map/all_to_all | solution.py:259
  183.9 2.3 collective-permute-start.41
  186.2 10.8 %all-to-all-done.4 = bf16[32,16,256]{2,1,0:T(8,128)(2,1)S(1)} async-done(((bf16[32,16,256]{2,1,0:T(8,128)(2,1)}), bf16[32,16,256]{2,1,0:T(8,128)(2,1)S(1)}, u32[]{:S(2)}, u32[]{:S(2)}) %all-to-all-start.4) | async-done | bytes 262176 | tf_op jit(solution)/shard_map/all_to_all | solution.py:259
  197.0 3.3 %shard_map.57.y0 = bf16[256,512]{1,0:T(8,128)(2,1)S(1)} custom-call(bf16[512,256]{1,0:T(8,128)(2,1)S(1)} %bitcast.15), custom_call_target="tpu_custom_call" | custom-call | bytes 524288 | tf_op jit(solution)/shard_map/pallas_call | solution.py:29
  200.3 2.1 collective-permute-start.40
  202.4 1.0 copy-done.6
  203.5 1.0 copy-done.8
  204.5 2.4 %shard_map.58 = (bf16[512,512]{1,0:T(8,128)(2,1)S(1)}, bf16[512,512]{1,0:T(8,128)(2,1)S(1)}, bf16[512,512]{1,0:T(8,128)(2,1)S(1)}) custom-call(s32[4]{0:T(128)S(1)} %add_convert_fusion.flags, f32[16,8,128]{2,1,0:T(8,128)S(1)} %all_to_all.47.total_ref.total, bf16[256,512]{1,0:T(8,128)(2,1)} %collective-permute-done.41.y_2, ...), custom_call_target="tpu_custom_call" | custom-call | bytes 6357008 | tf_op jit(solution)/shard_map/pallas_call | solution.py:29
  207.0 4.8 %collective-permute-done.40.y_1 = bf16[256,512]{1,0:T(8,128)(2,1)S(1)} collective-permute-done((bf16[256,512]{1,0:T(8,128)(2,1)S(1)}, bf16[256,512]{1,0:T(8,128)(2,1)S(1)}, u32[]{:S(2)}, u32[]{:S(2)}) %collective-permute-start.40) | collective-permute-done | bytes 262176 | tf_op jit(solution)/shard_map/ppermute | solution.py:255
  211.8 0.7 shard_map.59
  212.5 15.7 %all_to_all.48.parts_ref = f32[32,8,128]{2,1,0:T(8,128)S(1)} all-to-all(f32[32,8,128]{2,1,0:T(8,128)S(1)} %get-tuple-element.128), channel_id=1, replica_groups=mesh['kstr'=16,'pw'=32] {'pw'}, dimensions={0} | all-to-all | bytes 262144 | tf_op jit(solution)/shard_map/all_to_all | solution.py:259
  228.3 10.5 %all_to_all.49.total_ref = f32[16,8,128]{2,1,0:T(8,128)S(1)} all-to-all(f32[16,8,128]{2,1,0:T(8,128)S(1)} %shard_map.60), channel_id=1, replica_groups=mesh['kstr'=16,'pw'=32] {'kstr'}, dimensions={0} | all-to-all | bytes 131072 | tf_op jit(solution)/shard_map/all_to_all | solution.py:259
  238.8 1.1 shard_map.61
  (23 shorter events, 0.1 us)
Async XLA Ops:
  1.7 21.5 %collective-permute-start.32 = (bf16[512,512]{1,0:T(8,128)(2,1)S(1)}, bf16[512,512]{1,0:T(8,128)(2,1)S(1)}, u32[]{:S(2)}, u32[]{:S(2)}) collective-permute-start(bf16[512,512]{1,0:T(8,128)(2,1)S(1)} %pad_maximum_fusion.state_ref.p0), channel_id=1, source_target_pairs={{0,31},{32,63},{448,449},{480,481},{1,0},{33,32},{449,450},{481,48... | collective-permute-start | bytes 1572872 | tf_op jit(solution)/shard_map/ppermute | solution.py:297
  10.5 38.6 %collective-permute-start.35 = (bf16[512,512]{1,0:T(8,128)(2,1)S(1)}, bf16[512,512]{1,0:T(8,128)(2,1)S(1)}, u32[]{:S(2)}, u32[]{:S(2)}) collective-permute-start(bf16[512,512]{1,0:T(8,128)(2,1)S(1)} %pad_maximum_fusion.state_ref.p0), channel_id=1, source_target_pairs={{0,64},{32,96},{64,128},{96,160},{128,192},{160,224},{192,256},{22... | collective-permute-start | bytes 1572872 | tf_op jit(solution)/shard_map/ppermute | solution.py:255
  12.4 37.4 %collective-permute-start.34 = (bf16[512,512]{1,0:T(8,128)(2,1)S(1)}, bf16[512,512]{1,0:T(8,128)(2,1)S(1)}, u32[]{:S(2)}, u32[]{:S(2)}) collective-permute-start(bf16[512,512]{1,0:T(8,128)(2,1)S(1)} %pad_maximum_fusion.state_ref.p0), channel_id=1, source_target_pairs={{0,448},{32,480},{64,0},{96,32},{128,64},{160,96},{192,128},{224,1... | collective-permute-start | bytes 1572872 | tf_op jit(solution)/shard_map/ppermute | solution.py:255
  17.0 32.9 %collective-permute-start.33 = (bf16[512,512]{1,0:T(8,128)(2,1)S(1)}, bf16[512,512]{1,0:T(8,128)(2,1)S(1)}, u32[]{:S(2)}, u32[]{:S(2)}) collective-permute-start(bf16[512,512]{1,0:T(8,128)(2,1)S(1)} %pad_maximum_fusion.state_ref.p0), channel_id=1, source_target_pairs={{0,480},{32,0},{64,32},{96,64},{128,96},{160,128},{192,160},{224,1... | collective-permute-start | bytes 1572872 | tf_op jit(solution)/shard_map/ppermute | solution.py:255
  24.1 25.0 %collective-permute-start.15 = (bf16[512,512]{1,0:T(8,128)(2,1)S(1)}, bf16[512,512]{1,0:T(8,128)(2,1)}, u32[]{:S(2)}, u32[]{:S(2)}) collective-permute-start(bf16[512,512]{1,0:T(8,128)(2,1)S(1)} %param.15), channel_id=1, source_target_pairs={{0,497},{480,15},{32,465},{448,47},{1,498},{481,16},{33,466},{449,... | collective-permute-start | bytes 1572872 | tf_op jit(solution)/shard_map/cond/branch_15_fun/ppermute | solution.py:108
  49.0 0.8 copy-start.1
  49.8 2.5 %copy-start.3 = (bf16[512,512]{1,0:T(8,128)(2,1)}, bf16[512,512]{1,0:T(8,128)(2,1)S(1)}, u32[]{:S(2)}) copy-start(bf16[512,512]{1,0:T(8,128)(2,1)S(1)} %collective-permute-done.34.p2) | copy-start | bytes 1572868
  52.3 26.9 %all-to-all-start = ((bf16[32,16,256]{2,1,0:T(8,128)(2,1)}), bf16[32,16,256]{2,1,0:T(8,128)(2,1)S(1)}, u32[]{:S(2)}, u32[]{:S(2)}) async-start(bf16[32,16,256]{2,1,0:T(8,128)(2,1)} %bitcast.10), calls=%async_computation | async-start | bytes 524288 | tf_op jit(solution)/shard_map/all_to_all | solution.py:259
  66.7 21.4 %collective-permute-start.36 = (bf16[512,512]{1,0:T(8,128)(2,1)S(1)}, bf16[512,512]{1,0:T(8,128)(2,1)S(1)}, u32[]{:S(2)}, u32[]{:S(2)}) collective-permute-start(bf16[512,512]{1,0:T(8,128)(2,1)S(1)} %pad_maximum_fusion.state_ref.p0), channel_id=1, source_target_pairs={{0,32},{32,64},{64,96},{96,128},{128,160},{160,192},{192,224},{224... | collective-permute-start | bytes 1572872 | tf_op jit(solution)/shard_map/ppermute | solution.py:255
  80.0 30.6 %collective-permute-start.37 = (bf16[512,512]{1,0:T(8,128)(2,1)}, bf16[512,512]{1,0:T(8,128)(2,1)S(1)}, u32[]{:S(2)}, u32[]{:S(2)}) collective-permute-start(bf16[512,512]{1,0:T(8,128)(2,1)} %get-tuple-element.133.closing_ref.closing), channel_id=1, source_target_pairs={{0,32},{32,0},{448,480},{480,448},{1,33},{33,1},{449,481},{481,449... | collective-permute-start | bytes 1572872 | tf_op jit(solution)/shard_map/ppermute | solution.py:310
  81.9 25.4 %all-to-all-start.1 = ((bf16[32,16,256]{2,1,0:T(8,128)(2,1)}), bf16[32,16,256]{2,1,0:T(8,128)(2,1)S(1)}, u32[]{:S(2)}, u32[]{:S(2)}) async-start(bf16[32,16,256]{2,1,0:T(8,128)(2,1)} %get-tuple-element.106), calls=%async_computation.1 | async-start | bytes 524288 | tf_op jit(solution)/shard_map/all_to_all | solution.py:259
  88.1 0.8 copy-start.9
  107.3 22.8 %copy-start.10 = (bf16[512,512]{1,0:T(8,128)(2,1)S(1)}, bf16[512,512]{1,0:T(8,128)(2,1)}, u32[]{:S(2)}) copy-start(bf16[512,512]{1,0:T(8,128)(2,1)} %copy-done.9) | copy-start | bytes 1572868
  110.6 13.2 %collective-permute-start.39 = (bf16[256,512]{1,0:T(8,128)(2,1)S(1)}, bf16[256,512]{1,0:T(8,128)(2,1)S(1)}, u32[]{:S(2)}, u32[]{:S(2)}) collective-permute-start(bf16[256,512]{1,0:T(8,128)(2,1)S(1)} %shard_map.53.y0), channel_id=1, source_target_pairs={{0,480},{32,0},{64,32},{96,64},{128,96},{160,128},{192,160},{224,1... | collective-permute-start | bytes 786440 | tf_op jit(solution)/shard_map/ppermute | solution.py:255
  117.7 12.4 %collective-permute-start.38 = (bf16[256,512]{1,0:T(8,128)(2,1)S(1)}, bf16[256,512]{1,0:T(8,128)(2,1)S(1)}, u32[]{:S(2)}, u32[]{:S(2)}) collective-permute-start(bf16[256,512]{1,0:T(8,128)(2,1)S(1)} %shard_map.53.y0), channel_id=1, source_target_pairs={{0,32},{32,64},{64,96},{96,128},{128,160},{160,192},{192,224},{224... | collective-permute-start | bytes 786440 | tf_op jit(solution)/shard_map/ppermute | solution.py:255
  130.1 1.0 copy-start.4
  135.0 27.9 %copy-start.5 = (bf16[512,512]{1,0:T(8,128)(2,1)}, bf16[512,512]{1,0:T(8,128)(2,1)S(1)}, u32[]{:S(2)}) copy-start(bf16[512,512]{1,0:T(8,128)(2,1)S(1)} %get-tuple-element.125.g1) | copy-start | bytes 1572868
  135.0 27.9 %copy-start.7 = (bf16[512,512]{1,0:T(8,128)(2,1)}, bf16[512,512]{1,0:T(8,128)(2,1)S(1)}, u32[]{:S(2)}) copy-start(bf16[512,512]{1,0:T(8,128)(2,1)S(1)} %get-tuple-element.123.p_1) | copy-start | bytes 1572868
  177.6 0.7 copy-start
  178.3 18.7 %all-to-all-start.4 = ((bf16[32,16,256]{2,1,0:T(8,128)(2,1)}), bf16[32,16,256]{2,1,0:T(8,128)(2,1)S(1)}, u32[]{:S(2)}, u32[]{:S(2)}) async-start(bf16[32,16,256]{2,1,0:T(8,128)(2,1)} %copy-done), calls=%async_computation.4 | async-start | bytes 524288 | tf_op jit(solution)/shard_map/all_to_all | solution.py:259
  183.9 18.5 %collective-permute-start.41 = (bf16[256,512]{1,0:T(8,128)(2,1)S(1)}, bf16[256,512]{1,0:T(8,128)(2,1)}, u32[]{:S(2)}, u32[]{:S(2)}) collective-permute-start(bf16[256,512]{1,0:T(8,128)(2,1)S(1)} %shard_map.53.y0), channel_id=1, source_target_pairs={{0,64},{32,96},{64,128},{96,160},{128,192},{160,224},{192,256},{22... | collective-permute-start | bytes 786440 | tf_op jit(solution)/shard_map/ppermute | solution.py:255
  197.0 5.4 %copy-start.2 = (bf16[512,512]{1,0:T(8,128)(2,1)S(1)}, bf16[512,512]{1,0:T(8,128)(2,1)}, u32[]{:S(2)}) copy-start(bf16[512,512]{1,0:T(8,128)(2,1)} %copy-done.1) | copy-start | bytes 1572868
  200.3 11.5 %collective-permute-start.40 = (bf16[256,512]{1,0:T(8,128)(2,1)S(1)}, bf16[256,512]{1,0:T(8,128)(2,1)S(1)}, u32[]{:S(2)}, u32[]{:S(2)}) collective-permute-start(bf16[256,512]{1,0:T(8,128)(2,1)S(1)} %shard_map.57.y0), channel_id=1, source_target_pairs={{0,32},{32,64},{64,96},{96,128},{128,160},{160,192},{192,224},{224... | collective-permute-start | bytes 786440 | tf_op jit(solution)/shard_map/ppermute | solution.py:255
  202.4 1.0 copy-start.6
  203.5 1.0 copy-start.8

commit v11 on v10

--- a/solution.py
+++ b/solution.py
@@ -98,8 +98,9 @@
         for row in (0, 1):
             pairs.append((place(row, j), place(NK - 1 - row, j - by)))
             pairs.append((place(NK - 1 - row, j), place(row, j + by)))
-    for row in range(2, NK - 2):
-        pairs += [(place(row, j), place(row, j)) for j in range(PARTS)]
+    if by % 8 == 0:
+        for row in range(2, NK - 2):
+            pairs += [(place(row, j), place(row, j)) for j in range(PARTS)]
     return pairs
 
 
@@ -296,7 +297,7 @@
 
     beside = lax.ppermute(state, ("kstr", "pw"), beside_pairs())
     p1, p_2 = shifted(state, -1), shifted(state, 2)
-    p2 = shifted(state, -2)
+    p2 = lax.ppermute(state, "kstr", [(i + 2, i) for i in range(NK - 2)])
     merged = call(merge_kernel, fields, bounds, state, beside, smem=1)
     near = close_string(merged, blocks)
     near, p1, p2, p_2 = lax.optimization_barrier((near, p1, p2, p_2))

time: 241 us -> 252 us (1.046)
  starting transfers between devices: 69.6 us -> 100 us
  waiting for transfers between devices: 73.2 us -> 58.3 us
  blocking collectives: 68.5 us -> 64.4 us
    ppermute x8 -> x7, starting transfers between devices: 25.9 us -> 47.3 us  [shifted(): return lax.ppermute(value, 'kstr', [(i, (i + by) % NK) for i in range(NK)])]
    ppermute x1, starting transfers between devices: 1.91 us -> 12.5 us  [body(): lax.ppermute(near, 'kstr', [(0, 1), (1, 0), (end - 1, end), (end, end - 1)])]
    all_to_all x3, waiting for transfers between devices: 39.7 us -> 29.2 us  [exchange(): return lax.all_to_all(value, axis, 0, 0, tiled=True)]
    all_to_all x4, blocking collectives: 68.5 us -> 64.4 us  [exchange(): return lax.all_to_all(value, axis, 0, 0, tiled=True)]
    ppermute x8 -> x7, waiting for transfers between devices: 17.6 us -> 14 us  [shifted(): return lax.ppermute(value, 'kstr', [(i, (i + by) % NK) for i in range(NK)])]
    all_to_all x3, starting transfers between devices: 23.9 us -> 20.7 us  [exchange(): return lax.all_to_all(value, axis, 0, 0, tiled=True)]
  transfers between devices with their start and end apart: 14 -> 14, of which waited for: 8 -> 6; matrix products, arithmetic and copies ran while one was open for 1% -> 1% of each run, Pallas kernels for 4% -> 4%
where the time goes in v11:
time: 252 us; the launch traced here: 251 us
  starting transfers between devices  100 us (40%)
  blocking collectives  64.4 us (26%)
  waiting for transfers between devices  58.3 us (23%)
  Pallas kernels  19.1 us (8%)
  local copies, waits for them, and re-layouts  6.62 us (3%)
    all_to_all x4, blocking collectives, exchange(): return lax.all_to_all(value, axis, 0, 0, tiled=True)  64.4 us
    ppermute x7, starting transfers between devices, shifted(): return lax.ppermute(value, 'kstr', [(i, (i + by) % NK) for i in range(NK)])  47.3 us
    all_to_all x3, waiting for transfers between devices, exchange(): return lax.all_to_all(value, axis, 0, 0, tiled=True)  29.2 us
    all_to_all x3, starting transfers between devices, exchange(): return lax.all_to_all(value, axis, 0, 0, tiled=True)  20.7 us
    pallas_call x12, Pallas kernels, call(): pl.pallas_call(kernel, out_shape=outs, in_specs=specs, out_specs=tuple((p...  19.1 us
    ppermute x1, waiting for transfers between devices, branch(): return lambda block: lax.ppermute(block, ('kstr', 'pw'), closing_pairs(by))  15.1 us
    ppermute x7, waiting for transfers between devices, shifted(): return lax.ppermute(value, 'kstr', [(i, (i + by) % NK) for i in range(NK)])  14 us
    ppermute x1, starting transfers between devices, body(): lax.ppermute(near, 'kstr', [(0, 1), (1, 0), (end - 1, end), (end, end - 1)])  12.5 us
  transfers between devices with their start and end apart: 14, of which 6 were waited for; matrix products, arithmetic and copies ran while one was open for 1% of the time, Pallas kernels for 4%

profile of v11, /device:TPU:1, one launch (start us, length us, event | category | flops | bytes accessed | tf_op | source)
XLA Modules:
  0.0 251.4 jit_solution(17466528423516535351)
XLA Ops:
  0.6 1.1 pad_maximum_fusion.state_ref.p0
  1.7 8.8 %collective-permute-start.32 = (bf16[512,512]{1,0:T(8,128)(2,1)S(1)}, bf16[512,512]{1,0:T(8,128)(2,1)S(1)}, u32[]{:S(2)}, u32[]{:S(2)}) collective-permute-start(bf16[512,512]{1,0:T(8,128)(2,1)S(1)} %pad_maximum_fusion.state_ref.p0), channel_id=1, source_target_pairs={{0,31},{32,63},{448,449},{480,481},{1,0},{33,32},{449,450},{481,48... | collective-permute-start | bytes 1572872 | tf_op jit(solution)/shard_map/ppermute | solution.py:298
  10.5 1.9 collective-permute-start.35
  12.4 1.3 collective-permute-start.34
  13.7 7.4 %collective-permute-start.33 = (bf16[512,512]{1,0:T(8,128)(2,1)S(1)}, bf16[512,512]{1,0:T(8,128)(2,1)S(1)}, u32[]{:S(2)}, u32[]{:S(2)}) collective-permute-start(bf16[512,512]{1,0:T(8,128)(2,1)S(1)} %pad_maximum_fusion.state_ref.p0), channel_id=1, source_target_pairs={{0,480},{32,0},{64,32},{96,64},{128,96},{160,128},{192,160},{224,1... | collective-permute-start | bytes 1572872 | tf_op jit(solution)/shard_map/ppermute | solution.py:256
  21.1 1.2 slice.3
  23.1 0.1 pad_add_fusion.bounds
  23.1 0.1 add_convert_fusion.flags
  23.2 0.8 shard_map.50
  24.1 24.7 %conditional.1 = (bf16[512,512]{1,0:T(8,128)(2,1)}) conditional(s32[]{:T(128)} %clamp.3, bf16[512,512]{1,0:T(8,128)(2,1)S(1)} %shard_map.50, bf16[512,512]{1,0:T(8,128)(2,1)S(1)} %shard_map.50, bf16[512,512]{1,0:T(8,128)(2,1)S(1)} %shard_map.50, bf16[512,512]{1,0:T(8,128)(2,1)S(1)} %shard_map.50, ...), branch_computations={%region_0.1_spmd, %region_1.2_spmd, %region_2.3_spmd, %region_3.4_... | conditional | bytes 2097200 | solution.py:111
  24.1 9.6 %collective-permute-start.7 = (bf16[512,512]{1,0:T(8,128)(2,1)S(1)}, bf16[512,512]{1,0:T(8,128)(2,1)}, u32[]{:S(2)}, u32[]{:S(2)}) collective-permute-start(bf16[512,512]{1,0:T(8,128)(2,1)S(1)} %param.7), channel_id=1, source_target_pairs={{0,505},{480,7},{32,473},{448,39},{1,506},{481,8},{33,474},{449,40... | collective-permute-start | bytes 1572872 | tf_op jit(solution)/shard_map/cond/branch_7_fun/ppermute | solution.py:109
  33.6 15.1 %collective-permute-done.7 = bf16[512,512]{1,0:T(8,128)(2,1)} collective-permute-done((bf16[512,512]{1,0:T(8,128)(2,1)S(1)}, bf16[512,512]{1,0:T(8,128)(2,1)}, u32[]{:S(2)}, u32[]{:S(2)}) %collective-permute-start.7) | collective-permute-done | bytes 524320 | tf_op jit(solution)/shard_map/cond/branch_7_fun/ppermute | solution.py:109
  48.8 0.0 collective-permute-done.35.p_2
  48.8 0.8 copy-done.1
  49.6 2.5 shard_map.51
  52.0 10.9 %all-to-all-start = ((bf16[32,16,256]{2,1,0:T(8,128)(2,1)}), bf16[32,16,256]{2,1,0:T(8,128)(2,1)S(1)}, u32[]{:S(2)}, u32[]{:S(2)}) async-start(bf16[32,16,256]{2,1,0:T(8,128)(2,1)} %bitcast.10), calls=%async_computation | async-start | bytes 524288 | tf_op jit(solution)/shard_map/all_to_all | solution.py:260
  63.0 21.6 %collective-permute-start.36 = (bf16[512,512]{1,0:T(8,128)(2,1)S(1)}, bf16[512,512]{1,0:T(8,128)(2,1)S(1)}, u32[]{:S(2)}, u32[]{:S(2)}) collective-permute-start(bf16[512,512]{1,0:T(8,128)(2,1)S(1)} %pad_maximum_fusion.state_ref.p0), channel_id=1, source_target_pairs={{0,32},{32,64},{64,96},{96,128},{128,160},{160,192},{192,224},{224... | collective-permute-start | bytes 1572872 | tf_op jit(solution)/shard_map/ppermute | solution.py:256
  84.6 0.8 shard_map.52
  85.3 12.5 %collective-permute-start.37 = (bf16[512,512]{1,0:T(8,128)(2,1)}, bf16[512,512]{1,0:T(8,128)(2,1)S(1)}, u32[]{:S(2)}, u32[]{:S(2)}) collective-permute-start(bf16[512,512]{1,0:T(8,128)(2,1)} %get-tuple-element.133.closing_ref.closing), channel_id=1, source_target_pairs={{0,32},{32,0},{448,480},{480,448},{1,33},{33,1},{449,481},{481,449... | collective-permute-start | bytes 1572872 | tf_op jit(solution)/shard_map/ppermute | solution.py:311
  97.8 4.0 %all-to-all-start.1 = ((bf16[32,16,256]{2,1,0:T(8,128)(2,1)}), bf16[32,16,256]{2,1,0:T(8,128)(2,1)S(1)}, u32[]{:S(2)}, u32[]{:S(2)}) async-start(bf16[32,16,256]{2,1,0:T(8,128)(2,1)} %get-tuple-element.106), calls=%async_computation.1 | async-start | bytes 524288 | tf_op jit(solution)/shard_map/all_to_all | solution.py:260
  101.9 0.8 copy-done.9
  102.6 18.4 %all-to-all-done.1 = bf16[32,16,256]{2,1,0:T(8,128)(2,1)S(1)} async-done(((bf16[32,16,256]{2,1,0:T(8,128)(2,1)}), bf16[32,16,256]{2,1,0:T(8,128)(2,1)S(1)}, u32[]{:S(2)}, u32[]{:S(2)}) %all-to-all-start.1) | async-done | bytes 262176 | tf_op jit(solution)/shard_map/all_to_all | solution.py:260
  121.0 3.3 %shard_map.53.y0 = bf16[256,512]{1,0:T(8,128)(2,1)S(1)} custom-call(bf16[512,256]{1,0:T(8,128)(2,1)S(1)} %bitcast.16), custom_call_target="tpu_custom_call" | custom-call | bytes 524288 | tf_op jit(solution)/shard_map/pallas_call | solution.py:29
  124.3 10.0 %collective-permute-start.39 = (bf16[256,512]{1,0:T(8,128)(2,1)S(1)}, bf16[256,512]{1,0:T(8,128)(2,1)S(1)}, u32[]{:S(2)}, u32[]{:S(2)}) collective-permute-start(bf16[256,512]{1,0:T(8,128)(2,1)S(1)} %shard_map.53.y0), channel_id=1, source_target_pairs={{0,480},{32,0},{64,32},{96,64},{128,96},{160,128},{192,160},{224,1... | collective-permute-start | bytes 786440 | tf_op jit(solution)/shard_map/ppermute | solution.py:256
  134.4 1.9 collective-permute-start.38
  136.3 3.3 %collective-permute-done.39.y1 = bf16[256,512]{1,0:T(8,128)(2,1)S(1)} collective-permute-done((bf16[256,512]{1,0:T(8,128)(2,1)S(1)}, bf16[256,512]{1,0:T(8,128)(2,1)S(1)}, u32[]{:S(2)}, u32[]{:S(2)}) %collective-permute-start.39) | collective-permute-done | bytes 262176 | tf_op jit(solution)/shard_map/ppermute | solution.py:256
  139.6 5.9 %collective-permute-done.38.y_1 = bf16[256,512]{1,0:T(8,128)(2,1)S(1)} collective-permute-done((bf16[256,512]{1,0:T(8,128)(2,1)S(1)}, bf16[256,512]{1,0:T(8,128)(2,1)S(1)}, u32[]{:S(2)}, u32[]{:S(2)}) %collective-permute-start.38) | collective-permute-done | bytes 262176 | tf_op jit(solution)/shard_map/ppermute | solution.py:256
  145.5 1.0 copy-done.4
  146.6 3.9 %shard_map.54 = (f32[512,512]{1,0:T(8,128)S(1)}, bf16[512,512]{1,0:T(8,128)(2,1)S(1)}, bf16[512,512]{1,0:T(8,128)(2,1)S(1)}, bf16[32,80,128]{2,1,0:T(8,128)(2,1)S(1)}) custom-call(s32[4]{0:T(128)S(1)} %add_convert_fusion.flags, bf16[256,512]{1,0:T(8,128)(2,1)S(1)} %collective-permute-done.38.y_1, bf16[256,512]{1,0:T(8,128)(2,1)S(1)} %shard_map.53.y0, ...), custom_call_target="tpu_custom_call" | custom-call | bytes 6684688 | tf_op jit(solution)/shard_map/pallas_call | solution.py:29
  150.5 24.4 %all_to_all.46.parts_ref = bf16[32,80,128]{2,1,0:T(8,128)(2,1)S(1)} all-to-all(bf16[32,80,128]{2,1,0:T(8,128)(2,1)S(1)} %get-tuple-element.116), channel_id=1, replica_groups=mesh['kstr'=16,'pw'=32] {'pw'}, dimensions={0} | all-to-all | bytes 1310720 | tf_op jit(solution)/shard_map/all_to_all | solution.py:260
  174.9 0.1 shard_map.55
  175.0 13.8 %all_to_all.47.total_ref.total = f32[16,8,128]{2,1,0:T(8,128)S(1)} all-to-all(f32[16,8,128]{2,1,0:T(8,128)S(1)} %get-tuple-element.117), channel_id=1, replica_groups=mesh['kstr'=16,'pw'=32] {'kstr'}, dimensions={0} | all-to-all | bytes 131072 | tf_op jit(solution)/shard_map/all_to_all | solution.py:260
  188.7 0.1 shard_map.56
  188.9 0.0 copy-start
  188.9 0.7 copy-done
  189.6 5.7 %all-to-all-start.4 = ((bf16[32,16,256]{2,1,0:T(8,128)(2,1)}), bf16[32,16,256]{2,1,0:T(8,128)(2,1)S(1)}, u32[]{:S(2)}, u32[]{:S(2)}) async-start(bf16[32,16,256]{2,1,0:T(8,128)(2,1)} %copy-done), calls=%async_computation.4 | async-start | bytes 524288 | tf_op jit(solution)/shard_map/all_to_all | solution.py:260
  195.3 2.3 collective-permute-start.41
  197.6 10.8 %all-to-all-done.4 = bf16[32,16,256]{2,1,0:T(8,128)(2,1)S(1)} async-done(((bf16[32,16,256]{2,1,0:T(8,128)(2,1)}), bf16[32,16,256]{2,1,0:T(8,128)(2,1)S(1)}, u32[]{:S(2)}, u32[]{:S(2)}) %all-to-all-start.4) | async-done | bytes 262176 | tf_op jit(solution)/shard_map/all_to_all | solution.py:260
  208.5 3.3 %shard_map.57.y0 = bf16[256,512]{1,0:T(8,128)(2,1)S(1)} custom-call(bf16[512,256]{1,0:T(8,128)(2,1)S(1)} %bitcast.15), custom_call_target="tpu_custom_call" | custom-call | bytes 524288 | tf_op jit(solution)/shard_map/pallas_call | solution.py:29
  211.8 2.2 collective-permute-start.40
  214.0 1.0 copy-done.6
  215.0 1.0 copy-done.8
  216.0 2.4 shard_map.58
  218.5 4.8 %collective-permute-done.40.y_1 = bf16[256,512]{1,0:T(8,128)(2,1)S(1)} collective-permute-done((bf16[256,512]{1,0:T(8,128)(2,1)S(1)}, bf16[256,512]{1,0:T(8,128)(2,1)S(1)}, u32[]{:S(2)}, u32[]{:S(2)}) %collective-permute-start.40) | collective-permute-done | bytes 262176 | tf_op jit(solution)/shard_map/ppermute | solution.py:256
  223.3 0.7 shard_map.59
  224.0 15.7 %all_to_all.48.parts_ref = f32[32,8,128]{2,1,0:T(8,128)S(1)} all-to-all(f32[32,8,128]{2,1,0:T(8,128)S(1)} %get-tuple-element.128), channel_id=1, replica_groups=mesh['kstr'=16,'pw'=32] {'pw'}, dimensions={0} | all-to-all | bytes 262144 | tf_op jit(solution)/shard_map/all_to_all | solution.py:260
  239.8 10.5 %all_to_all.49.total_ref = f32[16,8,128]{2,1,0:T(8,128)S(1)} all-to-all(f32[16,8,128]{2,1,0:T(8,128)S(1)} %shard_map.60), channel_id=1, replica_groups=mesh['kstr'=16,'pw'=32] {'kstr'}, dimensions={0} | all-to-all | bytes 131072 | tf_op jit(solution)/shard_map/all_to_all | solution.py:260
  250.3 1.1 shard_map.61
  (23 shorter events, 0.1 us)
Async XLA Ops:
  1.7 21.5 %collective-permute-start.32 = (bf16[512,512]{1,0:T(8,128)(2,1)S(1)}, bf16[512,512]{1,0:T(8,128)(2,1)S(1)}, u32[]{:S(2)}, u32[]{:S(2)}) collective-permute-start(bf16[512,512]{1,0:T(8,128)(2,1)S(1)} %pad_maximum_fusion.state_ref.p0), channel_id=1, source_target_pairs={{0,31},{32,63},{448,449},{480,481},{1,0},{33,32},{449,450},{481,48... | collective-permute-start | bytes 1572872 | tf_op jit(solution)/shard_map/ppermute | solution.py:298
  10.5 38.3 %collective-permute-start.35 = (bf16[512,512]{1,0:T(8,128)(2,1)S(1)}, bf16[512,512]{1,0:T(8,128)(2,1)S(1)}, u32[]{:S(2)}, u32[]{:S(2)}) collective-permute-start(bf16[512,512]{1,0:T(8,128)(2,1)S(1)} %pad_maximum_fusion.state_ref.p0), channel_id=1, source_target_pairs={{0,64},{32,96},{64,128},{96,160},{128,192},{160,224},{192,256},{22... | collective-permute-start | bytes 1572872 | tf_op jit(solution)/shard_map/ppermute | solution.py:256
  12.4 37.1 %collective-permute-start.34 = (bf16[512,512]{1,0:T(8,128)(2,1)S(1)}, bf16[512,512]{1,0:T(8,128)(2,1)S(1)}, u32[]{:S(2)}, u32[]{:S(2)}) collective-permute-start(bf16[512,512]{1,0:T(8,128)(2,1)S(1)} %pad_maximum_fusion.state_ref.p0), channel_id=1, source_target_pairs={{64,0},{96,32},{128,64},{160,96},{192,128},{224,160},{256,192},{28... | collective-permute-start | bytes 1572872 | tf_op jit(solution)/shard_map/ppermute | solution.py:300
  13.7 35.8 %collective-permute-start.33 = (bf16[512,512]{1,0:T(8,128)(2,1)S(1)}, bf16[512,512]{1,0:T(8,128)(2,1)S(1)}, u32[]{:S(2)}, u32[]{:S(2)}) collective-permute-start(bf16[512,512]{1,0:T(8,128)(2,1)S(1)} %pad_maximum_fusion.state_ref.p0), channel_id=1, source_target_pairs={{0,480},{32,0},{64,32},{96,64},{128,96},{160,128},{192,160},{224,1... | collective-permute-start | bytes 1572872 | tf_op jit(solution)/shard_map/ppermute | solution.py:256
  24.1 24.7 %collective-permute-start.7 = (bf16[512,512]{1,0:T(8,128)(2,1)S(1)}, bf16[512,512]{1,0:T(8,128)(2,1)}, u32[]{:S(2)}, u32[]{:S(2)}) collective-permute-start(bf16[512,512]{1,0:T(8,128)(2,1)S(1)} %param.7), channel_id=1, source_target_pairs={{0,505},{480,7},{32,473},{448,39},{1,506},{481,8},{33,474},{449,40... | collective-permute-start | bytes 1572872 | tf_op jit(solution)/shard_map/cond/branch_7_fun/ppermute | solution.py:109
  48.8 0.8 copy-start.1
  49.6 2.5 copy-start.3
  52.0 32.5 %all-to-all-start = ((bf16[32,16,256]{2,1,0:T(8,128)(2,1)}), bf16[32,16,256]{2,1,0:T(8,128)(2,1)S(1)}, u32[]{:S(2)}, u32[]{:S(2)}) async-start(bf16[32,16,256]{2,1,0:T(8,128)(2,1)} %bitcast.10), calls=%async_computation | async-start | bytes 524288 | tf_op jit(solution)/shard_map/all_to_all | solution.py:260
  63.0 38.9 %collective-permute-start.36 = (bf16[512,512]{1,0:T(8,128)(2,1)S(1)}, bf16[512,512]{1,0:T(8,128)(2,1)S(1)}, u32[]{:S(2)}, u32[]{:S(2)}) collective-permute-start(bf16[512,512]{1,0:T(8,128)(2,1)S(1)} %pad_maximum_fusion.state_ref.p0), channel_id=1, source_target_pairs={{0,32},{32,64},{64,96},{96,128},{128,160},{160,192},{192,224},{224... | collective-permute-start | bytes 1572872 | tf_op jit(solution)/shard_map/ppermute | solution.py:256
  85.3 39.0 %collective-permute-start.37 = (bf16[512,512]{1,0:T(8,128)(2,1)}, bf16[512,512]{1,0:T(8,128)(2,1)S(1)}, u32[]{:S(2)}, u32[]{:S(2)}) collective-permute-start(bf16[512,512]{1,0:T(8,128)(2,1)} %get-tuple-element.133.closing_ref.closing), channel_id=1, source_target_pairs={{0,32},{32,0},{448,480},{480,448},{1,33},{33,1},{449,481},{481,449... | collective-permute-start | bytes 1572872 | tf_op jit(solution)/shard_map/ppermute | solution.py:311
  97.8 23.2 %all-to-all-start.1 = ((bf16[32,16,256]{2,1,0:T(8,128)(2,1)}), bf16[32,16,256]{2,1,0:T(8,128)(2,1)S(1)}, u32[]{:S(2)}, u32[]{:S(2)}) async-start(bf16[32,16,256]{2,1,0:T(8,128)(2,1)} %get-tuple-element.106), calls=%async_computation.1 | async-start | bytes 524288 | tf_op jit(solution)/shard_map/all_to_all | solution.py:260
  101.8 0.8 copy-start.9
  121.0 24.5 %copy-start.10 = (bf16[512,512]{1,0:T(8,128)(2,1)S(1)}, bf16[512,512]{1,0:T(8,128)(2,1)}, u32[]{:S(2)}) copy-start(bf16[512,512]{1,0:T(8,128)(2,1)} %copy-done.9) | copy-start | bytes 1572868
  124.3 15.3 %collective-permute-start.39 = (bf16[256,512]{1,0:T(8,128)(2,1)S(1)}, bf16[256,512]{1,0:T(8,128)(2,1)S(1)}, u32[]{:S(2)}, u32[]{:S(2)}) collective-permute-start(bf16[256,512]{1,0:T(8,128)(2,1)S(1)} %shard_map.53.y0), channel_id=1, source_target_pairs={{0,480},{32,0},{64,32},{96,64},{128,96},{160,128},{192,160},{224,1... | collective-permute-start | bytes 786440 | tf_op jit(solution)/shard_map/ppermute | solution.py:256
  134.4 11.1 %collective-permute-start.38 = (bf16[256,512]{1,0:T(8,128)(2,1)S(1)}, bf16[256,512]{1,0:T(8,128)(2,1)S(1)}, u32[]{:S(2)}, u32[]{:S(2)}) collective-permute-start(bf16[256,512]{1,0:T(8,128)(2,1)S(1)} %shard_map.53.y0), channel_id=1, source_target_pairs={{0,32},{32,64},{64,96},{96,128},{128,160},{160,192},{192,224},{224... | collective-permute-start | bytes 786440 | tf_op jit(solution)/shard_map/ppermute | solution.py:256
  145.5 1.0 copy-start.4
  150.5 24.4 %copy-start.5 = (bf16[512,512]{1,0:T(8,128)(2,1)}, bf16[512,512]{1,0:T(8,128)(2,1)S(1)}, u32[]{:S(2)}) copy-start(bf16[512,512]{1,0:T(8,128)(2,1)S(1)} %get-tuple-element.125.g1) | copy-start | bytes 1572868
  150.5 24.4 %copy-start.7 = (bf16[512,512]{1,0:T(8,128)(2,1)}, bf16[512,512]{1,0:T(8,128)(2,1)S(1)}, u32[]{:S(2)}) copy-start(bf16[512,512]{1,0:T(8,128)(2,1)S(1)} %get-tuple-element.123.p_1) | copy-start | bytes 1572868
  188.9 0.7 copy-start
  189.6 18.9 %all-to-all-start.4 = ((bf16[32,16,256]{2,1,0:T(8,128)(2,1)}), bf16[32,16,256]{2,1,0:T(8,128)(2,1)S(1)}, u32[]{:S(2)}, u32[]{:S(2)}) async-start(bf16[32,16,256]{2,1,0:T(8,128)(2,1)} %copy-done), calls=%async_computation.4 | async-start | bytes 524288 | tf_op jit(solution)/shard_map/all_to_all | solution.py:260
  195.3 18.6 %collective-permute-start.41 = (bf16[256,512]{1,0:T(8,128)(2,1)S(1)}, bf16[256,512]{1,0:T(8,128)(2,1)}, u32[]{:S(2)}, u32[]{:S(2)}) collective-permute-start(bf16[256,512]{1,0:T(8,128)(2,1)S(1)} %shard_map.53.y0), channel_id=1, source_target_pairs={{0,64},{32,96},{64,128},{96,160},{128,192},{160,224},{192,256},{22... | collective-permute-start | bytes 786440 | tf_op jit(solution)/shard_map/ppermute | solution.py:256
  208.5 5.5 %copy-start.2 = (bf16[512,512]{1,0:T(8,128)(2,1)S(1)}, bf16[512,512]{1,0:T(8,128)(2,1)}, u32[]{:S(2)}) copy-start(bf16[512,512]{1,0:T(8,128)(2,1)} %copy-done.1) | copy-start | bytes 1572868
  211.8 11.5 %collective-permute-start.40 = (bf16[256,512]{1,0:T(8,128)(2,1)S(1)}, bf16[256,512]{1,0:T(8,128)(2,1)S(1)}, u32[]{:S(2)}, u32[]{:S(2)}) collective-permute-start(bf16[256,512]{1,0:T(8,128)(2,1)S(1)} %shard_map.57.y0), channel_id=1, source_target_pairs={{0,32},{32,64},{64,96},{96,128},{128,160},{160,192},{192,224},{224... | collective-permute-start | bytes 786440 | tf_op jit(solution)/shard_map/ppermute | solution.py:256
  214.0 1.0 copy-start.6
  215.0 1.0 copy-start.8

commit v12 on v11

--- a/solution.py
+++ b/solution.py
@@ -305,14 +305,13 @@
     part, p1 = call(first_margin_kernel, (shape((full, NB), BF16), fields), flags, state, p1, near, smem=1)
     state, near, part = lax.optimization_barrier((state, near, part))
     p_1 = shifted(state, 1)
+    far = lax.ppermute(near, "kstr", [(0, 1), (1, 0), (end - 1, end), (end, end - 1)])
     parts = exchange(part, "pw").reshape(PARTS, CHUNK, NB)
     own, kept = call(collect_kernel, (chunks, chunk), parts)
-    own, near = lax.optimization_barrier((own, near))
-    far = lax.ppermute(near, "kstr", [(0, 1), (1, 0), (end - 1, end), (end, end - 1)])
     whole = exchange(own.reshape(full, NB), "pw")
-    whole, p_1 = lax.optimization_barrier((whole, p_1))
-
-    y0, far = lax.optimization_barrier((inverse(whole), far))
+    whole, far, p_1 = lax.optimization_barrier((whole, far, p_1))
+
+    y0 = inverse(whole)
     y_1 = shifted(y0, 1)
     y1 = shifted(y0, -1)
     g0, g1, p_1, part = call(

time: 252 us -> 243 us (0.964)
  starting transfers between devices: 100 us -> 79.3 us
  waiting for transfers between devices: 58.3 us -> 70 us
    ppermute x7, starting transfers between devices: 47.3 us -> 27 us  [shifted(): return lax.ppermute(value, 'kstr', [(i, (i + by) % NK) for i in range(NK)])]
    ppermute x1, waiting for transfers between devices: 0.01 us -> 14.8 us  [body(): lax.ppermute(near, 'kstr', [(0, 1), (1, 0), (end - 1, end), (end, end - 1)])]
    ppermute x1, starting transfers between devices: 12.5 us -> 5.25 us  [body(): lax.ppermute(near, 'kstr', [(0, 1), (1, 0), (end - 1, end), (end, end - 1)])]
    all_to_all x3, waiting for transfers between devices: 29.2 us -> 25.3 us  [exchange(): return lax.all_to_all(value, axis, 0, 0, tiled=True)]
    ppermute x1, starting transfers between devices: 9.55 us -> 13.5 us  [branch(): return lambda block: lax.ppermute(block, ('kstr', 'pw'), closing_pairs(by))]
    all_to_all x3, starting transfers between devices: 20.7 us -> 23.6 us  [exchange(): return lax.all_to_all(value, axis, 0, 0, tiled=True)]
  transfers between devices with their start and end apart: 14 -> 14, of which waited for: 6 -> 8; matrix products, arithmetic and copies ran while one was open for 1% -> 1% of each run, Pallas kernels for 4% -> 3%
where the time goes in v12:
time: 243 us; the launch traced here: 242 us
  starting transfers between devices  79.3 us (33%)
  waiting for transfers between devices  70 us (29%)
  blocking collectives  63.9 us (26%)
  Pallas kernels  19.1 us (8%)
  local copies, waits for them, and re-layouts  6.63 us (3%)
    all_to_all x4, blocking collectives, exchange(): return lax.all_to_all(value, axis, 0, 0, tiled=True)  63.9 us
    ppermute x7, starting transfers between devices, shifted(): return lax.ppermute(value, 'kstr', [(i, (i + by) % NK) for i in range(NK)])  27 us
    all_to_all x3, waiting for transfers between devices, exchange(): return lax.all_to_all(value, axis, 0, 0, tiled=True)  25.3 us
    all_to_all x3, starting transfers between devices, exchange(): return lax.all_to_all(value, axis, 0, 0, tiled=True)  23.6 us
    pallas_call x12, Pallas kernels, call(): pl.pallas_call(kernel, out_shape=outs, in_specs=specs, out_specs=tuple((p...  19.1 us
    ppermute x1, waiting for transfers between devices, branch(): return lambda block: lax.ppermute(block, ('kstr', 'pw'), closing_pairs(by))  15 us
    ppermute x7, waiting for transfers between devices, shifted(): return lax.ppermute(value, 'kstr', [(i, (i + by) % NK) for i in range(NK)])  14.9 us
    ppermute x1, waiting for transfers between devices, body(): lax.ppermute(near, 'kstr', [(0, 1), (1, 0), (end - 1, end), (end, end - 1)])  14.8 us
  transfers between devices with their start and end apart: 14, of which 8 were waited for; matrix products, arithmetic and copies ran while one was open for 1% of the time, Pallas kernels for 3%

profile of v12, /device:TPU:1, one launch (start us, length us, event | category | flops | bytes accessed | tf_op | source)
XLA Modules:
  0.0 241.8 jit_solution(14318377014285465925)
XLA Ops:
  0.6 1.1 pad_maximum_fusion.state_ref.p0
  1.7 8.8 %collective-permute-start.32 = (bf16[512,512]{1,0:T(8,128)(2,1)S(1)}, bf16[512,512]{1,0:T(8,128)(2,1)S(1)}, u32[]{:S(2)}, u32[]{:S(2)}) collective-permute-start(bf16[512,512]{1,0:T(8,128)(2,1)S(1)} %pad_maximum_fusion.state_ref.p0), channel_id=1, source_target_pairs={{0,31},{32,63},{448,449},{480,481},{1,0},{33,32},{449,450},{481,48... | collective-permute-start | bytes 1572872 | tf_op jit(solution)/shard_map/ppermute | solution.py:298
  10.5 1.9 collective-permute-start.35
  12.4 1.3 collective-permute-start.34
  13.7 7.4 %collective-permute-start.33 = (bf16[512,512]{1,0:T(8,128)(2,1)S(1)}, bf16[512,512]{1,0:T(8,128)(2,1)S(1)}, u32[]{:S(2)}, u32[]{:S(2)}) collective-permute-start(bf16[512,512]{1,0:T(8,128)(2,1)S(1)} %pad_maximum_fusion.state_ref.p0), channel_id=1, source_target_pairs={{0,480},{32,0},{64,32},{96,64},{128,96},{160,128},{192,160},{224,1... | collective-permute-start | bytes 1572872 | tf_op jit(solution)/shard_map/ppermute | solution.py:256
  21.1 1.2 slice.3
  23.1 0.1 pad_add_fusion.bounds
  23.1 0.1 add_convert_fusion.flags
  23.2 0.8 shard_map.50
  24.1 28.5 %conditional.1 = (bf16[512,512]{1,0:T(8,128)(2,1)}) conditional(s32[]{:T(128)} %clamp.3, bf16[512,512]{1,0:T(8,128)(2,1)S(1)} %shard_map.50, bf16[512,512]{1,0:T(8,128)(2,1)S(1)} %shard_map.50, bf16[512,512]{1,0:T(8,128)(2,1)S(1)} %shard_map.50, bf16[512,512]{1,0:T(8,128)(2,1)S(1)} %shard_map.50, ...), branch_computations={%region_0.1_spmd, %region_1.2_spmd, %region_2.3_spmd, %region_3.4_... | conditional | bytes 2097200 | solution.py:111
  24.1 13.5 %collective-permute-start.3 = (bf16[512,512]{1,0:T(8,128)(2,1)S(1)}, bf16[512,512]{1,0:T(8,128)(2,1)}, u32[]{:S(2)}, u32[]{:S(2)}) collective-permute-start(bf16[512,512]{1,0:T(8,128)(2,1)S(1)} %param.3), channel_id=1, source_target_pairs={{0,509},{480,3},{32,477},{448,35},{1,510},{481,4},{33,478},{449,36... | collective-permute-start | bytes 1572872 | tf_op jit(solution)/shard_map/cond/branch_3_fun/ppermute | solution.py:109
  37.5 15.0 %collective-permute-done.3 = bf16[512,512]{1,0:T(8,128)(2,1)} collective-permute-done((bf16[512,512]{1,0:T(8,128)(2,1)S(1)}, bf16[512,512]{1,0:T(8,128)(2,1)}, u32[]{:S(2)}, u32[]{:S(2)}) %collective-permute-start.3) | collective-permute-done | bytes 524320 | tf_op jit(solution)/shard_map/cond/branch_3_fun/ppermute | solution.py:109
  52.5 0.8 copy-done.1
  53.3 2.5 %shard_map.51 = (bf16[512,256]{1,0:T(8,128)(2,1)}, bf16[512,512]{1,0:T(8,128)(2,1)S(1)}) custom-call(s32[4]{0:T(128)S(1)} %add_convert_fusion.flags, bf16[512,512]{1,0:T(8,128)(2,1)S(1)} %pad_maximum_fusion.state_ref.p0, bf16[512,512]{1,0:T(8,128)(2,1)S(1)} %collective-permute-done.33.next_ref, bf16[512,512]{1,0:T(8,128)(2,1)} %get-tuple-element.127.closing_ref.closing), custom_call_target="tpu_custom_call" | custom-call | bytes 2359312 | tf_op jit(solution)/shard_map/pallas_call | solution.py:29
  55.8 14.0 %all-to-all-start = ((bf16[32,16,256]{2,1,0:T(8,128)(2,1)}), bf16[32,16,256]{2,1,0:T(8,128)(2,1)S(1)}, u32[]{:S(2)}, u32[]{:S(2)}) async-start(bf16[32,16,256]{2,1,0:T(8,128)(2,1)} %bitcast.10), calls=%async_computation | async-start | bytes 524288 | tf_op jit(solution)/shard_map/all_to_all | solution.py:260
  69.8 5.2 %collective-permute-start.36 = (bf16[512,512]{1,0:T(8,128)(2,1)}, bf16[512,512]{1,0:T(8,128)(2,1)S(1)}, u32[]{:S(2)}, u32[]{:S(2)}) collective-permute-start(bf16[512,512]{1,0:T(8,128)(2,1)} %get-tuple-element.127.closing_ref.closing), channel_id=1, source_target_pairs={{0,32},{32,0},{448,480},{480,448},{1,33},{33,1},{449,481},{481,449... | collective-permute-start | bytes 1572872 | tf_op jit(solution)/shard_map/ppermute | solution.py:308
  75.0 1.9 collective-permute-start.37
  76.9 6.2 %all-to-all-done.parts_ref = bf16[32,16,256]{2,1,0:T(8,128)(2,1)S(1)} async-done(((bf16[32,16,256]{2,1,0:T(8,128)(2,1)}), bf16[32,16,256]{2,1,0:T(8,128)(2,1)S(1)}, u32[]{:S(2)}, u32[]{:S(2)}) %all-to-all-start) | async-done | bytes 262176 | tf_op jit(solution)/shard_map/all_to_all | solution.py:260
  83.2 0.8 shard_map.52
  83.9 4.1 %all-to-all-start.1 = ((bf16[32,16,256]{2,1,0:T(8,128)(2,1)}), bf16[32,16,256]{2,1,0:T(8,128)(2,1)S(1)}, u32[]{:S(2)}, u32[]{:S(2)}) async-start(bf16[32,16,256]{2,1,0:T(8,128)(2,1)} %get-tuple-element.101), calls=%async_computation.1 | async-start | bytes 524288 | tf_op jit(solution)/shard_map/all_to_all | solution.py:260
  88.0 14.8 %collective-permute-done.36.beyond.closing = bf16[512,512]{1,0:T(8,128)(2,1)S(1)} collective-permute-done((bf16[512,512]{1,0:T(8,128)(2,1)}, bf16[512,512]{1,0:T(8,128)(2,1)S(1)}, u32[]{:S(2)}, u32[]{:S(2)}) %collective-permute-start.36) | collective-permute-done | bytes 524320 | tf_op jit(solution)/shard_map/ppermute | solution.py:308
  102.8 0.8 copy-done.9
  103.6 8.3 %all-to-all-done.1 = bf16[32,16,256]{2,1,0:T(8,128)(2,1)S(1)} async-done(((bf16[32,16,256]{2,1,0:T(8,128)(2,1)}), bf16[32,16,256]{2,1,0:T(8,128)(2,1)S(1)}, u32[]{:S(2)}, u32[]{:S(2)}) %all-to-all-start.1) | async-done | bytes 262176 | tf_op jit(solution)/shard_map/all_to_all | solution.py:260
  112.0 3.3 %shard_map.53.y0 = bf16[256,512]{1,0:T(8,128)(2,1)S(1)} custom-call(bf16[512,256]{1,0:T(8,128)(2,1)S(1)} %bitcast.15), custom_call_target="tpu_custom_call" | custom-call | bytes 524288 | tf_op jit(solution)/shard_map/pallas_call | solution.py:29
  115.3 9.4 %collective-permute-start.39 = (bf16[256,512]{1,0:T(8,128)(2,1)S(1)}, bf16[256,512]{1,0:T(8,128)(2,1)S(1)}, u32[]{:S(2)}, u32[]{:S(2)}) collective-permute-start(bf16[256,512]{1,0:T(8,128)(2,1)S(1)} %shard_map.53.y0), channel_id=1, source_target_pairs={{0,480},{32,0},{64,32},{96,64},{128,96},{160,128},{192,160},{224,1... | collective-permute-start | bytes 786440 | tf_op jit(solution)/shard_map/ppermute | solution.py:256
  124.7 1.9 collective-permute-start.38
  126.6 4.2 %collective-permute-done.39.y1 = bf16[256,512]{1,0:T(8,128)(2,1)S(1)} collective-permute-done((bf16[256,512]{1,0:T(8,128)(2,1)S(1)}, bf16[256,512]{1,0:T(8,128)(2,1)S(1)}, u32[]{:S(2)}, u32[]{:S(2)}) %collective-permute-start.39) | collective-permute-done | bytes 262176 | tf_op jit(solution)/shard_map/ppermute | solution.py:256
  130.8 5.9 %collective-permute-done.38.y_1 = bf16[256,512]{1,0:T(8,128)(2,1)S(1)} collective-permute-done((bf16[256,512]{1,0:T(8,128)(2,1)S(1)}, bf16[256,512]{1,0:T(8,128)(2,1)S(1)}, u32[]{:S(2)}, u32[]{:S(2)}) %collective-permute-start.38) | collective-permute-done | bytes 262176 | tf_op jit(solution)/shard_map/ppermute | solution.py:256
  136.7 1.0 copy-done.4
  137.7 3.9 %shard_map.54 = (f32[512,512]{1,0:T(8,128)S(1)}, bf16[512,512]{1,0:T(8,128)(2,1)S(1)}, bf16[512,512]{1,0:T(8,128)(2,1)S(1)}, bf16[32,80,128]{2,1,0:T(8,128)(2,1)S(1)}) custom-call(s32[4]{0:T(128)S(1)} %add_convert_fusion.flags, bf16[256,512]{1,0:T(8,128)(2,1)S(1)} %collective-permute-done.38.y_1, bf16[256,512]{1,0:T(8,128)(2,1)S(1)} %shard_map.53.y0, ...), custom_call_target="tpu_custom_call" | custom-call | bytes 6684688 | tf_op jit(solution)/shard_map/pallas_call | solution.py:29
  141.7 23.4 %all_to_all.46.parts_ref = bf16[32,80,128]{2,1,0:T(8,128)(2,1)S(1)} all-to-all(bf16[32,80,128]{2,1,0:T(8,128)(2,1)S(1)} %get-tuple-element.110), channel_id=1, replica_groups=mesh['kstr'=16,'pw'=32] {'pw'}, dimensions={0} | all-to-all | bytes 1310720 | tf_op jit(solution)/shard_map/all_to_all | solution.py:260
  165.1 0.1 shard_map.55
  165.2 14.3 %all_to_all.47.total_ref.total = f32[16,8,128]{2,1,0:T(8,128)S(1)} all-to-all(f32[16,8,128]{2,1,0:T(8,128)S(1)} %get-tuple-element.111), channel_id=1, replica_groups=mesh['kstr'=16,'pw'=32] {'kstr'}, dimensions={0} | all-to-all | bytes 131072 | tf_op jit(solution)/shard_map/all_to_all | solution.py:260
  179.5 0.1 shard_map.56
  179.6 0.7 copy-done
  180.3 5.5 %all-to-all-start.4 = ((bf16[32,16,256]{2,1,0:T(8,128)(2,1)}), bf16[32,16,256]{2,1,0:T(8,128)(2,1)S(1)}, u32[]{:S(2)}, u32[]{:S(2)}) async-start(bf16[32,16,256]{2,1,0:T(8,128)(2,1)} %copy-done), calls=%async_computation.4 | async-start | bytes 524288 | tf_op jit(solution)/shard_map/all_to_all | solution.py:260
  185.8 2.3 collective-permute-start.41
  188.1 10.7 %all-to-all-done.4 = bf16[32,16,256]{2,1,0:T(8,128)(2,1)S(1)} async-done(((bf16[32,16,256]{2,1,0:T(8,128)(2,1)}), bf16[32,16,256]{2,1,0:T(8,128)(2,1)S(1)}, u32[]{:S(2)}, u32[]{:S(2)}) %all-to-all-start.4) | async-done | bytes 262176 | tf_op jit(solution)/shard_map/all_to_all | solution.py:260
  198.9 3.3 %shard_map.57.y0 = bf16[256,512]{1,0:T(8,128)(2,1)S(1)} custom-call(bf16[512,256]{1,0:T(8,128)(2,1)S(1)} %bitcast.16), custom_call_target="tpu_custom_call" | custom-call | bytes 524288 | tf_op jit(solution)/shard_map/pallas_call | solution.py:29
  202.2 2.1 collective-permute-start.40
  204.3 1.0 copy-done.6
  205.4 1.0 copy-done.8
  206.4 2.4 %shard_map.58 = (bf16[512,512]{1,0:T(8,128)(2,1)S(1)}, bf16[512,512]{1,0:T(8,128)(2,1)S(1)}, bf16[512,512]{1,0:T(8,128)(2,1)S(1)}) custom-call(s32[4]{0:T(128)S(1)} %add_convert_fusion.flags, f32[16,8,128]{2,1,0:T(8,128)S(1)} %all_to_all.47.total_ref.total, bf16[256,512]{1,0:T(8,128)(2,1)} %collective-permute-done.41.y_2, ...), custom_call_target="tpu_custom_call" | custom-call | bytes 6357008 | tf_op jit(solution)/shard_map/pallas_call | solution.py:29
  208.9 4.8 %collective-permute-done.40.y_1 = bf16[256,512]{1,0:T(8,128)(2,1)S(1)} collective-permute-done((bf16[256,512]{1,0:T(8,128)(2,1)S(1)}, bf16[256,512]{1,0:T(8,128)(2,1)S(1)}, u32[]{:S(2)}, u32[]{:S(2)}) %collective-permute-start.40) | collective-permute-done | bytes 262176 | tf_op jit(solution)/shard_map/ppermute | solution.py:256
  213.7 0.7 shard_map.59
  214.4 15.7 %all_to_all.48.parts_ref = f32[32,8,128]{2,1,0:T(8,128)S(1)} all-to-all(f32[32,8,128]{2,1,0:T(8,128)S(1)} %get-tuple-element.122), channel_id=1, replica_groups=mesh['kstr'=16,'pw'=32] {'pw'}, dimensions={0} | all-to-all | bytes 262144 | tf_op jit(solution)/shard_map/all_to_all | solution.py:260
  230.1 10.5 %all_to_all.49.total_ref = f32[16,8,128]{2,1,0:T(8,128)S(1)} all-to-all(f32[16,8,128]{2,1,0:T(8,128)S(1)} %shard_map.60), channel_id=1, replica_groups=mesh['kstr'=16,'pw'=32] {'kstr'}, dimensions={0} | all-to-all | bytes 131072 | tf_op jit(solution)/shard_map/all_to_all | solution.py:260
  240.7 1.1 shard_map.61
  (23 shorter events, 0.1 us)
Async XLA Ops:
  1.7 21.5 %collective-permute-start.32 = (bf16[512,512]{1,0:T(8,128)(2,1)S(1)}, bf16[512,512]{1,0:T(8,128)(2,1)S(1)}, u32[]{:S(2)}, u32[]{:S(2)}) collective-permute-start(bf16[512,512]{1,0:T(8,128)(2,1)S(1)} %pad_maximum_fusion.state_ref.p0), channel_id=1, source_target_pairs={{0,31},{32,63},{448,449},{480,481},{1,0},{33,32},{449,450},{481,48... | collective-permute-start | bytes 1572872 | tf_op jit(solution)/shard_map/ppermute | solution.py:298
  10.5 42.0 %collective-permute-start.35 = (bf16[512,512]{1,0:T(8,128)(2,1)S(1)}, bf16[512,512]{1,0:T(8,128)(2,1)S(1)}, u32[]{:S(2)}, u32[]{:S(2)}) collective-permute-start(bf16[512,512]{1,0:T(8,128)(2,1)S(1)} %pad_maximum_fusion.state_ref.p0), channel_id=1, source_target_pairs={{0,64},{32,96},{64,128},{96,160},{128,192},{160,224},{192,256},{22... | collective-permute-start | bytes 1572872 | tf_op jit(solution)/shard_map/ppermute | solution.py:256
  12.4 40.9 %collective-permute-start.34 = (bf16[512,512]{1,0:T(8,128)(2,1)S(1)}, bf16[512,512]{1,0:T(8,128)(2,1)S(1)}, u32[]{:S(2)}, u32[]{:S(2)}) collective-permute-start(bf16[512,512]{1,0:T(8,128)(2,1)S(1)} %pad_maximum_fusion.state_ref.p0), channel_id=1, source_target_pairs={{64,0},{96,32},{128,64},{160,96},{192,128},{224,160},{256,192},{28... | collective-permute-start | bytes 1572872 | tf_op jit(solution)/shard_map/ppermute | solution.py:300
  13.7 39.6 %collective-permute-start.33 = (bf16[512,512]{1,0:T(8,128)(2,1)S(1)}, bf16[512,512]{1,0:T(8,128)(2,1)S(1)}, u32[]{:S(2)}, u32[]{:S(2)}) collective-permute-start(bf16[512,512]{1,0:T(8,128)(2,1)S(1)} %pad_maximum_fusion.state_ref.p0), channel_id=1, source_target_pairs={{0,480},{32,0},{64,32},{96,64},{128,96},{160,128},{192,160},{224,1... | collective-permute-start | bytes 1572872 | tf_op jit(solution)/shard_map/ppermute | solution.py:256
  24.1 28.4 %collective-permute-start.3 = (bf16[512,512]{1,0:T(8,128)(2,1)S(1)}, bf16[512,512]{1,0:T(8,128)(2,1)}, u32[]{:S(2)}, u32[]{:S(2)}) collective-permute-start(bf16[512,512]{1,0:T(8,128)(2,1)S(1)} %param.3), channel_id=1, source_target_pairs={{0,509},{480,3},{32,477},{448,35},{1,510},{481,4},{33,478},{449,36... | collective-permute-start | bytes 1572872 | tf_op jit(solution)/shard_map/cond/branch_3_fun/ppermute | solution.py:109
  52.5 0.8 copy-start.1
  53.3 2.5 %copy-start.3 = (bf16[512,512]{1,0:T(8,128)(2,1)}, bf16[512,512]{1,0:T(8,128)(2,1)S(1)}, u32[]{:S(2)}) copy-start(bf16[512,512]{1,0:T(8,128)(2,1)S(1)} %collective-permute-done.34.p2) | copy-start | bytes 1572868
  55.8 27.4 %all-to-all-start = ((bf16[32,16,256]{2,1,0:T(8,128)(2,1)}), bf16[32,16,256]{2,1,0:T(8,128)(2,1)S(1)}, u32[]{:S(2)}, u32[]{:S(2)}) async-start(bf16[32,16,256]{2,1,0:T(8,128)(2,1)} %bitcast.10), calls=%async_computation | async-start | bytes 524288 | tf_op jit(solution)/shard_map/all_to_all | solution.py:260
  69.8 33.1 %collective-permute-start.36 = (bf16[512,512]{1,0:T(8,128)(2,1)}, bf16[512,512]{1,0:T(8,128)(2,1)S(1)}, u32[]{:S(2)}, u32[]{:S(2)}) collective-permute-start(bf16[512,512]{1,0:T(8,128)(2,1)} %get-tuple-element.127.closing_ref.closing), channel_id=1, source_target_pairs={{0,32},{32,0},{448,480},{480,448},{1,33},{33,1},{449,481},{481,449... | collective-permute-start | bytes 1572872 | tf_op jit(solution)/shard_map/ppermute | solution.py:308
  75.0 27.8 %collective-permute-start.37 = (bf16[512,512]{1,0:T(8,128)(2,1)S(1)}, bf16[512,512]{1,0:T(8,128)(2,1)S(1)}, u32[]{:S(2)}, u32[]{:S(2)}) collective-permute-start(bf16[512,512]{1,0:T(8,128)(2,1)S(1)} %pad_maximum_fusion.state_ref.p0), channel_id=1, source_target_pairs={{0,32},{32,64},{64,96},{96,128},{128,160},{160,192},{192,224},{224... | collective-permute-start | bytes 1572872 | tf_op jit(solution)/shard_map/ppermute | solution.py:256
  83.9 28.1 %all-to-all-start.1 = ((bf16[32,16,256]{2,1,0:T(8,128)(2,1)}), bf16[32,16,256]{2,1,0:T(8,128)(2,1)S(1)}, u32[]{:S(2)}, u32[]{:S(2)}) async-start(bf16[32,16,256]{2,1,0:T(8,128)(2,1)} %get-tuple-element.101), calls=%async_computation.1 | async-start | bytes 524288 | tf_op jit(solution)/shard_map/all_to_all | solution.py:260
  102.8 0.8 copy-start.9
  112.0 24.7 %copy-start.10 = (bf16[512,512]{1,0:T(8,128)(2,1)S(1)}, bf16[512,512]{1,0:T(8,128)(2,1)}, u32[]{:S(2)}) copy-start(bf16[512,512]{1,0:T(8,128)(2,1)} %copy-done.9) | copy-start | bytes 1572868
  115.3 15.5 %collective-permute-start.39 = (bf16[256,512]{1,0:T(8,128)(2,1)S(1)}, bf16[256,512]{1,0:T(8,128)(2,1)S(1)}, u32[]{:S(2)}, u32[]{:S(2)}) collective-permute-start(bf16[256,512]{1,0:T(8,128)(2,1)S(1)} %shard_map.53.y0), channel_id=1, source_target_pairs={{0,480},{32,0},{64,32},{96,64},{128,96},{160,128},{192,160},{224,1... | collective-permute-start | bytes 786440 | tf_op jit(solution)/shard_map/ppermute | solution.py:256
  124.7 12.0 %collective-permute-start.38 = (bf16[256,512]{1,0:T(8,128)(2,1)S(1)}, bf16[256,512]{1,0:T(8,128)(2,1)S(1)}, u32[]{:S(2)}, u32[]{:S(2)}) collective-permute-start(bf16[256,512]{1,0:T(8,128)(2,1)S(1)} %shard_map.53.y0), channel_id=1, source_target_pairs={{0,32},{32,64},{64,96},{96,128},{128,160},{160,192},{192,224},{224... | collective-permute-start | bytes 786440 | tf_op jit(solution)/shard_map/ppermute | solution.py:256
  136.7 1.0 copy-start.4
  141.7 23.4 %copy-start.5 = (bf16[512,512]{1,0:T(8,128)(2,1)}, bf16[512,512]{1,0:T(8,128)(2,1)S(1)}, u32[]{:S(2)}) copy-start(bf16[512,512]{1,0:T(8,128)(2,1)S(1)} %get-tuple-element.119.g1) | copy-start | bytes 1572868
  141.7 23.4 %copy-start.7 = (bf16[512,512]{1,0:T(8,128)(2,1)}, bf16[512,512]{1,0:T(8,128)(2,1)S(1)}, u32[]{:S(2)}) copy-start(bf16[512,512]{1,0:T(8,128)(2,1)S(1)} %get-tuple-element.117.p_1) | copy-start | bytes 1572868
  179.6 0.7 copy-start
  180.3 18.5 %all-to-all-start.4 = ((bf16[32,16,256]{2,1,0:T(8,128)(2,1)}), bf16[32,16,256]{2,1,0:T(8,128)(2,1)S(1)}, u32[]{:S(2)}, u32[]{:S(2)}) async-start(bf16[32,16,256]{2,1,0:T(8,128)(2,1)} %copy-done), calls=%async_computation.4 | async-start | bytes 524288 | tf_op jit(solution)/shard_map/all_to_all | solution.py:260
  185.8 18.5 %collective-permute-start.41 = (bf16[256,512]{1,0:T(8,128)(2,1)S(1)}, bf16[256,512]{1,0:T(8,128)(2,1)}, u32[]{:S(2)}, u32[]{:S(2)}) collective-permute-start(bf16[256,512]{1,0:T(8,128)(2,1)S(1)} %shard_map.53.y0), channel_id=1, source_target_pairs={{0,64},{32,96},{64,128},{96,160},{128,192},{160,224},{192,256},{22... | collective-permute-start | bytes 786440 | tf_op jit(solution)/shard_map/ppermute | solution.py:256
  198.9 5.4 %copy-start.2 = (bf16[512,512]{1,0:T(8,128)(2,1)S(1)}, bf16[512,512]{1,0:T(8,128)(2,1)}, u32[]{:S(2)}) copy-start(bf16[512,512]{1,0:T(8,128)(2,1)} %copy-done.1) | copy-start | bytes 1572868
  202.2 11.5 %collective-permute-start.40 = (bf16[256,512]{1,0:T(8,128)(2,1)S(1)}, bf16[256,512]{1,0:T(8,128)(2,1)S(1)}, u32[]{:S(2)}, u32[]{:S(2)}) collective-permute-start(bf16[256,512]{1,0:T(8,128)(2,1)S(1)} %shard_map.57.y0), channel_id=1, source_target_pairs={{0,32},{32,64},{64,96},{96,128},{128,160},{160,192},{192,224},{224... | collective-permute-start | bytes 786440 | tf_op jit(solution)/shard_map/ppermute | solution.py:256
  204.3 1.0 copy-start.6
  205.4 1.0 copy-start.8

commit v13 on v12

--- a/solution.py
+++ b/solution.py
@@ -123,7 +123,7 @@
         lanes = pl.ds(128 * half, 128)
         first_ref[:, lanes] = total[CHUNK * half : CHUNK * (half + 1)] * (1.0 / NPW)
         second_ref[:, lanes] = total[CHUNK * (2 + half) : CHUNK * (3 + half)] * (1.0 / NPW)
-    part = total[4 * CHUNK : 4 * CHUNK + 8] + total[4 * CHUNK + 8 :]
+    part = jnp.sum(total[4 * CHUNK :], axis=0, keepdims=True)
     squares_ref[...] = jnp.broadcast_to(part[None], squares_ref.shape)
 
 
@@ -227,7 +227,8 @@
 def slope_kernel(y_1, y0, p_1, p1, g0, total_ref):
     grad = slope(y0[...], p1[...], y_1[...], p_1[...])
     g0[...] = grad
-    total_ref[...] = jnp.broadcast_to(squares(grad)[None], total_ref.shape)
+    part = jnp.sum(squares(grad), axis=0, keepdims=True)
+    total_ref[...] = jnp.broadcast_to(part[None], total_ref.shape)
 
 
 def step_size(total_ref):
@@ -262,7 +263,7 @@
 
 def whole_total(part):
     parts = exchange(part, "pw")
-    own = call(spread_kernel, shape((NK, 8, 128), F32), parts)
+    own = call(spread_kernel, shape((NK, 1, 128), F32), parts)
     return exchange(own, "kstr")
 
 
@@ -325,7 +326,7 @@
     y_2 = shifted(y0, 2)
     parts = exchange(part, "pw")
     first, second, total = call(
-        collect_orders_kernel, (chunk, chunk, shape((NK, 8, 128), F32)), parts
+        collect_orders_kernel, (chunk, chunk, shape((NK, 1, 128), F32)), parts
     )
     total = exchange(total, "kstr")
     own = call(combine_kernel, chunks, total, kept, first, second)
@@ -340,7 +341,7 @@
 
     y0 = inverse(whole)
     y_1 = shifted(y0, 1)
-    g0, total = call(slope_kernel, (grads, shape((PARTS, 8, 128), F32)), y_1, y0, q_1, q1)
+    g0, total = call(slope_kernel, (grads, shape((PARTS, 1, 128), F32)), y_1, y0, q_1, q1)
     total = whole_total(total)
     half = shape((NB, width), BF16)
     new_re, new_im = call(finish_kernel, (half, half), total, q0, g0)

time: 243 us -> 250 us (1.029)
  starting transfers between devices: 79.3 us -> 95 us
  waiting for transfers between devices: 70 us -> 63.9 us
    ppermute x1, starting transfers between devices: 5.25 us -> 21.8 us  [body(): lax.ppermute(near, 'kstr', [(0, 1), (1, 0), (end - 1, end), (end, end - 1)])]
    all_to_all x3, waiting for transfers between devices: 25.3 us -> 19.3 us  [exchange(): return lax.all_to_all(value, axis, 0, 0, tiled=True)]
    ppermute x1, starting transfers between devices: 13.5 us -> 9.82 us  [branch(): return lambda block: lax.ppermute(block, ('kstr', 'pw'), closing_pairs(by))]
    all_to_all x3, starting transfers between devices: 23.6 us -> 26.6 us  [exchange(): return lax.all_to_all(value, axis, 0, 0, tiled=True)]
  transfers between devices with their start and end apart: 14 -> 14, of which waited for: 8 -> 7; matrix products, arithmetic and copies ran while one was open for 1% -> 1% of each run, Pallas kernels for 3% -> 3%
where the time goes in v13:
time: 250 us; the launch traced here: 249 us
  starting transfers between devices  95 us (38%)
  waiting for transfers between devices  63.9 us (26%)
  blocking collectives  61.5 us (25%)
  Pallas kernels  19 us (8%)
  local copies, waits for them, and re-layouts  6.63 us (3%)
    all_to_all x4, blocking collectives, exchange(): return lax.all_to_all(value, axis, 0, 0, tiled=True)  61.5 us
    ppermute x7, starting transfers between devices, shifted(): return lax.ppermute(value, 'kstr', [(i, (i + by) % NK) for i in range(NK)])  26.7 us
    all_to_all x3, starting transfers between devices, exchange(): return lax.all_to_all(value, axis, 0, 0, tiled=True)  26.6 us
    ppermute x1, starting transfers between devices, body(): lax.ppermute(near, 'kstr', [(0, 1), (1, 0), (end - 1, end), (end, end - 1)])  21.8 us
    all_to_all x3, waiting for transfers between devices, exchange(): return lax.all_to_all(value, axis, 0, 0, tiled=True)  19.3 us
    pallas_call x12, Pallas kernels, call(): pl.pallas_call(kernel, out_shape=outs, in_specs=specs, out_specs=tuple((p...  19 us
    ppermute x1, waiting for transfers between devices, branch(): return lambda block: lax.ppermute(block, ('kstr', 'pw'), closing_pairs(by))  15.1 us
    ppermute x7, waiting for transfers between devices, shifted(): return lax.ppermute(value, 'kstr', [(i, (i + by) % NK) for i in range(NK)])  15 us
  transfers between devices with their start and end apart: 14, of which 7 were waited for; matrix products, arithmetic and copies ran while one was open for 1% of the time, Pallas kernels for 3%

profile of v13, /device:TPU:1, one launch (start us, length us, event | category | flops | bytes accessed | tf_op | source)
XLA Modules:
  0.0 248.9 jit_solution(1771838906845257853)
XLA Ops:
  0.6 1.1 pad_maximum_fusion.state_ref.p0
  1.7 8.8 %collective-permute-start.32 = (bf16[512,512]{1,0:T(8,128)(2,1)S(1)}, bf16[512,512]{1,0:T(8,128)(2,1)S(1)}, u32[]{:S(2)}, u32[]{:S(2)}) collective-permute-start(bf16[512,512]{1,0:T(8,128)(2,1)S(1)} %pad_maximum_fusion.state_ref.p0), channel_id=1, source_target_pairs={{0,31},{32,63},{448,449},{480,481},{1,0},{33,32},{449,450},{481,48... | collective-permute-start | bytes 1572872 | tf_op jit(solution)/shard_map/ppermute | solution.py:299
  10.5 1.9 collective-permute-start.35
  12.4 1.3 collective-permute-start.34
  13.7 7.4 %collective-permute-start.33 = (bf16[512,512]{1,0:T(8,128)(2,1)S(1)}, bf16[512,512]{1,0:T(8,128)(2,1)S(1)}, u32[]{:S(2)}, u32[]{:S(2)}) collective-permute-start(bf16[512,512]{1,0:T(8,128)(2,1)S(1)} %pad_maximum_fusion.state_ref.p0), channel_id=1, source_target_pairs={{0,480},{32,0},{64,32},{96,64},{128,96},{160,128},{192,160},{224,1... | collective-permute-start | bytes 1572872 | tf_op jit(solution)/shard_map/ppermute | solution.py:257
  21.1 1.2 slice.3
  23.1 0.1 pad_add_fusion.bounds
  23.1 0.1 add_convert_fusion.flags
  23.2 0.8 shard_map.50
  24.1 25.0 %conditional.1 = (bf16[512,512]{1,0:T(8,128)(2,1)}) conditional(s32[]{:T(128)} %clamp.3, bf16[512,512]{1,0:T(8,128)(2,1)S(1)} %shard_map.50, bf16[512,512]{1,0:T(8,128)(2,1)S(1)} %shard_map.50, bf16[512,512]{1,0:T(8,128)(2,1)S(1)} %shard_map.50, bf16[512,512]{1,0:T(8,128)(2,1)S(1)} %shard_map.50, ...), branch_computations={%region_0.1_spmd, %region_1.2_spmd, %region_2.3_spmd, %region_3.4_... | conditional | bytes 2097200 | solution.py:111
  24.1 9.8 %collective-permute-start.15 = (bf16[512,512]{1,0:T(8,128)(2,1)S(1)}, bf16[512,512]{1,0:T(8,128)(2,1)}, u32[]{:S(2)}, u32[]{:S(2)}) collective-permute-start(bf16[512,512]{1,0:T(8,128)(2,1)S(1)} %param.15), channel_id=1, source_target_pairs={{0,497},{480,15},{32,465},{448,47},{1,498},{481,16},{33,466},{449,... | collective-permute-start | bytes 1572872 | tf_op jit(solution)/shard_map/cond/branch_15_fun/ppermute | solution.py:109
  33.9 15.1 %collective-permute-done.15 = bf16[512,512]{1,0:T(8,128)(2,1)} collective-permute-done((bf16[512,512]{1,0:T(8,128)(2,1)S(1)}, bf16[512,512]{1,0:T(8,128)(2,1)}, u32[]{:S(2)}, u32[]{:S(2)}) %collective-permute-start.15) | collective-permute-done | bytes 524320 | tf_op jit(solution)/shard_map/cond/branch_15_fun/ppermute | solution.py:109
  49.0 0.8 copy-done.1
  49.8 2.5 shard_map.51
  52.3 11.0 %all-to-all-start = ((bf16[32,16,256]{2,1,0:T(8,128)(2,1)}), bf16[32,16,256]{2,1,0:T(8,128)(2,1)S(1)}, u32[]{:S(2)}, u32[]{:S(2)}) async-start(bf16[32,16,256]{2,1,0:T(8,128)(2,1)} %bitcast.10), calls=%async_computation | async-start | bytes 524288 | tf_op jit(solution)/shard_map/all_to_all | solution.py:261
  63.4 21.8 %collective-permute-start.36 = (bf16[512,512]{1,0:T(8,128)(2,1)}, bf16[512,512]{1,0:T(8,128)(2,1)S(1)}, u32[]{:S(2)}, u32[]{:S(2)}) collective-permute-start(bf16[512,512]{1,0:T(8,128)(2,1)} %get-tuple-element.127.closing_ref.closing), channel_id=1, source_target_pairs={{0,32},{32,0},{448,480},{480,448},{1,33},{33,1},{449,481},{481,449... | collective-permute-start | bytes 1572872 | tf_op jit(solution)/shard_map/ppermute | solution.py:309
  85.2 1.9 collective-permute-start.37
  87.1 0.8 shard_map.52
  87.8 10.1 %all-to-all-start.1 = ((bf16[32,16,256]{2,1,0:T(8,128)(2,1)}), bf16[32,16,256]{2,1,0:T(8,128)(2,1)S(1)}, u32[]{:S(2)}, u32[]{:S(2)}) async-start(bf16[32,16,256]{2,1,0:T(8,128)(2,1)} %get-tuple-element.101), calls=%async_computation.1 | async-start | bytes 524288 | tf_op jit(solution)/shard_map/all_to_all | solution.py:261
  97.9 14.5 %collective-permute-done.36.beyond.closing = bf16[512,512]{1,0:T(8,128)(2,1)S(1)} collective-permute-done((bf16[512,512]{1,0:T(8,128)(2,1)}, bf16[512,512]{1,0:T(8,128)(2,1)S(1)}, u32[]{:S(2)}, u32[]{:S(2)}) %collective-permute-start.36) | collective-permute-done | bytes 524320 | tf_op jit(solution)/shard_map/ppermute | solution.py:309
  112.4 0.8 copy-done.9
  113.2 8.6 %all-to-all-done.1 = bf16[32,16,256]{2,1,0:T(8,128)(2,1)S(1)} async-done(((bf16[32,16,256]{2,1,0:T(8,128)(2,1)}), bf16[32,16,256]{2,1,0:T(8,128)(2,1)S(1)}, u32[]{:S(2)}, u32[]{:S(2)}) %all-to-all-start.1) | async-done | bytes 262176 | tf_op jit(solution)/shard_map/all_to_all | solution.py:261
  121.8 3.3 %shard_map.53.y0 = bf16[256,512]{1,0:T(8,128)(2,1)S(1)} custom-call(bf16[512,256]{1,0:T(8,128)(2,1)S(1)} %bitcast.15), custom_call_target="tpu_custom_call" | custom-call | bytes 524288 | tf_op jit(solution)/shard_map/pallas_call | solution.py:29
  125.1 9.1 %collective-permute-start.39 = (bf16[256,512]{1,0:T(8,128)(2,1)S(1)}, bf16[256,512]{1,0:T(8,128)(2,1)S(1)}, u32[]{:S(2)}, u32[]{:S(2)}) collective-permute-start(bf16[256,512]{1,0:T(8,128)(2,1)S(1)} %shard_map.53.y0), channel_id=1, source_target_pairs={{0,480},{32,0},{64,32},{96,64},{128,96},{160,128},{192,160},{224,1... | collective-permute-start | bytes 786440 | tf_op jit(solution)/shard_map/ppermute | solution.py:257
  134.2 1.9 collective-permute-start.38
  136.2 4.2 %collective-permute-done.39.y1 = bf16[256,512]{1,0:T(8,128)(2,1)S(1)} collective-permute-done((bf16[256,512]{1,0:T(8,128)(2,1)S(1)}, bf16[256,512]{1,0:T(8,128)(2,1)S(1)}, u32[]{:S(2)}, u32[]{:S(2)}) %collective-permute-start.39) | collective-permute-done | bytes 262176 | tf_op jit(solution)/shard_map/ppermute | solution.py:257
  140.4 5.9 %collective-permute-done.38.y_1 = bf16[256,512]{1,0:T(8,128)(2,1)S(1)} collective-permute-done((bf16[256,512]{1,0:T(8,128)(2,1)S(1)}, bf16[256,512]{1,0:T(8,128)(2,1)S(1)}, u32[]{:S(2)}, u32[]{:S(2)}) %collective-permute-start.38) | collective-permute-done | bytes 262176 | tf_op jit(solution)/shard_map/ppermute | solution.py:257
  146.3 1.0 copy-done.4
  147.3 3.9 %shard_map.54 = (f32[512,512]{1,0:T(8,128)S(1)}, bf16[512,512]{1,0:T(8,128)(2,1)S(1)}, bf16[512,512]{1,0:T(8,128)(2,1)S(1)}, bf16[32,80,128]{2,1,0:T(8,128)(2,1)S(1)}) custom-call(s32[4]{0:T(128)S(1)} %add_convert_fusion.flags, bf16[256,512]{1,0:T(8,128)(2,1)S(1)} %collective-permute-done.38.y_1, bf16[256,512]{1,0:T(8,128)(2,1)S(1)} %shard_map.53.y0, ...), custom_call_target="tpu_custom_call" | custom-call | bytes 6684688 | tf_op jit(solution)/shard_map/pallas_call | solution.py:29
  151.3 23.4 %all_to_all.46.parts_ref = bf16[32,80,128]{2,1,0:T(8,128)(2,1)S(1)} all-to-all(bf16[32,80,128]{2,1,0:T(8,128)(2,1)S(1)} %get-tuple-element.110), channel_id=1, replica_groups=mesh['kstr'=16,'pw'=32] {'pw'}, dimensions={0} | all-to-all | bytes 1310720 | tf_op jit(solution)/shard_map/all_to_all | solution.py:261
  174.7 0.1 shard_map.55
  174.8 13.7 %all_to_all.47.total_ref.total = f32[16,1,128]{2,1,0:T(1,128)S(1)} all-to-all(f32[16,1,128]{2,1,0:T(1,128)S(1)} %get-tuple-element.111), channel_id=1, replica_groups=mesh['kstr'=16,'pw'=32] {'kstr'}, dimensions={0} | all-to-all | bytes 16384 | tf_op jit(solution)/shard_map/all_to_all | solution.py:261
  188.5 0.1 shard_map.56
  188.7 0.0 copy-start
  188.7 0.7 copy-done
  189.4 5.5 %all-to-all-start.4 = ((bf16[32,16,256]{2,1,0:T(8,128)(2,1)}), bf16[32,16,256]{2,1,0:T(8,128)(2,1)S(1)}, u32[]{:S(2)}, u32[]{:S(2)}) async-start(bf16[32,16,256]{2,1,0:T(8,128)(2,1)} %copy-done), calls=%async_computation.4 | async-start | bytes 524288 | tf_op jit(solution)/shard_map/all_to_all | solution.py:261
  194.9 2.4 collective-permute-start.41
  197.2 10.7 %all-to-all-done.4 = bf16[32,16,256]{2,1,0:T(8,128)(2,1)S(1)} async-done(((bf16[32,16,256]{2,1,0:T(8,128)(2,1)}), bf16[32,16,256]{2,1,0:T(8,128)(2,1)S(1)}, u32[]{:S(2)}, u32[]{:S(2)}) %all-to-all-start.4) | async-done | bytes 262176 | tf_op jit(solution)/shard_map/all_to_all | solution.py:261
  207.9 3.3 %shard_map.57.y0 = bf16[256,512]{1,0:T(8,128)(2,1)S(1)} custom-call(bf16[512,256]{1,0:T(8,128)(2,1)S(1)} %bitcast.16), custom_call_target="tpu_custom_call" | custom-call | bytes 524288 | tf_op jit(solution)/shard_map/pallas_call | solution.py:29
  211.2 2.1 collective-permute-start.40
  213.3 1.0 copy-done.6
  214.3 1.0 copy-done.8
  215.4 2.4 shard_map.58
  217.7 4.9 %collective-permute-done.40.y_1 = bf16[256,512]{1,0:T(8,128)(2,1)S(1)} collective-permute-done((bf16[256,512]{1,0:T(8,128)(2,1)S(1)}, bf16[256,512]{1,0:T(8,128)(2,1)S(1)}, u32[]{:S(2)}, u32[]{:S(2)}) %collective-permute-start.40) | collective-permute-done | bytes 262176 | tf_op jit(solution)/shard_map/ppermute | solution.py:257
  222.7 0.8 shard_map.59
  223.4 14.5 %all_to_all.48.parts_ref = f32[32,1,128]{2,1,0:T(1,128)S(1)} all-to-all(f32[32,1,128]{2,1,0:T(1,128)S(1)} %get-tuple-element.122), channel_id=1, replica_groups=mesh['kstr'=16,'pw'=32] {'pw'}, dimensions={0} | all-to-all | bytes 32768 | tf_op jit(solution)/shard_map/all_to_all | solution.py:261
  238.0 9.9 %all_to_all.49.total_ref = f32[16,1,128]{2,1,0:T(1,128)S(1)} all-to-all(f32[16,1,128]{2,1,0:T(1,128)S(1)} %shard_map.60), channel_id=1, replica_groups=mesh['kstr'=16,'pw'=32] {'kstr'}, dimensions={0} | all-to-all | bytes 16384 | tf_op jit(solution)/shard_map/all_to_all | solution.py:261
  247.9 1.1 shard_map.61
  (23 shorter events, 0.1 us)
Async XLA Ops:
  1.7 21.5 %collective-permute-start.32 = (bf16[512,512]{1,0:T(8,128)(2,1)S(1)}, bf16[512,512]{1,0:T(8,128)(2,1)S(1)}, u32[]{:S(2)}, u32[]{:S(2)}) collective-permute-start(bf16[512,512]{1,0:T(8,128)(2,1)S(1)} %pad_maximum_fusion.state_ref.p0), channel_id=1, source_target_pairs={{0,31},{32,63},{448,449},{480,481},{1,0},{33,32},{449,450},{481,48... | collective-permute-start | bytes 1572872 | tf_op jit(solution)/shard_map/ppermute | solution.py:299
  10.5 38.5 %collective-permute-start.35 = (bf16[512,512]{1,0:T(8,128)(2,1)S(1)}, bf16[512,512]{1,0:T(8,128)(2,1)S(1)}, u32[]{:S(2)}, u32[]{:S(2)}) collective-permute-start(bf16[512,512]{1,0:T(8,128)(2,1)S(1)} %pad_maximum_fusion.state_ref.p0), channel_id=1, source_target_pairs={{0,64},{32,96},{64,128},{96,160},{128,192},{160,224},{192,256},{22... | collective-permute-start | bytes 1572872 | tf_op jit(solution)/shard_map/ppermute | solution.py:257
  12.4 37.4 %collective-permute-start.34 = (bf16[512,512]{1,0:T(8,128)(2,1)S(1)}, bf16[512,512]{1,0:T(8,128)(2,1)S(1)}, u32[]{:S(2)}, u32[]{:S(2)}) collective-permute-start(bf16[512,512]{1,0:T(8,128)(2,1)S(1)} %pad_maximum_fusion.state_ref.p0), channel_id=1, source_target_pairs={{64,0},{96,32},{128,64},{160,96},{192,128},{224,160},{256,192},{28... | collective-permute-start | bytes 1572872 | tf_op jit(solution)/shard_map/ppermute | solution.py:301
  13.7 36.1 %collective-permute-start.33 = (bf16[512,512]{1,0:T(8,128)(2,1)S(1)}, bf16[512,512]{1,0:T(8,128)(2,1)S(1)}, u32[]{:S(2)}, u32[]{:S(2)}) collective-permute-start(bf16[512,512]{1,0:T(8,128)(2,1)S(1)} %pad_maximum_fusion.state_ref.p0), channel_id=1, source_target_pairs={{0,480},{32,0},{64,32},{96,64},{128,96},{160,128},{192,160},{224,1... | collective-permute-start | bytes 1572872 | tf_op jit(solution)/shard_map/ppermute | solution.py:257
  24.1 24.9 %collective-permute-start.15 = (bf16[512,512]{1,0:T(8,128)(2,1)S(1)}, bf16[512,512]{1,0:T(8,128)(2,1)}, u32[]{:S(2)}, u32[]{:S(2)}) collective-permute-start(bf16[512,512]{1,0:T(8,128)(2,1)S(1)} %param.15), channel_id=1, source_target_pairs={{0,497},{480,15},{32,465},{448,47},{1,498},{481,16},{33,466},{449,... | collective-permute-start | bytes 1572872 | tf_op jit(solution)/shard_map/cond/branch_15_fun/ppermute | solution.py:109
  49.0 0.8 copy-start.1
  49.8 2.5 copy-start.3
  52.3 34.8 %all-to-all-start = ((bf16[32,16,256]{2,1,0:T(8,128)(2,1)}), bf16[32,16,256]{2,1,0:T(8,128)(2,1)S(1)}, u32[]{:S(2)}, u32[]{:S(2)}) async-start(bf16[32,16,256]{2,1,0:T(8,128)(2,1)} %bitcast.10), calls=%async_computation | async-start | bytes 524288 | tf_op jit(solution)/shard_map/all_to_all | solution.py:261
  63.4 49.0 %collective-permute-start.36 = (bf16[512,512]{1,0:T(8,128)(2,1)}, bf16[512,512]{1,0:T(8,128)(2,1)S(1)}, u32[]{:S(2)}, u32[]{:S(2)}) collective-permute-start(bf16[512,512]{1,0:T(8,128)(2,1)} %get-tuple-element.127.closing_ref.closing), channel_id=1, source_target_pairs={{0,32},{32,0},{448,480},{480,448},{1,33},{33,1},{449,481},{481,449... | collective-permute-start | bytes 1572872 | tf_op jit(solution)/shard_map/ppermute | solution.py:309
  85.2 27.2 %collective-permute-start.37 = (bf16[512,512]{1,0:T(8,128)(2,1)S(1)}, bf16[512,512]{1,0:T(8,128)(2,1)S(1)}, u32[]{:S(2)}, u32[]{:S(2)}) collective-permute-start(bf16[512,512]{1,0:T(8,128)(2,1)S(1)} %pad_maximum_fusion.state_ref.p0), channel_id=1, source_target_pairs={{0,32},{32,64},{64,96},{96,128},{128,160},{160,192},{192,224},{224... | collective-permute-start | bytes 1572872 | tf_op jit(solution)/shard_map/ppermute | solution.py:257
  87.8 34.0 %all-to-all-start.1 = ((bf16[32,16,256]{2,1,0:T(8,128)(2,1)}), bf16[32,16,256]{2,1,0:T(8,128)(2,1)S(1)}, u32[]{:S(2)}, u32[]{:S(2)}) async-start(bf16[32,16,256]{2,1,0:T(8,128)(2,1)} %get-tuple-element.101), calls=%async_computation.1 | async-start | bytes 524288 | tf_op jit(solution)/shard_map/all_to_all | solution.py:261
  112.4 0.8 copy-start.9
  121.8 24.5 %copy-start.10 = (bf16[512,512]{1,0:T(8,128)(2,1)S(1)}, bf16[512,512]{1,0:T(8,128)(2,1)}, u32[]{:S(2)}) copy-start(bf16[512,512]{1,0:T(8,128)(2,1)} %copy-done.9) | copy-start | bytes 1572868
  125.1 15.3 %collective-permute-start.39 = (bf16[256,512]{1,0:T(8,128)(2,1)S(1)}, bf16[256,512]{1,0:T(8,128)(2,1)S(1)}, u32[]{:S(2)}, u32[]{:S(2)}) collective-permute-start(bf16[256,512]{1,0:T(8,128)(2,1)S(1)} %shard_map.53.y0), channel_id=1, source_target_pairs={{0,480},{32,0},{64,32},{96,64},{128,96},{160,128},{192,160},{224,1... | collective-permute-start | bytes 786440 | tf_op jit(solution)/shard_map/ppermute | solution.py:257
  134.2 12.0 %collective-permute-start.38 = (bf16[256,512]{1,0:T(8,128)(2,1)S(1)}, bf16[256,512]{1,0:T(8,128)(2,1)S(1)}, u32[]{:S(2)}, u32[]{:S(2)}) collective-permute-start(bf16[256,512]{1,0:T(8,128)(2,1)S(1)} %shard_map.53.y0), channel_id=1, source_target_pairs={{0,32},{32,64},{64,96},{96,128},{128,160},{160,192},{192,224},{224... | collective-permute-start | bytes 786440 | tf_op jit(solution)/shard_map/ppermute | solution.py:257
  146.3 1.0 copy-start.4
  151.3 23.4 %copy-start.5 = (bf16[512,512]{1,0:T(8,128)(2,1)}, bf16[512,512]{1,0:T(8,128)(2,1)S(1)}, u32[]{:S(2)}) copy-start(bf16[512,512]{1,0:T(8,128)(2,1)S(1)} %get-tuple-element.119.g1) | copy-start | bytes 1572868
  151.3 23.4 %copy-start.7 = (bf16[512,512]{1,0:T(8,128)(2,1)}, bf16[512,512]{1,0:T(8,128)(2,1)S(1)}, u32[]{:S(2)}) copy-start(bf16[512,512]{1,0:T(8,128)(2,1)S(1)} %get-tuple-element.117.p_1) | copy-start | bytes 1572868
  188.7 0.7 copy-start
  189.4 18.5 %all-to-all-start.4 = ((bf16[32,16,256]{2,1,0:T(8,128)(2,1)}), bf16[32,16,256]{2,1,0:T(8,128)(2,1)S(1)}, u32[]{:S(2)}, u32[]{:S(2)}) async-start(bf16[32,16,256]{2,1,0:T(8,128)(2,1)} %copy-done), calls=%async_computation.4 | async-start | bytes 524288 | tf_op jit(solution)/shard_map/all_to_all | solution.py:261
  194.9 18.4 %collective-permute-start.41 = (bf16[256,512]{1,0:T(8,128)(2,1)S(1)}, bf16[256,512]{1,0:T(8,128)(2,1)}, u32[]{:S(2)}, u32[]{:S(2)}) collective-permute-start(bf16[256,512]{1,0:T(8,128)(2,1)S(1)} %shard_map.53.y0), channel_id=1, source_target_pairs={{0,64},{32,96},{64,128},{96,160},{128,192},{160,224},{192,256},{22... | collective-permute-start | bytes 786440 | tf_op jit(solution)/shard_map/ppermute | solution.py:257
  207.9 5.4 %copy-start.2 = (bf16[512,512]{1,0:T(8,128)(2,1)S(1)}, bf16[512,512]{1,0:T(8,128)(2,1)}, u32[]{:S(2)}) copy-start(bf16[512,512]{1,0:T(8,128)(2,1)} %copy-done.1) | copy-start | bytes 1572868
  211.2 11.5 %collective-permute-start.40 = (bf16[256,512]{1,0:T(8,128)(2,1)S(1)}, bf16[256,512]{1,0:T(8,128)(2,1)S(1)}, u32[]{:S(2)}, u32[]{:S(2)}) collective-permute-start(bf16[256,512]{1,0:T(8,128)(2,1)S(1)} %shard_map.57.y0), channel_id=1, source_target_pairs={{0,32},{32,64},{64,96},{96,128},{128,160},{160,192},{192,224},{224... | collective-permute-start | bytes 786440 | tf_op jit(solution)/shard_map/ppermute | solution.py:257
  213.3 1.0 copy-start.6
  214.3 1.0 copy-start.8

commit v14 on v13

--- a/solution.py
+++ b/solution.py
@@ -98,9 +98,8 @@
         for row in (0, 1):
             pairs.append((place(row, j), place(NK - 1 - row, j - by)))
             pairs.append((place(NK - 1 - row, j), place(row, j + by)))
-    if by % 8 == 0:
-        for row in range(2, NK - 2):
-            pairs += [(place(row, j), place(row, j)) for j in range(PARTS)]
+    for row in range(2, NK - 2):
+        pairs += [(place(row, j), place(row, j)) for j in range(PARTS)]
     return pairs
 
 
@@ -298,7 +297,7 @@
 
     beside = lax.ppermute(state, ("kstr", "pw"), beside_pairs())
     p1, p_2 = shifted(state, -1), shifted(state, 2)
-    p2 = lax.ppermute(state, "kstr", [(i + 2, i) for i in range(NK - 2)])
+    p2 = shifted(state, -2)
     merged = call(merge_kernel, fields, bounds, state, beside, smem=1)
     near = close_string(merged, blocks)
     near, p1, p2, p_2 = lax.optimization_barrier((near, p1, p2, p_2))

time: 250 us -> 233 us (0.932)
  starting transfers between devices: 95 us -> 72.8 us
  waiting for transfers between devices: 63.9 us -> 70.9 us
    ppermute x1, starting transfers between devices: 21.8 us -> 1.92 us  [body(): lax.ppermute(near, 'kstr', [(0, 1), (1, 0), (end - 1, end), (end, end - 1)])]
    all_to_all x3, waiting for transfers between devices: 19.3 us -> 28.8 us  [exchange(): return lax.all_to_all(value, axis, 0, 0, tiled=True)]
    ppermute x1, starting transfers between devices: 9.82 us -> 6.62 us  [branch(): return lambda block: lax.ppermute(block, ('kstr', 'pw'), closing_pairs(by))]
    ppermute x1, waiting for transfers between devices: 14.5 us -> 11.7 us  [body(): lax.ppermute(near, 'kstr', [(0, 1), (1, 0), (end - 1, end), (end, end - 1)])]
    ppermute x7 -> x8, starting transfers between devices: 26.7 us -> 29 us  [shifted(): return lax.ppermute(value, 'kstr', [(i, (i + by) % NK) for i in range(NK)])]
    ppermute x7 -> x8, waiting for transfers between devices: 15 us -> 14.4 us  [shifted(): return lax.ppermute(value, 'kstr', [(i, (i + by) % NK) for i in range(NK)])]
  transfers between devices with their start and end apart: 14 -> 14, of which waited for: 7 -> 8; matrix products, arithmetic and copies ran while one was open for 1% -> 1% of each run, Pallas kernels for 3% -> 3%
where the time goes in v14:
time: 233 us
  starting transfers between devices  72.8 us (31%)
  waiting for transfers between devices  70.9 us (30%)
  blocking collectives  61.1 us (26%)
  Pallas kernels  19 us (8%)
  local copies, waits for them, and re-layouts  6.63 us (3%)
    all_to_all x4, blocking collectives, exchange(): return lax.all_to_all(value, axis, 0, 0, tiled=True)  61.1 us
    ppermute x8, starting transfers between devices, shifted(): return lax.ppermute(value, 'kstr', [(i, (i + by) % NK) for i in range(NK)])  29 us
    all_to_all x3, waiting for transfers between devices, exchange(): return lax.all_to_all(value, axis, 0, 0, tiled=True)  28.8 us
    all_to_all x3, starting transfers between devices, exchange(): return lax.all_to_all(value, axis, 0, 0, tiled=True)  26.4 us
    pallas_call x12, Pallas kernels, call(): pl.pallas_call(kernel, out_shape=outs, in_specs=specs, out_specs=tuple((p...  19 us
    ppermute x1, waiting for transfers between devices, branch(): return lambda block: lax.ppermute(block, ('kstr', 'pw'), closing_pairs(by))  15.9 us
    ppermute x8, waiting for transfers between devices, shifted(): return lax.ppermute(value, 'kstr', [(i, (i + by) % NK) for i in range(NK)])  14.4 us
    ppermute x1, waiting for transfers between devices, body(): lax.ppermute(near, 'kstr', [(0, 1), (1, 0), (end - 1, end), (end, end - 1)])  11.7 us
  transfers between devices with their start and end apart: 14, of which 8 were waited for; matrix products, arithmetic and copies ran while one was open for 1% of the time, Pallas kernels for 3%

profile of v14, /device:TPU:1, one launch (start us, length us, event | category | flops | bytes accessed | tf_op | source)
XLA Modules:
  0.0 233.3 jit_solution(880785927807846585)
XLA Ops:
  0.6 1.1 pad_maximum_fusion.state_ref.p0
  1.7 8.8 %collective-permute-start.32 = (bf16[512,512]{1,0:T(8,128)(2,1)S(1)}, bf16[512,512]{1,0:T(8,128)(2,1)S(1)}, u32[]{:S(2)}, u32[]{:S(2)}) collective-permute-start(bf16[512,512]{1,0:T(8,128)(2,1)S(1)} %pad_maximum_fusion.state_ref.p0), channel_id=1, source_target_pairs={{0,31},{32,63},{448,449},{480,481},{1,0},{33,32},{449,450},{481,48... | collective-permute-start | bytes 1572872 | tf_op jit(solution)/shard_map/ppermute | solution.py:298
  10.5 1.9 collective-permute-start.35
  12.4 4.6 %collective-permute-start.34 = (bf16[512,512]{1,0:T(8,128)(2,1)S(1)}, bf16[512,512]{1,0:T(8,128)(2,1)S(1)}, u32[]{:S(2)}, u32[]{:S(2)}) collective-permute-start(bf16[512,512]{1,0:T(8,128)(2,1)S(1)} %pad_maximum_fusion.state_ref.p0), channel_id=1, source_target_pairs={{0,448},{32,480},{64,0},{96,32},{128,64},{160,96},{192,128},{224,1... | collective-permute-start | bytes 1572872 | tf_op jit(solution)/shard_map/ppermute | solution.py:256
  17.0 4.1 %collective-permute-start.33 = (bf16[512,512]{1,0:T(8,128)(2,1)S(1)}, bf16[512,512]{1,0:T(8,128)(2,1)S(1)}, u32[]{:S(2)}, u32[]{:S(2)}) collective-permute-start(bf16[512,512]{1,0:T(8,128)(2,1)S(1)} %pad_maximum_fusion.state_ref.p0), channel_id=1, source_target_pairs={{0,480},{32,0},{64,32},{96,64},{128,96},{160,128},{192,160},{224,1... | collective-permute-start | bytes 1572872 | tf_op jit(solution)/shard_map/ppermute | solution.py:256
  21.1 1.2 slice.3
  23.0 0.1 pad_add_fusion.bounds
  23.1 0.1 add_convert_fusion.flags
  23.2 0.8 shard_map.50
  24.0 22.6 %conditional.1 = (bf16[512,512]{1,0:T(8,128)(2,1)}) conditional(s32[]{:T(128)} %clamp.3, bf16[512,512]{1,0:T(8,128)(2,1)S(1)} %shard_map.50, bf16[512,512]{1,0:T(8,128)(2,1)S(1)} %shard_map.50, bf16[512,512]{1,0:T(8,128)(2,1)S(1)} %shard_map.50, bf16[512,512]{1,0:T(8,128)(2,1)S(1)} %shard_map.50, ...), branch_computations={%region_0.1_spmd, %region_1.2_spmd, %region_2.3_spmd, %region_3.4_... | conditional | bytes 2097200 | solution.py:110
  24.1 6.6 %collective-permute-start.31 = (bf16[512,512]{1,0:T(8,128)(2,1)S(1)}, bf16[512,512]{1,0:T(8,128)(2,1)}, u32[]{:S(2)}, u32[]{:S(2)}) collective-permute-start(bf16[512,512]{1,0:T(8,128)(2,1)S(1)} %param.31), channel_id=1, source_target_pairs={{0,481},{480,31},{32,449},{448,63},{1,482},{481,0},{33,450},{449,3... | collective-permute-start | bytes 1572872 | tf_op jit(solution)/shard_map/cond/branch_31_fun/ppermute | solution.py:108
  30.7 15.9 %collective-permute-done.31 = bf16[512,512]{1,0:T(8,128)(2,1)} collective-permute-done((bf16[512,512]{1,0:T(8,128)(2,1)S(1)}, bf16[512,512]{1,0:T(8,128)(2,1)}, u32[]{:S(2)}, u32[]{:S(2)}) %collective-permute-start.31) | collective-permute-done | bytes 524320 | tf_op jit(solution)/shard_map/cond/branch_31_fun/ppermute | solution.py:108
  46.6 0.8 copy-done.1
  47.4 2.5 %shard_map.51 = (bf16[512,256]{1,0:T(8,128)(2,1)}, bf16[512,512]{1,0:T(8,128)(2,1)S(1)}) custom-call(s32[4]{0:T(128)S(1)} %add_convert_fusion.flags, bf16[512,512]{1,0:T(8,128)(2,1)S(1)} %pad_maximum_fusion.state_ref.p0, bf16[512,512]{1,0:T(8,128)(2,1)S(1)} %collective-permute-done.33.next_ref, bf16[512,512]{1,0:T(8,128)(2,1)} %get-tuple-element.127.closing_ref.closing), custom_call_target="tpu_custom_call" | custom-call | bytes 2359312 | tf_op jit(solution)/shard_map/pallas_call | solution.py:29
  49.9 16.8 %all-to-all-start = ((bf16[32,16,256]{2,1,0:T(8,128)(2,1)}), bf16[32,16,256]{2,1,0:T(8,128)(2,1)S(1)}, u32[]{:S(2)}, u32[]{:S(2)}) async-start(bf16[32,16,256]{2,1,0:T(8,128)(2,1)} %bitcast.10), calls=%async_computation | async-start | bytes 524288 | tf_op jit(solution)/shard_map/all_to_all | solution.py:260
  66.7 1.9 collective-permute-start.36
  68.6 3.4 %collective-permute-start.37 = (bf16[512,512]{1,0:T(8,128)(2,1)S(1)}, bf16[512,512]{1,0:T(8,128)(2,1)S(1)}, u32[]{:S(2)}, u32[]{:S(2)}) collective-permute-start(bf16[512,512]{1,0:T(8,128)(2,1)S(1)} %pad_maximum_fusion.state_ref.p0), channel_id=1, source_target_pairs={{0,32},{32,64},{64,96},{96,128},{128,160},{160,192},{192,224},{224... | collective-permute-start | bytes 1572872 | tf_op jit(solution)/shard_map/ppermute | solution.py:256
  72.0 7.2 %all-to-all-done.parts_ref = bf16[32,16,256]{2,1,0:T(8,128)(2,1)S(1)} async-done(((bf16[32,16,256]{2,1,0:T(8,128)(2,1)}), bf16[32,16,256]{2,1,0:T(8,128)(2,1)S(1)}, u32[]{:S(2)}, u32[]{:S(2)}) %all-to-all-start) | async-done | bytes 262176 | tf_op jit(solution)/shard_map/all_to_all | solution.py:260
  79.2 0.8 shard_map.52
  80.0 3.9 %all-to-all-start.1 = ((bf16[32,16,256]{2,1,0:T(8,128)(2,1)}), bf16[32,16,256]{2,1,0:T(8,128)(2,1)S(1)}, u32[]{:S(2)}, u32[]{:S(2)}) async-start(bf16[32,16,256]{2,1,0:T(8,128)(2,1)} %get-tuple-element.101), calls=%async_computation.1 | async-start | bytes 524288 | tf_op jit(solution)/shard_map/all_to_all | solution.py:260
  83.9 11.7 %collective-permute-done.36.beyond.closing = bf16[512,512]{1,0:T(8,128)(2,1)S(1)} collective-permute-done((bf16[512,512]{1,0:T(8,128)(2,1)}, bf16[512,512]{1,0:T(8,128)(2,1)S(1)}, u32[]{:S(2)}, u32[]{:S(2)}) %collective-permute-start.36) | collective-permute-done | bytes 524320 | tf_op jit(solution)/shard_map/ppermute | solution.py:308
  95.6 0.8 copy-done.9
  96.4 10.8 %all-to-all-done.1 = bf16[32,16,256]{2,1,0:T(8,128)(2,1)S(1)} async-done(((bf16[32,16,256]{2,1,0:T(8,128)(2,1)}), bf16[32,16,256]{2,1,0:T(8,128)(2,1)S(1)}, u32[]{:S(2)}, u32[]{:S(2)}) %all-to-all-start.1) | async-done | bytes 262176 | tf_op jit(solution)/shard_map/all_to_all | solution.py:260
  107.3 3.3 %shard_map.53.y0 = bf16[256,512]{1,0:T(8,128)(2,1)S(1)} custom-call(bf16[512,256]{1,0:T(8,128)(2,1)S(1)} %bitcast.15), custom_call_target="tpu_custom_call" | custom-call | bytes 524288 | tf_op jit(solution)/shard_map/pallas_call | solution.py:29
  110.6 8.7 %collective-permute-start.39 = (bf16[256,512]{1,0:T(8,128)(2,1)S(1)}, bf16[256,512]{1,0:T(8,128)(2,1)S(1)}, u32[]{:S(2)}, u32[]{:S(2)}) collective-permute-start(bf16[256,512]{1,0:T(8,128)(2,1)S(1)} %shard_map.53.y0), channel_id=1, source_target_pairs={{0,480},{32,0},{64,32},{96,64},{128,96},{160,128},{192,160},{224,1... | collective-permute-start | bytes 786440 | tf_op jit(solution)/shard_map/ppermute | solution.py:256
  119.3 1.9 collective-permute-start.38
  121.2 3.7 %collective-permute-done.39.y1 = bf16[256,512]{1,0:T(8,128)(2,1)S(1)} collective-permute-done((bf16[256,512]{1,0:T(8,128)(2,1)S(1)}, bf16[256,512]{1,0:T(8,128)(2,1)S(1)}, u32[]{:S(2)}, u32[]{:S(2)}) %collective-permute-start.39) | collective-permute-done | bytes 262176 | tf_op jit(solution)/shard_map/ppermute | solution.py:256
  124.8 5.9 %collective-permute-done.38.y_1 = bf16[256,512]{1,0:T(8,128)(2,1)S(1)} collective-permute-done((bf16[256,512]{1,0:T(8,128)(2,1)S(1)}, bf16[256,512]{1,0:T(8,128)(2,1)S(1)}, u32[]{:S(2)}, u32[]{:S(2)}) %collective-permute-start.38) | collective-permute-done | bytes 262176 | tf_op jit(solution)/shard_map/ppermute | solution.py:256
  130.7 1.0 copy-done.4
  131.7 3.9 %shard_map.54 = (f32[512,512]{1,0:T(8,128)S(1)}, bf16[512,512]{1,0:T(8,128)(2,1)S(1)}, bf16[512,512]{1,0:T(8,128)(2,1)S(1)}, bf16[32,80,128]{2,1,0:T(8,128)(2,1)S(1)}) custom-call(s32[4]{0:T(128)S(1)} %add_convert_fusion.flags, bf16[256,512]{1,0:T(8,128)(2,1)S(1)} %collective-permute-done.38.y_1, bf16[256,512]{1,0:T(8,128)(2,1)S(1)} %shard_map.53.y0, ...), custom_call_target="tpu_custom_call" | custom-call | bytes 6684688 | tf_op jit(solution)/shard_map/pallas_call | solution.py:29
  135.7 23.7 %all_to_all.46.parts_ref = bf16[32,80,128]{2,1,0:T(8,128)(2,1)S(1)} all-to-all(bf16[32,80,128]{2,1,0:T(8,128)(2,1)S(1)} %get-tuple-element.110), channel_id=1, replica_groups=mesh['kstr'=16,'pw'=32] {'pw'}, dimensions={0} | all-to-all | bytes 1310720 | tf_op jit(solution)/shard_map/all_to_all | solution.py:260
  159.4 0.1 shard_map.55
  159.5 13.0 %all_to_all.47.total_ref.total = f32[16,1,128]{2,1,0:T(1,128)S(1)} all-to-all(f32[16,1,128]{2,1,0:T(1,128)S(1)} %get-tuple-element.111), channel_id=1, replica_groups=mesh['kstr'=16,'pw'=32] {'kstr'}, dimensions={0} | all-to-all | bytes 16384 | tf_op jit(solution)/shard_map/all_to_all | solution.py:260
  172.5 0.1 shard_map.56
  172.7 0.7 copy-done
  173.4 5.7 %all-to-all-start.4 = ((bf16[32,16,256]{2,1,0:T(8,128)(2,1)}), bf16[32,16,256]{2,1,0:T(8,128)(2,1)S(1)}, u32[]{:S(2)}, u32[]{:S(2)}) async-start(bf16[32,16,256]{2,1,0:T(8,128)(2,1)} %copy-done), calls=%async_computation.4 | async-start | bytes 524288 | tf_op jit(solution)/shard_map/all_to_all | solution.py:260
  179.1 2.4 %collective-permute-start.41 = (bf16[256,512]{1,0:T(8,128)(2,1)S(1)}, bf16[256,512]{1,0:T(8,128)(2,1)}, u32[]{:S(2)}, u32[]{:S(2)}) collective-permute-start(bf16[256,512]{1,0:T(8,128)(2,1)S(1)} %shard_map.53.y0), channel_id=1, source_target_pairs={{0,64},{32,96},{64,128},{96,160},{128,192},{160,224},{192,256},{22... | collective-permute-start | bytes 786440 | tf_op jit(solution)/shard_map/ppermute | solution.py:256
  181.5 10.8 %all-to-all-done.4 = bf16[32,16,256]{2,1,0:T(8,128)(2,1)S(1)} async-done(((bf16[32,16,256]{2,1,0:T(8,128)(2,1)}), bf16[32,16,256]{2,1,0:T(8,128)(2,1)S(1)}, u32[]{:S(2)}, u32[]{:S(2)}) %all-to-all-start.4) | async-done | bytes 262176 | tf_op jit(solution)/shard_map/all_to_all | solution.py:260
  192.3 3.3 %shard_map.57.y0 = bf16[256,512]{1,0:T(8,128)(2,1)S(1)} custom-call(bf16[512,256]{1,0:T(8,128)(2,1)S(1)} %bitcast.16), custom_call_target="tpu_custom_call" | custom-call | bytes 524288 | tf_op jit(solution)/shard_map/pallas_call | solution.py:29
  195.6 2.1 collective-permute-start.40
  197.7 1.0 copy-done.6
  198.7 1.0 copy-done.8
  199.7 2.4 %shard_map.58 = (bf16[512,512]{1,0:T(8,128)(2,1)S(1)}, bf16[512,512]{1,0:T(8,128)(2,1)S(1)}, bf16[512,512]{1,0:T(8,128)(2,1)S(1)}) custom-call(s32[4]{0:T(128)S(1)} %add_convert_fusion.flags, f32[16,1,128]{2,1,0:T(1,128)S(1)} %all_to_all.47.total_ref.total, bf16[256,512]{1,0:T(8,128)(2,1)} %collective-permute-done.41.y_2, ...), custom_call_target="tpu_custom_call" | custom-call | bytes 6299664 | tf_op jit(solution)/shard_map/pallas_call | solution.py:29
  202.1 4.9 %collective-permute-done.40.y_1 = bf16[256,512]{1,0:T(8,128)(2,1)S(1)} collective-permute-done((bf16[256,512]{1,0:T(8,128)(2,1)S(1)}, bf16[256,512]{1,0:T(8,128)(2,1)S(1)}, u32[]{:S(2)}, u32[]{:S(2)}) %collective-permute-start.40) | collective-permute-done | bytes 262176 | tf_op jit(solution)/shard_map/ppermute | solution.py:256
  207.0 0.8 shard_map.59
  207.8 14.5 %all_to_all.48.parts_ref = f32[32,1,128]{2,1,0:T(1,128)S(1)} all-to-all(f32[32,1,128]{2,1,0:T(1,128)S(1)} %get-tuple-element.122), channel_id=1, replica_groups=mesh['kstr'=16,'pw'=32] {'pw'}, dimensions={0} | all-to-all | bytes 32768 | tf_op jit(solution)/shard_map/all_to_all | solution.py:260
  222.3 9.9 %all_to_all.49.total_ref = f32[16,1,128]{2,1,0:T(1,128)S(1)} all-to-all(f32[16,1,128]{2,1,0:T(1,128)S(1)} %shard_map.60), channel_id=1, replica_groups=mesh['kstr'=16,'pw'=32] {'kstr'}, dimensions={0} | all-to-all | bytes 16384 | tf_op jit(solution)/shard_map/all_to_all | solution.py:260
  232.2 1.1 shard_map.61
  (23 shorter events, 0.1 us)
Async XLA Ops:
  1.7 21.5 %collective-permute-start.32 = (bf16[512,512]{1,0:T(8,128)(2,1)S(1)}, bf16[512,512]{1,0:T(8,128)(2,1)S(1)}, u32[]{:S(2)}, u32[]{:S(2)}) collective-permute-start(bf16[512,512]{1,0:T(8,128)(2,1)S(1)} %pad_maximum_fusion.state_ref.p0), channel_id=1, source_target_pairs={{0,31},{32,63},{448,449},{480,481},{1,0},{33,32},{449,450},{481,48... | collective-permute-start | bytes 1572872 | tf_op jit(solution)/shard_map/ppermute | solution.py:298
  10.5 36.1 %collective-permute-start.35 = (bf16[512,512]{1,0:T(8,128)(2,1)S(1)}, bf16[512,512]{1,0:T(8,128)(2,1)S(1)}, u32[]{:S(2)}, u32[]{:S(2)}) collective-permute-start(bf16[512,512]{1,0:T(8,128)(2,1)S(1)} %pad_maximum_fusion.state_ref.p0), channel_id=1, source_target_pairs={{0,64},{32,96},{64,128},{96,160},{128,192},{160,224},{192,256},{22... | collective-permute-start | bytes 1572872 | tf_op jit(solution)/shard_map/ppermute | solution.py:256
  12.4 35.0 %collective-permute-start.34 = (bf16[512,512]{1,0:T(8,128)(2,1)S(1)}, bf16[512,512]{1,0:T(8,128)(2,1)S(1)}, u32[]{:S(2)}, u32[]{:S(2)}) collective-permute-start(bf16[512,512]{1,0:T(8,128)(2,1)S(1)} %pad_maximum_fusion.state_ref.p0), channel_id=1, source_target_pairs={{0,448},{32,480},{64,0},{96,32},{128,64},{160,96},{192,128},{224,1... | collective-permute-start | bytes 1572872 | tf_op jit(solution)/shard_map/ppermute | solution.py:256
  17.0 30.4 %collective-permute-start.33 = (bf16[512,512]{1,0:T(8,128)(2,1)S(1)}, bf16[512,512]{1,0:T(8,128)(2,1)S(1)}, u32[]{:S(2)}, u32[]{:S(2)}) collective-permute-start(bf16[512,512]{1,0:T(8,128)(2,1)S(1)} %pad_maximum_fusion.state_ref.p0), channel_id=1, source_target_pairs={{0,480},{32,0},{64,32},{96,64},{128,96},{160,128},{192,160},{224,1... | collective-permute-start | bytes 1572872 | tf_op jit(solution)/shard_map/ppermute | solution.py:256
  24.1 22.6 %collective-permute-start.31 = (bf16[512,512]{1,0:T(8,128)(2,1)S(1)}, bf16[512,512]{1,0:T(8,128)(2,1)}, u32[]{:S(2)}, u32[]{:S(2)}) collective-permute-start(bf16[512,512]{1,0:T(8,128)(2,1)S(1)} %param.31), channel_id=1, source_target_pairs={{0,481},{480,31},{32,449},{448,63},{1,482},{481,0},{33,450},{449,3... | collective-permute-start | bytes 1572872 | tf_op jit(solution)/shard_map/cond/branch_31_fun/ppermute | solution.py:108
  46.6 0.8 copy-start.1
  47.4 2.5 %copy-start.3 = (bf16[512,512]{1,0:T(8,128)(2,1)}, bf16[512,512]{1,0:T(8,128)(2,1)S(1)}, u32[]{:S(2)}) copy-start(bf16[512,512]{1,0:T(8,128)(2,1)S(1)} %collective-permute-done.34.p2) | copy-start | bytes 1572868
  49.9 29.3 %all-to-all-start = ((bf16[32,16,256]{2,1,0:T(8,128)(2,1)}), bf16[32,16,256]{2,1,0:T(8,128)(2,1)S(1)}, u32[]{:S(2)}, u32[]{:S(2)}) async-start(bf16[32,16,256]{2,1,0:T(8,128)(2,1)} %bitcast.10), calls=%async_computation | async-start | bytes 524288 | tf_op jit(solution)/shard_map/all_to_all | solution.py:260
  66.7 28.9 %collective-permute-start.36 = (bf16[512,512]{1,0:T(8,128)(2,1)}, bf16[512,512]{1,0:T(8,128)(2,1)S(1)}, u32[]{:S(2)}, u32[]{:S(2)}) collective-permute-start(bf16[512,512]{1,0:T(8,128)(2,1)} %get-tuple-element.127.closing_ref.closing), channel_id=1, source_target_pairs={{0,32},{32,0},{448,480},{480,448},{1,33},{33,1},{449,481},{481,449... | collective-permute-start | bytes 1572872 | tf_op jit(solution)/shard_map/ppermute | solution.py:308
  68.6 27.0 %collective-permute-start.37 = (bf16[512,512]{1,0:T(8,128)(2,1)S(1)}, bf16[512,512]{1,0:T(8,128)(2,1)S(1)}, u32[]{:S(2)}, u32[]{:S(2)}) collective-permute-start(bf16[512,512]{1,0:T(8,128)(2,1)S(1)} %pad_maximum_fusion.state_ref.p0), channel_id=1, source_target_pairs={{0,32},{32,64},{64,96},{96,128},{128,160},{160,192},{192,224},{224... | collective-permute-start | bytes 1572872 | tf_op jit(solution)/shard_map/ppermute | solution.py:256
  80.0 27.3 %all-to-all-start.1 = ((bf16[32,16,256]{2,1,0:T(8,128)(2,1)}), bf16[32,16,256]{2,1,0:T(8,128)(2,1)S(1)}, u32[]{:S(2)}, u32[]{:S(2)}) async-start(bf16[32,16,256]{2,1,0:T(8,128)(2,1)} %get-tuple-element.101), calls=%async_computation.1 | async-start | bytes 524288 | tf_op jit(solution)/shard_map/all_to_all | solution.py:260
  95.6 0.8 copy-start.9
  107.3 23.4 %copy-start.10 = (bf16[512,512]{1,0:T(8,128)(2,1)S(1)}, bf16[512,512]{1,0:T(8,128)(2,1)}, u32[]{:S(2)}) copy-start(bf16[512,512]{1,0:T(8,128)(2,1)} %copy-done.9) | copy-start | bytes 1572868
  110.6 14.3 %collective-permute-start.39 = (bf16[256,512]{1,0:T(8,128)(2,1)S(1)}, bf16[256,512]{1,0:T(8,128)(2,1)S(1)}, u32[]{:S(2)}, u32[]{:S(2)}) collective-permute-start(bf16[256,512]{1,0:T(8,128)(2,1)S(1)} %shard_map.53.y0), channel_id=1, source_target_pairs={{0,480},{32,0},{64,32},{96,64},{128,96},{160,128},{192,160},{224,1... | collective-permute-start | bytes 786440 | tf_op jit(solution)/shard_map/ppermute | solution.py:256
  119.3 11.4 %collective-permute-start.38 = (bf16[256,512]{1,0:T(8,128)(2,1)S(1)}, bf16[256,512]{1,0:T(8,128)(2,1)S(1)}, u32[]{:S(2)}, u32[]{:S(2)}) collective-permute-start(bf16[256,512]{1,0:T(8,128)(2,1)S(1)} %shard_map.53.y0), channel_id=1, source_target_pairs={{0,32},{32,64},{64,96},{96,128},{128,160},{160,192},{192,224},{224... | collective-permute-start | bytes 786440 | tf_op jit(solution)/shard_map/ppermute | solution.py:256
  130.7 1.0 copy-start.4
  135.7 23.7 %copy-start.5 = (bf16[512,512]{1,0:T(8,128)(2,1)}, bf16[512,512]{1,0:T(8,128)(2,1)S(1)}, u32[]{:S(2)}) copy-start(bf16[512,512]{1,0:T(8,128)(2,1)S(1)} %get-tuple-element.119.g1) | copy-start | bytes 1572868
  135.7 23.7 %copy-start.7 = (bf16[512,512]{1,0:T(8,128)(2,1)}, bf16[512,512]{1,0:T(8,128)(2,1)S(1)}, u32[]{:S(2)}) copy-start(bf16[512,512]{1,0:T(8,128)(2,1)S(1)} %get-tuple-element.117.p_1) | copy-start | bytes 1572868
  172.7 0.7 copy-start
  173.4 18.9 %all-to-all-start.4 = ((bf16[32,16,256]{2,1,0:T(8,128)(2,1)}), bf16[32,16,256]{2,1,0:T(8,128)(2,1)S(1)}, u32[]{:S(2)}, u32[]{:S(2)}) async-start(bf16[32,16,256]{2,1,0:T(8,128)(2,1)} %copy-done), calls=%async_computation.4 | async-start | bytes 524288 | tf_op jit(solution)/shard_map/all_to_all | solution.py:260
  179.1 18.5 %collective-permute-start.41 = (bf16[256,512]{1,0:T(8,128)(2,1)S(1)}, bf16[256,512]{1,0:T(8,128)(2,1)}, u32[]{:S(2)}, u32[]{:S(2)}) collective-permute-start(bf16[256,512]{1,0:T(8,128)(2,1)S(1)} %shard_map.53.y0), channel_id=1, source_target_pairs={{0,64},{32,96},{64,128},{96,160},{128,192},{160,224},{192,256},{22... | collective-permute-start | bytes 786440 | tf_op jit(solution)/shard_map/ppermute | solution.py:256
  192.3 5.4 %copy-start.2 = (bf16[512,512]{1,0:T(8,128)(2,1)S(1)}, bf16[512,512]{1,0:T(8,128)(2,1)}, u32[]{:S(2)}) copy-start(bf16[512,512]{1,0:T(8,128)(2,1)} %copy-done.1) | copy-start | bytes 1572868
  195.6 11.5 %collective-permute-start.40 = (bf16[256,512]{1,0:T(8,128)(2,1)S(1)}, bf16[256,512]{1,0:T(8,128)(2,1)S(1)}, u32[]{:S(2)}, u32[]{:S(2)}) collective-permute-start(bf16[256,512]{1,0:T(8,128)(2,1)S(1)} %shard_map.57.y0), channel_id=1, source_target_pairs={{0,32},{32,64},{64,96},{96,128},{128,160},{160,192},{192,224},{224... | collective-permute-start | bytes 786440 | tf_op jit(solution)/shard_map/ppermute | solution.py:256
  197.7 1.0 copy-start.6
  198.7 1.0 copy-start.8
